TPU v7x, 128 devices: a whole 4x4x4 slice. The times are simulated.
128 devices in a mesh: section: 2 (over core), dp: 64 (over y, z, x).
Axes of the slice: x: 4, y: 4, z: 4, core: 2. Of those that a mesh axis runs over, the one named last changes fastest.
Arguments:
- layer_input: bfloat16 [2, 8192, 1024], P(None, 'dp'), may hold values from -6 to 6
- out_grad: bfloat16 [2, 8192, 1024], P(None, 'dp'), may hold values from -6 to 6
- in_weight: bfloat16 [2, 1024, 3352], P('section', 'dp'), may hold values from -0.1875 to 0.1875
- query_weight: bfloat16 [2, 1024, 512], P('section', 'dp'), may hold values from -0.1875 to 0.1875
- key_weight: bfloat16 [2, 1024, 128], P('section', 'dp'), may hold values from -0.1875 to 0.1875
- value_weight: bfloat16 [2, 1024, 128], P('section', 'dp'), may hold values from -0.1875 to 0.1875
- out_weight: bfloat16 [2, 1536, 1024], P('section', 'dp'), may hold values from -0.15625 to 0.15625
- heads_weight: bfloat16 [2, 512, 1024], P('section', 'dp'), may hold values from -1 to 1
- gate_weight: bfloat16 [2, 1024, 2048], P('section', 'dp'), may hold values from -0.1875 to 0.1875
- up_weight: bfloat16 [2, 1024, 2048], P('section', 'dp'), may hold values from -0.1875 to 0.1875
- down_weight: bfloat16 [2, 2048, 1024], P('section', 'dp'), may hold values from -0.1875 to 0.1875
- input_gain: float32 [2, 1024], P('section'), may hold values from 0.25 to 1.75
- conv_kernel: float32 [2, 4, 1792], P('section'), may hold values from -3 to 3
- conv_bias: float32 [2, 1792], P('section'), may hold values from -0.5 to 0.5
- step_bias: float32 [2, 24], P('section'), may hold values from -4 to -0.5
- decay_log: float32 [2, 24], P('section'), may hold values from -2 to 1
- skip_gain: float32 [2, 24], P('section'), may hold values from 0.5 to 2
- mixer_gain: float32 [2, 1536], P('section'), may hold values from 0.25 to 1.75
- feed_gain: float32 [2, 1024], P('section'), may hold values from 0.25 to 1.75
Outputs:
- layer_outputs: bfloat16 [2, 2, 8192, 1024], P('section', None, 'dp')
- input_grads: float32 [2, 2, 8192, 1024], P('section', None, 'dp')
- in_weight_grad: float32 [2, 1024, 3352], P('section', 'dp')
- query_weight_grad: float32 [2, 1024, 512], P('section', 'dp')
- key_weight_grad: float32 [2, 1024, 128], P('section', 'dp')
- value_weight_grad: float32 [2, 1024, 128], P('section', 'dp')
- out_weight_grad: float32 [2, 1536, 1024], P('section', 'dp')
- heads_weight_grad: float32 [2, 512, 1024], P('section', 'dp')
- gate_weight_grad: float32 [2, 1024, 2048], P('section', 'dp')
- up_weight_grad: float32 [2, 1024, 2048], P('section', 'dp')
- down_weight_grad: float32 [2, 2048, 1024], P('section', 'dp')
- input_gain_grad: float32 [2, 1024], P('section')
- conv_kernel_grad: float32 [2, 4, 1792], P('section')
- conv_bias_grad: float32 [2, 1792], P('section')
- step_bias_grad: float32 [2, 24], P('section')
- decay_log_grad: float32 [2, 24], P('section')
- skip_gain_grad: float32 [2, 24], P('section')
- mixer_gain_grad: float32 [2, 1536], P('section')
- feed_gain_grad: float32 [2, 1024], P('section')
All inputs are finite; a program needn't handle non-finite values.
Results may differ from a plain program's by a relative error of at most 0.025.
Values may be sent and summed in bfloat16 or wider, within the bound.
No kernel may reach another device: no remote copies, remote signals or barrier semaphores. Data moves between devices by JAX's collectives and lax.ppermute only.
A program may use at most 256 MiB of HBM per device.

v0:
```python
import jax
import jax.numpy as jnp
from jax import lax
from jax.sharding import Mesh
from jax.sharding import PartitionSpec as P

QH = 8
KVH = 2
HD = 64
LEN = 128
DP = ("dp_0", "dp_1", "dp_2")


def side_by_side(arrays, axis, dim, along):
    widths = [a.shape[along] for a in arrays]
    both = jnp.concatenate(arrays, axis=along)
    whole = lax.all_gather(both, axis, axis=dim, tiled=True)
    return tuple(jnp.split(whole, [sum(widths[:k]) for k in range(1, len(widths))], axis=along))


def shifted(shard, axis, by):
    length = lax.axis_size(axis)
    pairs = [(i, i + by) for i in range(length) if 0 <= i + by < length]
    return lax.ppermute(shard, axis, pairs)


def in_one_piece(arrays, axis, dim, along):
    ends, at = ([], 0)
    for a in arrays[:-1]:
        at += a.shape[along]
        ends.append(at)
    both = jnp.concatenate(arrays, axis=along)
    return tuple(
        jnp.split(lax.psum_scatter(both, axis, scatter_dimension=dim, tiled=True), ends, axis=along)
    )


def one_axis_at_a_time(shard, axes):
    for axis in axes:
        shard = lax.psum(shard, axis)
    return shard


def matmul(left, right):
    return jnp.dot(left, right, preferred_element_type=jnp.float32)


def transposed(left, right):
    return lax.dot_general(
        left, right, (((0,), (0,)), ((), ())), preferred_element_type=jnp.float32
    )


def backward_product(grad, weight):
    return lax.dot_general(
        grad, weight, (((1,), (1,)), ((), ())), preferred_element_type=jnp.float32
    )


def rms_scale(value, gain):
    return value * lax.rsqrt(jnp.mean(value * value, axis=-1, keepdims=True) + 1e-05) * gain


def rotate(value, cosine, sine, sign):
    half = value.shape[-1] // 2
    turned = jnp.concatenate([-value[..., half:], value[..., :half]], axis=-1)
    return value * cosine + sign * turned * sine


def tables(length, width):
    position = jnp.arange(length).astype(jnp.float32)
    inverse = 10000.0 ** (-(jnp.arange(width // 2).astype(jnp.float32) * 2.0) / width)
    angle = position[:, None] * inverse[None, :]
    angle = jnp.concatenate([angle, angle], axis=-1)
    return (jnp.cos(angle)[:, None, :], jnp.sin(angle)[:, None, :])


def mamba_core(proj, conv_kernel, conv_bias, step_bias, decay_log, skip_gain, mixer_gain):
    seqs, length = (proj.shape[0], proj.shape[1])
    heads = step_bias.shape[0]
    inner = mixer_gain.shape[0]
    channels = conv_bias.shape[0]
    state = (channels - inner) // 2
    taps = conv_kernel.shape[0]
    gate_z = proj[..., :inner]
    mixed = proj[..., inner : inner + channels]
    step_raw = proj[..., inner + channels :]
    padded = jnp.pad(mixed, ((0, 0), (taps - 1, 0), (0, 0)))
    total = conv_bias + padded[:, 0:length] * conv_kernel[0]
    for tap in range(1, taps):
        total = total + padded[:, tap : tap + length] * conv_kernel[tap]
    active = jax.nn.silu(total)
    inputs = active[..., :inner].reshape(seqs, length, heads, inner // heads)
    state_in = active[..., inner : inner + state]
    state_out = active[..., inner + state :]
    step = jax.nn.softplus(step_raw + step_bias)
    rate = -step * jnp.exp(decay_log)
    cumul = jnp.cumsum(rate, axis=1)
    spread = cumul[:, :, None, :] - cumul[:, None, :, :]
    causal = (jnp.arange(length)[:, None] >= jnp.arange(length)[None, :])[None, :, :, None]
    decay = jnp.where(causal, jnp.exp(jnp.where(causal, spread, 0.0)), 0.0)
    intersection = jnp.einsum("sin,sjn->sij", state_out, state_in)
    mixing = intersection[..., None] * decay * step[:, None, :, :]
    output = jnp.einsum("sijh,sjhp->sihp", mixing, inputs)
    output = output + skip_gain[:, None] * inputs
    output = output.reshape(seqs, length, inner)
    return rms_scale(output * jax.nn.silu(gate_z), mixer_gain)


def masked_scores(queries, keys):
    seqs, length, heads, size = queries.shape
    groups = keys.shape[2]
    grouped = queries.reshape(seqs, length, groups, heads // groups, size)
    scores = jnp.einsum(
        "sigrd,sjgd->sgrij", grouped, keys, preferred_element_type=jnp.float32
    ) * size ** (-0.5)
    causal = jnp.arange(length)[:, None] >= jnp.arange(length)[None, :]
    return (grouped, jnp.where(causal, scores, -1e30))


def attend_forward(queries, keys, values):
    seqs, length, heads, size = queries.shape
    grouped, scores = masked_scores(queries, keys)
    top = jnp.max(scores, axis=-1, keepdims=True)
    expo = jnp.exp(scores - top)
    total = jnp.sum(expo, axis=-1, keepdims=True)
    probs = (expo / total).astype(jnp.bfloat16)
    mixed = jnp.einsum("sgrij,sjgd->sigrd", probs, values, preferred_element_type=jnp.float32)
    return (mixed.reshape(seqs, length, heads * size).astype(jnp.bfloat16), top + jnp.log(total))


def attend_backward(queries, keys, values, logsum, grad_out):
    seqs, length, heads, size = queries.shape
    groups = keys.shape[2]
    grouped, scores = masked_scores(queries, keys)
    probs = jnp.exp(scores - logsum)
    rounded = probs.astype(jnp.bfloat16)
    grad_grouped = grad_out.reshape(seqs, length, groups, heads // groups, size)
    grad_values = jnp.einsum(
        "sgrij,sigrd->sjgd", rounded, grad_grouped, preferred_element_type=jnp.float32
    )
    grad_probs = jnp.einsum(
        "sigrd,sjgd->sgrij", grad_grouped, values, preferred_element_type=jnp.float32
    )
    grad_scores = probs * (grad_probs - jnp.sum(probs * grad_probs, axis=-1, keepdims=True))
    grad_scores = grad_scores.astype(jnp.bfloat16)
    scale = size ** (-0.5)
    grad_queries = (
        jnp.einsum("sgrij,sjgd->sigrd", grad_scores, keys, preferred_element_type=jnp.float32)
        * scale
    )
    grad_keys = (
        jnp.einsum("sgrij,sigrd->sjgd", grad_scores, grouped, preferred_element_type=jnp.float32)
        * scale
    )
    return (grad_queries.reshape(seqs, length, heads, size), grad_keys, grad_values)


def silu_product(gate, upper):
    return jax.nn.silu(gate) * upper


def run_forward(start, mats, small):
    (
        in_weight,
        query_weight,
        key_weight,
        value_weight,
        out_weight,
        heads_weight,
        gate_weight,
        up_weight,
        down_weight,
    ) = mats
    input_gain, conv_kernel, conv_bias, step_bias, decay_log, skip_gain, mixer_gain, feed_gain = (
        small
    )
    rows = start.shape[0]
    seqs = rows // LEN
    cosine, sine = tables(LEN, HD)
    state = start.astype(jnp.float32)
    normed = rms_scale(state, input_gain).astype(jnp.bfloat16)
    proj = matmul(normed, in_weight)
    q_raw = matmul(normed, query_weight)
    k_raw = matmul(normed, key_weight)
    values = matmul(normed, value_weight).astype(jnp.bfloat16)
    mamba = (
        mamba_core(
            proj.reshape(seqs, LEN, -1),
            conv_kernel,
            conv_bias,
            step_bias,
            decay_log,
            skip_gain,
            mixer_gain,
        )
        .reshape(rows, -1)
        .astype(jnp.bfloat16)
    )
    queries = rotate(q_raw.reshape(seqs, LEN, QH, HD), cosine, sine, 1.0).astype(jnp.bfloat16)
    keys = rotate(k_raw.reshape(seqs, LEN, KVH, HD), cosine, sine, 1.0).astype(jnp.bfloat16)
    attended, logsum = attend_forward(queries, keys, values.reshape(seqs, LEN, KVH, HD))
    attended = attended.reshape(rows, QH * HD)
    middle = state + matmul(mamba, out_weight) + matmul(attended, heads_weight)
    ffin = rms_scale(middle, feed_gain).astype(jnp.bfloat16)
    gate = matmul(ffin, gate_weight)
    upper = matmul(ffin, up_weight)
    hidden = silu_product(gate, upper).astype(jnp.bfloat16)
    result = middle + matmul(hidden, down_weight)
    kept = (
        state,
        normed,
        proj,
        queries,
        keys,
        values,
        mamba,
        attended,
        logsum,
        middle,
        ffin,
        gate,
        upper,
        hidden,
    )
    return (result.astype(jnp.bfloat16), kept)


def run_backward(kept, mats, small, grad_top):
    (
        in_weight,
        query_weight,
        key_weight,
        value_weight,
        out_weight,
        heads_weight,
        gate_weight,
        up_weight,
        down_weight,
    ) = mats
    input_gain, conv_kernel, conv_bias, step_bias, decay_log, skip_gain, mixer_gain, feed_gain = (
        small
    )
    (
        state,
        normed,
        proj,
        queries,
        keys,
        values,
        mamba,
        attended,
        logsum,
        middle,
        ffin,
        gate,
        upper,
        hidden,
    ) = kept
    rows = state.shape[0]
    seqs = rows // LEN
    cosine, sine = tables(LEN, HD)
    grad_low = grad_top.astype(jnp.bfloat16)
    grad_hidden = backward_product(grad_low, down_weight)
    unused, swiglu_pull = jax.vjp(silu_product, gate, upper)
    grad_gate, grad_upper = swiglu_pull(grad_hidden)
    grad_gate = grad_gate.astype(jnp.bfloat16)
    grad_upper = grad_upper.astype(jnp.bfloat16)
    grad_ffin = backward_product(grad_gate, gate_weight) + backward_product(grad_upper, up_weight)
    unused, feed_pull = jax.vjp(rms_scale, middle, feed_gain)
    grad_part, feed_grad = feed_pull(grad_ffin)
    grad_middle = grad_top + grad_part
    grad_branch = grad_middle.astype(jnp.bfloat16)
    grad_mamba = backward_product(grad_branch, out_weight)
    grad_attended = backward_product(grad_branch, heads_weight).astype(jnp.bfloat16)
    grad_queries, grad_keys, grad_values = attend_backward(
        queries,
        keys,
        values.reshape(seqs, LEN, KVH, HD),
        logsum,
        grad_attended.reshape(seqs, LEN, QH, HD),
    )
    grad_query = rotate(grad_queries, cosine, sine, -1.0).reshape(rows, -1).astype(jnp.bfloat16)
    grad_key = rotate(grad_keys, cosine, sine, -1.0).reshape(rows, -1).astype(jnp.bfloat16)
    grad_value = grad_values.reshape(rows, -1).astype(jnp.bfloat16)
    unused, mamba_pull = jax.vjp(
        mamba_core,
        proj.reshape(seqs, LEN, -1),
        conv_kernel,
        conv_bias,
        step_bias,
        decay_log,
        skip_gain,
        mixer_gain,
    )
    grad_proj, kernel_grad, bias_grad, step_grad, decay_grad, skip_grad, mixer_grad = mamba_pull(
        grad_mamba.reshape(seqs, LEN, -1)
    )
    grad_proj = grad_proj.reshape(rows, -1).astype(jnp.bfloat16)
    grad_normed = backward_product(grad_proj, in_weight) + backward_product(
        grad_query, query_weight
    )
    grad_normed = (
        grad_normed
        + backward_product(grad_key, key_weight)
        + backward_product(grad_value, value_weight)
    )
    unused, input_pull = jax.vjp(rms_scale, state, input_gain)
    grad_state, input_grad = input_pull(grad_normed)
    lefts = (normed, mamba, attended, ffin, hidden)
    rights = (
        grad_proj,
        grad_query,
        grad_key,
        grad_value,
        grad_branch,
        grad_gate,
        grad_upper,
        grad_low,
    )
    small_grads = (
        input_grad,
        kernel_grad,
        bias_grad,
        step_grad,
        decay_grad,
        skip_grad,
        mixer_grad,
        feed_grad,
    )
    return (grad_middle + grad_state, (lefts, rights), small_grads)


def weight_grads(lefts, rights):
    normed, mamba, attended, ffin, hidden = lefts
    grad_proj, grad_query, grad_key, grad_value, grad_branch, grad_gate, grad_upper, grad_low = (
        rights
    )
    return (
        transposed(normed, grad_proj),
        transposed(normed, grad_query),
        transposed(normed, grad_key),
        transposed(normed, grad_value),
        transposed(mamba, grad_branch),
        transposed(attended, grad_branch),
        transposed(ffin, grad_gate),
        transposed(ffin, grad_upper),
        transposed(hidden, grad_low),
    )


def zero_like(array):
    return jnp.zeros(array.shape, array.dtype)


def skip_forward(start, mats, small):
    return jax.tree.map(zero_like, run_forward(start, mats, small))


def skip_backward(kept, mats, small, grad_top):
    return jax.tree.map(zero_like, run_backward(kept, mats, small, grad_top))


def on_device(
    layer_input,
    out_grad,
    in_weight,
    query_weight,
    key_weight,
    value_weight,
    out_weight,
    heads_weight,
    gate_weight,
    up_weight,
    down_weight,
    input_gain,
    conv_kernel,
    conv_bias,
    step_bias,
    decay_log,
    skip_gain,
    mixer_gain,
    feed_gain,
):
    gathered = (
        *side_by_side((in_weight, query_weight, key_weight, value_weight), DP, 1, 2),
        lax.all_gather(out_weight, DP, axis=1, tiled=True),
        lax.all_gather(heads_weight, DP, axis=1, tiled=True),
        *side_by_side((gate_weight, up_weight), DP, 1, 0),
        lax.all_gather(down_weight, DP, axis=1, tiled=True),
    )
    mats = tuple((piece[0] for piece in gathered))
    small = tuple(
        (
            piece[0]
            for piece in (
                input_gain,
                conv_kernel,
                conv_bias,
                step_bias,
                decay_log,
                skip_gain,
                mixer_gain,
                feed_gain,
            )
        )
    )
    micro = layer_input.shape[0]
    rows = layer_input.shape[1]
    width = layer_input.shape[2]
    first = lax.axis_index("section") == 0
    incoming = jnp.zeros((rows, width), jnp.bfloat16)
    results = []
    kept = []
    for tick in range(micro + 1):
        start = jnp.where(first, layer_input[min(tick, micro - 1)], incoming)
        active = jnp.where(first, tick < micro, tick >= 1)
        result, keep = lax.cond(active, run_forward, skip_forward, start, mats, small)
        results.append(result)
        kept.append(keep)
        if tick < micro:
            incoming = shifted(result, "section", 1)
    layer_outputs = jnp.stack(
        [jnp.where(first, results[index], results[index + 1]) for index in range(micro)]
    )[None]
    small_totals = tuple((jnp.zeros(piece.shape, jnp.float32) for piece in small))
    outgoing = jnp.zeros((rows, width), jnp.bfloat16)
    grads_in = []
    factor_list = []
    for tick in range(micro + 1):
        later = max(micro - 1 - tick, 0)
        grad_top = jnp.where(
            first, outgoing.astype(jnp.float32), out_grad[later].astype(jnp.float32)
        )
        active = jnp.where(first, tick >= 1, tick < micro)
        grad_start, factors, small_grads = lax.cond(
            active, run_backward, skip_backward, kept[micro - tick], mats, small, grad_top
        )
        factor_list.append(factors)
        small_totals = tuple((total + part for total, part in zip(small_totals, small_grads)))
        grads_in.append(grad_start)
        if tick < micro:
            outgoing = shifted(grad_start.astype(jnp.bfloat16), "section", -1)
    chosen = [
        jax.tree.map(
            lambda upper_item, lower_item: jnp.where(first, upper_item, lower_item),
            factor_list[index + 1],
            factor_list[index],
        )
        for index in range(micro)
    ]
    lefts = tuple(
        (jnp.concatenate([item[0][slot] for item in chosen], axis=0) for slot in range(5))
    )
    rights = tuple(
        (jnp.concatenate([item[1][slot] for item in chosen], axis=0) for slot in range(8))
    )
    mat_full = weight_grads(lefts, rights)
    mat_shards = (
        *in_one_piece(
            (mat_full[0][None], mat_full[1][None], mat_full[2][None], mat_full[3][None]), DP, 1, 2
        ),
        lax.psum_scatter(mat_full[4][None], DP, scatter_dimension=1, tiled=True),
        lax.psum_scatter(mat_full[5][None], DP, scatter_dimension=1, tiled=True),
        *in_one_piece((mat_full[6][None], mat_full[7][None]), DP, 1, 0),
        lax.psum_scatter(mat_full[8][None], DP, scatter_dimension=1, tiled=True),
    )
    summed = (
        one_axis_at_a_time(small_totals[0], DP),
        one_axis_at_a_time(small_totals[1], DP),
        one_axis_at_a_time(small_totals[2], DP),
        one_axis_at_a_time(small_totals[3], DP),
        one_axis_at_a_time(small_totals[4], DP),
        one_axis_at_a_time(small_totals[5], DP),
        one_axis_at_a_time(small_totals[6], DP),
        one_axis_at_a_time(small_totals[7], DP),
    )
    input_grads = jnp.stack(
        [
            jnp.where(first, grads_in[micro - index], grads_in[micro - 1 - index])
            for index in range(micro)
        ]
    )[None]
    return (
        layer_outputs,
        input_grads,
        mat_shards[0],
        mat_shards[1],
        mat_shards[2],
        mat_shards[3],
        mat_shards[4],
        mat_shards[5],
        mat_shards[6],
        mat_shards[7],
        mat_shards[8],
        summed[0][None],
        summed[1][None],
        summed[2][None],
        summed[3][None],
        summed[4][None],
        summed[5][None],
        summed[6][None],
        summed[7][None],
    )


def solution(mesh):
    torus = Mesh(
        mesh.devices.reshape(mesh.shape["section"], 4, 4, 4), ("section", "dp_0", "dp_1", "dp_2")
    )
    in_specs = (
        P(None, DP, None),
        P(None, DP, None),
        P("section", DP, None),
        P("section", DP, None),
        P("section", DP, None),
        P("section", DP, None),
        P("section", DP, None),
        P("section", DP, None),
        P("section", DP, None),
        P("section", DP, None),
        P("section", DP, None),
        P("section", None),
        P("section", None, None),
        P("section", None),
        P("section", None),
        P("section", None),
        P("section", None),
        P("section", None),
        P("section", None),
    )
    out_specs = (
        P("section", None, DP, None),
        P("section", None, DP, None),
        P("section", DP, None),
        P("section", DP, None),
        P("section", DP, None),
        P("section", DP, None),
        P("section", DP, None),
        P("section", DP, None),
        P("section", DP, None),
        P("section", DP, None),
        P("section", DP, None),
        P("section", None),
        P("section", None, None),
        P("section", None),
        P("section", None),
        P("section", None),
        P("section", None),
        P("section", None),
        P("section", None),
    )
    return jax.shard_map(
        on_device, mesh=torus, in_specs=in_specs, out_specs=out_specs, check_vma=False
    )
```

profile of v0, /device:TPU:0, one launch (start us, length us, event | category | flops | bytes accessed | tf_op | source)
XLA Modules:
  0.0 2363.4 jit_solution(2238103732358101359)
XLA Ops:
  14.9 78.3 %all-gather.12.cloned.1.call-done = bf16[2,1024,2048]{2,1,0:T(8,128)(2,1)} async-done(((bf16[2,16,2048]{2,1,0:T(8,128)(2,1)}), bf16[2,1024,2048]{2,1,0:T(8,128)(2,1)}) %all-gather.12.cloned.1.call-update) | async-done | bytes 8388624 | tf_op jit(solution)/shard_map/all_gather | solution.py:17
  93.2 6.2 slice_bitcast_fusion.23
  99.3 76.1 %all-gather.6.cloned.1.call-done = bf16[1,1024,4120]{2,1,0:T(8,128)(2,1)} async-done(((bf16[1,16,4120]{2,1,0:T(8,128)(2,1)}), bf16[1,1024,4120]{2,1,0:T(8,128)(2,1)}) %all-gather.6.cloned.1.call-update) | async-done | bytes 8437776 | tf_op jit(solution)/shard_map/all_gather | solution.py:17
  179.0 6.8 slice_bitcast_fusion.22
  185.8 56.1 %all-gather.10.cloned.1.call-done = bf16[1,512,1024]{2,1,0:T(8,128)(2,1)} async-done(((bf16[1,8,1024]{2,1,0:T(8,128)(2,1)}), bf16[1,512,1024]{2,1,0:T(8,128)(2,1)}) %all-gather.10.cloned.1.call-update) | async-done | bytes 1048592 | tf_op jit(solution)/shard_map/all_gather | solution.py:388
  241.9 67.2 %all-gather.8.cloned.1.call-done = bf16[1,1536,1024]{2,1,0:T(8,128)(2,1)} async-done(((bf16[1,24,1024]{2,1,0:T(8,128)(2,1)}), bf16[1,1536,1024]{2,1,0:T(8,128)(2,1)}) %all-gather.8.cloned.1.call-update) | async-done | bytes 3145744 | tf_op jit(solution)/shard_map/all_gather | solution.py:387
  309.1 69.4 %all-gather.14.cloned.1.call-done = bf16[1,2048,1024]{2,1,0:T(8,128)(2,1)} async-done(((bf16[1,32,1024]{2,1,0:T(8,128)(2,1)}), bf16[1,2048,1024]{2,1,0:T(8,128)(2,1)}) %all-gather.14.cloned.1.call-update) | async-done | bytes 4194320 | tf_op jit(solution)/shard_map/all_gather | solution.py:390
  378.6 34.7 %conditional.4 = (bf16[128,1024]{1,0:T(8,128)(2,1)}, f32[128,1024]{1,0:T(8,128)}, bf16[128,1024]{1,0:T(8,128)(2,1)}, f32[128,3352]{0,1:T(8,128)}, bf16[1,128,8,6...) conditional(s32[]{:T(128)} %convert_element_type.545, () %tuple.71, ...), branch_computations={%region_0.1_spmd, %region_1.8_spmd} | conditional | flops 3328781824 | bytes 162139616 | solution.py:418
  418.1 5.9 convolution_bitcast_fusion.11
  454.1 12.1 conditional.5
  466.2 18.9 conditional.6
  488.8 102.0 %collective-permute-done.2 = bf16[128,1024]{1,0:T(8,128)(2,1)S(1)} collective-permute-done((bf16[128,1024]{1,0:T(8,128)(2,1)S(1)}, bf16[128,1024]{1,0:T(8,128)(2,1)S(1)}, u32[]{:S(2)}, u32[]{:S(2)}) %collective-permute-start.2) | collective-permute-done | bytes 262176 | tf_op jit(solution)/shard_map/ppermute | solution.py:24
  652.2 96.4 %conditional.7 = (f32[128,1024]{1,0:T(8,128)}, bf16[128,1024]{1,0:T(8,128)(2,1)}, bf16[128,1024]{1,0:T(8,128)(2,1)}, bf16[128,2048]{1,0:T(8,128)(2,1)}, bf16[128...) conditional(s32[]{:T(128)} %convert_element_type.545, () %tuple.75, ...), branch_computations={%region_60.62_spmd, %region_61.0_spmd} | conditional | flops 3513079040 | bytes 223001840 | solution.py:436
  757.1 14.1 pad_maximum_fusion.6
  771.2 37.3 %copy.409 = f32[1,1024,4120]{2,0,1:T(1,128)} copy(f32[1,1024,4120]{1,2,0:T(8,128)} %pad_maximum_fusion.6) | data formatting | bytes 33751040 | tf_op jit(solution)/shard_map/concatenate | solution.py:32
  814.8 6.0 pad_maximum_fusion.7
  847.3 17.9 all-reduce.50
  865.2 17.1 all-reduce.49
  882.3 16.8 all-reduce.48
  901.2 123.1 %all-reduce.53.cloned.1.call-done = f32[1,1024,4120]{2,0,1:T(1,128)} async-done(((f32[1,1024,4120]{2,0,1:T(1,128)}), f32[1,1024,4120]{2,0,1:T(1,128)}) %all-reduce.53.cloned.1.call-update) | async-done | bytes 16875536
  1029.0 384.7 %reduce-scatter.9.cloned.1.call-done = f32[2,16,2048]{2,1,0:T(8,128)} async-done(((f32[2,1024,2048]{2,1,0:T(8,128)}), f32[2,16,2048]{2,1,0:T(8,128)}) %reduce-scatter.9.cloned.1.call-update) | async-done | bytes 262160 | tf_op jit(solution)/shard_map/reduce_scatter | solution.py:34
  1415.4 349.7 %reduce-scatter.7.cloned.1.call-done = f32[1,8,1024]{2,1,0:T(8,128)} async-done(((f32[1,512,1024]{2,1,0:T(8,128)}), f32[1,8,1024]{2,1,0:T(8,128)}) %reduce-scatter.7.cloned.1.call-update) | async-done | bytes 32784 | tf_op jit(solution)/shard_map/reduce_scatter | solution.py:464
  1765.1 223.9 %reduce-scatter.5.cloned.1.call-done = f32[1,24,1024]{2,1,0:T(8,128)} async-done(((f32[1,1536,1024]{2,1,0:T(8,128)}), f32[1,24,1024]{2,1,0:T(8,128)}) %reduce-scatter.5.cloned.1.call-update) | async-done | bytes 98320 | tf_op jit(solution)/shard_map/reduce_scatter | solution.py:463
  1989.0 367.1 %reduce-scatter.11.cloned.1.call-done = f32[1,32,1024]{2,1,0:T(8,128)} async-done(((f32[1,2048,1024]{2,1,0:T(8,128)}), f32[1,32,1024]{2,1,0:T(8,128)}) %reduce-scatter.11.cloned.1.call-update) | async-done | bytes 131088 | tf_op jit(solution)/shard_map/reduce_scatter | solution.py:466
  (770 shorter events, 313.5 us)
Async XLA Ops:
  7.2 86.0 %all-gather.12.cloned.1.call-start = ((), (), s32[]{:S(2)}) async-start(), calls=%async_computation.7 | async-start | bytes 8519680 | tf_op jit(solution)/shard_map/all_gather | solution.py:17
  8.8 166.6 %all-gather.6.cloned.1.call-start = ((), (), s32[]{:S(2)}) async-start(), calls=%async_computation.4 | async-start | bytes 8785920 | tf_op jit(solution)/shard_map/all_gather | solution.py:17
  10.5 231.4 %all-gather.10.cloned.1.call-start = ((), (), s32[]{:S(2)}) async-start(), calls=%async_computation.6 | async-start | bytes 1064960 | tf_op jit(solution)/shard_map/all_gather | solution.py:388
  11.3 297.9 %all-gather.8.cloned.1.call-start = ((), (), s32[]{:S(2)}) async-start(), calls=%async_computation.5 | async-start | bytes 3194880 | tf_op jit(solution)/shard_map/all_gather | solution.py:387
  11.9 366.7 %all-gather.14.cloned.1.call-start = ((), (), s32[]{:S(2)}) async-start(), calls=%async_computation.8 | async-start | bytes 4259840 | tf_op jit(solution)/shard_map/all_gather | solution.py:390
  12.4 1011.9 %all-reduce.53.cloned.1.call-start = ((), (), s32[]{:S(2)}) async-start(), calls=%async_computation.13 | async-start | bytes 34603008
  176.9 201.7 %copy-start.58 = (bf16[1024,128]{1,0:T(8,128)(2,1)}, bf16[1024,128]{1,0:T(8,128)(2,1)S(1)}, u32[]{:S(2)}) copy-start(bf16[1024,128]{1,0:T(8,128)(2,1)S(1)} %get-tuple-element.1399) | copy-start | bytes 786436
  176.9 201.7 %copy-start.62 = (bf16[1024,128]{1,0:T(8,128)(2,1)}, bf16[1024,128]{1,0:T(8,128)(2,1)S(1)}, u32[]{:S(2)}) copy-start(bf16[1024,128]{1,0:T(8,128)(2,1)S(1)} %get-tuple-element.1400) | copy-start | bytes 786436
  178.9 199.7 %copy-start.23 = (bf16[1024,512]{1,0:T(8,128)(2,1)}, bf16[1024,512]{1,0:T(8,128)(2,1)S(1)}, u32[]{:S(2)}) copy-start(bf16[1024,512]{1,0:T(8,128)(2,1)S(1)} %slice_bitcast_fusion.25) | copy-start | bytes 3145732
  178.9 199.6 %copy-start.107 = (bf16[2,128,1024]{2,1,0:T(8,128)(2,1)S(1)}, bf16[2,128,1024]{2,1,0:T(8,128)(2,1)}, u32[]{:S(2)}) copy-start(bf16[2,128,1024]{2,1,0:T(8,128)(2,1)} %param.28) | copy-start | bytes 1572868
  178.9 199.6 %copy-start.136 = (f32[1,4,1792]{2,1,0:T(4,128)S(1)}, f32[1,4,1792]{2,1,0:T(4,128)}, u32[]{:S(2)}) copy-start(f32[1,4,1792]{2,1,0:T(4,128)} %param.40) | copy-start | bytes 86020
  178.9 199.6 %copy-start.154 = (f32[1,1024]{1,0:T(1,128)S(1)}, f32[1,1024]{1,0:T(1,128)}, u32[]{:S(2)}) copy-start(f32[1,1024]{1,0:T(1,128)} %param.46) | copy-start | bytes 12292
  179.0 199.6 %copy-start.155 = (f32[1,1024]{1,0:T(1,128)S(1)}, f32[1,1024]{1,0:T(1,128)}, u32[]{:S(2)}) copy-start(f32[1,1024]{1,0:T(1,128)} %param.39) | copy-start | bytes 12292
  179.0 199.6 %copy-start.168 = (f32[1,1792]{1,0:T(1,128)S(1)}, f32[1,1792]{1,0:T(1,128)}, u32[]{:S(2)}) copy-start(f32[1,1792]{1,0:T(1,128)} %param.41) | copy-start | bytes 21508
  179.0 199.6 %copy-start.222 = (f32[1,24]{1,0:T(1,128)S(1)}, f32[1,24]{1,0:T(1,128)}, u32[]{:S(2)}) copy-start(f32[1,24]{1,0:T(1,128)} %param.42) | copy-start | bytes 292
  179.0 199.6 %copy-start.302 = (f32[1,24]{1,0:T(1,128)S(1)}, f32[1,24]{1,0:T(1,128)}, u32[]{:S(2)}) copy-start(f32[1,24]{1,0:T(1,128)} %param.43) | copy-start | bytes 292
  413.3 3.1 collective-permute-start
  450.7 3.5 collective-permute-start.1
  486.2 104.6 %collective-permute-start.2 = (bf16[128,1024]{1,0:T(8,128)(2,1)S(1)}, bf16[128,1024]{1,0:T(8,128)(2,1)S(1)}, u32[]{:S(2)}, u32[]{:S(2)}) collective-permute-start(bf16[128,1024]{1,0:T(8,128)(2,1)S(1)} %convert_element_type.564), channel_id=1, source_target_pairs={{64,0},{65,1},{66,2},{67,3},{68,4},{69,5},{70,6},{71,7},{72,8},{73... | collective-permute-start | bytes 786440 | tf_op jit(solution)/shard_map/ppermute | solution.py:24
  648.0 3.4 collective-permute-start.3
  808.6 605.1 %reduce-scatter.9.cloned.1.call-start = ((), (), s32[]{:S(2)}) async-start(), calls=%async_computation.11 | async-start | bytes 17039360 | tf_op jit(solution)/shard_map/reduce_scatter | solution.py:34
  820.9 944.2 %reduce-scatter.7.cloned.1.call-start = ((), (), s32[]{:S(2)}) async-start(), calls=%async_computation.10 | async-start | bytes 2129920 | tf_op jit(solution)/shard_map/reduce_scatter | solution.py:464
  824.7 1164.4 %reduce-scatter.5.cloned.1.call-start = ((), (), s32[]{:S(2)}) async-start(), calls=%async_computation.9 | async-start | bytes 6389760 | tf_op jit(solution)/shard_map/reduce_scatter | solution.py:463
  830.7 1525.4 %reduce-scatter.11.cloned.1.call-start = ((), (), s32[]{:S(2)}) async-start(), calls=%async_computation.12 | async-start | bytes 8519680 | tf_op jit(solution)/shard_map/reduce_scatter | solution.py:466
  (215 other events, 1113.5 us)
Sparse Core Ops, SparseCore 0:
  11.5 81.6 all-gather.11
  96.5 78.8 all-gather.5
  178.3 63.5 all-gather.9
  244.6 64.4 all-gather.7
  311.9 66.6 all-gather.13
  808.7 215.5 all-reduce.52
  1026.7 386.9 reduce-scatter.8
  1416.6 348.4 reduce-scatter.6
  1770.8 218.2 reduce-scatter.4
  1991.8 364.2 reduce-scatter.10
where the time goes:
time: 2370 us; the launch traced here: 2360 us
  waiting for transfers between devices  1900 us (80%)
  matrix products  135 us (6%)
  local copies, waits for them, and re-layouts  126 us (5%)
  other arithmetic  119 us (5%)
  blocking collectives  51.7 us (2%)
    reduce_scatter x1, waiting for transfers between devices, in_one_piece(): lax.psum_scatter(both, axis, scatter_dimension=dim, tiled=True)  385 us
    reduce_scatter x1, waiting for transfers between devices, on_device(): lax.psum_scatter(mat_full[8][None], DP, scatter_dimension=1, tiled=True)  367 us
    reduce_scatter x1, waiting for transfers between devices, on_device(): lax.psum_scatter(mat_full[5][None], DP, scatter_dimension=1, tiled=True)  350 us
    reduce_scatter x1, waiting for transfers between devices, on_device(): lax.psum_scatter(mat_full[4][None], DP, scatter_dimension=1, tiled=True)  224 us
    all_gather x2, waiting for transfers between devices, side_by_side(): whole = lax.all_gather(both, axis, axis=dim, tiled=True)  154 us
    unnamed x11, waiting for transfers between devices  125 us
    ppermute x4, waiting for transfers between devices, shifted(): return lax.ppermute(shard, axis, pairs)  103 us
    all_gather x1, waiting for transfers between devices, on_device(): lax.all_gather(down_weight, DP, axis=1, tiled=True)  69.4 us
  transfers between devices with their start and end apart: 14, of which 12 were waited for; matrix products, arithmetic and copies ran while one was open for 3% of the time, Pallas kernels for 0%

commit v1 on v0

v1 whole, which is shorter than its diff:
```python
import jax
import jax.numpy as jnp
from jax import lax
from jax.sharding import Mesh
from jax.sharding import PartitionSpec as P

QH = 8
KVH = 2
HD = 64
LEN = 128
DP = ("dp_0", "dp_1", "dp_2")


def matmul(left, right):
    return jnp.dot(left, right, preferred_element_type=jnp.float32)


def transposed(left, right):
    return lax.dot_general(
        left, right, (((0,), (0,)), ((), ())), preferred_element_type=jnp.float32
    )


def backward_product(grad, weight):
    return lax.dot_general(
        grad, weight, (((1,), (1,)), ((), ())), preferred_element_type=jnp.float32
    )


def rms_scale(value, gain):
    return value * lax.rsqrt(jnp.mean(value * value, axis=-1, keepdims=True) + 1e-05) * gain


def rotate(value, cosine, sine, sign):
    half = value.shape[-1] // 2
    turned = jnp.concatenate([-value[..., half:], value[..., :half]], axis=-1)
    return value * cosine + sign * turned * sine


def tables(length, width):
    position = jnp.arange(length).astype(jnp.float32)
    inverse = 10000.0 ** (-(jnp.arange(width // 2).astype(jnp.float32) * 2.0) / width)
    angle = position[:, None] * inverse[None, :]
    angle = jnp.concatenate([angle, angle], axis=-1)
    return (jnp.cos(angle)[:, None, :], jnp.sin(angle)[:, None, :])


def mamba_core(proj, conv_kernel, conv_bias, step_bias, decay_log, skip_gain, mixer_gain):
    seqs, length = (proj.shape[0], proj.shape[1])
    heads = step_bias.shape[0]
    inner = mixer_gain.shape[0]
    channels = conv_bias.shape[0]
    state = (channels - inner) // 2
    taps = conv_kernel.shape[0]
    gate_z = proj[..., :inner]
    mixed = proj[..., inner : inner + channels]
    step_raw = proj[..., inner + channels :]
    padded = jnp.pad(mixed, ((0, 0), (taps - 1, 0), (0, 0)))
    total = conv_bias + padded[:, 0:length] * conv_kernel[0]
    for tap in range(1, taps):
        total = total + padded[:, tap : tap + length] * conv_kernel[tap]
    active = jax.nn.silu(total)
    inputs = active[..., :inner].reshape(seqs, length, heads, inner // heads)
    state_in = active[..., inner : inner + state]
    state_out = active[..., inner + state :]
    step = jax.nn.softplus(step_raw + step_bias)
    rate = -step * jnp.exp(decay_log)
    cumul = jnp.cumsum(rate, axis=1)
    spread = cumul[:, :, None, :] - cumul[:, None, :, :]
    causal = (jnp.arange(length)[:, None] >= jnp.arange(length)[None, :])[None, :, :, None]
    decay = jnp.where(causal, jnp.exp(jnp.where(causal, spread, 0.0)), 0.0)
    intersection = jnp.einsum("sin,sjn->sij", state_out, state_in)
    mixing = intersection[..., None] * decay * step[:, None, :, :]
    output = jnp.einsum("sijh,sjhp->sihp", mixing, inputs)
    output = output + skip_gain[:, None] * inputs
    output = output.reshape(seqs, length, inner)
    return rms_scale(output * jax.nn.silu(gate_z), mixer_gain)


def masked_scores(queries, keys):
    seqs, length, heads, size = queries.shape
    groups = keys.shape[2]
    grouped = queries.reshape(seqs, length, groups, heads // groups, size)
    scores = jnp.einsum(
        "sigrd,sjgd->sgrij", grouped, keys, preferred_element_type=jnp.float32
    ) * size ** (-0.5)
    causal = jnp.arange(length)[:, None] >= jnp.arange(length)[None, :]
    return (grouped, jnp.where(causal, scores, -1e30))


def attend_forward(queries, keys, values):
    seqs, length, heads, size = queries.shape
    grouped, scores = masked_scores(queries, keys)
    top = jnp.max(scores, axis=-1, keepdims=True)
    expo = jnp.exp(scores - top)
    total = jnp.sum(expo, axis=-1, keepdims=True)
    probs = (expo / total).astype(jnp.bfloat16)
    mixed = jnp.einsum("sgrij,sjgd->sigrd", probs, values, preferred_element_type=jnp.float32)
    return (mixed.reshape(seqs, length, heads * size).astype(jnp.bfloat16), top + jnp.log(total))


def attend_backward(queries, keys, values, logsum, grad_out):
    seqs, length, heads, size = queries.shape
    groups = keys.shape[2]
    grouped, scores = masked_scores(queries, keys)
    probs = jnp.exp(scores - logsum)
    rounded = probs.astype(jnp.bfloat16)
    grad_grouped = grad_out.reshape(seqs, length, groups, heads // groups, size)
    grad_values = jnp.einsum(
        "sgrij,sigrd->sjgd", rounded, grad_grouped, preferred_element_type=jnp.float32
    )
    grad_probs = jnp.einsum(
        "sigrd,sjgd->sgrij", grad_grouped, values, preferred_element_type=jnp.float32
    )
    grad_scores = probs * (grad_probs - jnp.sum(probs * grad_probs, axis=-1, keepdims=True))
    grad_scores = grad_scores.astype(jnp.bfloat16)
    scale = size ** (-0.5)
    grad_queries = (
        jnp.einsum("sgrij,sjgd->sigrd", grad_scores, keys, preferred_element_type=jnp.float32)
        * scale
    )
    grad_keys = (
        jnp.einsum("sgrij,sigrd->sjgd", grad_scores, grouped, preferred_element_type=jnp.float32)
        * scale
    )
    return (grad_queries.reshape(seqs, length, heads, size), grad_keys, grad_values)


def silu_product(gate, upper):
    return jax.nn.silu(gate) * upper


CAT = 4224


def run_forward(start, mats, small):
    cat_weight, out_weight, heads_weight, gate_weight, up_weight, down_weight = mats
    input_gain, conv_kernel, conv_bias, step_bias, decay_log, skip_gain, mixer_gain, feed_gain = (
        small
    )
    rows = start.shape[0]
    seqs = rows // LEN
    cosine, sine = tables(LEN, HD)
    state = start.astype(jnp.float32)
    normed = rms_scale(state, input_gain).astype(jnp.bfloat16)
    proj = matmul(normed, cat_weight)
    values = proj[:, 640:768].astype(jnp.bfloat16)
    mamba = (
        mamba_core(
            proj[:, 768:4120].reshape(seqs, LEN, -1),
            conv_kernel,
            conv_bias,
            step_bias,
            decay_log,
            skip_gain,
            mixer_gain,
        )
        .reshape(rows, -1)
        .astype(jnp.bfloat16)
    )
    queries = rotate(proj[:, :512].reshape(seqs, LEN, QH, HD), cosine, sine, 1.0)
    keys = rotate(proj[:, 512:640].reshape(seqs, LEN, KVH, HD), cosine, sine, 1.0)
    queries = queries.astype(jnp.bfloat16)
    keys = keys.astype(jnp.bfloat16)
    attended, logsum = attend_forward(queries, keys, values.reshape(seqs, LEN, KVH, HD))
    attended = attended.reshape(rows, QH * HD)
    middle = state + matmul(mamba, out_weight) + matmul(attended, heads_weight)
    ffin = rms_scale(middle, feed_gain).astype(jnp.bfloat16)
    gate = matmul(ffin, gate_weight)
    upper = matmul(ffin, up_weight)
    hidden = silu_product(gate, upper).astype(jnp.bfloat16)
    result = middle + matmul(hidden, down_weight)
    kept = (state, normed, proj, queries, keys, values, mamba, attended, logsum, middle, ffin)
    return (result.astype(jnp.bfloat16), (*kept, gate, upper, hidden))


def backward_feed(kept, mats, small, grad_top):
    gate_weight, up_weight, down_weight = mats[3:]
    middle, ffin, gate, upper, hidden = kept[9:]
    feed_gain = small[7]
    grad_low = grad_top.astype(jnp.bfloat16)
    grad_hidden = backward_product(grad_low, down_weight)
    unused, swiglu_pull = jax.vjp(silu_product, gate, upper)
    grad_gate, grad_upper = swiglu_pull(grad_hidden)
    grad_gate = grad_gate.astype(jnp.bfloat16)
    grad_upper = grad_upper.astype(jnp.bfloat16)
    grad_ffin = backward_product(grad_gate, gate_weight) + backward_product(grad_upper, up_weight)
    unused, feed_pull = jax.vjp(rms_scale, middle, feed_gain)
    grad_part, feed_grad = feed_pull(grad_ffin)
    return (grad_top + grad_part, feed_grad, (hidden, ffin, grad_low, grad_gate, grad_upper))


def backward_mix(kept, mats, small, grad_middle):
    cat_weight, out_weight, heads_weight = mats[:3]
    input_gain, conv_kernel, conv_bias, step_bias, decay_log, skip_gain, mixer_gain, feed_gain = (
        small
    )
    state, normed, proj, queries, keys, values, mamba, attended, logsum = kept[:9]
    rows = state.shape[0]
    seqs = rows // LEN
    cosine, sine = tables(LEN, HD)
    grad_branch = grad_middle.astype(jnp.bfloat16)
    grad_mamba = backward_product(grad_branch, out_weight)
    grad_attended = backward_product(grad_branch, heads_weight).astype(jnp.bfloat16)
    grad_queries, grad_keys, grad_values = attend_backward(
        queries,
        keys,
        values.reshape(seqs, LEN, KVH, HD),
        logsum,
        grad_attended.reshape(seqs, LEN, QH, HD),
    )
    grad_query = rotate(grad_queries, cosine, sine, -1.0).reshape(rows, -1).astype(jnp.bfloat16)
    grad_key = rotate(grad_keys, cosine, sine, -1.0).reshape(rows, -1).astype(jnp.bfloat16)
    grad_value = grad_values.reshape(rows, -1).astype(jnp.bfloat16)
    unused, mamba_pull = jax.vjp(
        mamba_core,
        proj[:, 768:4120].reshape(seqs, LEN, -1),
        conv_kernel,
        conv_bias,
        step_bias,
        decay_log,
        skip_gain,
        mixer_gain,
    )
    grad_proj, kernel_grad, bias_grad, step_grad, decay_grad, skip_grad, mixer_grad = mamba_pull(
        grad_mamba.reshape(seqs, LEN, -1)
    )
    grad_proj = grad_proj.reshape(rows, -1).astype(jnp.bfloat16)
    pad = jnp.zeros((rows, CAT - 4120), jnp.bfloat16)
    grad_cat = jnp.concatenate([grad_query, grad_key, grad_value, grad_proj, pad], axis=1)
    grad_normed = backward_product(grad_cat, cat_weight)
    unused, input_pull = jax.vjp(rms_scale, state, input_gain)
    grad_state, input_grad = input_pull(grad_normed)
    small_grads = (
        input_grad,
        kernel_grad,
        bias_grad,
        step_grad,
        decay_grad,
        skip_grad,
        mixer_grad,
    )
    factors = (normed, mamba, attended, grad_branch, grad_cat)
    return (grad_middle + grad_state, small_grads, factors)


def around(axis, by):
    length = lax.axis_size(axis)
    return [(i, (i + by) % length) for i in range(length)]


def send(shard, axis, by):
    return lax.ppermute(shard, axis, around(axis, by))


def columns(left, place, piece):
    shape = left.shape
    parts = left.reshape(shape[0], 4, 4, 4, shape[1] // 64)
    return lax.dynamic_index_in_dim(parts, piece, 1 + place, keepdims=False)


def scatter_first(left, right, place):
    axis = DP[place]
    me = lax.axis_index(axis)
    pieces = [columns(left, place, lax.rem(me + by, 4)) for by in range(4)]
    low = [p[:, :2] for p in pieces]
    high = [p[:, 2:] for p in pieces]

    def product(part):
        flat = part.reshape(part.shape[0], -1)
        return transposed(flat, right)

    up_one = product(jnp.concatenate([low[2], high[1]], axis=1)).astype(jnp.bfloat16)
    down_one = product(jnp.concatenate([high[2], low[3]], axis=1)).astype(jnp.bfloat16)
    from_below = send(up_one, axis, 1)
    from_above = send(down_one, axis, -1)
    half = up_one.shape[0] // 2
    up_two = (product(low[1]) + from_below[:half].astype(jnp.float32)).astype(jnp.bfloat16)
    down_two = (product(high[3]) + from_above[:half].astype(jnp.float32)).astype(jnp.bfloat16)
    below_two = send(up_two, axis, 1)
    above_two = send(down_two, axis, -1)
    own_low = product(low[0]) + below_two.astype(jnp.float32) + from_above[half:].astype(jnp.float32)
    own_high = product(high[0]) + above_two.astype(jnp.float32) + from_below[half:].astype(jnp.float32)
    own = jnp.concatenate([own_low, own_high], axis=0).astype(jnp.bfloat16)
    return own.reshape(4, 4, left.shape[1] // 64, right.shape[1])


def scatter_next(array, axis, dim):
    me = lax.axis_index(axis)

    def piece(by):
        return lax.dynamic_index_in_dim(array, lax.rem(me + by, 4), dim, keepdims=False)

    one = send(piece(1), axis, 1)
    three = send(piece(3), axis, -1)
    two = send(piece(2), axis, 2)
    total = piece(0).astype(jnp.float32) + one.astype(jnp.float32)
    return total + three.astype(jnp.float32) + two.astype(jnp.float32)


def scattered(left, right, order):
    array = scatter_first(left, right, order[0])
    rest = [0, 1, 2]
    rest.remove(order[0])
    array = scatter_next(array, DP[order[1]], rest.index(order[1])).astype(jnp.bfloat16)
    return scatter_next(array, DP[order[2]], 0)


def summed_over(vector):
    for axis in DP:
        one = send(vector, axis, 1)
        two = send(vector, axis, 2)
        three = send(vector, axis, 3)
        me = lax.axis_index(axis)
        terms = jnp.stack([vector, one, two, three])
        total = lax.dynamic_index_in_dim(terms, me, 0, keepdims=False)
        for place in range(1, 4):
            total = total + lax.dynamic_index_in_dim(
                terms, lax.rem(me + 4 - place, 4), 0, keepdims=False
            )
        vector = total
    return vector


def on_device(
    layer_input,
    out_grad,
    in_weight,
    query_weight,
    key_weight,
    value_weight,
    out_weight,
    heads_weight,
    gate_weight,
    up_weight,
    down_weight,
    input_gain,
    conv_kernel,
    conv_bias,
    step_bias,
    decay_log,
    skip_gain,
    mixer_gain,
    feed_gain,
):
    micro, part, width = layer_input.shape
    rows = micro * part
    own = jnp.concatenate(
        [
            query_weight[0],
            key_weight[0],
            value_weight[0],
            in_weight[0],
            jnp.zeros((16, CAT - 4120), jnp.bfloat16),
            gate_weight[0],
            up_weight[0],
            down_weight[0].reshape(16, 2048),
            out_weight[0].reshape(16, 1536),
            heads_weight[0].reshape(16, 512),
        ],
        axis=1,
    )
    whole = lax.all_gather(own, DP, axis=0, tiled=True)
    mats = (
        whole[:, :CAT],
        whole[:, CAT + 6144 : CAT + 7680].reshape(1536, 1024),
        whole[:, CAT + 7680 :].reshape(512, 1024),
        whole[:, CAT : CAT + 2048],
        whole[:, CAT + 2048 : CAT + 4096],
        whole[:, CAT + 4096 : CAT + 6144].reshape(2048, 1024),
    )
    small = tuple(
        (
            piece[0]
            for piece in (
                input_gain,
                conv_kernel,
                conv_bias,
                step_bias,
                decay_log,
                skip_gain,
                mixer_gain,
                feed_gain,
            )
        )
    )
    first = lax.axis_index("section") == 0
    start = layer_input.reshape(rows, width)
    result_low, kept_low = run_forward(start, mats, small)
    handed = lax.ppermute(result_low, "section", [(0, 1)])
    result_high, kept_high = run_forward(handed, mats, small)
    layer_outputs = jnp.where(first, result_low, result_high).reshape(1, micro, part, width)

    def backward(kept, grad_top):
        grad_middle, feed_grad, feed_factors = backward_feed(kept, mats, small, grad_top)
        grad_start, small_grads, mix_factors = backward_mix(kept, mats, small, grad_middle)
        return (grad_start, (*small_grads, feed_grad), feed_factors, mix_factors)

    high = backward(kept_high, out_grad.reshape(rows, width).astype(jnp.float32))
    handed = lax.ppermute(high[0].astype(jnp.bfloat16), "section", [(1, 0)])
    input_grads, small_grads, feed_factors, mix_factors = lax.cond(
        first,
        lambda kept, grad, other: backward(kept, grad.astype(jnp.float32)),
        lambda kept, grad, other: other,
        kept_low,
        handed,
        high,
    )
    hidden, ffin, grad_low, grad_gate, grad_upper = feed_factors
    normed, mamba, attended, grad_branch, grad_cat = mix_factors
    down_grad = scattered(hidden, grad_low, (2, 0, 1))
    gate_grad = scattered(ffin, grad_gate, (0, 1, 2))
    up_grad = scattered(ffin, grad_upper, (1, 2, 0))
    cat_left = scattered(normed, grad_cat[:, :2048], (0, 1, 2))
    cat_right = scattered(normed, grad_cat[:, 2048:], (1, 2, 0))
    out_grad_own = scattered(mamba, grad_branch, (2, 0, 1))
    heads_grad = scattered(attended, grad_branch, (2, 0, 1))
    cat_grad = jnp.concatenate([cat_left, cat_right], axis=1)
    packed = jnp.concatenate([piece.reshape(-1) for piece in small_grads])
    packed = jnp.pad(packed, (0, -packed.shape[0] % 1024)).reshape(-1, 128)
    total = summed_over(packed).reshape(-1)
    summed, at = ([], 0)
    for piece in small_grads:
        summed.append(total[at : at + piece.size].reshape(1, *piece.shape))
        at += piece.size
    return (
        layer_outputs,
        input_grads.reshape(1, micro, part, width),
        cat_grad[None, :, 768:4120],
        cat_grad[None, :, :512],
        cat_grad[None, :, 512:640],
        cat_grad[None, :, 640:768],
        out_grad_own[None],
        heads_grad[None],
        gate_grad[None],
        up_grad[None],
        down_grad[None],
        *summed,
    )


def solution(mesh):
    torus = Mesh(
        mesh.devices.reshape(mesh.shape["section"], 4, 4, 4), ("section", "dp_0", "dp_1", "dp_2")
    )
    in_specs = (
        P(None, DP, None),
        P(None, DP, None),
        P("section", DP, None),
        P("section", DP, None),
        P("section", DP, None),
        P("section", DP, None),
        P("section", DP, None),
        P("section", DP, None),
        P("section", DP, None),
        P("section", DP, None),
        P("section", DP, None),
        P("section", None),
        P("section", None, None),
        P("section", None),
        P("section", None),
        P("section", None),
        P("section", None),
        P("section", None),
        P("section", None),
    )
    out_specs = (
        P("section", None, DP, None),
        P("section", None, DP, None),
        P("section", DP, None),
        P("section", DP, None),
        P("section", DP, None),
        P("section", DP, None),
        P("section", DP, None),
        P("section", DP, None),
        P("section", DP, None),
        P("section", DP, None),
        P("section", DP, None),
        P("section", None),
        P("section", None, None),
        P("section", None),
        P("section", None),
        P("section", None),
        P("section", None),
        P("section", None),
        P("section", None),
    )
    return jax.shard_map(
        on_device, mesh=torus, in_specs=in_specs, out_specs=out_specs, check_vma=False
    )
```

time: 2370 us -> 805 us (0.34)
  waiting for transfers between devices: 1900 us -> 210 us
  starting transfers between devices: 7.3 us -> 97.4 us
  blocking collectives: 51.7 us -> 0 us
  local copies, waits for them, and re-layouts: 126 us -> 173 us
  matrix products: 135 us -> 172 us
    reduce_scatter x4 -> x0, waiting for transfers between devices: 1330 us -> none  [the longest x1 385 us: in_one_piece(): lax.psum_scatter(both, axis, scatter_dimension=dim, tiled=True)]
    all_gather x5 -> x1, waiting for transfers between devices: 347 us -> 131 us  [on_device(): whole = lax.all_gather(own, DP, axis=0, tiled=True)]
    unnamed x11 -> x1, waiting for transfers between devices: 125 us -> 0.02 us
    ppermute x4 -> x81, starting transfers between devices: 6.61 us -> 97.3 us  [the longest x79 93.5 us: send(): return lax.ppermute(shard, axis, around(axis, by))]
    psum x3 -> x0, blocking collectives: 51.7 us -> none  [one_axis_at_a_time(): shard = lax.psum(shard, axis)]
    slice x0 -> x49, local copies, waits for them, and re-layouts: none -> 50.4 us  [the longest x22 11.7 us: scatter_first(): low = [p[:, :2] for p in pieces]]
    reshape x0 -> x19, local copies, waits for them, and re-layouts: none -> 31.4 us  [the longest x2 8.17 us: on_device(): whole[:, CAT + 6144:CAT + 7680].reshape(1536, 1024)]
    concatenate x2 -> x4, local copies, waits for them, and re-layouts: 39 us -> 9.46 us  [the longest x2 7.57 us: backward_mix(): jnp.concatenate([grad_query, grad_key, grad_value, grad_proj, pad], axis=1)]
  transfers between devices with their start and end apart: 14 -> 82, of which waited for: 12 -> 43; matrix products, arithmetic and copies ran while one was open for 3% -> 13% of each run, Pallas kernels for 0% -> 0%
where the time goes in v1:
time: 805 us; the launch traced here: 794 us
  waiting for transfers between devices  210 us (26%)
  local copies, waits for them, and re-layouts  173 us (21%)
  matrix products  172 us (21%)
  other arithmetic  123 us (15%)
  starting transfers between devices  97.4 us (12%)
  between operations  17.2 us (2%)
    all_gather x1, waiting for transfers between devices, on_device(): whole = lax.all_gather(own, DP, axis=0, tiled=True)  131 us
    ppermute x79, starting transfers between devices, send(): return lax.ppermute(shard, axis, around(axis, by))  93.5 us
    ppermute x79, waiting for transfers between devices, send(): return lax.ppermute(shard, axis, around(axis, by))  79.5 us
    dot_general x42, matrix products, transposed(): lax.dot_general(left, right, (((0,), (0,)), ((), ())), preferred_element_...  44.7 us
    dot_general x12, matrix products, matmul(): return jnp.dot(left, right, preferred_element_type=jnp.float32)  41 us
    dot_general x12, matrix products, backward_product(): lax.dot_general(grad, weight, (((1,), (1,)), ((), ())), preferred_element...  40 us
    dot_general x7, matrix products, mamba_core(): output = jnp.einsum('sijh,sjhp->sihp', mixing, inputs)  30 us
    mul x3, other arithmetic, mamba_core(): active = jax.nn.silu(total)  16.2 us
  transfers between devices with their start and end apart: 82, of which 43 were waited for; matrix products, arithmetic and copies ran while one was open for 13% of the time, Pallas kernels for 0%

profile of v1, /device:TPU:0, one launch (start us, length us, event | category | flops | bytes accessed | tf_op | source)
XLA Modules:
  0.0 794.0 jit_solution(17397822230670330960)
XLA Ops:
  18.3 130.8 %all-gather.2.cloned.1.call-done = bf16[1024,12416]{1,0:T(8,128)(2,1)} async-done(((bf16[16,12416]{1,0:T(8,128)(2,1)}), bf16[1024,12416]{1,0:T(8,128)(2,1)}) %all-gather.2.cloned.1.call-update) | async-done | bytes 25427984 | tf_op jit(solution)/shard_map/all_gather | solution.py:363
  149.1 5.9 fusion.297
  190.1 4.9 reshape.1029
  215.9 9.5 %fusion.308 = (bf16[1024,2048]{1,0:T(8,128)(2,1)}, bf16[1024,2048]{1,0:T(8,128)(2,1)}, bf16[1024,2048]{1,0:T(8,128)(2,1)}) fusion(bf16[1024,12416]{1,0:T(8,128)(2,1)} %all-gather.2.cloned.1.call-done), kind=kLoop, calls=%fused_computation.669 | loop fusion | bytes 25165824 | tf_op jit(solution)/shard_map/slice | solution.py:369
  225.4 7.1 reshape.1035
  236.3 5.9 multiply_convert_fusion.4
  254.2 6.1 fusion.295
  274.0 7.9 fusion.116
  319.5 4.7 multiply_reduce_fusion.21
  343.3 5.4 fusion.120
  365.0 5.0 broadcast_multiply_fusion.9
  389.8 6.8 fusion.179
  402.7 7.5 slice.727
  410.4 4.8 fusion.167
  415.8 105.4 %conditional.1 = (bf16[256,1024]{1,0:T(8,128)(2,1)}, bf16[256,2048]{1,0:T(8,128)(2,1)}, bf16[256,2048]{1,0:T(8,128)(2,1)}, bf16[256,1024]{1,0:T(8,128)(2,1)S(1)}...) conditional(s32[]{:T(128)} %convert_element_type.775, ...), branch_computations={%region_23.25_spmd, %region_24.39_spmd} | conditional | flops 7078396928 | bytes 323846080 | solution.py:401
  416.9 5.6 multiply_convert_fusion
  435.2 7.2 fusion.13
  451.4 4.6 bitcast_add_fusion.1
  461.9 4.6 fusion.45
  473.3 4.9 fusion.15
  506.9 7.0 multiply_reduce_fusion.4
  521.2 4.9 fusion.299
  658.0 5.7 collective-permute-done.42
  673.4 6.4 collective-permute-done.62
  (1003 shorter events, 512.2 us)
Async XLA Ops:
  7.3 141.8 %all-gather.2.cloned.1.call-start = ((), (), s32[]{:S(2)}) async-start(), calls=%async_computation | async-start | bytes 25825280 | tf_op jit(solution)/shard_map/all_gather | solution.py:363
  400.3 15.0 %collective-permute-start.1 = (bf16[256,1024]{1,0:T(8,128)(2,1)}, bf16[256,1024]{1,0:T(8,128)(2,1)S(1)}, u32[]{:S(2)}, u32[]{:S(2)}) collective-permute-start(bf16[256,1024]{1,0:T(8,128)(2,1)} %get-tuple-element.973), channel_id=1, source_target_pairs={{64,0},{65,1},{66,2},{67,3},{68,4},{69,5},{70,6},{71,7},{72,8},{73... | collective-permute-start | bytes 1572872 | tf_op jit(solution)/shard_map/ppermute | solution.py:400
  533.3 52.4 %collective-permute-start.74 = (f32[104,128]{1,0:T(8,128)}, f32[104,128]{1,0:T(8,128)}, u32[]{:S(2)}, u32[]{:S(2)}) collective-permute-start(f32[104,128]{1,0:T(8,128)} %get-tuple-element.1177), channel_id=1, source_target_pairs={{0,48},{16,0},{32,16},{48,32},{1,49},{17,1},{33,17},{49,33},{2,50}... | collective-permute-start | bytes 159752 | tf_op jit(solution)/shard_map/ppermute | solution.py:253
  536.0 49.7 %collective-permute-start.73 = (f32[104,128]{1,0:T(8,128)}, f32[104,128]{1,0:T(8,128)}, u32[]{:S(2)}, u32[]{:S(2)}) collective-permute-start(f32[104,128]{1,0:T(8,128)} %get-tuple-element.1177), channel_id=1, source_target_pairs={{0,32},{16,48},{32,0},{48,16},{1,33},{17,49},{33,1},{49,17},{2,34}... | collective-permute-start | bytes 159752 | tf_op jit(solution)/shard_map/ppermute | solution.py:253
  536.8 48.9 %collective-permute-start.72 = (f32[104,128]{1,0:T(8,128)}, f32[104,128]{1,0:T(8,128)}, u32[]{:S(2)}, u32[]{:S(2)}) collective-permute-start(f32[104,128]{1,0:T(8,128)} %get-tuple-element.1177), channel_id=1, source_target_pairs={{0,16},{16,32},{32,48},{48,0},{1,17},{17,33},{33,49},{49,1},{2,18}... | collective-permute-start | bytes 159752 | tf_op jit(solution)/shard_map/ppermute | solution.py:253
  548.7 98.3 %collective-permute-start.4 = (bf16[256,2048]{1,0:T(8,128)(2,1)}, bf16[256,2048]{1,0:T(8,128)(2,1)}, u32[]{:S(2)}, u32[]{:S(2)}) collective-permute-start(bf16[256,2048]{1,0:T(8,128)(2,1)} %convolution_convert_fusion.7), channel_id=1, source_target_pairs={{0,48},{16,0},{32,16},{48,32},{1,49},{17,1},{33,17},{49,33},{2,50}... | collective-permute-start | bytes 3145736 | tf_op jit(solution)/shard_map/ppermute | solution.py:253
  557.5 83.1 %collective-permute-start.24 = (bf16[384,1024]{1,0:T(8,128)(2,1)}, bf16[384,1024]{1,0:T(8,128)(2,1)S(1)}, u32[]{:S(2)}, u32[]{:S(2)}) collective-permute-start(bf16[384,1024]{1,0:T(8,128)(2,1)} %convolution_convert_fusion.11), channel_id=1, source_target_pairs={{0,3},{1,0},{2,1},{3,2},{4,7},{5,4},{6,5},{7,6},{8,11},{9,8},{10,9... | collective-permute-start | bytes 2359304 | tf_op jit(solution)/shard_map/ppermute | solution.py:253
  622.8 22.8 %collective-permute-start.22 = (bf16[384,1024]{1,0:T(8,128)(2,1)}, bf16[384,1024]{1,0:T(8,128)(2,1)}, u32[]{:S(2)}, u32[]{:S(2)}) collective-permute-start(bf16[384,1024]{1,0:T(8,128)(2,1)} %convolution_convert_fusion.12), channel_id=1, source_target_pairs={{0,1},{1,2},{2,3},{3,0},{4,5},{5,6},{6,7},{7,4},{8,9},{9,10},{10,1... | collective-permute-start | bytes 2359304 | tf_op jit(solution)/shard_map/ppermute | solution.py:253
  630.9 20.4 %collective-permute-start.2 = (bf16[256,2048]{1,0:T(8,128)(2,1)}, bf16[256,2048]{1,0:T(8,128)(2,1)}, u32[]{:S(2)}, u32[]{:S(2)}) collective-permute-start(bf16[256,2048]{1,0:T(8,128)(2,1)} %convolution_convert_fusion.8), channel_id=1, source_target_pairs={{0,16},{16,32},{32,48},{48,0},{1,17},{17,33},{33,49},{49,1},{2,18}... | collective-permute-start | bytes 3145736 | tf_op jit(solution)/shard_map/ppermute | solution.py:253
  636.5 51.2 %collective-permute-start.14 = (bf16[256,2176]{1,0:T(8,128)(2,1)}, bf16[256,2176]{1,0:T(8,128)(2,1)S(1)}, u32[]{:S(2)}, u32[]{:S(2)}) collective-permute-start(bf16[256,2176]{1,0:T(8,128)(2,1)} %convolution_convert_fusion.1), channel_id=1, source_target_pairs={{0,12},{4,0},{8,4},{12,8},{1,13},{5,1},{9,5},{13,9},{2,14},{6,2},{... | collective-permute-start | bytes 3342344 | tf_op jit(solution)/shard_map/ppermute | solution.py:253
  640.7 16.5 %collective-permute-start.44 = (bf16[256,2048]{1,0:T(8,128)(2,1)}, bf16[256,2048]{1,0:T(8,128)(2,1)S(1)}, u32[]{:S(2)}, u32[]{:S(2)}) collective-permute-start(bf16[256,2048]{1,0:T(8,128)(2,1)} %convolution_convert_fusion.5), channel_id=1, source_target_pairs={{0,48},{16,0},{32,16},{48,32},{1,49},{17,1},{33,17},{49,33},{2,50}... | collective-permute-start | bytes 3145736 | tf_op jit(solution)/shard_map/ppermute | solution.py:253
  645.6 18.1 %collective-permute-start.42 = (bf16[256,2048]{1,0:T(8,128)(2,1)}, bf16[256,2048]{1,0:T(8,128)(2,1)S(1)}, u32[]{:S(2)}, u32[]{:S(2)}) collective-permute-start(bf16[256,2048]{1,0:T(8,128)(2,1)} %convolution_convert_fusion.6), channel_id=1, source_target_pairs={{0,16},{16,32},{32,48},{48,0},{1,17},{17,33},{33,49},{49,1},{2,18}... | collective-permute-start | bytes 3145736 | tf_op jit(solution)/shard_map/ppermute | solution.py:253
  647.0 18.2 %collective-permute-start.54 = (bf16[256,2048]{1,0:T(8,128)(2,1)S(1)}, bf16[256,2048]{1,0:T(8,128)(2,1)S(1)}, u32[]{:S(2)}, u32[]{:S(2)}) collective-permute-start(bf16[256,2048]{1,0:T(8,128)(2,1)S(1)} %copy-done.100), channel_id=1, source_target_pairs={{0,12},{4,0},{8,4},{12,8},{1,13},{5,1},{9,5},{13,9},{2,14},{6,2},{... | collective-permute-start | bytes 3145736 | tf_op jit(solution)/shard_map/ppermute | solution.py:253
  651.2 17.0 %collective-permute-start.52 = (bf16[256,2048]{1,0:T(8,128)(2,1)S(1)}, bf16[256,2048]{1,0:T(8,128)(2,1)S(1)}, u32[]{:S(2)}, u32[]{:S(2)}) collective-permute-start(bf16[256,2048]{1,0:T(8,128)(2,1)S(1)} %copy-done.99), channel_id=1, source_target_pairs={{0,4},{4,8},{8,12},{12,0},{1,5},{5,9},{9,13},{13,1},{2,6},{6,10},{... | collective-permute-start | bytes 3145736 | tf_op jit(solution)/shard_map/ppermute | solution.py:253
  657.2 14.8 %collective-permute-start.64 = (bf16[512,1024]{1,0:T(8,128)(2,1)S(1)}, bf16[512,1024]{1,0:T(8,128)(2,1)S(1)}, u32[]{:S(2)}, u32[]{:S(2)}) collective-permute-start(bf16[512,1024]{1,0:T(8,128)(2,1)S(1)} %copy-done.94), channel_id=1, source_target_pairs={{0,3},{1,0},{2,1},{3,2},{4,7},{5,4},{6,5},{7,6},{8,11},{9,8},{10,9... | collective-permute-start | bytes 3145736 | tf_op jit(solution)/shard_map/ppermute | solution.py:253
  663.8 16.0 %collective-permute-start.62 = (bf16[512,1024]{1,0:T(8,128)(2,1)S(1)}, bf16[512,1024]{1,0:T(8,128)(2,1)S(1)}, u32[]{:S(2)}, u32[]{:S(2)}) collective-permute-start(bf16[512,1024]{1,0:T(8,128)(2,1)S(1)} %copy-done.93), channel_id=1, source_target_pairs={{0,1},{1,2},{2,3},{3,0},{4,5},{5,6},{6,7},{7,4},{8,9},{9,10},{10,1... | collective-permute-start | bytes 3145736 | tf_op jit(solution)/shard_map/ppermute | solution.py:253
  665.2 32.1 %collective-permute-start.12 = (bf16[256,2176]{1,0:T(8,128)(2,1)S(1)}, bf16[256,2176]{1,0:T(8,128)(2,1)S(1)}, u32[]{:S(2)}, u32[]{:S(2)}) collective-permute-start(bf16[256,2176]{1,0:T(8,128)(2,1)S(1)} %copy-done.92), channel_id=1, source_target_pairs={{0,4},{4,8},{8,12},{12,0},{1,5},{5,9},{9,13},{13,1},{2,6},{6,10},{... | collective-permute-start | bytes 3342344 | tf_op jit(solution)/shard_map/ppermute | solution.py:253
  679.8 25.2 %collective-permute-start.5 = (bf16[128,2048]{1,0:T(8,128)(2,1)S(1)}, bf16[128,2048]{1,0:T(8,128)(2,1)S(1)}, u32[]{:S(2)}, u32[]{:S(2)}) collective-permute-start(bf16[128,2048]{1,0:T(8,128)(2,1)S(1)} %fusion.101), channel_id=1, source_target_pairs={{0,48},{16,0},{32,16},{48,32},{1,49},{17,1},{33,17},{49,33},{2,50}... | collective-permute-start | bytes 1572872 | tf_op jit(solution)/shard_map/ppermute | solution.py:253
  691.7 15.4 %collective-permute-start.3 = (bf16[128,2048]{1,0:T(8,128)(2,1)S(1)}, bf16[128,2048]{1,0:T(8,128)(2,1)S(1)}, u32[]{:S(2)}, u32[]{:S(2)}) collective-permute-start(bf16[128,2048]{1,0:T(8,128)(2,1)S(1)} %fusion.99), channel_id=1, source_target_pairs={{0,16},{16,32},{32,48},{48,0},{1,17},{17,33},{33,49},{49,1},{2,18}... | collective-permute-start | bytes 1572872 | tf_op jit(solution)/shard_map/ppermute | solution.py:253
  715.0 13.6 %collective-permute-start.13 = (bf16[128,2176]{1,0:T(8,128)(2,1)S(1)}, bf16[128,2176]{1,0:T(8,128)(2,1)S(1)}, u32[]{:S(2)}, u32[]{:S(2)}) collective-permute-start(bf16[128,2176]{1,0:T(8,128)(2,1)S(1)} %fusion.75), channel_id=1, source_target_pairs={{0,4},{4,8},{8,12},{12,0},{1,5},{5,9},{9,13},{13,1},{2,6},{6,10},{... | collective-permute-start | bytes 1671176 | tf_op jit(solution)/shard_map/ppermute | solution.py:253
  717.5 13.8 %collective-permute-start.7 = (bf16[4,16,2048]{2,1,0:T(8,128)(2,1)S(1)}, bf16[4,16,2048]{2,1,0:T(8,128)(2,1)S(1)}, u32[]{:S(2)}, u32[]{:S(2)}) collective-permute-start(bf16[4,16,2048]{2,1,0:T(8,128)(2,1)S(1)} %get-tuple-element.1049), channel_id=1, source_target_pairs={{0,12},{4,0},{8,4},{12,8},{1,13},{5,1},{9,5},{13,9},{2,14},{6,2},{... | collective-permute-start | bytes 786440 | tf_op jit(solution)/shard_map/ppermute | solution.py:253
  740.6 36.8 %collective-permute-start.18 = (bf16[4,16,2176]{2,1,0:T(8,128)(2,1)S(1)}, bf16[4,16,2176]{2,1,0:T(8,128)(2,1)S(1)}, u32[]{:S(2)}, u32[]{:S(2)}) collective-permute-start(bf16[4,16,2176]{2,1,0:T(8,128)(2,1)S(1)} %get-tuple-element.1032), channel_id=1, source_target_pairs={{0,2},{1,3},{2,0},{3,1},{4,6},{5,7},{6,4},{7,5},{8,10},{9,11},{10,... | collective-permute-start | bytes 835592 | tf_op jit(solution)/shard_map/ppermute | solution.py:253
  743.3 34.1 %collective-permute-start.17 = (bf16[4,16,2176]{2,1,0:T(8,128)(2,1)S(1)}, bf16[4,16,2176]{2,1,0:T(8,128)(2,1)S(1)}, u32[]{:S(2)}, u32[]{:S(2)}) collective-permute-start(bf16[4,16,2176]{2,1,0:T(8,128)(2,1)S(1)} %get-tuple-element.1033), channel_id=1, source_target_pairs={{0,3},{1,0},{2,1},{3,2},{4,7},{5,4},{6,5},{7,6},{8,11},{9,8},{10,9... | collective-permute-start | bytes 835592 | tf_op jit(solution)/shard_map/ppermute | solution.py:253
  763.2 14.2 %collective-permute-start.16 = (bf16[4,16,2176]{2,1,0:T(8,128)(2,1)S(1)}, bf16[4,16,2176]{2,1,0:T(8,128)(2,1)S(1)}, u32[]{:S(2)}, u32[]{:S(2)}) collective-permute-start(bf16[4,16,2176]{2,1,0:T(8,128)(2,1)S(1)} %get-tuple-element.1031), channel_id=1, source_target_pairs={{0,1},{1,2},{2,3},{3,0},{4,5},{5,6},{6,7},{7,4},{8,9},{9,10},{10,1... | collective-permute-start | bytes 835592 | tf_op jit(solution)/shard_map/ppermute | solution.py:253
  (283 other events, 1993.3 us)
Sparse Core Ops, SparseCore 0:
  13.7 135.3 all-gather.1

commit v2 on v1

v2 whole, which is shorter than its diff:
```python
import jax
import jax.numpy as jnp
from jax import lax
from jax.experimental import pallas as pl
from jax.experimental.pallas import tpu as pltpu
from jax.sharding import Mesh
from jax.sharding import PartitionSpec as P

LEN = 128
ROWS = 256
WIDTH = 1024
FEED = 2048
INNER = 1536
MIXED = 1792
CAT = 4224
HEADS = 24
DP = ("dp_0", "dp_1", "dp_2")
F32 = jnp.float32
BF16 = jnp.bfloat16
HIDE = -1e30
Q0, K0, V0, Z0, X0, T0 = 0, 512, 640, 768, 2304, 4096
GATE0, UP0, DOWN0, OUT0, HEADS0, DT0, PACKED = 64, 96, 128, 160, 184, 192, 200


def dot(left, right):
    return jnp.dot(left, right, preferred_element_type=F32)


def dot_nt(left, right):
    return lax.dot_general(left, right, (((1,), (1,)), ((), ())), preferred_element_type=F32)


def dot_tn(left, right):
    return lax.dot_general(left, right, (((0,), (0,)), ((), ())), preferred_element_type=F32)


def dot_full(left, right):
    return jnp.dot(left, right, precision=lax.Precision.HIGHEST, preferred_element_type=F32)


def iota(shape, dim):
    return lax.broadcasted_iota(jnp.int32, shape, dim)


def sigmoid(v):
    return 1.0 / (1.0 + jnp.exp(-v))


def softplus(v):
    return jnp.maximum(v, 0.0) + jnp.log(1.0 + jnp.exp(-jnp.abs(v)))


def swap_halves(v):
    width = v.shape[1]
    near = lax.rem(iota(v.shape, 1), 64) < 32
    return jnp.where(near, pltpu.roll(v, width - 32, 1), pltpu.roll(v, 32, 1))


def shifted_down(v, by):
    if by == 0:
        return v
    return jnp.where(iota(v.shape, 0) >= by, pltpu.roll(v, by, 0), 0.0)


def shifted_up(v, by):
    if by == 0:
        return v
    rows = v.shape[0]
    return jnp.where(iota(v.shape, 0) < rows - by, pltpu.roll(v, rows - by, 0), 0.0)


def rms(v):
    return lax.rsqrt(jnp.mean(v * v, axis=-1, keepdims=True) + 1e-05)


def rms_backward(v, gain, grad):
    scale = rms(v)
    gained = grad * gain
    inner = jnp.mean(gained * v, axis=-1, keepdims=True)
    grad_v = scale * gained - v * (scale * scale * scale * inner)
    return grad_v, jnp.sum(grad * v * scale, axis=0, keepdims=True)


def left_half():
    return iota((LEN, 128), 1) < 64


def both_halves(v, group, left):
    turned = pltpu.roll(v, 64, 1)
    return jnp.where(left, v, turned) if group == 0 else jnp.where(left, turned, v)


def stacked(pairs, left):
    parts = []
    for pair in pairs:
        parts.append(jnp.where(left, pair, 0.0))
        parts.append(jnp.where(left, 0.0, pair))
    return jnp.concatenate(parts, axis=0).astype(BF16)


def unstacked(rows, index, left):
    low = rows[2 * index * LEN : (2 * index + 1) * LEN]
    high = rows[(2 * index + 1) * LEN : (2 * index + 2) * LEN]
    return jnp.where(left, low, high)


def attention_parts(proj, rows, cosine, sine):
    left = left_half()
    query = proj[rows, Q0:K0]
    query = query * cosine[...] + swap_halves(query) * sine[...]
    key = proj[rows, K0:V0]
    key = key * cosine[:, :128] + swap_halves(key) * sine[:, :128]
    value = proj[rows, V0:Z0]
    groups = []
    for group in range(2):
        pairs = [query[:, 128 * p : 128 * p + 128] for p in (2 * group, 2 * group + 1)]
        queries = stacked(pairs, left)
        keys = both_halves(key, group, left).astype(BF16)
        values = both_halves(value, group, left).astype(BF16)
        scores = dot_nt(queries, keys) * 0.125
        time = lax.rem(iota(scores.shape, 0), LEN)
        scores = jnp.where(iota(scores.shape, 1) <= time, scores, HIDE)
        top = jnp.max(scores, axis=-1, keepdims=True)
        expo = jnp.exp(scores - top)
        probs = expo / jnp.sum(expo, axis=-1, keepdims=True)
        groups.append((queries, keys, values, probs))
    return left, groups


def attention_forward(proj, rows, cosine, sine, attended):
    left, groups = attention_parts(proj, rows, cosine, sine)
    for group, (queries, keys, values, probs) in enumerate(groups):
        mixed = dot(probs.astype(BF16), values)
        for index in range(2):
            at = 256 * group + 128 * index
            attended[rows, at : at + 128] = unstacked(mixed, index, left).astype(BF16)


def attention_backward(proj, rows, cosine, sine, grad_attended, grad_cat):
    left, groups = attention_parts(proj, rows, cosine, sine)
    key_parts, value_parts = [], []
    for group, (queries, keys, values, probs) in enumerate(groups):
        pairs = [grad_attended[:, 128 * p : 128 * p + 128] for p in (2 * group, 2 * group + 1)]
        grads = stacked(pairs, left)
        grad_values = dot_tn(probs.astype(BF16), grads)
        grad_probs = dot_nt(grads, values)
        inner = jnp.sum(probs * grad_probs, axis=-1, keepdims=True)
        grad_scores = (probs * (grad_probs - inner)).astype(BF16)
        grad_queries = dot(grad_scores, keys) * 0.125
        grad_keys = dot_tn(grad_scores, queries) * 0.125
        for index in range(2):
            at = 256 * group + 128 * index
            grad = unstacked(grad_queries, index, left)
            grad = grad * cosine[:, :128] - swap_halves(grad) * sine[:, :128]
            grad_cat[rows, at : at + 128] = grad.astype(BF16)
        key_parts.append(grad_keys + pltpu.roll(grad_keys, 64, 1))
        value_parts.append(grad_values + pltpu.roll(grad_values, 64, 1))
    grad = jnp.where(left, key_parts[0], key_parts[1])
    grad = grad * cosine[:, :128] - swap_halves(grad) * sine[:, :128]
    grad_cat[rows, K0:V0] = grad.astype(BF16)
    grad_cat[rows, V0:Z0] = jnp.where(left, value_parts[0], value_parts[1]).astype(BF16)


def mamba_parts(proj, rows, kernel, bias, step_bias, decay_log):
    mixed = proj[rows, X0:T0]
    total = bias[...] + mixed * kernel[3:4, :]
    for tap in range(3):
        total = total + shifted_down(mixed, 3 - tap) * kernel[tap : tap + 1, :]
    active = total * sigmoid(total)
    step = softplus(proj[rows, T0:CAT] + step_bias[...])
    rate = -step * jnp.exp(decay_log[...])
    earlier = (iota((LEN, LEN), 0) >= iota((LEN, LEN), 1)).astype(F32)
    cumul = dot_full(earlier, rate)
    state_in = active[:, INNER : INNER + 128].astype(BF16)
    state_out = active[:, INNER + 128 :].astype(BF16)
    return mixed, total, active, step, rate, cumul, state_in, state_out


def stepped(step, pair, left):
    return jnp.where(left, step[:, 2 * pair : 2 * pair + 1], step[:, 2 * pair + 1 : 2 * pair + 2])


def mamba_forward(proj, rows, kernel, bias, step_bias, decay_log, skip, gain, ssm, mamba):
    left = left_half()
    parts = mamba_parts(proj, rows, kernel, bias, step_bias, decay_log)
    mixed, total, active, step, rate, cumul, state_in, state_out = parts
    across = cumul.T
    hidden = jnp.where(iota((LEN, LEN), 0) >= iota((LEN, LEN), 1), 0.0, HIDE)
    meeting = dot_nt(state_out, state_in)
    for pair in range(HEADS // 2):
        at = 128 * pair
        inputs = active[:, at : at + 128]
        scaled = (inputs * stepped(step, pair, left)).astype(BF16)
        mixing = []
        for head in (2 * pair, 2 * pair + 1):
            spread = cumul[:, head : head + 1] - across[head : head + 1, :] + hidden
            mixing.append((meeting * jnp.exp(spread)).astype(BF16))
        both = dot(jnp.concatenate(mixing, axis=0), scaled)
        out = unstacked(both, 0, left) + skip[:, at : at + 128] * inputs
        ssm[rows, at : at + 128] = out
    z = proj[rows, Z0:X0]
    gated = ssm[rows, :] * (z * sigmoid(z))
    mamba[rows, :] = (gated * rms(gated) * gain[...]).astype(BF16)


def head_sums(v, pick):
    high = v.astype(BF16)
    low = (v - high.astype(F32)).astype(BF16)
    return dot(high, pick) + dot(low, pick)


def mamba_backward(
    proj, rows, kernel, bias, step_bias, decay_log, skip, gain, pick, ssm, grad_mamba, grad_cat,
    across_scratch, balance_scratch, touch_scratch, grad_active, add_small,
):
    left = left_half()
    parts = mamba_parts(proj, rows, kernel, bias, step_bias, decay_log)
    mixed, total, active, step, rate, cumul, state_in, state_out = parts
    across = cumul.T
    hidden = jnp.where(iota((LEN, LEN), 1) >= iota((LEN, LEN), 0), 0.0, HIDE)
    meeting = dot_nt(state_out, state_in).T
    z = proj[rows, Z0:X0]
    out = ssm[rows, :]
    gate = sigmoid(z)
    gated = out * (z * gate)
    grad_gated, grad_gain = rms_backward(gated, gain[...], grad_mamba)
    add_small(6, grad_gain)
    grad_cat[rows, Z0:X0] = (grad_gated * out * (gate * (1.0 + z * (1.0 - gate)))).astype(BF16)
    grad_out = grad_gated * (z * gate)
    add_small(5, jnp.sum(grad_out * active[:, :INNER], axis=0, keepdims=True))
    grad_meeting = jnp.zeros((LEN, LEN), F32)
    for pair in range(HEADS // 2):
        at = 128 * pair
        inputs = active[:, at : at + 128]
        steps = stepped(step, pair, left)
        scaled = (inputs * steps).astype(BF16)
        grad_pair = grad_out[:, at : at + 128]
        grad_low = grad_pair.astype(BF16)
        halves = jnp.concatenate(
            [jnp.where(left, scaled, jnp.zeros_like(scaled)), jnp.where(left, jnp.zeros_like(scaled), scaled)],
            axis=0,
        )
        grad_mixing = dot_nt(halves, grad_low)
        mixing = []
        for place, head in enumerate((2 * pair, 2 * pair + 1)):
            spread = across[head : head + 1, :] - cumul[:, head : head + 1] + hidden
            decay = jnp.exp(spread)
            mixing.append((meeting * decay).astype(BF16))
            grad_meeting = grad_meeting + grad_mixing[LEN * place : LEN * place + LEN] * decay
        both = dot(jnp.concatenate(mixing, axis=0), grad_low)
        grad_scaled = unstacked(both, 0, left)
        skips = skip[:, at : at + 128]
        grad_active[:, at : at + 128] = grad_scaled * steps + skips * grad_pair
        touch_scratch[:, at : at + 128] = grad_scaled * inputs
        balance_scratch[:, at : at + 128] = grad_low.astype(F32) * (
            out[:, at : at + 128] - skips * inputs
        ) - scaled.astype(F32) * grad_scaled
    grad_low = grad_meeting.astype(BF16)
    grad_active[:, INNER : INNER + 128] = dot(grad_low, state_out)
    grad_active[:, INNER + 128 :] = dot_tn(grad_low, state_in)
    later = (iota((LEN, LEN), 1) >= iota((LEN, LEN), 0)).astype(F32)
    grad_rate = dot_full(later, head_sums(balance_scratch[...], pick[...]))
    add_small(4, jnp.sum(grad_rate * rate, axis=0, keepdims=True))
    grad_step = head_sums(touch_scratch[...], pick[...]) - grad_rate * jnp.exp(decay_log[...])
    grad_dt = grad_step * sigmoid(proj[rows, T0:CAT] + step_bias[...])
    add_small(3, jnp.sum(grad_dt, axis=0, keepdims=True))
    grad_cat[rows, T0:CAT] = grad_dt.astype(BF16)
    slope = sigmoid(total)
    grad_total = grad_active[...] * (slope * (1.0 + total * (1.0 - slope)))
    add_small(2, jnp.sum(grad_total, axis=0, keepdims=True))
    grad_mixed = grad_total * kernel[3:4, :]
    taps = []
    for tap in range(4):
        taps.append(jnp.sum(grad_total * shifted_down(mixed, 3 - tap), axis=0, keepdims=True))
        if tap < 3:
            grad_mixed = grad_mixed + shifted_up(grad_total, 3 - tap) * kernel[tap : tap + 1, :]
    add_small(1, jnp.concatenate(taps, axis=0))
    grad_cat[rows, X0:T0] = grad_mixed.astype(BF16)


def flat(block):
    return block.reshape(block.shape[0] * block.shape[1], block.shape[2])


def start_all(copies):
    for copy in copies:
        copy.start()


def forward_kernel(
    x, packed, dt_weight, out_weight, heads_weight, input_gain, kernel, bias, step_bias, decay_log, skip,
    mixer_gain, feed_gain, cosine, sine,
    result, normed, proj, ssm, mamba, attended, middle, ffin, gate, upper, hidden,
    cat, gate_up, down, out_mat, heads_mat, sems,
):
    copies = [
        pltpu.make_async_copy(packed.at[:, pl.ds(16 * j, 16), :], cat.at[j], sems.at[j])
        for j in range(4)
    ]
    copies.append(pltpu.make_async_copy(out_weight, out_mat, sems.at[4]))
    copies.append(pltpu.make_async_copy(heads_weight, heads_mat, sems.at[5]))
    for j in range(4):
        copies.append(
            pltpu.make_async_copy(
                packed.at[:, pl.ds(GATE0 + 16 * j, 16), :], gate_up.at[j], sems.at[6 + j]
            )
        )
    copies.append(pltpu.make_async_copy(packed.at[:, pl.ds(DOWN0, 32), :], down, sems.at[10]))
    start_all(copies)
    state = x[...].astype(F32)
    normed[...] = (state * rms(state) * input_gain[...]).astype(BF16)
    proj[:, T0:CAT] = dot(normed[...], dt_weight[...])
    for j in range(4):
        copies[j].wait()

        def columns(tile, carry, j=j):
            at = pl.multiple_of(tile * 256, 256)
            block = flat(cat[j, :, :, pl.ds(at, 256)])
            proj[:, pl.ds(pl.multiple_of(j * 1024 + at, 256), 256)] = dot(normed[...], block)
            return carry

        lax.fori_loop(0, 4, columns, 0)

    def sequence(index, carry):
        rows = pl.ds(pl.multiple_of(index * LEN, LEN), LEN)
        attention_forward(proj, rows, cosine, sine, attended)
        mamba_forward(proj, rows, kernel, bias, step_bias, decay_log, skip, mixer_gain, ssm, mamba)
        return carry

    lax.fori_loop(0, 2, sequence, 0)
    copies[4].wait()
    copies[5].wait()

    def joined(tile, carry):
        at = pl.ds(pl.multiple_of(tile * 256, 256), 256)
        part = dot(mamba[...], out_mat[:, at]) + dot(attended[...], heads_mat[:, at])
        middle[:, at] = x[:, at].astype(F32) + part
        return carry

    lax.fori_loop(0, 4, joined, 0)
    value = middle[...]
    ffin[...] = (value * rms(value) * feed_gain[...]).astype(BF16)
    for j in range(2):
        copies[6 + j].wait()
        copies[8 + j].wait()

        def feed(tile, carry, j=j):
            at = pl.multiple_of(tile * 256, 256)
            to = pl.ds(pl.multiple_of(j * 1024 + at, 256), 256)
            low = dot(ffin[...], flat(gate_up[j, :, :, pl.ds(at, 256)]))
            high = dot(ffin[...], flat(gate_up[2 + j, :, :, pl.ds(at, 256)]))
            gate[:, to] = low
            upper[:, to] = high
            hidden[:, to] = (low * sigmoid(low) * high).astype(BF16)
            return carry

        lax.fori_loop(0, 4, feed, 0)
    copies[10].wait()

    def last(tile, carry):
        at = pl.ds(pl.multiple_of(tile * 256, 256), 256)
        result[:, at] = (middle[:, at] + dot(hidden[...], flat(down[:, :, at]))).astype(BF16)
        return carry

    lax.fori_loop(0, 4, last, 0)


def feed_backward_kernel(
    grad_top, packed, gate, upper, middle, feed_gain,
    grad_gate, grad_upper, grad_middle, feed_grad,
    gate_up, down, grad_ffin, sems,
):
    copies = [pltpu.make_async_copy(packed.at[:, pl.ds(DOWN0, 32), :], down, sems.at[4])]
    for j in range(4):
        copies.append(
            pltpu.make_async_copy(
                packed.at[:, pl.ds(GATE0 + 16 * j, 16), :], gate_up.at[j], sems.at[j]
            )
        )
    start_all(copies)
    copies[0].wait()

    def through(tile, carry):
        at = pl.ds(pl.multiple_of(tile * 256, 256), 256)
        block = flat(down[pl.ds(tile * 8, 8)])
        grad_hidden = dot_nt(grad_top[...], block)
        low, high = gate[:, at], upper[:, at]
        slope = sigmoid(low)
        grad_upper[:, at] = (grad_hidden * (low * slope)).astype(BF16)
        part = grad_hidden * high * (slope * (1.0 + low * (1.0 - slope)))
        grad_gate[:, at] = part.astype(BF16)
        return carry

    lax.fori_loop(0, 8, through, 0)
    for copy in copies[1:]:
        copy.wait()

    def back(tile, carry):
        at = pl.ds(pl.multiple_of(tile * 256, 256), 256)
        total = jnp.zeros((ROWS, 256), F32)
        for j in range(2):
            block = flat(gate_up[j, pl.ds(tile * 16, 16)])
            total = total + dot_nt(grad_gate[:, 1024 * j : 1024 * j + 1024], block)
            block = flat(gate_up[2 + j, pl.ds(tile * 16, 16)])
            total = total + dot_nt(grad_upper[:, 1024 * j : 1024 * j + 1024], block)
        grad_ffin[:, at] = total
        return carry

    lax.fori_loop(0, 4, back, 0)
    grad_part, grad_gain = rms_backward(middle[...], feed_gain[...], grad_ffin[...])
    feed_grad[...] = grad_gain
    grad_middle[...] = grad_top[...].astype(F32) + grad_part


def mix_backward_kernel(
    grad_middle, x, packed, dt_weight, out_weight, heads_weight, proj, ssm, input_gain, kernel, bias,
    step_bias, decay_log, skip, mixer_gain, cosine, sine, pick,
    grad_branch, grad_cat, grad_start, input_grad, kernel_grad, bias_grad, step_grad, decay_grad,
    skip_grad, mixer_grad,
    cat, out_mat, heads_mat, grad_mamba, grad_attended, balance, touch, grad_active, grad_normed, sems,
):
    copies = [
        pltpu.make_async_copy(out_weight, out_mat, sems.at[4]),
        pltpu.make_async_copy(heads_weight, heads_mat, sems.at[5]),
    ]
    for j in range(4):
        copies.append(
            pltpu.make_async_copy(packed.at[:, pl.ds(16 * j, 16), :], cat.at[j], sems.at[j])
        )
    start_all(copies)
    grad_branch[...] = grad_middle[...].astype(BF16)
    copies[0].wait()
    copies[1].wait()

    def through(tile, carry):
        at = pl.ds(pl.multiple_of(tile * 256, 256), 256)
        grad_mamba[:, at] = dot_nt(grad_branch[...], out_mat[at, :])
        return carry

    lax.fori_loop(0, 6, through, 0)

    def through_heads(tile, carry):
        at = pl.ds(pl.multiple_of(tile * 256, 256), 256)
        grad_attended[:, at] = dot_nt(grad_branch[...], heads_mat[at, :])
        return carry

    lax.fori_loop(0, 2, through_heads, 0)
    small = {
        1: kernel_grad,
        2: bias_grad,
        3: step_grad,
        4: decay_grad,
        5: skip_grad,
        6: mixer_grad,
    }
    for ref in small.values():
        ref[...] = jnp.zeros_like(ref)

    def add_small(slot, value):
        small[slot][...] += value

    def sequence(index, carry):
        rows = pl.ds(pl.multiple_of(index * LEN, LEN), LEN)
        grads = grad_attended[rows, :]
        attention_backward(proj, rows, cosine, sine, grads, grad_cat)
        mamba_backward(
            proj, rows, kernel, bias, step_bias, decay_log, skip, mixer_gain, pick, ssm,
            grad_mamba[rows, :], grad_cat, None, balance, touch, grad_active, add_small,
        )
        return carry

    lax.fori_loop(0, 2, sequence, 0)
    for copy in copies[2:]:
        copy.wait()

    def back(tile, carry):
        at = pl.ds(pl.multiple_of(tile * 256, 256), 256)
        total = dot_nt(grad_cat[:, T0:CAT], dt_weight[at, :])
        for j in range(4):
            block = flat(cat[j, pl.ds(tile * 16, 16)])
            total = total + dot_nt(grad_cat[:, 1024 * j : 1024 * j + 1024], block)
        grad_normed[:, at] = total
        return carry

    lax.fori_loop(0, 4, back, 0)
    state = x[...].astype(F32)
    grad_state, grad_gain = rms_backward(state, input_gain[...], grad_normed[...])
    input_grad[...] = grad_gain
    grad_start[...] = grad_middle[...] + grad_state


VMEM = pl.BlockSpec(memory_space=pltpu.VMEM)
ANY = pl.BlockSpec(memory_space=pl.ANY)
LIMIT = 60 * 1024 * 1024


def shape(rows, columns, dtype):
    return jax.ShapeDtypeStruct((rows, columns), dtype)


def scratch(*dims, dtype=BF16):
    return pltpu.VMEM(dims, dtype)


def run_forward(start, mats, small, rope):
    packed, dt_weight, out_weight, heads_weight = mats
    input_gain, kernel, bias, step_bias, decay_log, skip, mixer_gain, feed_gain = small
    return pl.pallas_call(
        forward_kernel,
        out_shape=(
            shape(ROWS, WIDTH, BF16),
            shape(ROWS, WIDTH, BF16),
            shape(ROWS, CAT, F32),
            shape(ROWS, INNER, F32),
            shape(ROWS, INNER, BF16),
            shape(ROWS, 512, BF16),
            shape(ROWS, WIDTH, F32),
            shape(ROWS, WIDTH, BF16),
            shape(ROWS, FEED, F32),
            shape(ROWS, FEED, F32),
            shape(ROWS, FEED, BF16),
        ),
        in_specs=[VMEM, ANY, VMEM, ANY, ANY] + [VMEM] * 10,
        out_specs=(VMEM,) * 11,
        scratch_shapes=[
            scratch(4, 64, 16, 1024),
            scratch(4, 64, 16, 1024),
            scratch(64, 32, 1024),
            scratch(INNER, WIDTH),
            scratch(512, WIDTH),
            pltpu.SemaphoreType.DMA((11,)),
        ],
        compiler_params=pltpu.CompilerParams(vmem_limit_bytes=LIMIT),
        cost_estimate=pl.CostEstimate(
            flops=2 * ROWS * 12_600_000, bytes_accessed=40_000_000, transcendentals=2_000_000
        ),
        name="forward",
    )(start, packed, dt_weight, out_weight, heads_weight, *small, *rope)


def run_feed_backward(grad_top, mats, gate, upper, middle, feed_gain):
    return pl.pallas_call(
        feed_backward_kernel,
        out_shape=(
            shape(ROWS, FEED, BF16),
            shape(ROWS, FEED, BF16),
            shape(ROWS, WIDTH, F32),
            shape(1, WIDTH, F32),
        ),
        in_specs=[VMEM, ANY] + [VMEM] * 4,
        out_specs=(VMEM,) * 4,
        scratch_shapes=[
            scratch(4, 64, 16, 1024),
            scratch(64, 32, 1024),
            scratch(ROWS, WIDTH, dtype=F32),
            pltpu.SemaphoreType.DMA((5,)),
        ],
        compiler_params=pltpu.CompilerParams(vmem_limit_bytes=LIMIT),
        cost_estimate=pl.CostEstimate(
            flops=2 * ROWS * 6_300_000, bytes_accessed=22_000_000, transcendentals=1_000_000
        ),
        name="feed_backward",
    )(grad_top, mats[0], gate, upper, middle, feed_gain)


def run_mix_backward(grad_middle, start, mats, proj, ssm, small, rope, pick):
    packed, dt_weight, out_weight, heads_weight = mats
    return pl.pallas_call(
        mix_backward_kernel,
        out_shape=(
            shape(ROWS, WIDTH, BF16),
            shape(ROWS, CAT, BF16),
            shape(ROWS, WIDTH, F32),
            shape(1, WIDTH, F32),
            shape(4, MIXED, F32),
            shape(1, MIXED, F32),
            shape(1, 128, F32),
            shape(1, 128, F32),
            shape(1, INNER, F32),
            shape(1, INNER, F32),
        ),
        in_specs=[VMEM, VMEM, ANY, VMEM, ANY, ANY] + [VMEM] * 12,
        out_specs=(VMEM,) * 10,
        scratch_shapes=[
            scratch(4, 64, 16, 1024),
            scratch(INNER, WIDTH),
            scratch(512, WIDTH),
            scratch(ROWS, INNER, dtype=F32),
            scratch(ROWS, 512, dtype=F32),
            scratch(LEN, INNER, dtype=F32),
            scratch(LEN, INNER, dtype=F32),
            scratch(LEN, MIXED, dtype=F32),
            scratch(ROWS, WIDTH, dtype=F32),
            pltpu.SemaphoreType.DMA((6,)),
        ],
        compiler_params=pltpu.CompilerParams(vmem_limit_bytes=LIMIT),
        cost_estimate=pl.CostEstimate(
            flops=2 * ROWS * 6_300_000, bytes_accessed=25_000_000, transcendentals=4_000_000
        ),
        name="mix_backward",
    )(
        grad_middle, start, packed, dt_weight, out_weight, heads_weight, proj, ssm, *small[:7], *rope, pick
    )


def rope_tables():
    position = jnp.arange(LEN).astype(F32)
    inverse = 10000.0 ** (-(jnp.arange(32).astype(F32) * 2.0) / 64)
    angle = position[:, None] * inverse[None, :]
    cosine = jnp.tile(jnp.cos(angle), (1, 16))
    sine = jnp.sin(angle)
    return cosine, jnp.tile(jnp.concatenate([-sine, sine], axis=1), (1, 8))


def head_pick():
    lanes = lax.broadcasted_iota(jnp.int32, (INNER, 128), 0) // 64
    return (lanes == lax.broadcasted_iota(jnp.int32, (INNER, 128), 1)).astype(BF16)


def prepared_small(pieces):
    input_gain, kernel, bias, step_bias, decay_log, skip, mixer_gain, feed_gain = pieces

    def padded(v):
        return jnp.pad(v, (0, 128 - HEADS))[None]

    return (
        input_gain[None],
        kernel,
        bias[None],
        padded(step_bias),
        padded(decay_log),
        jnp.repeat(skip, 64)[None],
        mixer_gain[None],
        feed_gain[None],
    )


FIRST = (1, 0, 3, 2)
SECOND = (3, 2, 1, 0)


def partners(axis, turn):
    order = (FIRST, SECOND) if turn == 0 else (SECOND, FIRST)
    me = lax.axis_index(axis)
    near = me + 1 - 2 * lax.rem(me, 2)
    found = (near, 3 - me) if turn == 0 else (3 - me, near)
    return me, found, [[(i, table[i]) for i in range(4)] for table in order]


def halved(part, axis, turn):
    me, (one, two), (swap_one, swap_two) = partners(axis, turn)
    sent = part([one, lax.rem(me + 2, 4)])
    got = lax.ppermute(sent.astype(BF16), axis, swap_one)
    half = got.shape[0] // 2
    handed = part([two]) + got[half:].astype(F32)
    last = lax.ppermute(handed.astype(BF16), axis, swap_two)
    return part([me]) + got[:half].astype(F32) + last.astype(F32)


def scattered(left, right, order, turn):
    depth = left.shape[0] // 64
    blocks = left.reshape(4, 4, 4, depth, left.shape[1])

    def product(places):
        picked = [lax.dynamic_index_in_dim(blocks, p, order[0], keepdims=False) for p in places]
        return dot(jnp.concatenate(picked, axis=0).reshape(-1, left.shape[1]), right)

    array = halved(product, DP[order[0]], turn).astype(BF16)
    array = array.reshape(4, 4, depth, right.shape[1])
    rest = [0, 1, 2]
    rest.remove(order[0])

    def quarters(array, dim):
        def part(places):
            picked = [lax.dynamic_index_in_dim(array, p, dim, keepdims=False) for p in places]
            return jnp.concatenate(picked, axis=0).reshape(-1, array.shape[-1]).astype(F32)

        return part

    array = halved(quarters(array, rest.index(order[1])), DP[order[1]], turn).astype(BF16)
    array = array.reshape(4, depth, right.shape[1])
    return halved(quarters(array, 0), DP[order[2]], turn)


def summed_over(vector):
    for axis in DP:
        for table in (FIRST, SECOND):
            vector = vector + lax.ppermute(vector, axis, [(i, table[i]) for i in range(4)])
    return vector


def column_blocks(matrix):
    return [matrix[:, at : at + 1024] for at in range(0, matrix.shape[1], 1024)]


def on_device(
    layer_input,
    out_grad,
    in_weight,
    query_weight,
    key_weight,
    value_weight,
    out_weight,
    heads_weight,
    gate_weight,
    up_weight,
    down_weight,
    *pieces,
):
    micro, part, width = layer_input.shape
    rows = micro * part
    cat = jnp.concatenate(
        [query_weight[0], key_weight[0], value_weight[0], in_weight[0, :, :3328]], axis=1
    )
    steps = jnp.pad(in_weight[0, :, 3328:].reshape(1, -1), ((0, 7), (0, 1024 - 16 * HEADS)))
    own = jnp.concatenate(
        [
            *column_blocks(cat),
            *column_blocks(gate_weight[0]),
            *column_blocks(up_weight[0]),
            down_weight[0],
            out_weight[0],
            heads_weight[0],
            steps,
        ],
        axis=0,
    )
    packed = lax.all_gather(own, DP, axis=0, tiled=False)
    dt_weight = packed[:, DT0, : 16 * HEADS].reshape(WIDTH, HEADS)
    mats = (
        packed,
        jnp.pad(dt_weight, ((0, 0), (0, 128 - HEADS))),
        packed[:, OUT0:HEADS0].reshape(INNER, WIDTH),
        packed[:, HEADS0:DT0].reshape(512, WIDTH),
    )
    small = prepared_small([piece[0] for piece in pieces])
    rope = rope_tables()
    pick = head_pick()
    first = lax.axis_index("section") == 0

    start_low = layer_input.reshape(rows, width)
    kept_low = run_forward(start_low, mats, small, rope)
    start_high = lax.ppermute(kept_low[0], "section", [(0, 1)])
    kept_high = run_forward(start_high, mats, small, rope)
    layer_outputs = jnp.where(first, kept_low[0], kept_high[0]).reshape(1, micro, part, width)

    def feed_backward(kept, grad_top):
        result, normed, proj, ssm, mamba, attended, middle, ffin, gate, upper, hidden = kept
        out = run_feed_backward(grad_top, mats, gate, upper, middle, small[7])
        return (*out, grad_top, hidden.T, ffin.T)

    def mix_backward(kept, start, grad_middle):
        result, normed, proj, ssm, mamba, attended, middle, ffin, gate, upper, hidden = kept
        out = run_mix_backward(grad_middle, start, mats, proj, ssm, small, rope, pick)
        joined = jnp.concatenate(
            [mamba.T.reshape(64, 24, rows), attended.T.reshape(64, 8, rows)], axis=1
        )
        return (*out, normed.T, joined.reshape(2048, rows))

    top = out_grad.reshape(rows, width)
    feed_high = feed_backward(kept_high, top)
    mix_high = mix_backward(kept_high, start_high, feed_high[2])
    top = lax.ppermute(mix_high[2].astype(BF16), "section", [(1, 0)])
    feed = lax.cond(
        first,
        lambda kept, grad, other: feed_backward(kept, grad),
        lambda kept, grad, other: other,
        kept_low,
        top,
        feed_high,
    )
    grad_gate, grad_upper, grad_middle, feed_grad, grad_low, hidden_t, ffin_t = feed
    down_grad = scattered(hidden_t, grad_low, (2, 0, 1), 0)
    gate_grad = scattered(ffin_t, grad_gate, (0, 1, 2), 0)
    up_grad = scattered(ffin_t, grad_upper, (1, 2, 0), 0)
    mix = lax.cond(
        first,
        lambda kept, start, grad, other: mix_backward(kept, start, grad),
        lambda kept, start, grad, other: other,
        kept_low,
        start_low,
        grad_middle,
        mix_high,
    )
    grad_branch, grad_cat, grad_start, *small_grads, normed_t, joined_t = mix
    joined_grad = scattered(joined_t, grad_branch, (2, 0, 1), 1)
    cat_left = scattered(normed_t, grad_cat[:, :2048], (0, 1, 2), 1)
    cat_right = scattered(normed_t, grad_cat[:, 2048:], (1, 2, 0), 1)
    cat_grad = jnp.concatenate([cat_left, cat_right], axis=1)

    input_g, kernel_g, bias_g, step_g, decay_g, skip_g, mixer_g = small_grads
    small_grads = (
        input_g[0],
        kernel_g,
        bias_g[0],
        step_g[0, :HEADS],
        decay_g[0, :HEADS],
        skip_g.reshape(HEADS, 64).sum(axis=1),
        mixer_g[0],
        feed_grad[0],
    )
    vector = jnp.concatenate([piece.reshape(-1) for piece in small_grads])
    vector = jnp.pad(vector, (0, -vector.shape[0] % 1024)).reshape(-1, 128)
    total = summed_over(vector).reshape(-1)
    summed, at = ([], 0)
    for piece in small_grads:
        summed.append(total[at : at + piece.size].reshape(1, *piece.shape))
        at += piece.size
    return (
        layer_outputs,
        grad_start.reshape(1, micro, part, width),
        cat_grad[None, :, Z0 : T0 + HEADS],
        cat_grad[None, :, :K0],
        cat_grad[None, :, K0:V0],
        cat_grad[None, :, V0:Z0],
        joined_grad[None, :24],
        joined_grad[None, 24:],
        gate_grad[None],
        up_grad[None],
        down_grad[None],
        *summed,
    )


def solution(mesh):
    torus = Mesh(
        mesh.devices.reshape(mesh.shape["section"], 4, 4, 4), ("section", "dp_0", "dp_1", "dp_2")
    )
    in_specs = (
        P(None, DP, None),
        P(None, DP, None),
        P("section", DP, None),
        P("section", DP, None),
        P("section", DP, None),
        P("section", DP, None),
        P("section", DP, None),
        P("section", DP, None),
        P("section", DP, None),
        P("section", DP, None),
        P("section", DP, None),
        P("section", None),
        P("section", None, None),
        P("section", None),
        P("section", None),
        P("section", None),
        P("section", None),
        P("section", None),
        P("section", None),
    )
    out_specs = (
        P("section", None, DP, None),
        P("section", None, DP, None),
        P("section", DP, None),
        P("section", DP, None),
        P("section", DP, None),
        P("section", DP, None),
        P("section", DP, None),
        P("section", DP, None),
        P("section", DP, None),
        P("section", DP, None),
        P("section", DP, None),
        P("section", None),
        P("section", None, None),
        P("section", None),
        P("section", None),
        P("section", None),
        P("section", None),
        P("section", None),
        P("section", None),
    )
    return jax.shard_map(
        on_device, mesh=torus, in_specs=in_specs, out_specs=out_specs, check_vma=False
    )
```

time: 805 us -> 505 us (0.63)
  matrix products: 172 us -> 33.6 us
  Pallas kernels: 0 us -> 123 us
  local copies, waits for them, and re-layouts: 173 us -> 57.2 us
  other arithmetic: 123 us -> 22.2 us
  waiting for transfers between devices: 210 us -> 179 us
  starting transfers between devices: 97.4 us -> 66.5 us
    dot_general x93 -> x18, matrix products: 172 us -> 33.6 us  [dot(): return jnp.dot(left, right, preferred_element_type=F32)]
    pallas_call x0 -> x6, Pallas kernels: none -> 123 us  [the longest x2 51.5 us: run_forward(): pl.pallas_call(forward_kernel, out_shape=(shape(ROWS, WIDTH, BF16), shape...]
    slice x56 -> x3, local copies, waits for them, and re-layouts: 62.9 us -> 4.14 us  [the longest x1 2.21 us: on_device(): packed[:, OUT0:HEADS0].reshape(INNER, WIDTH)]
    mul x26 -> x0, other arithmetic: 56.4 us -> none  [the longest x3 16.2 us: mamba_core(): active = jax.nn.silu(total)]
    reshape x21 -> x4, local copies, waits for them, and re-layouts: 41.6 us -> 2.41 us  [the longest x1 2.32 us: on_device(): packed[:, HEADS0:DT0].reshape(512, WIDTH)]
    ppermute x81 -> x44, waiting for transfers between devices: 79.5 us -> 42.9 us  [the longest x6 18.1 us: summed_over(): lax.ppermute(vector, axis, [(i, table[i]) for i in range(4)])]
    ppermute x81 -> x44, starting transfers between devices: 97.3 us -> 66.5 us  [the longest x18 26.1 us: halved(): got = lax.ppermute(sent.astype(BF16), axis, swap_one)]
    reduce_sum x13 -> x1, other arithmetic: 20.1 us -> 0.12 us  [on_device(): skip_g.reshape(HEADS, 64).sum(axis=1)]
  transfers between devices with their start and end apart: 82 -> 45, of which waited for: 43 -> 14; matrix products, arithmetic and copies ran while one was open for 13% -> 13% of each run, Pallas kernels for 0% -> 0%
where the time goes in v2:
time: 505 us; the launch traced here: 498 us
  waiting for transfers between devices  179 us (35%)
  Pallas kernels  123 us (24%)
  starting transfers between devices  66.5 us (13%)
  local copies, waits for them, and re-layouts  57.2 us (11%)
  matrix products  33.6 us (7%)
  other arithmetic  22.2 us (4%)
  between operations  15.5 us (3%)
    all_gather x1, waiting for transfers between devices, on_device(): packed = lax.all_gather(own, DP, axis=0, tiled=False)  136 us
    pallas_call x2, Pallas kernels, run_forward(): pl.pallas_call(forward_kernel, out_shape=(shape(ROWS, WIDTH, BF16), shape...  51.5 us
    pallas_call x2, Pallas kernels, run_mix_backward(): pl.pallas_call(mix_backward_kernel, out_shape=(shape(ROWS, WIDTH, BF16),...  47.6 us
    dot_general x18, matrix products, dot(): return jnp.dot(left, right, preferred_element_type=F32)  33.6 us
    ppermute x18, starting transfers between devices, halved(): got = lax.ppermute(sent.astype(BF16), axis, swap_one)  26.1 us
    ppermute x18, starting transfers between devices, halved(): last = lax.ppermute(handed.astype(BF16), axis, swap_two)  24.2 us
    pallas_call x2, Pallas kernels, run_feed_backward(): pl.pallas_call(feed_backward_kernel, out_shape=(shape(ROWS, FEED, BF16),...  24 us
    ppermute x6, waiting for transfers between devices, summed_over(): lax.ppermute(vector, axis, [(i, table[i]) for i in range(4)])  18.1 us
  transfers between devices with their start and end apart: 45, of which 14 were waited for; matrix products, arithmetic and copies ran while one was open for 13% of the time, Pallas kernels for 0%

profile of v2, /device:TPU:0, one launch (start us, length us, event | category | flops | bytes accessed | tf_op | source)
XLA Modules:
  0.0 497.6 jit_solution(3322527411161764363)
XLA Ops:
  19.2 136.1 %all-gather.3.cloned.1.call-done = bf16[12800,1024]{1,0:T(8,128)(2,1)} async-done(((bf16[200,1024]{1,0:T(8,128)(2,1)}), bf16[12800,1024]{1,0:T(8,128)(2,1)}) %all-gather.3.cloned.1.call-update) | async-done | bytes 26214416 | tf_op jit(solution)/shard_map/all_gather | solution.py:728
  163.4 25.7 %forward.2 = (bf16[256,1024]{1,0:T(8,128)(2,1)}, bf16[256,1024]{1,0:T(8,128)(2,1)}, f32[256,4224]{1,0:T(8,128)}, f32[256,1536]{1,0:T(8,128)}, bf16[256,1536]{1,0...) custom-call(bf16[256,1024]{1,0:T(8,128)(2,1)} %bitcast.339, ...), custom_call_target="tpu_custom_call" | custom-call | flops 6451200000 | bytes 40000000 | tf_op jit(solution)/shard_map/forward/pallas_call | solution.py:508
  189.1 3.1 collective-permute-start
  194.3 25.8 %forward.3 = (bf16[256,1024]{1,0:T(8,128)(2,1)}, bf16[256,1024]{1,0:T(8,128)(2,1)}, f32[256,4224]{1,0:T(8,128)}, f32[256,1536]{1,0:T(8,128)}, bf16[256,1536]{1,0...) custom-call(bf16[256,1024]{1,0:T(8,128)(2,1)} %collective-permute-do, ...), custom_call_target="tpu_custom_call" | custom-call | flops 6451200000 | bytes 40000000 | tf_op jit(solution)/shard_map/forward/pallas_call | solution.py:508
  220.1 11.8 %feed_backward.3 = (bf16[256,2048]{1,0:T(8,128)(2,1)}, bf16[256,2048]{1,0:T(8,128)(2,1)}, f32[256,1024]{1,0:T(8,128)}, f32[1,1024]{1,0:T(1,128)}) custom-call(bf16[256,1024]{1,0:T(8,128)(2,1)S(1)} %bitcast.320, bf16[64,200,1024]{2,1,0:T(8,128)(2,1)} %bitcast.311, f32[256,2048]{1,0:T(8,128)} %get-tuple-element.332.gate, ...), custom_call_target="tpu_custom_call" | custom-call | flops 3225600000 | bytes 22000000 | tf_op jit(solution)/shard_map/feed_backward/pallas_call | solution.py:542
  231.9 23.9 %mix_backward.4 = (bf16[256,1024]{1,0:T(8,128)(2,1)}, bf16[256,4224]{1,0:T(8,128)(2,1)}, f32[256,1024]{1,0:T(8,128)}, f32[1,1024]{1,0:T(1,128)}, f32[4,1792]{1,0...) custom-call(f32[256,1024]{1,0:T(8,128)} %get-tuple-element.335.grad_, ...), custom_call_target="tpu_custom_call" | custom-call | flops 3225600000 | bytes 25000000 | tf_op jit(solution)/shard_map/mix_backward/pallas_call | solution.py:568
  266.7 17.2 %conditional.2 = (bf16[256,2048]{1,0:T(8,128)(2,1)}, bf16[256,2048]{1,0:T(8,128)(2,1)}, f32[256,1024]{1,0:T(8,128)}, bf16[256,1024]{1,0:T(8,128)(2,1)}, f32[1,10...) conditional(s32[]{:T(128)} %convert_element_type.495, (bf16[2048,256]{0,1:T(8,128)(2,1)}, ...), branch_computations={%region_0.1_spmd, %region_1.2_spmd} | conditional | flops 3225600000 | bytes 26194360 | solution.py:764
  266.7 12.1 %feed_backward.2 = (bf16[256,2048]{1,0:T(8,128)(2,1)}, bf16[256,2048]{1,0:T(8,128)(2,1)}, f32[256,1024]{1,0:T(8,128)}, f32[1,1024]{1,0:T(1,128)}) custom-call(bf16[256,1024]{1,0:T(8,128)(2,1)} %get-tuple-element.505.grad_top, bf16[64,200,1024]{2,1,0:T(8,128)(2,1)} %get-tuple-element.199.packed, f32[256,2048]{1,0:T(8,128)} %get-tuple-element.200.gate, ...), custom_call_target="tpu_custom_call" | custom-call | flops 3225600000 | bytes 22000000 | tf_op jit(solution)/shard_map/cond/branch_1_fun/feed_backward/pallas_call | solution.py:542
  283.9 30.1 %conditional.3 = (bf16[256,1024]{1,0:T(8,128)(2,1)}, bf16[256,4224]{1,0:T(8,128)(2,1)}, f32[256,1024]{1,0:T(8,128)}, f32[1,1024]{1,0:T(1,128)}, f32[4,1792]{1,0:...) conditional(s32[]{:T(128)} %convert_element_type.495, ...), branch_computations={%region_2.3_spmd, %region_3.4_spmd} | conditional | flops 3227697152 | bytes 38631640 | solution.py:776
  287.4 23.7 %mix_backward.3 = (bf16[256,1024]{1,0:T(8,128)(2,1)}, bf16[256,4224]{1,0:T(8,128)(2,1)}, f32[256,1024]{1,0:T(8,128)}, f32[1,1024]{1,0:T(1,128)}, f32[4,1792]{1,0...) custom-call(f32[256,1024]{1,0:T(8,128)} %get-tuple-element.222.grad_, ...), custom_call_target="tpu_custom_call" | custom-call | flops 3225600000 | bytes 25000000 | tf_op jit(solution)/shard_map/cond/branch_1_fun/mix_backward/pallas_call | solution.py:568
  326.5 2.7 collective-permute-start.2
  334.1 2.7 collective-permute-start.14
  342.1 14.6 %collective-permute-done.39 = f32[104,128]{1,0:T(8,128)S(1)} collective-permute-done((f32[104,128]{1,0:T(8,128)S(1)}, f32[104,128]{1,0:T(8,128)S(1)}, u32[]{:S(2)}, u32[]{:S(2)}) %collective-permute-start.39) | collective-permute-done | bytes 53280 | tf_op jit(solution)/shard_map/ppermute | solution.py:688
  357.4 2.7 collective-permute-start.40
  365.3 3.0 collective-permute-start.41
  370.7 2.7 collective-permute-start.42
  383.6 3.0 collective-permute-start.8
  402.0 3.7 collective-permute-done.26
  405.7 3.4 collective-permute-start.21
  412.6 3.0 collective-permute-start.27
  422.0 6.7 %collective-permute-done.15 = bf16[512,1024]{1,0:T(8,128)(2,1)S(1)} collective-permute-done((bf16[512,1024]{1,0:T(8,128)(2,1)S(1)}, bf16[512,1024]{1,0:T(8,128)(2,1)S(1)}, u32[]{:S(2)}, u32[]{:S(2)}) %collective-permute-start.15) | collective-permute-done | bytes 1048608 | tf_op jit(solution)/shard_map/ppermute | solution.py:656
  444.3 2.5 collective-permute-start.10
  480.9 4.5 collective-permute-done.12
  486.1 3.7 collective-permute-done.13
  (332 shorter events, 160.3 us)
Async XLA Ops:
  7.2 148.2 %all-gather.3.cloned.1.call-start = ((), (), s32[]{:S(2)}) async-start(), calls=%async_computation | async-start | bytes 26624000 | tf_op jit(solution)/shard_map/all_gather | solution.py:728
  326.5 57.2 %collective-permute-start.2 = (bf16[512,2048]{1,0:T(8,128)(2,1)}, bf16[512,2048]{1,0:T(8,128)(2,1)}, u32[]{:S(2)}, u32[]{:S(2)}) collective-permute-start(bf16[512,2048]{1,0:T(8,128)(2,1)} %convolution_convert_fusion.3), channel_id=1, source_target_pairs={{0,48},{16,32},{32,16},{48,0},{1,49},{17,33},{33,17},{49,1},{2,50}... | collective-permute-start | bytes 6291464 | tf_op jit(solution)/shard_map/ppermute | solution.py:653
  334.1 62.9 %collective-permute-start.14 = (bf16[1024,1024]{1,0:T(8,128)(2,1)}, bf16[1024,1024]{1,0:T(8,128)(2,1)}, u32[]{:S(2)}, u32[]{:S(2)}) collective-permute-start(bf16[1024,1024]{1,0:T(8,128)(2,1)} %convolution_convert_fusion.5), channel_id=1, source_target_pairs={{0,3},{1,2},{2,1},{3,0},{4,7},{5,6},{6,5},{7,4},{8,11},{9,10},{10,... | collective-permute-start | bytes 6291464 | tf_op jit(solution)/shard_map/ppermute | solution.py:653
  339.7 59.1 %collective-permute-start.20 = (bf16[512,2048]{1,0:T(8,128)(2,1)}, bf16[512,2048]{1,0:T(8,128)(2,1)}, u32[]{:S(2)}, u32[]{:S(2)}) collective-permute-start(bf16[512,2048]{1,0:T(8,128)(2,1)} %convolution_convert_fusion.2), channel_id=1, source_target_pairs={{0,16},{16,0},{32,48},{48,32},{1,17},{17,1},{33,49},{49,33},{2,18}... | collective-permute-start | bytes 6291464 | tf_op jit(solution)/shard_map/ppermute | solution.py:653
  341.5 15.2 %collective-permute-start.39 = (f32[104,128]{1,0:T(8,128)S(1)}, f32[104,128]{1,0:T(8,128)S(1)}, u32[]{:S(2)}, u32[]{:S(2)}) collective-permute-start(f32[104,128]{1,0:T(8,128)S(1)} %fusion.60), channel_id=1, source_target_pairs={{0,48},{16,32},{32,16},{48,0},{1,49},{17,33},{33,17},{49,1},{2,50}... | collective-permute-start | bytes 159752 | tf_op jit(solution)/shard_map/ppermute | solution.py:688
  362.1 43.6 %collective-permute-start.26 = (bf16[512,2048]{1,0:T(8,128)(2,1)}, bf16[512,2048]{1,0:T(8,128)(2,1)}, u32[]{:S(2)}, u32[]{:S(2)}) collective-permute-start(bf16[512,2048]{1,0:T(8,128)(2,1)} %convolution_convert_fusion.1), channel_id=1, source_target_pairs={{0,4},{4,0},{8,12},{12,8},{1,5},{5,1},{9,13},{13,9},{2,6},{6,2},{1... | collective-permute-start | bytes 6291464 | tf_op jit(solution)/shard_map/ppermute | solution.py:653
  381.0 31.5 %collective-permute-start.32 = (bf16[1024,1024]{1,0:T(8,128)(2,1)}, bf16[1024,1024]{1,0:T(8,128)(2,1)}, u32[]{:S(2)}, u32[]{:S(2)}) collective-permute-start(bf16[1024,1024]{1,0:T(8,128)(2,1)} %convolution_convert_fusion.4), channel_id=1, source_target_pairs={{0,1},{1,0},{2,3},{3,2},{4,5},{5,4},{6,7},{7,6},{8,9},{9,8},{10,11... | collective-permute-start | bytes 6291464 | tf_op jit(solution)/shard_map/ppermute | solution.py:653
  383.6 33.6 %collective-permute-start.8 = (bf16[512,2176]{1,0:T(8,128)(2,1)}, bf16[512,2176]{1,0:T(8,128)(2,1)}, u32[]{:S(2)}, u32[]{:S(2)}) collective-permute-start(bf16[512,2176]{1,0:T(8,128)(2,1)} %convolution_convert_fusion), channel_id=1, source_target_pairs={{0,12},{4,8},{8,4},{12,0},{1,13},{5,9},{9,5},{13,1},{2,14},{6,10},... | collective-permute-start | bytes 6684680 | tf_op jit(solution)/shard_map/ppermute | solution.py:653
  397.0 23.0 %collective-permute-start.3 = (bf16[256,2048]{1,0:T(8,128)(2,1)S(1)}, bf16[256,2048]{1,0:T(8,128)(2,1)S(1)}, u32[]{:S(2)}, u32[]{:S(2)}) collective-permute-start(bf16[256,2048]{1,0:T(8,128)(2,1)S(1)} %add_convert_fusion.7), channel_id=1, source_target_pairs={{0,16},{16,0},{32,48},{48,32},{1,17},{17,1},{33,49},{49,33},{2,18}... | collective-permute-start | bytes 3145736 | tf_op jit(solution)/shard_map/ppermute | solution.py:656
  398.8 30.0 %collective-permute-start.15 = (bf16[512,1024]{1,0:T(8,128)(2,1)S(1)}, bf16[512,1024]{1,0:T(8,128)(2,1)S(1)}, u32[]{:S(2)}, u32[]{:S(2)}) collective-permute-start(bf16[512,1024]{1,0:T(8,128)(2,1)S(1)} %add_convert_fusion.5), channel_id=1, source_target_pairs={{0,1},{1,0},{2,3},{3,2},{4,5},{5,4},{6,7},{7,6},{8,9},{9,8},{10,11... | collective-permute-start | bytes 3145736 | tf_op jit(solution)/shard_map/ppermute | solution.py:656
  405.7 26.3 %collective-permute-start.21 = (bf16[256,2048]{1,0:T(8,128)(2,1)S(1)}, bf16[256,2048]{1,0:T(8,128)(2,1)S(1)}, u32[]{:S(2)}, u32[]{:S(2)}) collective-permute-start(bf16[256,2048]{1,0:T(8,128)(2,1)S(1)} %fusion.4), channel_id=1, source_target_pairs={{0,48},{16,32},{32,16},{48,0},{1,49},{17,33},{33,17},{49,1},{2,50}... | collective-permute-start | bytes 3145736 | tf_op jit(solution)/shard_map/ppermute | solution.py:656
  412.6 22.2 %collective-permute-start.27 = (bf16[256,2048]{1,0:T(8,128)(2,1)S(1)}, bf16[256,2048]{1,0:T(8,128)(2,1)S(1)}, u32[]{:S(2)}, u32[]{:S(2)}) collective-permute-start(bf16[256,2048]{1,0:T(8,128)(2,1)S(1)} %fusion.5), channel_id=1, source_target_pairs={{0,12},{4,8},{8,4},{12,0},{1,13},{5,9},{9,5},{13,1},{2,14},{6,10},... | collective-permute-start | bytes 3145736 | tf_op jit(solution)/shard_map/ppermute | solution.py:656
  417.3 19.9 %collective-permute-start.33 = (bf16[512,1024]{1,0:T(8,128)(2,1)S(1)}, bf16[512,1024]{1,0:T(8,128)(2,1)S(1)}, u32[]{:S(2)}, u32[]{:S(2)}) collective-permute-start(bf16[512,1024]{1,0:T(8,128)(2,1)S(1)} %add_convert_fusion.3), channel_id=1, source_target_pairs={{0,3},{1,2},{2,1},{3,0},{4,7},{5,6},{6,5},{7,4},{8,11},{9,10},{10,... | collective-permute-start | bytes 3145736 | tf_op jit(solution)/shard_map/ppermute | solution.py:656
  420.0 21.0 %collective-permute-start.9 = (bf16[256,2176]{1,0:T(8,128)(2,1)S(1)}, bf16[256,2176]{1,0:T(8,128)(2,1)S(1)}, u32[]{:S(2)}, u32[]{:S(2)}) collective-permute-start(bf16[256,2176]{1,0:T(8,128)(2,1)S(1)} %add_convert_fusion.1), channel_id=1, source_target_pairs={{0,4},{4,0},{8,12},{12,8},{1,5},{5,1},{9,13},{13,9},{2,6},{6,2},{1... | collective-permute-start | bytes 3342344 | tf_op jit(solution)/shard_map/ppermute | solution.py:656
  428.8 15.5 %collective-permute-start.4 = (bf16[128,2048]{1,0:T(8,128)(2,1)S(1)}, bf16[128,2048]{1,0:T(8,128)(2,1)S(1)}, u32[]{:S(2)}, u32[]{:S(2)}) collective-permute-start(bf16[128,2048]{1,0:T(8,128)(2,1)S(1)} %bitcast.381), channel_id=1, source_target_pairs={{0,12},{4,8},{8,4},{12,0},{1,13},{5,9},{9,5},{13,1},{2,14},{6,10},... | collective-permute-start | bytes 1572872 | tf_op jit(solution)/shard_map/ppermute | solution.py:653
  432.1 14.8 %collective-permute-start.16 = (bf16[256,1024]{1,0:T(8,128)(2,1)S(1)}, bf16[256,1024]{1,0:T(8,128)(2,1)S(1)}, u32[]{:S(2)}, u32[]{:S(2)}) collective-permute-start(bf16[256,1024]{1,0:T(8,128)(2,1)S(1)} %bitcast.382), channel_id=1, source_target_pairs={{0,48},{16,32},{32,16},{48,0},{1,49},{17,33},{33,17},{49,1},{2,50}... | collective-permute-start | bytes 1572872 | tf_op jit(solution)/shard_map/ppermute | solution.py:653
  434.8 14.3 %collective-permute-start.22 = (bf16[128,2048]{1,0:T(8,128)(2,1)S(1)}, bf16[128,2048]{1,0:T(8,128)(2,1)S(1)}, u32[]{:S(2)}, u32[]{:S(2)}) collective-permute-start(bf16[128,2048]{1,0:T(8,128)(2,1)S(1)} %bitcast.383), channel_id=1, source_target_pairs={{0,4},{4,0},{8,12},{12,8},{1,5},{5,1},{9,13},{13,9},{2,6},{6,2},{1... | collective-permute-start | bytes 1572872 | tf_op jit(solution)/shard_map/ppermute | solution.py:653
  437.2 12.8 %collective-permute-start.28 = (bf16[128,2048]{1,0:T(8,128)(2,1)S(1)}, bf16[128,2048]{1,0:T(8,128)(2,1)S(1)}, u32[]{:S(2)}, u32[]{:S(2)}) collective-permute-start(bf16[128,2048]{1,0:T(8,128)(2,1)S(1)} %bitcast.384), channel_id=1, source_target_pairs={{0,1},{1,0},{2,3},{3,2},{4,5},{5,4},{6,7},{7,6},{8,9},{9,8},{10,11... | collective-permute-start | bytes 1572872 | tf_op jit(solution)/shard_map/ppermute | solution.py:653
  441.0 11.0 %collective-permute-start.34 = (bf16[256,1024]{1,0:T(8,128)(2,1)S(1)}, bf16[256,1024]{1,0:T(8,128)(2,1)S(1)}, u32[]{:S(2)}, u32[]{:S(2)}) collective-permute-start(bf16[256,1024]{1,0:T(8,128)(2,1)S(1)} %bitcast.385), channel_id=1, source_target_pairs={{0,16},{16,0},{32,48},{48,32},{1,17},{17,1},{33,49},{49,33},{2,18}... | collective-permute-start | bytes 1572872 | tf_op jit(solution)/shard_map/ppermute | solution.py:653
  444.3 10.8 %collective-permute-start.10 = (bf16[128,2176]{1,0:T(8,128)(2,1)S(1)}, bf16[128,2176]{1,0:T(8,128)(2,1)S(1)}, u32[]{:S(2)}, u32[]{:S(2)}) collective-permute-start(bf16[128,2176]{1,0:T(8,128)(2,1)S(1)} %bitcast.375), channel_id=1, source_target_pairs={{0,3},{1,2},{2,1},{3,0},{4,7},{5,6},{6,5},{7,4},{8,11},{9,10},{10,... | collective-permute-start | bytes 1671176 | tf_op jit(solution)/shard_map/ppermute | solution.py:653
  446.9 10.6 %collective-permute-start.5 = (bf16[64,2048]{1,0:T(8,128)(2,1)S(1)}, bf16[64,2048]{1,0:T(8,128)(2,1)S(1)}, u32[]{:S(2)}, u32[]{:S(2)}) collective-permute-start(bf16[64,2048]{1,0:T(8,128)(2,1)S(1)} %fusion.36), channel_id=1, source_target_pairs={{0,4},{4,0},{8,12},{12,8},{1,5},{5,1},{9,13},{13,9},{2,6},{6,2},{1... | collective-permute-start | bytes 786440 | tf_op jit(solution)/shard_map/ppermute | solution.py:656
  449.9 10.7 %collective-permute-start.23 = (bf16[64,2048]{1,0:T(8,128)(2,1)S(1)}, bf16[64,2048]{1,0:T(8,128)(2,1)S(1)}, u32[]{:S(2)}, u32[]{:S(2)}) collective-permute-start(bf16[64,2048]{1,0:T(8,128)(2,1)S(1)} %fusion.30), channel_id=1, source_target_pairs={{0,12},{4,8},{8,4},{12,0},{1,13},{5,9},{9,5},{13,1},{2,14},{6,10},... | collective-permute-start | bytes 786440 | tf_op jit(solution)/shard_map/ppermute | solution.py:656
  452.0 10.2 %collective-permute-start.29 = (bf16[64,2048]{1,0:T(8,128)(2,1)S(1)}, bf16[64,2048]{1,0:T(8,128)(2,1)S(1)}, u32[]{:S(2)}, u32[]{:S(2)}) collective-permute-start(bf16[64,2048]{1,0:T(8,128)(2,1)S(1)} %fusion.27), channel_id=1, source_target_pairs={{0,3},{1,2},{2,1},{3,0},{4,7},{5,6},{6,5},{7,4},{8,11},{9,10},{10,... | collective-permute-start | bytes 786440 | tf_op jit(solution)/shard_map/ppermute | solution.py:656
  457.5 21.3 %collective-permute-start.11 = (bf16[64,2176]{1,0:T(8,128)(2,1)S(1)}, bf16[64,2176]{1,0:T(8,128)(2,1)S(1)}, u32[]{:S(2)}, u32[]{:S(2)}) collective-permute-start(bf16[64,2176]{1,0:T(8,128)(2,1)S(1)} %fusion.21), channel_id=1, source_target_pairs={{0,1},{1,0},{2,3},{3,2},{4,5},{5,4},{6,7},{7,6},{8,9},{9,8},{10,11... | collective-permute-start | bytes 835592 | tf_op jit(solution)/shard_map/ppermute | solution.py:656
  (67 other events, 693.2 us)
Sparse Core Ops, SparseCore 0:
  17.2 138.0 all-gather.2

commit v3 on v2

--- a/solution.py
+++ b/solution.py
@@ -1,3 +1,5 @@
+import functools
+
 import jax
 import jax.numpy as jnp
 from jax import lax
@@ -290,9 +292,19 @@
 def forward_kernel(
     x, packed, dt_weight, out_weight, heads_weight, input_gain, kernel, bias, step_bias, decay_log, skip,
     mixer_gain, feed_gain, cosine, sine,
+    result_out, normed_out, proj_out, ssm_out, mamba_out, attended_out, middle_out, ffin_out, gate_out,
+    upper_out, hidden_out,
     result, normed, proj, ssm, mamba, attended, middle, ffin, gate, upper, hidden,
-    cat, gate_up, down, out_mat, heads_mat, sems,
+    cat, gate_up, down, out_mat, heads_mat, sems, out_sems,
 ):
+    leaving = []
+
+    def leave(*pairs):
+        for source, target in pairs:
+            copy = pltpu.make_async_copy(source, target, out_sems.at[len(leaving)])
+            copy.start()
+            leaving.append(copy)
+
     copies = [
         pltpu.make_async_copy(packed.at[:, pl.ds(16 * j, 16), :], cat.at[j], sems.at[j])
         for j in range(4)
@@ -320,6 +332,7 @@
             return carry
 
         lax.fori_loop(0, 4, columns, 0)
+    leave((normed, normed_out), (proj, proj_out))
 
     def sequence(index, carry):
         rows = pl.ds(pl.multiple_of(index * LEN, LEN), LEN)
@@ -328,6 +341,7 @@
         return carry
 
     lax.fori_loop(0, 2, sequence, 0)
+    leave((ssm, ssm_out), (mamba, mamba_out), (attended, attended_out))
     copies[4].wait()
     copies[5].wait()
 
@@ -340,6 +354,7 @@
     lax.fori_loop(0, 4, joined, 0)
     value = middle[...]
     ffin[...] = (value * rms(value) * feed_gain[...]).astype(BF16)
+    leave((middle, middle_out), (ffin, ffin_out))
     for j in range(2):
         copies[6 + j].wait()
         copies[8 + j].wait()
@@ -355,6 +370,7 @@
             return carry
 
         lax.fori_loop(0, 4, feed, 0)
+    leave((gate, gate_out), (upper, upper_out), (hidden, hidden_out))
     copies[10].wait()
 
     def last(tile, carry):
@@ -363,22 +379,49 @@
         return carry
 
     lax.fori_loop(0, 4, last, 0)
-
-
-def feed_backward_kernel(
-    grad_top, packed, gate, upper, middle, feed_gain,
+    leave((result, result_out))
+    for copy in leaving:
+        copy.wait()
+
+
+def leave_all(pairs, sems):
+    copies = [
+        pltpu.make_async_copy(source, target, sems.at[k]) for k, (source, target) in enumerate(pairs)
+    ]
+    start_all(copies)
+    return copies
+
+
+def feed_backward_kernel(earlier, active, *refs):
+    @pl.when(active[0] == 1)
+    def run():
+        feed_backward_body(*refs[:6], *refs[6 + earlier :])
+
+
+def feed_backward_body(
+    grad_top, packed, gate_in, upper_in, middle_in, feed_gain,
+    grad_gate_out, grad_upper_out, grad_middle_out, feed_grad_out,
     grad_gate, grad_upper, grad_middle, feed_grad,
-    gate_up, down, grad_ffin, sems,
+    gate, upper, middle, gate_up, down, grad_ffin, sems, out_sems,
 ):
-    copies = [pltpu.make_async_copy(packed.at[:, pl.ds(DOWN0, 32), :], down, sems.at[4])]
+    inputs = [
+        pltpu.make_async_copy(gate_in, gate, sems.at[5]),
+        pltpu.make_async_copy(upper_in, upper, sems.at[6]),
+        pltpu.make_async_copy(middle_in, middle, sems.at[7]),
+    ]
+    copies = [
+        pltpu.make_async_copy(packed.at[:, pl.ds(DOWN0, 32), :], down, sems.at[4]),
+    ]
     for j in range(4):
         copies.append(
             pltpu.make_async_copy(
                 packed.at[:, pl.ds(GATE0 + 16 * j, 16), :], gate_up.at[j], sems.at[j]
             )
         )
-    start_all(copies)
+    start_all(copies[:1] + inputs + copies[1:])
     copies[0].wait()
+    for copy in inputs:
+        copy.wait()
 
     def through(tile, carry):
         at = pl.ds(pl.multiple_of(tile * 256, 256), 256)
@@ -392,6 +435,7 @@
         return carry
 
     lax.fori_loop(0, 8, through, 0)
+    leaving = leave_all(((grad_gate, grad_gate_out), (grad_upper, grad_upper_out)), out_sems)
     for copy in copies[1:]:
         copy.wait()
 
@@ -410,23 +454,36 @@
     grad_part, grad_gain = rms_backward(middle[...], feed_gain[...], grad_ffin[...])
     feed_grad[...] = grad_gain
     grad_middle[...] = grad_top[...].astype(F32) + grad_part
-
-
-def mix_backward_kernel(
-    grad_middle, x, packed, dt_weight, out_weight, heads_weight, proj, ssm, input_gain, kernel, bias,
+    leaving += leave_all(
+        ((grad_middle, grad_middle_out), (feed_grad, feed_grad_out)), out_sems.at[pl.ds(2, 2)]
+    )
+    for copy in leaving:
+        copy.wait()
+
+
+def mix_backward_kernel(earlier, active, *refs):
+    @pl.when(active[0] == 1)
+    def run():
+        mix_backward_body(*refs[:14], *refs[14 + earlier :])
+
+
+def mix_backward_body(
+    grad_middle, out_weight, heads_weight, proj_in, ssm_in, kernel, bias,
     step_bias, decay_log, skip, mixer_gain, cosine, sine, pick,
-    grad_branch, grad_cat, grad_start, input_grad, kernel_grad, bias_grad, step_grad, decay_grad,
+    grad_branch_out, grad_cat_out, kernel_grad_out, bias_grad_out,
+    step_grad_out, decay_grad_out, skip_grad_out, mixer_grad_out,
+    grad_branch, grad_cat, kernel_grad, bias_grad, step_grad, decay_grad,
     skip_grad, mixer_grad,
-    cat, out_mat, heads_mat, grad_mamba, grad_attended, balance, touch, grad_active, grad_normed, sems,
+    proj, ssm,
+    out_mat, heads_mat, grad_mamba, grad_attended, balance, touch, grad_active, sems,
+    out_sems,
 ):
     copies = [
-        pltpu.make_async_copy(out_weight, out_mat, sems.at[4]),
-        pltpu.make_async_copy(heads_weight, heads_mat, sems.at[5]),
+        pltpu.make_async_copy(out_weight, out_mat, sems.at[0]),
+        pltpu.make_async_copy(heads_weight, heads_mat, sems.at[1]),
+        pltpu.make_async_copy(proj_in, proj, sems.at[2]),
+        pltpu.make_async_copy(ssm_in, ssm, sems.at[3]),
     ]
-    for j in range(4):
-        copies.append(
-            pltpu.make_async_copy(packed.at[:, pl.ds(16 * j, 16), :], cat.at[j], sems.at[j])
-        )
     start_all(copies)
     grad_branch[...] = grad_middle[...].astype(BF16)
     copies[0].wait()
@@ -459,6 +516,9 @@
     def add_small(slot, value):
         small[slot][...] += value
 
+    copies[2].wait()
+    copies[3].wait()
+
     def sequence(index, carry):
         rows = pl.ds(pl.multiple_of(index * LEN, LEN), LEN)
         grads = grad_attended[rows, :]
@@ -470,7 +530,41 @@
         return carry
 
     lax.fori_loop(0, 2, sequence, 0)
-    for copy in copies[2:]:
+    leaving = leave_all(
+        (
+            (grad_branch, grad_branch_out),
+            (grad_cat, grad_cat_out),
+            (kernel_grad, kernel_grad_out),
+            (bias_grad, bias_grad_out),
+            (step_grad, step_grad_out),
+            (decay_grad, decay_grad_out),
+            (skip_grad, skip_grad_out),
+            (mixer_grad, mixer_grad_out),
+        ),
+        out_sems,
+    )
+    for copy in leaving:
+        copy.wait()
+
+
+def input_backward_kernel(earlier, active, *refs):
+    @pl.when(active[0] == 1)
+    def run():
+        input_backward_body(*refs[:6], *refs[6 + earlier :])
+
+
+def input_backward_body(
+    grad_cat, grad_middle, x, packed, dt_weight, input_gain,
+    grad_start_out, input_grad_out,
+    grad_start, input_grad,
+    cat, grad_normed, sems, out_sems,
+):
+    copies = [
+        pltpu.make_async_copy(packed.at[:, pl.ds(16 * j, 16), :], cat.at[j], sems.at[j])
+        for j in range(4)
+    ]
+    start_all(copies)
+    for copy in copies:
         copy.wait()
 
     def back(tile, carry):
@@ -487,9 +581,13 @@
     grad_state, grad_gain = rms_backward(state, input_gain[...], grad_normed[...])
     input_grad[...] = grad_gain
     grad_start[...] = grad_middle[...] + grad_state
+    leaving = leave_all(((grad_start, grad_start_out), (input_grad, input_grad_out)), out_sems)
+    for copy in leaving:
+        copy.wait()
 
 
 VMEM = pl.BlockSpec(memory_space=pltpu.VMEM)
+SMEM = pl.BlockSpec(memory_space=pltpu.SMEM)
 ANY = pl.BlockSpec(memory_space=pl.ANY)
 LIMIT = 60 * 1024 * 1024
 
@@ -502,33 +600,39 @@
     return pltpu.VMEM(dims, dtype)
 
 
+def mirrored(shapes):
+    return [pltpu.VMEM(s.shape, s.dtype) for s in shapes]
+
+
 def run_forward(start, mats, small, rope):
     packed, dt_weight, out_weight, heads_weight = mats
-    input_gain, kernel, bias, step_bias, decay_log, skip, mixer_gain, feed_gain = small
+    shapes = (
+        shape(ROWS, WIDTH, BF16),
+        shape(ROWS, WIDTH, BF16),
+        shape(ROWS, CAT, F32),
+        shape(ROWS, INNER, F32),
+        shape(ROWS, INNER, BF16),
+        shape(ROWS, 512, BF16),
+        shape(ROWS, WIDTH, F32),
+        shape(ROWS, WIDTH, BF16),
+        shape(ROWS, FEED, F32),
+        shape(ROWS, FEED, F32),
+        shape(ROWS, FEED, BF16),
+    )
     return pl.pallas_call(
         forward_kernel,
-        out_shape=(
-            shape(ROWS, WIDTH, BF16),
-            shape(ROWS, WIDTH, BF16),
-            shape(ROWS, CAT, F32),
-            shape(ROWS, INNER, F32),
-            shape(ROWS, INNER, BF16),
-            shape(ROWS, 512, BF16),
-            shape(ROWS, WIDTH, F32),
-            shape(ROWS, WIDTH, BF16),
-            shape(ROWS, FEED, F32),
-            shape(ROWS, FEED, F32),
-            shape(ROWS, FEED, BF16),
-        ),
+        out_shape=shapes,
         in_specs=[VMEM, ANY, VMEM, ANY, ANY] + [VMEM] * 10,
-        out_specs=(VMEM,) * 11,
+        out_specs=(ANY,) * len(shapes),
         scratch_shapes=[
+            *mirrored(shapes),
             scratch(4, 64, 16, 1024),
             scratch(4, 64, 16, 1024),
             scratch(64, 32, 1024),
             scratch(INNER, WIDTH),
             scratch(512, WIDTH),
             pltpu.SemaphoreType.DMA((11,)),
+            pltpu.SemaphoreType.DMA((len(shapes),)),
         ],
         compiler_params=pltpu.CompilerParams(vmem_limit_bytes=LIMIT),
         cost_estimate=pl.CostEstimate(
@@ -538,51 +642,59 @@
     )(start, packed, dt_weight, out_weight, heads_weight, *small, *rope)
 
 
-def run_feed_backward(grad_top, mats, gate, upper, middle, feed_gain):
+def run_feed_backward(active, grad_top, mats, gate, upper, middle, feed_gain, earlier=()):
+    shapes = (
+        shape(ROWS, FEED, BF16),
+        shape(ROWS, FEED, BF16),
+        shape(ROWS, WIDTH, F32),
+        shape(1, WIDTH, F32),
+    )
     return pl.pallas_call(
-        feed_backward_kernel,
-        out_shape=(
-            shape(ROWS, FEED, BF16),
-            shape(ROWS, FEED, BF16),
-            shape(ROWS, WIDTH, F32),
-            shape(1, WIDTH, F32),
-        ),
-        in_specs=[VMEM, ANY] + [VMEM] * 4,
-        out_specs=(VMEM,) * 4,
+        functools.partial(feed_backward_kernel, len(earlier)),
+        out_shape=shapes,
+        in_specs=[SMEM, VMEM, ANY, ANY, ANY, ANY, VMEM] + [ANY] * len(earlier),
+        out_specs=(ANY,) * len(shapes),
         scratch_shapes=[
+            *mirrored(shapes),
+            scratch(ROWS, FEED, dtype=F32),
+            scratch(ROWS, FEED, dtype=F32),
+            scratch(ROWS, WIDTH, dtype=F32),
             scratch(4, 64, 16, 1024),
             scratch(64, 32, 1024),
             scratch(ROWS, WIDTH, dtype=F32),
-            pltpu.SemaphoreType.DMA((5,)),
+            pltpu.SemaphoreType.DMA((8,)),
+            pltpu.SemaphoreType.DMA((4,)),
         ],
+        input_output_aliases={7 + k: k for k in range(len(earlier))},
         compiler_params=pltpu.CompilerParams(vmem_limit_bytes=LIMIT),
         cost_estimate=pl.CostEstimate(
             flops=2 * ROWS * 6_300_000, bytes_accessed=22_000_000, transcendentals=1_000_000
         ),
         name="feed_backward",
-    )(grad_top, mats[0], gate, upper, middle, feed_gain)
-
-
-def run_mix_backward(grad_middle, start, mats, proj, ssm, small, rope, pick):
+    )(active, grad_top, mats[0], gate, upper, middle, feed_gain, *earlier)
+
+
+def run_mix_backward(active, grad_middle, mats, proj, ssm, small, rope, pick, earlier=()):
     packed, dt_weight, out_weight, heads_weight = mats
+    shapes = (
+        shape(ROWS, WIDTH, BF16),
+        shape(ROWS, CAT, BF16),
+        shape(4, MIXED, F32),
+        shape(1, MIXED, F32),
+        shape(1, 128, F32),
+        shape(1, 128, F32),
+        shape(1, INNER, F32),
+        shape(1, INNER, F32),
+    )
     return pl.pallas_call(
-        mix_backward_kernel,
-        out_shape=(
-            shape(ROWS, WIDTH, BF16),
-            shape(ROWS, CAT, BF16),
-            shape(ROWS, WIDTH, F32),
-            shape(1, WIDTH, F32),
-            shape(4, MIXED, F32),
-            shape(1, MIXED, F32),
-            shape(1, 128, F32),
-            shape(1, 128, F32),
-            shape(1, INNER, F32),
-            shape(1, INNER, F32),
-        ),
-        in_specs=[VMEM, VMEM, ANY, VMEM, ANY, ANY] + [VMEM] * 12,
-        out_specs=(VMEM,) * 10,
+        functools.partial(mix_backward_kernel, len(earlier)),
+        out_shape=shapes,
+        in_specs=[SMEM, VMEM] + [ANY] * 4 + [VMEM] * 9 + [ANY] * len(earlier),
+        out_specs=(ANY,) * len(shapes),
         scratch_shapes=[
-            scratch(4, 64, 16, 1024),
+            *mirrored(shapes),
+            scratch(ROWS, CAT, dtype=F32),
+            scratch(ROWS, INNER, dtype=F32),
             scratch(INNER, WIDTH),
             scratch(512, WIDTH),
             scratch(ROWS, INNER, dtype=F32),
@@ -590,17 +702,41 @@
             scratch(LEN, INNER, dtype=F32),
             scratch(LEN, INNER, dtype=F32),
             scratch(LEN, MIXED, dtype=F32),
-            scratch(ROWS, WIDTH, dtype=F32),
-            pltpu.SemaphoreType.DMA((6,)),
+            pltpu.SemaphoreType.DMA((4,)),
+            pltpu.SemaphoreType.DMA((8,)),
         ],
+        input_output_aliases={15 + k: k for k in range(len(earlier))},
         compiler_params=pltpu.CompilerParams(vmem_limit_bytes=LIMIT),
         cost_estimate=pl.CostEstimate(
-            flops=2 * ROWS * 6_300_000, bytes_accessed=25_000_000, transcendentals=4_000_000
+            flops=2 * ROWS * 2_100_000, bytes_accessed=14_000_000, transcendentals=4_000_000
         ),
         name="mix_backward",
     )(
-        grad_middle, start, packed, dt_weight, out_weight, heads_weight, proj, ssm, *small[:7], *rope, pick
-    )
+        active, grad_middle, out_weight, heads_weight, proj, ssm, *small[1:7], *rope, pick, *earlier
+    )
+
+
+def run_input_backward(active, grad_cat, grad_middle, start, mats, input_gain, earlier=()):
+    shapes = (shape(ROWS, WIDTH, F32), shape(1, WIDTH, F32))
+    return pl.pallas_call(
+        functools.partial(input_backward_kernel, len(earlier)),
+        out_shape=shapes,
+        in_specs=[SMEM, VMEM, VMEM, VMEM, ANY, VMEM, VMEM] + [ANY] * len(earlier),
+        out_specs=(ANY,) * len(shapes),
+        scratch_shapes=[
+            *mirrored(shapes),
+            scratch(4, 64, 16, 1024),
+            scratch(ROWS, WIDTH, dtype=F32),
+            pltpu.SemaphoreType.DMA((4,)),
+            pltpu.SemaphoreType.DMA((2,)),
+        ],
+        input_output_aliases={7 + k: k for k in range(len(earlier))},
+        compiler_params=pltpu.CompilerParams(vmem_limit_bytes=LIMIT),
+        cost_estimate=pl.CostEstimate(
+            flops=2 * ROWS * 4_200_000, bytes_accessed=13_000_000, transcendentals=1000
+        ),
+        name="input_backward",
+    )(active, grad_cat, grad_middle, start, *mats[:2], input_gain, *earlier)
 
 
 def rope_tables():
@@ -647,46 +783,55 @@
     return me, found, [[(i, table[i]) for i in range(4)] for table in order]
 
 
-def halved(part, axis, turn):
+def first_sent(part, axis, turn):
+    me, (one, two), swaps = partners(axis, turn)
+    return part([one, lax.rem(me + 2, 4)]).astype(BF16)
+
+
+def first_got(sent, axis, turn):
+    return lax.ppermute(sent, axis, partners(axis, turn)[2][0])
+
+
+def exchanged(part, got, axis, turn):
     me, (one, two), (swap_one, swap_two) = partners(axis, turn)
-    sent = part([one, lax.rem(me + 2, 4)])
-    got = lax.ppermute(sent.astype(BF16), axis, swap_one)
     half = got.shape[0] // 2
     handed = part([two]) + got[half:].astype(F32)
     last = lax.ppermute(handed.astype(BF16), axis, swap_two)
     return part([me]) + got[:half].astype(F32) + last.astype(F32)
 
 
-def scattered(left, right, order, turn):
-    depth = left.shape[0] // 64
-    blocks = left.reshape(4, 4, 4, depth, left.shape[1])
-
-    def product(places):
-        picked = [lax.dynamic_index_in_dim(blocks, p, order[0], keepdims=False) for p in places]
+def product_of(left, right, place):
+    blocks = left.reshape(4, 4, 4, left.shape[0] // 64, left.shape[1])
+
+    def part(places):
+        picked = [lax.dynamic_index_in_dim(blocks, p, place, keepdims=False) for p in places]
         return dot(jnp.concatenate(picked, axis=0).reshape(-1, left.shape[1]), right)
 
-    array = halved(product, DP[order[0]], turn).astype(BF16)
-    array = array.reshape(4, 4, depth, right.shape[1])
+    return part
+
+
+def quarters_of(array, dim):
+    def part(places):
+        picked = [lax.dynamic_index_in_dim(array, p, dim, keepdims=False) for p in places]
+        return jnp.concatenate(picked, axis=0).reshape(-1, array.shape[-1]).astype(F32)
+
+    return part
+
+
+def summed_on(array, axis, dim, turn):
+    part = quarters_of(array, dim)
+    got = first_got(first_sent(part, axis, turn), axis, turn)
+    return exchanged(part, got, axis, turn)
+
+
+def finished(parts, order, depth):
+    array = jnp.concatenate([p.astype(BF16) for p in parts], axis=1)
+    width = array.shape[1]
     rest = [0, 1, 2]
     rest.remove(order[0])
-
-    def quarters(array, dim):
-        def part(places):
-            picked = [lax.dynamic_index_in_dim(array, p, dim, keepdims=False) for p in places]
-            return jnp.concatenate(picked, axis=0).reshape(-1, array.shape[-1]).astype(F32)
-
-        return part
-
-    array = halved(quarters(array, rest.index(order[1])), DP[order[1]], turn).astype(BF16)
-    array = array.reshape(4, depth, right.shape[1])
-    return halved(quarters(array, 0), DP[order[2]], turn)
-
-
-def summed_over(vector):
-    for axis in DP:
-        for table in (FIRST, SECOND):
-            vector = vector + lax.ppermute(vector, axis, [(i, table[i]) for i in range(4)])
-    return vector
+    array = array.reshape(4, 4, depth, width)
+    array = summed_on(array, DP[order[1]], rest.index(order[1]), 0).astype(BF16)
+    return summed_on(array.reshape(4, depth, width), DP[order[2]], 0, 0)
 
 
 def column_blocks(matrix):
@@ -744,49 +889,76 @@
     kept_high = run_forward(start_high, mats, small, rope)
     layer_outputs = jnp.where(first, kept_low[0], kept_high[0]).reshape(1, micro, part, width)
 
-    def feed_backward(kept, grad_top):
-        result, normed, proj, ssm, mamba, attended, middle, ffin, gate, upper, hidden = kept
-        out = run_feed_backward(grad_top, mats, gate, upper, middle, small[7])
-        return (*out, grad_top, hidden.T, ffin.T)
-
-    def mix_backward(kept, start, grad_middle):
-        result, normed, proj, ssm, mamba, attended, middle, ffin, gate, upper, hidden = kept
-        out = run_mix_backward(grad_middle, start, mats, proj, ssm, small, rope, pick)
-        joined = jnp.concatenate(
-            [mamba.T.reshape(64, 24, rows), attended.T.reshape(64, 8, rows)], axis=1
+    on_high = jnp.where(first, 0, 1).astype(jnp.int32).reshape(1)
+    on_low = 1 - on_high
+    top_high = out_grad.reshape(rows, width)
+    feed_high = run_feed_backward(
+        on_high, top_high, mats, kept_high[8], kept_high[9], kept_high[6], small[7]
+    )
+    mix_high = run_mix_backward(
+        on_high, feed_high[2], mats, kept_high[2], kept_high[3], small, rope, pick
+    )
+    input_high = run_input_backward(
+        on_high, mix_high[1], feed_high[2], start_high, mats, small[0]
+    )
+    top_low = lax.ppermute(input_high[0].astype(BF16), "section", [(1, 0)])
+
+    def chosen(slot):
+        return jnp.where(first, kept_low[slot], kept_high[slot])
+
+    normed_t, ffin_t, hidden_t = (chosen(slot).T for slot in (1, 7, 10))
+    joined_t = jnp.concatenate(
+        [chosen(4).T.reshape(64, 24, rows), chosen(5).T.reshape(64, 8, rows)], axis=1
+    ).reshape(2048, rows)
+
+    feed = run_feed_backward(
+        on_low, top_low, mats, kept_low[8], kept_low[9], kept_low[6], small[7], feed_high
+    )
+    grad_gate, grad_upper, grad_middle, feed_grad = feed
+    grad_low = jnp.where(first, top_low, top_high)
+    orders = ((2, 0, 1), (0, 1, 2), (1, 2, 0))
+    products = [
+        product_of(left, right, order[0])
+        for left, right, order in zip(
+            (hidden_t, ffin_t, ffin_t), (grad_low, grad_gate, grad_upper), orders
         )
-        return (*out, normed.T, joined.reshape(2048, rows))
-
-    top = out_grad.reshape(rows, width)
-    feed_high = feed_backward(kept_high, top)
-    mix_high = mix_backward(kept_high, start_high, feed_high[2])
-    top = lax.ppermute(mix_high[2].astype(BF16), "section", [(1, 0)])
-    feed = lax.cond(
-        first,
-        lambda kept, grad, other: feed_backward(kept, grad),
-        lambda kept, grad, other: other,
-        kept_low,
-        top,
-        feed_high,
-    )
-    grad_gate, grad_upper, grad_middle, feed_grad, grad_low, hidden_t, ffin_t = feed
-    down_grad = scattered(hidden_t, grad_low, (2, 0, 1), 0)
-    gate_grad = scattered(ffin_t, grad_gate, (0, 1, 2), 0)
-    up_grad = scattered(ffin_t, grad_upper, (1, 2, 0), 0)
-    mix = lax.cond(
-        first,
-        lambda kept, start, grad, other: mix_backward(kept, start, grad),
-        lambda kept, start, grad, other: other,
-        kept_low,
-        start_low,
-        grad_middle,
-        mix_high,
-    )
-    grad_branch, grad_cat, grad_start, *small_grads, normed_t, joined_t = mix
-    joined_grad = scattered(joined_t, grad_branch, (2, 0, 1), 1)
-    cat_left = scattered(normed_t, grad_cat[:, :2048], (0, 1, 2), 1)
-    cat_right = scattered(normed_t, grad_cat[:, 2048:], (1, 2, 0), 1)
-    cat_grad = jnp.concatenate([cat_left, cat_right], axis=1)
+    ]
+    sents = [first_sent(p, DP[order[0]], 0) for p, order in zip(products, orders)]
+    grad_middle, *sents = lax.optimization_barrier((grad_middle, *sents))
+    gots = [first_got(sent, DP[order[0]], 0) for sent, order in zip(sents, orders)]
+    mix = run_mix_backward(
+        on_low, grad_middle, mats, kept_low[2], kept_low[3], small, rope, pick, mix_high
+    )
+    grad_branch, grad_cat, *small_grads = mix
+    grad_branch, grad_cat, *gots = lax.optimization_barrier((grad_branch, grad_cat, *gots))
+    feed_parts = [
+        exchanged(p, got, DP[order[0]], 0) for p, got, order in zip(products, gots, orders)
+    ]
+    products = [
+        product_of(left, right, order[0])
+        for left, right, order in zip(
+            (joined_t, normed_t, normed_t),
+            (grad_branch, grad_cat[:, :2048], grad_cat[:, 2048:]),
+            orders,
+        )
+    ]
+    sents = [first_sent(p, DP[order[0]], 1) for p, order in zip(products, orders)]
+    grad_middle, *sents = lax.optimization_barrier((grad_middle, *sents))
+    mix_parts = []
+    for p, sent, order in zip(products, sents, orders):
+        got = first_got(sent, DP[order[0]], 1)
+        mix_parts.append(exchanged(p, got, DP[order[0]], 1))
+    grad_start, input_grad = run_input_backward(
+        on_low, grad_cat, grad_middle, start_low, mats, small[0], input_high
+    )
+    small_grads = [input_grad, *small_grads]
+    rows_grad, gate_cat, up_cat = (
+        finished(pair, order, depth)
+        for pair, order, depth in zip(zip(feed_parts, mix_parts), orders, (32, 16, 16))
+    )
+    down_grad, joined_grad = rows_grad[:, :WIDTH], rows_grad[:, WIDTH:]
+    gate_grad, up_grad = gate_cat[:, :FEED], up_cat[:, :FEED]
+    cat_grad = jnp.concatenate([gate_cat[:, FEED:], up_cat[:, FEED:]], axis=1)
 
     input_g, kernel_g, bias_g, step_g, decay_g, skip_g, mixer_g = small_grads
     small_grads = (
@@ -801,7 +973,7 @@
     )
     vector = jnp.concatenate([piece.reshape(-1) for piece in small_grads])
     vector = jnp.pad(vector, (0, -vector.shape[0] % 1024)).reshape(-1, 128)
-    total = summed_over(vector).reshape(-1)
+    total = jnp.sum(lax.all_gather(vector, DP, axis=0, tiled=False), axis=0).reshape(-1)
     summed, at = ([], 0)
     for piece in small_grads:
         summed.append(total[at : at + piece.size].reshape(1, *piece.shape))

time: 505 us -> 512 us (1.014)
  waiting for transfers between devices: 179 us -> 265 us
  Pallas kernels: 123 us -> 90.6 us
  starting transfers between devices: 66.5 us -> 36.5 us
  local copies, waits for them, and re-layouts: 57.2 us -> 38.2 us
  matrix products: 33.6 us -> 40.5 us
    ppermute x43 -> x25, waiting for transfers between devices: 42.9 us -> 130 us  [the longest x12 61.6 us: exchanged(): last = lax.ppermute(handed.astype(BF16), axis, swap_two)]
    pallas_call x6 -> x8, Pallas kernels: 123 us -> 90.6 us  [the longest x2 43.9 us: run_forward(): pl.pallas_call(forward_kernel, out_shape=shapes, in_specs=[VMEM, ANY, VME...]
    ppermute x43 -> x25, starting transfers between devices: 63.4 us -> 34.1 us  [the longest x12 17.3 us: exchanged(): last = lax.ppermute(handed.astype(BF16), axis, swap_two)]
    unnamed x104 -> x102, local copies, waits for them, and re-layouts: 16.5 us -> 8.53 us
    dot_general x18, matrix products: 33.6 us -> 40.5 us  [dot(): return jnp.dot(left, right, preferred_element_type=F32)]
    cond x9 -> x0, local copies, waits for them, and re-layouts: 5.92 us -> none
    convert_element_type x23 -> x12, other arithmetic: 10.5 us -> 7.55 us  [the longest x2 3.94 us: finished(): array = jnp.concatenate([p.astype(BF16) for p in parts], axis=1)]
  transfers between devices with their start and end apart: 45 -> 28, of which waited for: 14 -> 17; matrix products, arithmetic and copies ran while one was open for 13% -> 11% of each run, Pallas kernels for 0% -> 6%
where the time goes in v3:
time: 512 us; the launch traced here: 505 us
  waiting for transfers between devices  265 us (52%)
  Pallas kernels  90.6 us (18%)
  matrix products  40.5 us (8%)
  local copies, waits for them, and re-layouts  38.2 us (7%)
  starting transfers between devices  36.5 us (7%)
  other arithmetic  19.6 us (4%)
  between operations  15.2 us (3%)
    all_gather x1, waiting for transfers between devices, on_device(): packed = lax.all_gather(own, DP, axis=0, tiled=False)  134 us
    ppermute x12, waiting for transfers between devices, exchanged(): last = lax.ppermute(handed.astype(BF16), axis, swap_two)  61.6 us
    pallas_call x2, Pallas kernels, run_forward(): pl.pallas_call(forward_kernel, out_shape=shapes, in_specs=[VMEM, ANY, VME...  43.9 us
    dot_general x18, matrix products, dot(): return jnp.dot(left, right, preferred_element_type=F32)  40.5 us
    ppermute x1, waiting for transfers between devices, on_device(): top_low = lax.ppermute(input_high[0].astype(BF16), 'section', [(1, 0)])  35 us
    ppermute x12, waiting for transfers between devices, first_got(): return lax.ppermute(sent, axis, partners(axis, turn)[2][0])  33.8 us
    pallas_call x2, Pallas kernels, run_mix_backward(): pl.pallas_call(functools.partial(mix_backward_kernel, len(earlier)), out_...  20.9 us
    ppermute x12, starting transfers between devices, exchanged(): last = lax.ppermute(handed.astype(BF16), axis, swap_two)  17.3 us
  transfers between devices with their start and end apart: 28, of which 17 were waited for; matrix products, arithmetic and copies ran while one was open for 11% of the time, Pallas kernels for 6%

profile of v3, /device:TPU:0, one launch (start us, length us, event | category | flops | bytes accessed | tf_op | source)
XLA Modules:
  0.0 505.3 jit_solution(5484783567864926149)
XLA Ops:
  19.9 134.3 %all-gather.6.cloned.1.call-done = bf16[12800,1024]{1,0:T(8,128)(2,1)} async-done(((bf16[200,1024]{1,0:T(8,128)(2,1)}), bf16[12800,1024]{1,0:T(8,128)(2,1)}) %all-gather.6.cloned.1.call-update) | async-done | bytes 26214416 | tf_op jit(solution)/shard_map/all_gather | solution.py:873
  157.8 3.8 slice.257
  162.7 22.0 %forward.2 = (bf16[256,1024]{1,0:T(8,128)(2,1)}, bf16[256,1024]{1,0:T(8,128)(2,1)}, f32[256,4224]{1,0:T(8,128)}, f32[256,1536]{1,0:T(8,128)}, bf16[256,1536]{1,0...) custom-call(bf16[256,1024]{1,0:T(8,128)(2,1)} %bitcast.256, ...), custom_call_target="tpu_custom_call" | custom-call | flops 6451200000 | bytes 40000000 | tf_op jit(solution)/shard_map/forward/pallas_call | solution.py:622
  189.9 22.0 %forward.3 = (bf16[256,1024]{1,0:T(8,128)(2,1)}, bf16[256,1024]{1,0:T(8,128)(2,1)}, f32[256,4224]{1,0:T(8,128)}, f32[256,1536]{1,0:T(8,128)}, bf16[256,1536]{1,0...) custom-call(bf16[256,1024]{1,0:T(8,128)(2,1)} %copy-done.11, ...), custom_call_target="tpu_custom_call" | custom-call | flops 6451200000 | bytes 40000000 | tf_op jit(solution)/shard_map/forward/pallas_call | solution.py:622
  224.5 35.0 %collective-permute-done.1.refs_0_ = bf16[256,1024]{1,0:T(8,128)(2,1)} collective-permute-done((bf16[256,1024]{1,0:T(8,128)(2,1)}, bf16[256,1024]{1,0:T(8,128)(2,1)}, u32[]{:S(2)}, u32[]{:S(2)}) %collective-permute-start.1) | collective-permute-done | bytes 524320 | tf_op jit(solution)/shard_map/ppermute | solution.py:904
  263.4 12.0 %feed_backward.3 = (bf16[256,2048]{1,0:T(8,128)(2,1)}, bf16[256,2048]{1,0:T(8,128)(2,1)}, f32[256,1024]{1,0:T(8,128)}, f32[1,1024]{1,0:T(1,128)}) custom-call(s32[1]{0:T(128)S(6)} %sub.23.active, bf16[256,1024]{1,0:T(8,128)(2,1)} %collective-permute-done.1.refs_0_, ...), custom_call_target="tpu_custom_call", output_to_operand_aliasing={{0}: (7, {}), {1}: (8, {}), {2}: (9, {}), {3}: (10, {})} | custom-call | flops 3225600000 | bytes 22000000 | tf_op jit(solution)/shard_map/feed_backward/pallas_call | solution.py:652
  275.5 3.3 convolution_convert_fusion.3
  290.4 19.1 %mix_backward.3 = (bf16[256,1024]{1,0:T(8,128)(2,1)}, bf16[256,4224]{1,0:T(8,128)(2,1)}, f32[4,1792]{1,0:T(4,128)}, f32[1,1792]{1,0:T(1,128)}, f32[1,128]{1,0:T(...) custom-call(s32[1]{0:T(128)S(6)} %sub.23.active, ...), custom_call_target="tpu_custom_call", output_to_operand_aliasing={{0}: (15, {}), {1}: (16, {}), {2}: (17, {}), {3}: (18, {}),... | custom-call | flops 1075200000 | bytes 14000000 | tf_op jit(solution)/shard_map/mix_backward/pallas_call | solution.py:689
  309.5 2.8 fusion.46
  312.3 7.1 %collective-permute-done.2 = bf16[1024,1024]{1,0:T(8,128)(2,1)} collective-permute-done((bf16[1024,1024]{1,0:T(8,128)(2,1)}, bf16[1024,1024]{1,0:T(8,128)(2,1)}, u32[]{:S(2)}, u32[]{:S(2)}) %collective-permute-start.2) | collective-permute-done | bytes 2097184 | tf_op jit(solution)/shard_map/ppermute | solution.py:792
  330.9 2.6 fusion.11
  334.6 2.6 fusion.9
  342.6 10.4 %input_backward.3 = (f32[256,1024]{1,0:T(8,128)}, f32[1,1024]{1,0:T(1,128)}) custom-call(s32[1]{0:T(128)S(6)} %sub.23.active, bf16[256,4224]{1,0:T(8,128)(2,1)} %get-tuple-element.120.refs_0_, f32[256,1024]{1,0:T(8,128)} %get-tuple-element.128.refs_0_.refs_1_, bf16[256,1024]{1,0:T(8,128)(2,1)} %bitcast.257, ...), custom_call_target="tpu_custom_call", output_to_operand_aliasing={{0}: (7, {}), {1}: (8, {})} | custom-call | flops 2150400000 | bytes 13000000 | tf_op jit(solution)/shard_map/input_backward/pallas_call | solution.py:721
  353.9 2.8 fusion.47
  356.7 2.7 add_convert_fusion.3
  366.2 12.0 %collective-permute-done.6 = bf16[512,2048]{1,0:T(8,128)(2,1)} collective-permute-done((bf16[512,2048]{1,0:T(8,128)(2,1)}, bf16[512,2048]{1,0:T(8,128)(2,1)}, u32[]{:S(2)}, u32[]{:S(2)}) %collective-permute-start.6) | collective-permute-done | bytes 2097184 | tf_op jit(solution)/shard_map/ppermute | solution.py:792
  380.0 9.8 %collective-permute-done.5 = bf16[256,2048]{1,0:T(8,128)(2,1)} collective-permute-done((bf16[256,2048]{1,0:T(8,128)(2,1)}, bf16[256,2048]{1,0:T(8,128)(2,1)}, u32[]{:S(2)}, u32[]{:S(2)}) %collective-permute-start.5) | collective-permute-done | bytes 1048608 | tf_op jit(solution)/shard_map/ppermute | solution.py:799
  392.2 8.6 %collective-permute-done.19 = bf16[512,1024]{1,0:T(8,128)(2,1)} collective-permute-done((bf16[512,1024]{1,0:T(8,128)(2,1)}, bf16[512,1024]{1,0:T(8,128)(2,1)}, u32[]{:S(2)}, u32[]{:S(2)}) %collective-permute-start.19) | collective-permute-done | bytes 1048608 | tf_op jit(solution)/shard_map/ppermute | solution.py:799
  411.2 23.5 %collective-permute-done.21 = bf16[512,1024]{1,0:T(8,128)(2,1)S(1)} collective-permute-done((bf16[512,1024]{1,0:T(8,128)(2,1)S(1)}, bf16[512,1024]{1,0:T(8,128)(2,1)S(1)}, u32[]{:S(2)}, u32[]{:S(2)}) %collective-permute-start.21) | collective-permute-done | bytes 1048608 | tf_op jit(solution)/shard_map/ppermute | solution.py:799
  437.2 4.2 collective-permute-done.14
  445.5 7.2 %collective-permute-done.8 = bf16[128,4096]{1,0:T(8,128)(2,1)S(1)} collective-permute-done((bf16[128,4096]{1,0:T(8,128)(2,1)S(1)}, bf16[128,4096]{1,0:T(8,128)(2,1)S(1)}, u32[]{:S(2)}, u32[]{:S(2)}) %collective-permute-start.8) | collective-permute-done | bytes 1048608 | tf_op jit(solution)/shard_map/ppermute | solution.py:792
  456.9 4.8 collective-permute-done.15
  466.5 6.0 %collective-permute-done.16 = bf16[64,4224]{1,0:T(8,128)(2,1)S(1)} collective-permute-done((bf16[64,4224]{1,0:T(8,128)(2,1)S(1)}, bf16[64,4224]{1,0:T(8,128)(2,1)S(1)}, u32[]{:S(2)}, u32[]{:S(2)}) %collective-permute-start.16) | collective-permute-done | bytes 540704 | tf_op jit(solution)/shard_map/ppermute | solution.py:799
  486.9 4.0 collective-permute-done.18
  (267 shorter events, 127.5 us)
Async XLA Ops:
  7.2 147.0 %all-gather.6.cloned.1.call-start = ((), (), s32[]{:S(2)}) async-start(), calls=%async_computation.1 | async-start | bytes 26624000 | tf_op jit(solution)/shard_map/all_gather | solution.py:873
  16.0 476.4 %all-gather.4.cloned.1.call-start = ((), (), s32[]{:S(2)}) async-start(), calls=%async_computation | async-start | bytes 3461120 | tf_op jit(solution)/shard_map/all_gather | solution.py:976
  219.7 39.8 %collective-permute-start.1 = (bf16[256,1024]{1,0:T(8,128)(2,1)}, bf16[256,1024]{1,0:T(8,128)(2,1)}, u32[]{:S(2)}, u32[]{:S(2)}) collective-permute-start(bf16[256,1024]{1,0:T(8,128)(2,1)} %convert_element_type.327), channel_id=1, source_target_pairs={{64,0},{65,1},{66,2},{67,3},{68,4},{69,5},{70,6},{71,7},{72,8},{73... | collective-permute-start | bytes 1572872 | tf_op jit(solution)/shard_map/ppermute | solution.py:904
  280.8 38.6 %collective-permute-start.2 = (bf16[1024,1024]{1,0:T(8,128)(2,1)}, bf16[1024,1024]{1,0:T(8,128)(2,1)}, u32[]{:S(2)}, u32[]{:S(2)}) collective-permute-start(bf16[1024,1024]{1,0:T(8,128)(2,1)} %convolution_convert_fusion.5), channel_id=1, source_target_pairs={{0,1},{1,0},{2,3},{3,2},{4,5},{5,4},{6,7},{7,6},{8,9},{9,8},{10,11... | collective-permute-start | bytes 6291464 | tf_op jit(solution)/shard_map/ppermute | solution.py:792
  282.3 38.7 %collective-permute-start.3 = (bf16[512,2048]{1,0:T(8,128)(2,1)}, bf16[512,2048]{1,0:T(8,128)(2,1)}, u32[]{:S(2)}, u32[]{:S(2)}) collective-permute-start(bf16[512,2048]{1,0:T(8,128)(2,1)} %convolution_convert_fusion.3), channel_id=1, source_target_pairs={{0,16},{16,0},{32,48},{48,32},{1,17},{17,1},{33,49},{49,33},{2,18}... | collective-permute-start | bytes 6291464 | tf_op jit(solution)/shard_map/ppermute | solution.py:792
  284.1 38.0 %collective-permute-start.4 = (bf16[512,2048]{1,0:T(8,128)(2,1)}, bf16[512,2048]{1,0:T(8,128)(2,1)}, u32[]{:S(2)}, u32[]{:S(2)}) collective-permute-start(bf16[512,2048]{1,0:T(8,128)(2,1)} %convolution_convert_fusion.2), channel_id=1, source_target_pairs={{0,4},{4,0},{8,12},{12,8},{1,5},{5,1},{9,13},{13,9},{2,6},{6,2},{1... | collective-permute-start | bytes 6291464 | tf_op jit(solution)/shard_map/ppermute | solution.py:792
  328.5 49.7 %collective-permute-start.6 = (bf16[512,2048]{1,0:T(8,128)(2,1)}, bf16[512,2048]{1,0:T(8,128)(2,1)}, u32[]{:S(2)}, u32[]{:S(2)}) collective-permute-start(bf16[512,2048]{1,0:T(8,128)(2,1)} %convolution_convert_fusion.1), channel_id=1, source_target_pairs={{0,48},{16,32},{32,16},{48,0},{1,49},{17,33},{33,17},{49,1},{2,50}... | collective-permute-start | bytes 6291464 | tf_op jit(solution)/shard_map/ppermute | solution.py:792
  333.5 27.6 %collective-permute-start.12 = (bf16[256,2048]{1,0:T(8,128)(2,1)}, bf16[256,2048]{1,0:T(8,128)(2,1)}, u32[]{:S(2)}, u32[]{:S(2)}) collective-permute-start(bf16[256,2048]{1,0:T(8,128)(2,1)} %fusion.11), channel_id=1, source_target_pairs={{0,12},{4,8},{8,4},{12,0},{1,13},{5,9},{9,5},{13,1},{2,14},{6,10},... | collective-permute-start | bytes 3145736 | tf_op jit(solution)/shard_map/ppermute | solution.py:799
  337.3 52.5 %collective-permute-start.5 = (bf16[256,2048]{1,0:T(8,128)(2,1)}, bf16[256,2048]{1,0:T(8,128)(2,1)}, u32[]{:S(2)}, u32[]{:S(2)}) collective-permute-start(bf16[256,2048]{1,0:T(8,128)(2,1)} %fusion.9), channel_id=1, source_target_pairs={{0,48},{16,32},{32,16},{48,0},{1,49},{17,33},{33,17},{49,1},{2,50}... | collective-permute-start | bytes 3145736 | tf_op jit(solution)/shard_map/ppermute | solution.py:799
  338.5 64.4 %collective-permute-start.20 = (bf16[1024,1024]{1,0:T(8,128)(2,1)}, bf16[1024,1024]{1,0:T(8,128)(2,1)}, u32[]{:S(2)}, u32[]{:S(2)}) collective-permute-start(bf16[1024,1024]{1,0:T(8,128)(2,1)} %convolution_convert_fusion.4), channel_id=1, source_target_pairs={{0,3},{1,2},{2,1},{3,0},{4,7},{5,6},{6,5},{7,4},{8,11},{9,10},{10,... | collective-permute-start | bytes 6291464 | tf_op jit(solution)/shard_map/ppermute | solution.py:792
  340.6 64.3 %collective-permute-start.13 = (bf16[512,2176]{1,0:T(8,128)(2,1)}, bf16[512,2176]{1,0:T(8,128)(2,1)}, u32[]{:S(2)}, u32[]{:S(2)}) collective-permute-start(bf16[512,2176]{1,0:T(8,128)(2,1)} %convolution_convert_fusion), channel_id=1, source_target_pairs={{0,12},{4,8},{8,4},{12,0},{1,13},{5,9},{9,5},{13,1},{2,14},{6,10},... | collective-permute-start | bytes 6684680 | tf_op jit(solution)/shard_map/ppermute | solution.py:792
  361.2 39.6 %collective-permute-start.19 = (bf16[512,1024]{1,0:T(8,128)(2,1)}, bf16[512,1024]{1,0:T(8,128)(2,1)}, u32[]{:S(2)}, u32[]{:S(2)}) collective-permute-start(bf16[512,1024]{1,0:T(8,128)(2,1)} %add_convert_fusion.3), channel_id=1, source_target_pairs={{0,3},{1,2},{2,1},{3,0},{4,7},{5,6},{6,5},{7,4},{8,11},{9,10},{10,... | collective-permute-start | bytes 3145736 | tf_op jit(solution)/shard_map/ppermute | solution.py:799
  379.9 26.9 %collective-permute-start.7 = (bf16[256,2048]{1,0:T(8,128)(2,1)S(1)}, bf16[256,2048]{1,0:T(8,128)(2,1)S(1)}, u32[]{:S(2)}, u32[]{:S(2)}) collective-permute-start(bf16[256,2048]{1,0:T(8,128)(2,1)S(1)} %fusion.10), channel_id=1, source_target_pairs={{0,16},{16,0},{32,48},{48,32},{1,17},{17,1},{33,49},{49,33},{2,18}... | collective-permute-start | bytes 3145736 | tf_op jit(solution)/shard_map/ppermute | solution.py:799
  404.6 30.1 %collective-permute-start.21 = (bf16[512,1024]{1,0:T(8,128)(2,1)S(1)}, bf16[512,1024]{1,0:T(8,128)(2,1)S(1)}, u32[]{:S(2)}, u32[]{:S(2)}) collective-permute-start(bf16[512,1024]{1,0:T(8,128)(2,1)S(1)} %add_convert_fusion.1), channel_id=1, source_target_pairs={{0,1},{1,0},{2,3},{3,2},{4,5},{5,4},{6,7},{7,6},{8,9},{9,8},{10,11... | collective-permute-start | bytes 3145736 | tf_op jit(solution)/shard_map/ppermute | solution.py:799
  406.7 34.7 %collective-permute-start.14 = (bf16[256,2176]{1,0:T(8,128)(2,1)S(1)}, bf16[256,2176]{1,0:T(8,128)(2,1)S(1)}, u32[]{:S(2)}, u32[]{:S(2)}) collective-permute-start(bf16[256,2176]{1,0:T(8,128)(2,1)S(1)} %fusion.2), channel_id=1, source_target_pairs={{0,4},{4,0},{8,12},{12,8},{1,5},{5,1},{9,13},{13,9},{2,6},{6,2},{1... | collective-permute-start | bytes 3342344 | tf_op jit(solution)/shard_map/ppermute | solution.py:799
  409.1 43.5 %collective-permute-start.8 = (bf16[128,4096]{1,0:T(8,128)(2,1)S(1)}, bf16[128,4096]{1,0:T(8,128)(2,1)S(1)}, u32[]{:S(2)}, u32[]{:S(2)}) collective-permute-start(bf16[128,4096]{1,0:T(8,128)(2,1)S(1)} %bitcast.270), channel_id=1, source_target_pairs={{0,4},{4,0},{8,12},{12,8},{1,5},{5,1},{9,13},{13,9},{2,6},{6,2},{1... | collective-permute-start | bytes 3145736 | tf_op jit(solution)/shard_map/ppermute | solution.py:792
  437.1 17.5 %collective-permute-start.22 = (bf16[256,2048]{1,0:T(8,128)(2,1)S(1)}, bf16[256,2048]{1,0:T(8,128)(2,1)S(1)}, u32[]{:S(2)}, u32[]{:S(2)}) collective-permute-start(bf16[256,2048]{1,0:T(8,128)(2,1)S(1)} %bitcast.271), channel_id=1, source_target_pairs={{0,16},{16,0},{32,48},{48,32},{1,17},{17,1},{33,49},{49,33},{2,18}... | collective-permute-start | bytes 3145736 | tf_op jit(solution)/shard_map/ppermute | solution.py:792
  443.7 18.0 %collective-permute-start.15 = (bf16[128,4224]{1,0:T(8,128)(2,1)S(1)}, bf16[128,4224]{1,0:T(8,128)(2,1)S(1)}, u32[]{:S(2)}, u32[]{:S(2)}) collective-permute-start(bf16[128,4224]{1,0:T(8,128)(2,1)S(1)} %bitcast.267), channel_id=1, source_target_pairs={{0,1},{1,0},{2,3},{3,2},{4,5},{5,4},{6,7},{7,6},{8,9},{9,8},{10,11... | collective-permute-start | bytes 3244040 | tf_op jit(solution)/shard_map/ppermute | solution.py:792
  452.8 11.3 %collective-permute-start.9 = (bf16[64,4096]{1,0:T(8,128)(2,1)S(1)}, bf16[64,4096]{1,0:T(8,128)(2,1)S(1)}, u32[]{:S(2)}, u32[]{:S(2)}) collective-permute-start(bf16[64,4096]{1,0:T(8,128)(2,1)S(1)} %fusion.18), channel_id=1, source_target_pairs={{0,12},{4,8},{8,4},{12,0},{1,13},{5,9},{9,5},{13,1},{2,14},{6,10},... | collective-permute-start | bytes 1572872 | tf_op jit(solution)/shard_map/ppermute | solution.py:799
  454.7 11.3 %collective-permute-start.23 = (bf16[128,2048]{1,0:T(8,128)(2,1)S(1)}, bf16[128,2048]{1,0:T(8,128)(2,1)S(1)}, u32[]{:S(2)}, u32[]{:S(2)}) collective-permute-start(bf16[128,2048]{1,0:T(8,128)(2,1)S(1)} %fusion.15), channel_id=1, source_target_pairs={{0,48},{16,32},{32,16},{48,0},{1,49},{17,33},{33,17},{49,1},{2,50}... | collective-permute-start | bytes 1572872 | tf_op jit(solution)/shard_map/ppermute | solution.py:799
  461.9 10.6 %collective-permute-start.16 = (bf16[64,4224]{1,0:T(8,128)(2,1)S(1)}, bf16[64,4224]{1,0:T(8,128)(2,1)S(1)}, u32[]{:S(2)}, u32[]{:S(2)}) collective-permute-start(bf16[64,4224]{1,0:T(8,128)(2,1)S(1)} %fusion.12), channel_id=1, source_target_pairs={{0,3},{1,2},{2,1},{3,0},{4,7},{5,6},{6,5},{7,4},{8,11},{9,10},{10,... | collective-permute-start | bytes 1622024 | tf_op jit(solution)/shard_map/ppermute | solution.py:799
  464.4 8.6 %collective-permute-start.10 = (bf16[32,4096]{1,0:T(8,128)(2,1)S(1)}, bf16[32,4096]{1,0:T(8,128)(2,1)S(1)}, u32[]{:S(2)}, u32[]{:S(2)}) collective-permute-start(bf16[32,4096]{1,0:T(8,128)(2,1)S(1)} %pad_maximum_fusion.13), channel_id=1, source_target_pairs={{0,1},{1,0},{2,3},{3,2},{4,5},{5,4},{6,7},{7,6},{8,9},{9,8},{10,11... | collective-permute-start | bytes 786440 | tf_op jit(solution)/shard_map/ppermute | solution.py:792
  466.4 9.2 %collective-permute-start.24 = (bf16[64,2048]{1,0:T(8,128)(2,1)S(1)}, bf16[64,2048]{1,0:T(8,128)(2,1)S(1)}, u32[]{:S(2)}, u32[]{:S(2)}) collective-permute-start(bf16[64,2048]{1,0:T(8,128)(2,1)S(1)} %pad_maximum_fusion.14), channel_id=1, source_target_pairs={{0,4},{4,0},{8,12},{12,8},{1,5},{5,1},{9,13},{13,9},{2,6},{6,2},{1... | collective-permute-start | bytes 786440 | tf_op jit(solution)/shard_map/ppermute | solution.py:792
  472.9 11.7 %collective-permute-start.17 = (bf16[32,4224]{1,0:T(8,128)(2,1)S(1)}, bf16[32,4224]{1,0:T(8,128)(2,1)S(1)}, u32[]{:S(2)}, u32[]{:S(2)}) collective-permute-start(bf16[32,4224]{1,0:T(8,128)(2,1)S(1)} %pad_maximum_fusion.8), channel_id=1, source_target_pairs={{0,16},{16,0},{32,48},{48,32},{1,17},{17,1},{33,49},{49,33},{2,18}... | collective-permute-start | bytes 811016 | tf_op jit(solution)/shard_map/ppermute | solution.py:792
  (49 other events, 384.5 us)
Sparse Core Ops, SparseCore 0:
  16.1 138.0 all-gather.5
  364.0 68.5 all-gather.3

commit v4 on v3

--- a/solution.py
+++ b/solution.py
@@ -555,8 +555,8 @@
 
 def input_backward_body(
     grad_cat, grad_middle, x, packed, dt_weight, input_gain,
-    grad_start_out, input_grad_out,
-    grad_start, input_grad,
+    grad_start_out, start_low_out, input_grad_out,
+    grad_start, start_low, input_grad,
     cat, grad_normed, sems, out_sems,
 ):
     copies = [
@@ -580,8 +580,13 @@
     state = x[...].astype(F32)
     grad_state, grad_gain = rms_backward(state, input_gain[...], grad_normed[...])
     input_grad[...] = grad_gain
-    grad_start[...] = grad_middle[...] + grad_state
-    leaving = leave_all(((grad_start, grad_start_out), (input_grad, input_grad_out)), out_sems)
+    total = grad_middle[...] + grad_state
+    grad_start[...] = total
+    start_low[...] = total.astype(BF16)
+    leaving = leave_all(
+        ((grad_start, grad_start_out), (start_low, start_low_out), (input_grad, input_grad_out)),
+        out_sems,
+    )
     for copy in leaving:
         copy.wait()
 
@@ -717,7 +722,7 @@
 
 
 def run_input_backward(active, grad_cat, grad_middle, start, mats, input_gain, earlier=()):
-    shapes = (shape(ROWS, WIDTH, F32), shape(1, WIDTH, F32))
+    shapes = (shape(ROWS, WIDTH, F32), shape(ROWS, WIDTH, BF16), shape(1, WIDTH, F32))
     return pl.pallas_call(
         functools.partial(input_backward_kernel, len(earlier)),
         out_shape=shapes,
@@ -728,7 +733,7 @@
             scratch(4, 64, 16, 1024),
             scratch(ROWS, WIDTH, dtype=F32),
             pltpu.SemaphoreType.DMA((4,)),
-            pltpu.SemaphoreType.DMA((2,)),
+            pltpu.SemaphoreType.DMA((3,)),
         ],
         input_output_aliases={7 + k: k for k in range(len(earlier))},
         compiler_params=pltpu.CompilerParams(vmem_limit_bytes=LIMIT),
@@ -776,11 +781,19 @@
 
 
 def partners(axis, turn):
-    order = (FIRST, SECOND) if turn == 0 else (SECOND, FIRST)
     me = lax.axis_index(axis)
-    near = me + 1 - 2 * lax.rem(me, 2)
-    found = (near, 3 - me) if turn == 0 else (3 - me, near)
-    return me, found, [[(i, table[i]) for i in range(4)] for table in order]
+    near, far = me + 1 - 2 * lax.rem(me, 2), 3 - me
+    flipped = lax.rem(lax.axis_index("section") + turn, 2) == 1
+    found = (jnp.where(flipped, far, near), jnp.where(flipped, near, far))
+    swaps = []
+    for step in range(2):
+        tables = [(FIRST, SECOND)[(core + turn + step) % 2] for core in range(2)]
+        swaps.append([(4 * c + i, 4 * c + tables[c][i]) for c in range(2) for i in range(4)])
+    return me, found, swaps
+
+
+def exchange(array, axis, pairs):
+    return lax.ppermute(array, ("section", axis), pairs)
 
 
 def first_sent(part, axis, turn):
@@ -789,14 +802,14 @@
 
 
 def first_got(sent, axis, turn):
-    return lax.ppermute(sent, axis, partners(axis, turn)[2][0])
+    return exchange(sent, axis, partners(axis, turn)[2][0])
 
 
 def exchanged(part, got, axis, turn):
     me, (one, two), (swap_one, swap_two) = partners(axis, turn)
     half = got.shape[0] // 2
     handed = part([two]) + got[half:].astype(F32)
-    last = lax.ppermute(handed.astype(BF16), axis, swap_two)
+    last = exchange(handed.astype(BF16), axis, swap_two)
     return part([me]) + got[:half].astype(F32) + last.astype(F32)
 
 
@@ -824,14 +837,14 @@
     return exchanged(part, got, axis, turn)
 
 
-def finished(parts, order, depth):
+def second_summed(parts, order, depth):
     array = jnp.concatenate([p.astype(BF16) for p in parts], axis=1)
     width = array.shape[1]
     rest = [0, 1, 2]
     rest.remove(order[0])
     array = array.reshape(4, 4, depth, width)
     array = summed_on(array, DP[order[1]], rest.index(order[1]), 0).astype(BF16)
-    return summed_on(array.reshape(4, depth, width), DP[order[2]], 0, 0)
+    return array.reshape(4, depth, width)
 
 
 def column_blocks(matrix):
@@ -901,7 +914,7 @@
     input_high = run_input_backward(
         on_high, mix_high[1], feed_high[2], start_high, mats, small[0]
     )
-    top_low = lax.ppermute(input_high[0].astype(BF16), "section", [(1, 0)])
+    top_low = lax.ppermute(input_high[1], "section", [(1, 0)])
 
     def chosen(slot):
         return jnp.where(first, kept_low[slot], kept_high[slot])
@@ -916,6 +929,7 @@
     )
     grad_gate, grad_upper, grad_middle, feed_grad = feed
     grad_low = jnp.where(first, top_low, top_high)
+    grad_low, grad_gate, grad_upper = lax.optimization_barrier((grad_low, grad_gate, grad_upper))
     orders = ((2, 0, 1), (0, 1, 2), (1, 2, 0))
     products = [
         product_of(left, right, order[0])
@@ -948,18 +962,10 @@
     for p, sent, order in zip(products, sents, orders):
         got = first_got(sent, DP[order[0]], 1)
         mix_parts.append(exchanged(p, got, DP[order[0]], 1))
-    grad_start, input_grad = run_input_backward(
+    grad_start, unused, input_grad = run_input_backward(
         on_low, grad_cat, grad_middle, start_low, mats, small[0], input_high
     )
     small_grads = [input_grad, *small_grads]
-    rows_grad, gate_cat, up_cat = (
-        finished(pair, order, depth)
-        for pair, order, depth in zip(zip(feed_parts, mix_parts), orders, (32, 16, 16))
-    )
-    down_grad, joined_grad = rows_grad[:, :WIDTH], rows_grad[:, WIDTH:]
-    gate_grad, up_grad = gate_cat[:, :FEED], up_cat[:, :FEED]
-    cat_grad = jnp.concatenate([gate_cat[:, FEED:], up_cat[:, FEED:]], axis=1)
-
     input_g, kernel_g, bias_g, step_g, decay_g, skip_g, mixer_g = small_grads
     small_grads = (
         input_g[0],
@@ -974,6 +980,18 @@
     vector = jnp.concatenate([piece.reshape(-1) for piece in small_grads])
     vector = jnp.pad(vector, (0, -vector.shape[0] % 1024)).reshape(-1, 128)
     total = jnp.sum(lax.all_gather(vector, DP, axis=0, tiled=False), axis=0).reshape(-1)
+    seconds = [
+        second_summed(pair, order, depth)
+        for pair, order, depth in zip(zip(feed_parts, mix_parts), orders, (32, 16, 16))
+    ]
+    total, *seconds = lax.optimization_barrier((total, *seconds))
+    rows_grad, gate_cat, up_cat = (
+        summed_on(array, DP[order[2]], 0, 0) for array, order in zip(seconds, orders)
+    )
+    down_grad, joined_grad = rows_grad[:, :WIDTH], rows_grad[:, WIDTH:]
+    gate_grad, up_grad = gate_cat[:, :FEED], up_cat[:, :FEED]
+    cat_grad = jnp.concatenate([gate_cat[:, FEED:], up_cat[:, FEED:]], axis=1)
+
     summed, at = ([], 0)
     for piece in small_grads:
         summed.append(total[at : at + piece.size].reshape(1, *piece.shape))

time: 512 us -> 478 us (0.934)
  waiting for transfers between devices: 265 us -> 228 us
  starting transfers between devices: 36.5 us -> 41.7 us
    ppermute x25, waiting for transfers between devices: 130 us -> 94.6 us  [the longest x24 63 us: exchange(): return lax.ppermute(array, ('section', axis), pairs)]
    ppermute x25, starting transfers between devices: 34.1 us -> 39.3 us  [the longest x24 37.9 us: exchange(): return lax.ppermute(array, ('section', axis), pairs)]
  transfers between devices with their start and end apart: 28 -> 28, of which waited for: 17 -> 14; matrix products, arithmetic and copies ran while one was open for 11% -> 12% of each run, Pallas kernels for 6% -> 6%
where the time goes in v4:
time: 478 us; the launch traced here: 472 us
  waiting for transfers between devices  228 us (48%)
  Pallas kernels  91.1 us (19%)
  starting transfers between devices  41.7 us (9%)
  local copies, waits for them, and re-layouts  38.7 us (8%)
  matrix products  38.6 us (8%)
  other arithmetic  17.7 us (4%)
  between operations  15.3 us (3%)
    all_gather x1, waiting for transfers between devices, on_device(): packed = lax.all_gather(own, DP, axis=0, tiled=False)  134 us
    ppermute x24, waiting for transfers between devices, exchange(): return lax.ppermute(array, ('section', axis), pairs)  63 us
    pallas_call x2, Pallas kernels, run_forward(): pl.pallas_call(forward_kernel, out_shape=shapes, in_specs=[VMEM, ANY, VME...  43.9 us
    dot_general x18, matrix products, dot(): return jnp.dot(left, right, preferred_element_type=F32)  38.6 us
    ppermute x24, starting transfers between devices, exchange(): return lax.ppermute(array, ('section', axis), pairs)  37.9 us
    ppermute x1, waiting for transfers between devices, on_device(): top_low = lax.ppermute(input_high[1], 'section', [(1, 0)])  31.6 us
    pallas_call x2, Pallas kernels, run_mix_backward(): pl.pallas_call(functools.partial(mix_backward_kernel, len(earlier)), out_...  20.9 us
    pallas_call x2, Pallas kernels, run_feed_backward(): pl.pallas_call(functools.partial(feed_backward_kernel, len(earlier)), out...  13.6 us
  transfers between devices with their start and end apart: 28, of which 14 were waited for; matrix products, arithmetic and copies ran while one was open for 12% of the time, Pallas kernels for 6%

profile of v4, /device:TPU:0, one launch (start us, length us, event | category | flops | bytes accessed | tf_op | source)
XLA Modules:
  0.0 471.5 jit_solution(7392868614998223645)
XLA Ops:
  20.4 133.8 %all-gather.6.cloned.1.call-done = bf16[12800,1024]{1,0:T(8,128)(2,1)} async-done(((bf16[200,1024]{1,0:T(8,128)(2,1)}), bf16[12800,1024]{1,0:T(8,128)(2,1)}) %all-gather.6.cloned.1.call-update) | async-done | bytes 26214416 | tf_op jit(solution)/shard_map/all_gather | solution.py:886
  157.8 3.8 slice.254
  162.7 22.0 %forward.2 = (bf16[256,1024]{1,0:T(8,128)(2,1)}, bf16[256,1024]{1,0:T(8,128)(2,1)}, f32[256,4224]{1,0:T(8,128)}, f32[256,1536]{1,0:T(8,128)}, bf16[256,1536]{1,0...) custom-call(bf16[256,1024]{1,0:T(8,128)(2,1)} %bitcast.249, ...), custom_call_target="tpu_custom_call" | custom-call | flops 6451200000 | bytes 40000000 | tf_op jit(solution)/shard_map/forward/pallas_call | solution.py:627
  190.0 22.0 %forward.3 = (bf16[256,1024]{1,0:T(8,128)(2,1)}, bf16[256,1024]{1,0:T(8,128)(2,1)}, f32[256,4224]{1,0:T(8,128)}, f32[256,1536]{1,0:T(8,128)}, bf16[256,1536]{1,0...) custom-call(bf16[256,1024]{1,0:T(8,128)(2,1)} %copy-done.10, ...), custom_call_target="tpu_custom_call" | custom-call | flops 6451200000 | bytes 40000000 | tf_op jit(solution)/shard_map/forward/pallas_call | solution.py:627
  227.0 31.6 %collective-permute-done.1.refs_0_ = bf16[256,1024]{1,0:T(8,128)(2,1)} collective-permute-done((bf16[256,1024]{1,0:T(8,128)(2,1)}, bf16[256,1024]{1,0:T(8,128)(2,1)}, u32[]{:S(2)}, u32[]{:S(2)}) %collective-permute-start.1) | collective-permute-done | bytes 524320 | tf_op jit(solution)/shard_map/ppermute | solution.py:917
  259.7 12.4 %feed_backward.3 = (bf16[256,2048]{1,0:T(8,128)(2,1)}, bf16[256,2048]{1,0:T(8,128)(2,1)}, f32[256,1024]{1,0:T(8,128)}, f32[1,1024]{1,0:T(1,128)}) custom-call(s32[1]{0:T(128)S(6)} %sub.23.active, bf16[256,1024]{1,0:T(8,128)(2,1)} %collective-permute-done.1.refs_0_, ...), custom_call_target="tpu_custom_call", output_to_operand_aliasing={{0}: (7, {}), {1}: (8, {}), {2}: (9, {}), {3}: (10, {})} | custom-call | flops 3225600000 | bytes 22000000 | tf_op jit(solution)/shard_map/feed_backward/pallas_call | solution.py:657
  284.2 19.0 %mix_backward.3 = (bf16[256,1024]{1,0:T(8,128)(2,1)}, bf16[256,4224]{1,0:T(8,128)(2,1)}, f32[4,1792]{1,0:T(4,128)}, f32[1,1792]{1,0:T(1,128)}, f32[1,128]{1,0:T(...) custom-call(s32[1]{0:T(128)S(6)} %sub.23.active, ...), custom_call_target="tpu_custom_call", output_to_operand_aliasing={{0}: (15, {}), {1}: (16, {}), {2}: (17, {}), {3}: (18, {}),... | custom-call | flops 1075200000 | bytes 14000000 | tf_op jit(solution)/shard_map/mix_backward/pallas_call | solution.py:694
  307.6 3.2 convolution_convert_fusion.1
  320.1 2.7 fusion.11
  323.7 2.6 add_convert_fusion.3
  331.9 10.4 %input_backward.3 = (f32[256,1024]{1,0:T(8,128)}, bf16[256,1024]{1,0:T(8,128)(2,1)}, f32[1,1024]{1,0:T(1,128)}) custom-call(s32[1]{0:T(128)S(6)} %sub.23.active, bf16[256,4224]{1,0:T(8,128)(2,1)} %get-tuple-element.131.refs_0_, f32[256,1024]{1,0:T(8,128)} %get-tuple-element.139.refs_0_.refs_1_, ...), custom_call_target="tpu_custom_call", output_to_operand_aliasing={{0}: (7, {}), {1}: (8, {}), {2}: (9, {})} | custom-call | flops 2150400000 | bytes 13000000 | tf_op jit(solution)/shard_map/input_backward/pallas_call | solution.py:726
  345.6 2.7 fusion.9
  354.1 11.7 %collective-permute-done.5 = bf16[512,1024]{1,0:T(8,128)(2,1)} collective-permute-done((bf16[512,1024]{1,0:T(8,128)(2,1)}, bf16[512,1024]{1,0:T(8,128)(2,1)}, u32[]{:S(2)}, u32[]{:S(2)}) %collective-permute-start.5) | collective-permute-done | bytes 1048608 | tf_op jit(solution)/shard_map/ppermute | solution.py:796
  378.5 10.4 %collective-permute-done.12 = bf16[256,2048]{1,0:T(8,128)(2,1)S(1)} collective-permute-done((bf16[256,2048]{1,0:T(8,128)(2,1)S(1)}, bf16[256,2048]{1,0:T(8,128)(2,1)S(1)}, u32[]{:S(2)}, u32[]{:S(2)}) %collective-permute-start.12) | collective-permute-done | bytes 1048608 | tf_op jit(solution)/shard_map/ppermute | solution.py:796
  395.7 17.3 %collective-permute-done.8 = bf16[256,2048]{1,0:T(8,128)(2,1)S(1)} collective-permute-done((bf16[256,2048]{1,0:T(8,128)(2,1)S(1)}, bf16[256,2048]{1,0:T(8,128)(2,1)S(1)}, u32[]{:S(2)}, u32[]{:S(2)}) %collective-permute-start.8) | collective-permute-done | bytes 1048608 | tf_op jit(solution)/shard_map/ppermute | solution.py:796
  413.2 4.4 collective-permute-start.9
  417.6 3.6 collective-permute-done.13
  421.4 3.5 collective-permute-start.14
  425.8 2.9 collective-permute-start.19
  428.7 4.9 %collective-permute-done.14 = bf16[64,4096]{1,0:T(8,128)(2,1)S(1)} collective-permute-done((bf16[64,4096]{1,0:T(8,128)(2,1)S(1)}, bf16[64,4096]{1,0:T(8,128)(2,1)S(1)}, u32[]{:S(2)}, u32[]{:S(2)}) %collective-permute-start.14) | collective-permute-done | bytes 524320 | tf_op jit(solution)/shard_map/ppermute | solution.py:796
  434.2 5.1 %collective-permute-done.19 = bf16[64,4224]{1,0:T(8,128)(2,1)S(1)} collective-permute-done((bf16[64,4224]{1,0:T(8,128)(2,1)S(1)}, bf16[64,4224]{1,0:T(8,128)(2,1)S(1)}, u32[]{:S(2)}, u32[]{:S(2)}) %collective-permute-start.19) | collective-permute-done | bytes 540704 | tf_op jit(solution)/shard_map/ppermute | solution.py:796
  447.8 3.0 collective-permute-done.24
  453.2 2.5 collective-permute-start.21
  455.7 3.4 collective-permute-start.23
  (269 shorter events, 117.3 us)
Async XLA Ops:
  7.2 147.0 %all-gather.6.cloned.1.call-start = ((), (), s32[]{:S(2)}) async-start(), calls=%async_computation.1 | async-start | bytes 26624000 | tf_op jit(solution)/shard_map/all_gather | solution.py:886
  16.0 423.6 %all-gather.4.cloned.1.call-start = ((), (), s32[]{:S(2)}) async-start(), calls=%async_computation | async-start | bytes 3461120 | tf_op jit(solution)/shard_map/all_gather | solution.py:982
  218.5 40.1 %collective-permute-start.1 = (bf16[256,1024]{1,0:T(8,128)(2,1)}, bf16[256,1024]{1,0:T(8,128)(2,1)}, u32[]{:S(2)}, u32[]{:S(2)}) collective-permute-start(bf16[256,1024]{1,0:T(8,128)(2,1)} %get-tuple-element.99.refs_7_), channel_id=1, source_target_pairs={{64,0},{65,1},{66,2},{67,3},{68,4},{69,5},{70,6},{71,7},{72,8},{73... | collective-permute-start | bytes 1572872 | tf_op jit(solution)/shard_map/ppermute | solution.py:917
  278.3 26.4 %collective-permute-start.2 = (bf16[1024,1024]{1,0:T(8,128)(2,1)}, bf16[1024,1024]{1,0:T(8,128)(2,1)}, u32[]{:S(2)}, u32[]{:S(2)}) collective-permute-start(bf16[1024,1024]{1,0:T(8,128)(2,1)} %convolution_convert_fusion.5), channel_id=1, source_target_pairs={{0,1},{1,0},{2,3},{3,2},{64,67},{65,66},{66,65},{67,64},{4,5},{5,4... | collective-permute-start | bytes 6291464 | tf_op jit(solution)/shard_map/ppermute | solution.py:796
  279.8 26.4 %collective-permute-start.3 = (bf16[512,2048]{1,0:T(8,128)(2,1)}, bf16[512,2048]{1,0:T(8,128)(2,1)}, u32[]{:S(2)}, u32[]{:S(2)}) collective-permute-start(bf16[512,2048]{1,0:T(8,128)(2,1)} %convolution_convert_fusion.3), channel_id=1, source_target_pairs={{0,16},{16,0},{32,48},{48,32},{64,112},{80,96},{96,80},{112,64},{1... | collective-permute-start | bytes 6291464 | tf_op jit(solution)/shard_map/ppermute | solution.py:796
  281.3 26.4 %collective-permute-start.4 = (bf16[512,2048]{1,0:T(8,128)(2,1)}, bf16[512,2048]{1,0:T(8,128)(2,1)}, u32[]{:S(2)}, u32[]{:S(2)}) collective-permute-start(bf16[512,2048]{1,0:T(8,128)(2,1)} %convolution_convert_fusion.2), channel_id=1, source_target_pairs={{0,4},{4,0},{8,12},{12,8},{64,76},{68,72},{72,68},{76,64},{1,5},{5... | collective-permute-start | bytes 6291464 | tf_op jit(solution)/shard_map/ppermute | solution.py:796
  315.2 37.1 %collective-permute-start.6 = (bf16[1024,1024]{1,0:T(8,128)(2,1)}, bf16[1024,1024]{1,0:T(8,128)(2,1)}, u32[]{:S(2)}, u32[]{:S(2)}) collective-permute-start(bf16[1024,1024]{1,0:T(8,128)(2,1)} %convolution_convert_fusion.4), channel_id=1, source_target_pairs={{0,3},{1,2},{2,1},{3,0},{64,65},{65,64},{66,67},{67,66},{4,7},{5,6... | collective-permute-start | bytes 6291464 | tf_op jit(solution)/shard_map/ppermute | solution.py:796
  322.7 25.6 %collective-permute-start.15 = (bf16[256,2048]{1,0:T(8,128)(2,1)}, bf16[256,2048]{1,0:T(8,128)(2,1)}, u32[]{:S(2)}, u32[]{:S(2)}) collective-permute-start(bf16[256,2048]{1,0:T(8,128)(2,1)} %fusion.11), channel_id=1, source_target_pairs={{0,12},{4,8},{8,4},{12,0},{64,68},{68,64},{72,76},{76,72},{1,13},{... | collective-permute-start | bytes 3145736 | tf_op jit(solution)/shard_map/ppermute | solution.py:796
  326.4 39.5 %collective-permute-start.5 = (bf16[512,1024]{1,0:T(8,128)(2,1)}, bf16[512,1024]{1,0:T(8,128)(2,1)}, u32[]{:S(2)}, u32[]{:S(2)}) collective-permute-start(bf16[512,1024]{1,0:T(8,128)(2,1)} %add_convert_fusion.3), channel_id=1, source_target_pairs={{0,3},{1,2},{2,1},{3,0},{64,65},{65,64},{66,67},{67,66},{4,7},{5,6... | collective-permute-start | bytes 3145736 | tf_op jit(solution)/shard_map/ppermute | solution.py:796
  327.5 42.7 %collective-permute-start.11 = (bf16[512,2048]{1,0:T(8,128)(2,1)}, bf16[512,2048]{1,0:T(8,128)(2,1)}, u32[]{:S(2)}, u32[]{:S(2)}) collective-permute-start(bf16[512,2048]{1,0:T(8,128)(2,1)} %convolution_convert_fusion.1), channel_id=1, source_target_pairs={{0,48},{16,32},{32,16},{48,0},{64,80},{80,64},{96,112},{112,96},{1... | collective-permute-start | bytes 6291464 | tf_op jit(solution)/shard_map/ppermute | solution.py:796
  329.6 44.0 %collective-permute-start.16 = (bf16[512,2176]{1,0:T(8,128)(2,1)}, bf16[512,2176]{1,0:T(8,128)(2,1)}, u32[]{:S(2)}, u32[]{:S(2)}) collective-permute-start(bf16[512,2176]{1,0:T(8,128)(2,1)} %convolution_convert_fusion), channel_id=1, source_target_pairs={{0,12},{4,8},{8,4},{12,0},{64,68},{68,64},{72,76},{76,72},{1,13},{... | collective-permute-start | bytes 6684680 | tf_op jit(solution)/shard_map/ppermute | solution.py:796
  348.3 19.6 %collective-permute-start.10 = (bf16[256,2048]{1,0:T(8,128)(2,1)}, bf16[256,2048]{1,0:T(8,128)(2,1)}, u32[]{:S(2)}, u32[]{:S(2)}) collective-permute-start(bf16[256,2048]{1,0:T(8,128)(2,1)} %fusion.9), channel_id=1, source_target_pairs={{0,48},{16,32},{32,16},{48,0},{64,80},{80,64},{96,112},{112,96},{1... | collective-permute-start | bytes 3145736 | tf_op jit(solution)/shard_map/ppermute | solution.py:796
  354.0 21.4 %collective-permute-start.7 = (bf16[512,1024]{1,0:T(8,128)(2,1)S(1)}, bf16[512,1024]{1,0:T(8,128)(2,1)S(1)}, u32[]{:S(2)}, u32[]{:S(2)}) collective-permute-start(bf16[512,1024]{1,0:T(8,128)(2,1)S(1)} %add_convert_fusion.1), channel_id=1, source_target_pairs={{0,1},{1,0},{2,3},{3,2},{64,67},{65,66},{66,65},{67,64},{4,5},{5,4... | collective-permute-start | bytes 3145736 | tf_op jit(solution)/shard_map/ppermute | solution.py:796
  372.0 17.0 %collective-permute-start.12 = (bf16[256,2048]{1,0:T(8,128)(2,1)S(1)}, bf16[256,2048]{1,0:T(8,128)(2,1)S(1)}, u32[]{:S(2)}, u32[]{:S(2)}) collective-permute-start(bf16[256,2048]{1,0:T(8,128)(2,1)S(1)} %fusion.10), channel_id=1, source_target_pairs={{0,16},{16,0},{32,48},{48,32},{64,112},{80,96},{96,80},{112,64},{1... | collective-permute-start | bytes 3145736 | tf_op jit(solution)/shard_map/ppermute | solution.py:796
  375.3 17.8 %collective-permute-start.17 = (bf16[256,2176]{1,0:T(8,128)(2,1)S(1)}, bf16[256,2176]{1,0:T(8,128)(2,1)S(1)}, u32[]{:S(2)}, u32[]{:S(2)}) collective-permute-start(bf16[256,2176]{1,0:T(8,128)(2,1)S(1)} %fusion.2), channel_id=1, source_target_pairs={{0,4},{4,0},{8,12},{12,8},{64,76},{68,72},{72,68},{76,64},{1,5},{5... | collective-permute-start | bytes 3342344 | tf_op jit(solution)/shard_map/ppermute | solution.py:796
  377.8 35.2 %collective-permute-start.8 = (bf16[256,2048]{1,0:T(8,128)(2,1)S(1)}, bf16[256,2048]{1,0:T(8,128)(2,1)S(1)}, u32[]{:S(2)}, u32[]{:S(2)}) collective-permute-start(bf16[256,2048]{1,0:T(8,128)(2,1)S(1)} %bitcast.264), channel_id=1, source_target_pairs={{0,16},{16,0},{32,48},{48,32},{64,112},{80,96},{96,80},{112,64},{1... | collective-permute-start | bytes 3145736 | tf_op jit(solution)/shard_map/ppermute | solution.py:796
  391.3 30.0 %collective-permute-start.13 = (bf16[128,4096]{1,0:T(8,128)(2,1)S(1)}, bf16[128,4096]{1,0:T(8,128)(2,1)S(1)}, u32[]{:S(2)}, u32[]{:S(2)}) collective-permute-start(bf16[128,4096]{1,0:T(8,128)(2,1)S(1)} %bitcast.265), channel_id=1, source_target_pairs={{0,4},{4,0},{8,12},{12,8},{64,76},{68,72},{72,68},{76,64},{1,5},{5... | collective-permute-start | bytes 3145736 | tf_op jit(solution)/shard_map/ppermute | solution.py:796
  395.5 30.1 %collective-permute-start.18 = (bf16[128,4224]{1,0:T(8,128)(2,1)S(1)}, bf16[128,4224]{1,0:T(8,128)(2,1)S(1)}, u32[]{:S(2)}, u32[]{:S(2)}) collective-permute-start(bf16[128,4224]{1,0:T(8,128)(2,1)S(1)} %bitcast.260), channel_id=1, source_target_pairs={{0,1},{1,0},{2,3},{3,2},{64,67},{65,66},{66,65},{67,64},{4,5},{5,4... | collective-permute-start | bytes 3244040 | tf_op jit(solution)/shard_map/ppermute | solution.py:796
  413.2 20.7 %collective-permute-start.9 = (bf16[128,2048]{1,0:T(8,128)(2,1)S(1)}, bf16[128,2048]{1,0:T(8,128)(2,1)S(1)}, u32[]{:S(2)}, u32[]{:S(2)}) collective-permute-start(bf16[128,2048]{1,0:T(8,128)(2,1)S(1)} %fusion.18), channel_id=1, source_target_pairs={{0,48},{16,32},{32,16},{48,0},{64,80},{80,64},{96,112},{112,96},{1... | collective-permute-start | bytes 1572872 | tf_op jit(solution)/shard_map/ppermute | solution.py:796
  421.4 12.2 %collective-permute-start.14 = (bf16[64,4096]{1,0:T(8,128)(2,1)S(1)}, bf16[64,4096]{1,0:T(8,128)(2,1)S(1)}, u32[]{:S(2)}, u32[]{:S(2)}) collective-permute-start(bf16[64,4096]{1,0:T(8,128)(2,1)S(1)} %fusion.15), channel_id=1, source_target_pairs={{0,12},{4,8},{8,4},{12,0},{64,68},{68,64},{72,76},{76,72},{1,13},{... | collective-permute-start | bytes 1572872 | tf_op jit(solution)/shard_map/ppermute | solution.py:796
  425.8 13.5 %collective-permute-start.19 = (bf16[64,4224]{1,0:T(8,128)(2,1)S(1)}, bf16[64,4224]{1,0:T(8,128)(2,1)S(1)}, u32[]{:S(2)}, u32[]{:S(2)}) collective-permute-start(bf16[64,4224]{1,0:T(8,128)(2,1)S(1)} %fusion.12), channel_id=1, source_target_pairs={{0,3},{1,2},{2,1},{3,0},{64,65},{65,64},{66,67},{67,66},{4,7},{5,6... | collective-permute-start | bytes 1622024 | tf_op jit(solution)/shard_map/ppermute | solution.py:796
  444.9 8.3 %collective-permute-start.20 = (bf16[32,4096]{1,0:T(8,128)(2,1)S(1)}, bf16[32,4096]{1,0:T(8,128)(2,1)S(1)}, u32[]{:S(2)}, u32[]{:S(2)}) collective-permute-start(bf16[32,4096]{1,0:T(8,128)(2,1)S(1)} %pad_maximum_fusion.13), channel_id=1, source_target_pairs={{0,1},{1,0},{2,3},{3,2},{64,67},{65,66},{66,65},{67,64},{4,5},{5,4... | collective-permute-start | bytes 786440 | tf_op jit(solution)/shard_map/ppermute | solution.py:796
  445.0 10.7 %collective-permute-start.22 = (bf16[32,4224]{1,0:T(8,128)(2,1)S(1)}, bf16[32,4224]{1,0:T(8,128)(2,1)S(1)}, u32[]{:S(2)}, u32[]{:S(2)}) collective-permute-start(bf16[32,4224]{1,0:T(8,128)(2,1)S(1)} %pad_maximum_fusion.8), channel_id=1, source_target_pairs={{0,16},{16,0},{32,48},{48,32},{64,112},{80,96},{96,80},{112,64},{1... | collective-permute-start | bytes 811016 | tf_op jit(solution)/shard_map/ppermute | solution.py:796
  450.8 8.4 %collective-permute-start.25 = (bf16[32,2048]{1,0:T(8,128)(2,1)S(1)}, bf16[32,2048]{1,0:T(8,128)(2,1)S(1)}, u32[]{:S(2)}, u32[]{:S(2)}) collective-permute-start(bf16[32,2048]{1,0:T(8,128)(2,1)S(1)} %fusion.36), channel_id=1, source_target_pairs={{0,12},{4,8},{8,4},{12,0},{64,68},{68,64},{72,76},{76,72},{1,13},{... | collective-permute-start | bytes 393224 | tf_op jit(solution)/shard_map/ppermute | solution.py:796
  (52 other events, 330.6 us)
Sparse Core Ops, SparseCore 0:
  16.1 138.0 all-gather.5
  350.2 69.4 all-gather.3

commit v5 on v4

--- a/solution.py
+++ b/solution.py
@@ -21,7 +21,7 @@
 BF16 = jnp.bfloat16
 HIDE = -1e30
 Q0, K0, V0, Z0, X0, T0 = 0, 512, 640, 768, 2304, 4096
-GATE0, UP0, DOWN0, OUT0, HEADS0, DT0, PACKED = 64, 96, 128, 160, 184, 192, 200
+OUT0, HEADS0, DT0, PACKED = 64, 88, 96, 104
 
 
 def dot(left, right):
@@ -289,13 +289,29 @@
         copy.start()
 
 
+def feed_copies(places, pieces, buffers, sems):
+    copies = []
+    for k, buffer in enumerate(buffers):
+        own, got, far = pieces[3 * k : 3 * k + 3]
+        for q, source in enumerate((own, got, far.at[0], far.at[1])):
+            target = buffer.at[(slice(None),) * k + (places[4 * k + q],)]
+            copies.append(pltpu.make_async_copy(source, target, sems.at[4 * k + q]))
+    return copies
+
+
+def rows_of(block):
+    return block.reshape(-1, block.shape[-1])
+
+
 def forward_kernel(
-    x, packed, dt_weight, out_weight, heads_weight, input_gain, kernel, bias, step_bias, decay_log, skip,
+    x, packed, dt_weight, out_weight, heads_weight,
+    places, gate_own, gate_got, gate_far, up_own, up_got, up_far, down_own, down_got, down_far,
+    input_gain, kernel, bias, step_bias, decay_log, skip,
     mixer_gain, feed_gain, cosine, sine,
     result_out, normed_out, proj_out, ssm_out, mamba_out, attended_out, middle_out, ffin_out, gate_out,
     upper_out, hidden_out,
     result, normed, proj, ssm, mamba, attended, middle, ffin, gate, upper, hidden,
-    cat, gate_up, down, out_mat, heads_mat, sems, out_sems,
+    cat, gate_mat, up_mat, down_mat, out_mat, heads_mat, sems, out_sems, feed_sems,
 ):
     leaving = []
 
@@ -311,14 +327,9 @@
     ]
     copies.append(pltpu.make_async_copy(out_weight, out_mat, sems.at[4]))
     copies.append(pltpu.make_async_copy(heads_weight, heads_mat, sems.at[5]))
-    for j in range(4):
-        copies.append(
-            pltpu.make_async_copy(
-                packed.at[:, pl.ds(GATE0 + 16 * j, 16), :], gate_up.at[j], sems.at[6 + j]
-            )
-        )
-    copies.append(pltpu.make_async_copy(packed.at[:, pl.ds(DOWN0, 32), :], down, sems.at[10]))
-    start_all(copies)
+    pieces = (gate_own, gate_got, gate_far, up_own, up_got, up_far, down_own, down_got, down_far)
+    feeds = feed_copies(places, pieces, (gate_mat, up_mat, down_mat), feed_sems)
+    start_all(copies + feeds)
     state = x[...].astype(F32)
     normed[...] = (state * rms(state) * input_gain[...]).astype(BF16)
     proj[:, T0:CAT] = dot(normed[...], dt_weight[...])
@@ -355,27 +366,27 @@
     value = middle[...]
     ffin[...] = (value * rms(value) * feed_gain[...]).astype(BF16)
     leave((middle, middle_out), (ffin, ffin_out))
-    for j in range(2):
-        copies[6 + j].wait()
-        copies[8 + j].wait()
-
-        def feed(tile, carry, j=j):
-            at = pl.multiple_of(tile * 256, 256)
-            to = pl.ds(pl.multiple_of(j * 1024 + at, 256), 256)
-            low = dot(ffin[...], flat(gate_up[j, :, :, pl.ds(at, 256)]))
-            high = dot(ffin[...], flat(gate_up[2 + j, :, :, pl.ds(at, 256)]))
-            gate[:, to] = low
-            upper[:, to] = high
-            hidden[:, to] = (low * sigmoid(low) * high).astype(BF16)
-            return carry
-
-        lax.fori_loop(0, 4, feed, 0)
+    for copy in feeds[:8]:
+        copy.wait()
+
+    def feed(tile, carry):
+        at = pl.ds(pl.multiple_of(tile * 256, 256), 256)
+        low = dot(ffin[...], rows_of(gate_mat[:, :, :, :, at]))
+        high = dot(ffin[...], rows_of(up_mat[:, :, :, :, at]))
+        gate[:, at] = low
+        upper[:, at] = high
+        hidden[:, at] = (low * sigmoid(low) * high).astype(BF16)
+        return carry
+
+    lax.fori_loop(0, 8, feed, 0)
     leave((gate, gate_out), (upper, upper_out), (hidden, hidden_out))
-    copies[10].wait()
+    for copy in feeds[8:]:
+        copy.wait()
 
     def last(tile, carry):
         at = pl.ds(pl.multiple_of(tile * 256, 256), 256)
-        result[:, at] = (middle[:, at] + dot(hidden[...], flat(down[:, :, at]))).astype(BF16)
+        part = dot(hidden[...], rows_of(down_mat[:, :, :, :, at]))
+        result[:, at] = (middle[:, at] + part).astype(BF16)
         return carry
 
     lax.fori_loop(0, 4, last, 0)
@@ -395,38 +406,31 @@
 def feed_backward_kernel(earlier, active, *refs):
     @pl.when(active[0] == 1)
     def run():
-        feed_backward_body(*refs[:6], *refs[6 + earlier :])
+        feed_backward_body(*refs[:15], *refs[15 + earlier :])
 
 
 def feed_backward_body(
-    grad_top, packed, gate_in, upper_in, middle_in, feed_gain,
+    grad_top, places, gate_own, gate_got, gate_far, up_own, up_got, up_far, down_own, down_got, down_far,
+    gate_in, upper_in, middle_in, feed_gain,
     grad_gate_out, grad_upper_out, grad_middle_out, feed_grad_out,
     grad_gate, grad_upper, grad_middle, feed_grad,
-    gate, upper, middle, gate_up, down, grad_ffin, sems, out_sems,
+    gate, upper, middle, gate_mat, up_mat, down_mat, grad_ffin, sems, out_sems, feed_sems,
 ):
     inputs = [
-        pltpu.make_async_copy(gate_in, gate, sems.at[5]),
-        pltpu.make_async_copy(upper_in, upper, sems.at[6]),
-        pltpu.make_async_copy(middle_in, middle, sems.at[7]),
+        pltpu.make_async_copy(gate_in, gate, sems.at[0]),
+        pltpu.make_async_copy(upper_in, upper, sems.at[1]),
+        pltpu.make_async_copy(middle_in, middle, sems.at[2]),
     ]
-    copies = [
-        pltpu.make_async_copy(packed.at[:, pl.ds(DOWN0, 32), :], down, sems.at[4]),
-    ]
-    for j in range(4):
-        copies.append(
-            pltpu.make_async_copy(
-                packed.at[:, pl.ds(GATE0 + 16 * j, 16), :], gate_up.at[j], sems.at[j]
-            )
-        )
-    start_all(copies[:1] + inputs + copies[1:])
-    copies[0].wait()
-    for copy in inputs:
+    pieces = (gate_own, gate_got, gate_far, up_own, up_got, up_far, down_own, down_got, down_far)
+    feeds = feed_copies(places, pieces, (gate_mat, up_mat, down_mat), feed_sems)
+    start_all(feeds[8:] + inputs + feeds[:8])
+    for copy in feeds[8:] + inputs:
         copy.wait()
 
     def through(tile, carry):
         at = pl.ds(pl.multiple_of(tile * 256, 256), 256)
-        block = flat(down[pl.ds(tile * 8, 8)])
-        grad_hidden = dot_nt(grad_top[...], block)
+        block = down_mat[tile // 2, pl.ds(lax.rem(tile, 2) * 2, 2)]
+        grad_hidden = dot_nt(grad_top[...], rows_of(block))
         low, high = gate[:, at], upper[:, at]
         slope = sigmoid(low)
         grad_upper[:, at] = (grad_hidden * (low * slope)).astype(BF16)
@@ -436,18 +440,13 @@
 
     lax.fori_loop(0, 8, through, 0)
     leaving = leave_all(((grad_gate, grad_gate_out), (grad_upper, grad_upper_out)), out_sems)
-    for copy in copies[1:]:
+    for copy in feeds[:8]:
         copy.wait()
 
     def back(tile, carry):
         at = pl.ds(pl.multiple_of(tile * 256, 256), 256)
-        total = jnp.zeros((ROWS, 256), F32)
-        for j in range(2):
-            block = flat(gate_up[j, pl.ds(tile * 16, 16)])
-            total = total + dot_nt(grad_gate[:, 1024 * j : 1024 * j + 1024], block)
-            block = flat(gate_up[2 + j, pl.ds(tile * 16, 16)])
-            total = total + dot_nt(grad_upper[:, 1024 * j : 1024 * j + 1024], block)
-        grad_ffin[:, at] = total
+        total = dot_nt(grad_gate[...], rows_of(gate_mat[tile]))
+        grad_ffin[:, at] = total + dot_nt(grad_upper[...], rows_of(up_mat[tile]))
         return carry
 
     lax.fori_loop(0, 4, back, 0)
@@ -605,12 +604,19 @@
     return pltpu.VMEM(dims, dtype)
 
 
+FEED_MATS = (
+    scratch(4, 4, 4, 16, FEED),
+    scratch(4, 4, 4, 16, FEED),
+    scratch(4, 4, 4, 32, WIDTH),
+)
+
+
 def mirrored(shapes):
     return [pltpu.VMEM(s.shape, s.dtype) for s in shapes]
 
 
 def run_forward(start, mats, small, rope):
-    packed, dt_weight, out_weight, heads_weight = mats
+    packed, dt_weight, out_weight, heads_weight, feeds = mats
     shapes = (
         shape(ROWS, WIDTH, BF16),
         shape(ROWS, WIDTH, BF16),
@@ -627,24 +633,24 @@
     return pl.pallas_call(
         forward_kernel,
         out_shape=shapes,
-        in_specs=[VMEM, ANY, VMEM, ANY, ANY] + [VMEM] * 10,
+        in_specs=[VMEM, ANY, VMEM, ANY, ANY, SMEM] + [ANY] * 9 + [VMEM] * 10,
         out_specs=(ANY,) * len(shapes),
         scratch_shapes=[
             *mirrored(shapes),
             scratch(4, 64, 16, 1024),
-            scratch(4, 64, 16, 1024),
-            scratch(64, 32, 1024),
+            *FEED_MATS,
             scratch(INNER, WIDTH),
             scratch(512, WIDTH),
-            pltpu.SemaphoreType.DMA((11,)),
+            pltpu.SemaphoreType.DMA((6,)),
             pltpu.SemaphoreType.DMA((len(shapes),)),
+            pltpu.SemaphoreType.DMA((12,)),
         ],
         compiler_params=pltpu.CompilerParams(vmem_limit_bytes=LIMIT),
         cost_estimate=pl.CostEstimate(
             flops=2 * ROWS * 12_600_000, bytes_accessed=40_000_000, transcendentals=2_000_000
         ),
         name="forward",
-    )(start, packed, dt_weight, out_weight, heads_weight, *small, *rope)
+    )(start, packed, dt_weight, out_weight, heads_weight, *feeds, *small, *rope)
 
 
 def run_feed_backward(active, grad_top, mats, gate, upper, middle, feed_gain, earlier=()):
@@ -657,30 +663,30 @@
     return pl.pallas_call(
         functools.partial(feed_backward_kernel, len(earlier)),
         out_shape=shapes,
-        in_specs=[SMEM, VMEM, ANY, ANY, ANY, ANY, VMEM] + [ANY] * len(earlier),
+        in_specs=[SMEM, VMEM, SMEM] + [ANY] * 12 + [VMEM] + [ANY] * len(earlier),
         out_specs=(ANY,) * len(shapes),
         scratch_shapes=[
             *mirrored(shapes),
             scratch(ROWS, FEED, dtype=F32),
             scratch(ROWS, FEED, dtype=F32),
             scratch(ROWS, WIDTH, dtype=F32),
-            scratch(4, 64, 16, 1024),
-            scratch(64, 32, 1024),
+            *FEED_MATS,
             scratch(ROWS, WIDTH, dtype=F32),
-            pltpu.SemaphoreType.DMA((8,)),
+            pltpu.SemaphoreType.DMA((3,)),
             pltpu.SemaphoreType.DMA((4,)),
+            pltpu.SemaphoreType.DMA((12,)),
         ],
-        input_output_aliases={7 + k: k for k in range(len(earlier))},
+        input_output_aliases={16 + k: k for k in range(len(earlier))},
         compiler_params=pltpu.CompilerParams(vmem_limit_bytes=LIMIT),
         cost_estimate=pl.CostEstimate(
             flops=2 * ROWS * 6_300_000, bytes_accessed=22_000_000, transcendentals=1_000_000
         ),
         name="feed_backward",
-    )(active, grad_top, mats[0], gate, upper, middle, feed_gain, *earlier)
+    )(active, grad_top, *mats[4], gate, upper, middle, feed_gain, *earlier)
 
 
 def run_mix_backward(active, grad_middle, mats, proj, ssm, small, rope, pick, earlier=()):
-    packed, dt_weight, out_weight, heads_weight = mats
+    packed, dt_weight, out_weight, heads_weight, feeds = mats
     shapes = (
         shape(ROWS, WIDTH, BF16),
         shape(ROWS, CAT, BF16),
@@ -847,6 +853,27 @@
     return array.reshape(4, depth, width)
 
 
+def gathered_on(array, axis):
+    me, (one, two), (swap_one, swap_two) = partners(axis, 0)
+    got = exchange(array, axis, swap_one)
+    far = exchange(jnp.stack([array, got]), axis, swap_two)
+    return (array, got, far), (me, one, two, lax.rem(me + 2, 4))
+
+
+def placed(blocks, places, dim):
+    own, got, far = blocks
+    whole = jnp.zeros((*own.shape[:dim], 4, *own.shape[dim:]), own.dtype)
+    for block, place in zip((own, got, far[0], far[1]), places):
+        whole = lax.dynamic_update_index_in_dim(whole, block, place, dim)
+    return whole
+
+
+def gathered(block, order):
+    block = placed(*gathered_on(block, DP[order[2]]), 0)
+    block = placed(*gathered_on(block, DP[order[1]]), 0 if order[1] < order[2] else 1)
+    return gathered_on(block, DP[order[0]])
+
+
 def column_blocks(matrix):
     return [matrix[:, at : at + 1024] for at in range(0, matrix.shape[1], 1024)]
 
@@ -874,9 +901,6 @@
     own = jnp.concatenate(
         [
             *column_blocks(cat),
-            *column_blocks(gate_weight[0]),
-            *column_blocks(up_weight[0]),
-            down_weight[0],
             out_weight[0],
             heads_weight[0],
             steps,
@@ -885,11 +909,21 @@
     )
     packed = lax.all_gather(own, DP, axis=0, tiled=False)
     dt_weight = packed[:, DT0, : 16 * HEADS].reshape(WIDTH, HEADS)
+    feeds = [
+        gathered(weight[0], order)
+        for weight, order in (
+            (gate_weight, (0, 1, 2)),
+            (up_weight, (1, 2, 0)),
+            (down_weight, (2, 0, 1)),
+        )
+    ]
+    places = jnp.stack([place for blocks, found in feeds for place in found]).astype(jnp.int32)
     mats = (
         packed,
         jnp.pad(dt_weight, ((0, 0), (0, 128 - HEADS))),
         packed[:, OUT0:HEADS0].reshape(INNER, WIDTH),
         packed[:, HEADS0:DT0].reshape(512, WIDTH),
+        (places, *(piece for blocks, found in feeds for piece in blocks)),
     )
     small = prepared_small([piece[0] for piece in pieces])
     rope = rope_tables()

time: 478 us -> 464 us (0.971)
  waiting for transfers between devices: 228 us -> 173 us
  starting transfers between devices: 41.7 us -> 71.6 us
  Pallas kernels: 91.1 us -> 97.6 us
  other arithmetic: 17.7 us -> 22.6 us
    all_gather x1, waiting for transfers between devices: 134 us -> 44.9 us  [on_device(): packed = lax.all_gather(own, DP, axis=0, tiled=False)]
    ppermute x24 -> x42, waiting for transfers between devices: 63 us -> 95.1 us  [exchange(): return lax.ppermute(array, ('section', axis), pairs)]
    ppermute x24 -> x42, starting transfers between devices: 37.9 us -> 68.1 us  [exchange(): return lax.ppermute(array, ('section', axis), pairs)]
    another operation x0 -> x9, other arithmetic: none -> 5.15 us  [gathered_on(): far = exchange(jnp.stack([array, got]), axis, swap_two)]
  transfers between devices with their start and end apart: 28 -> 46, of which waited for: 14 -> 22; matrix products, arithmetic and copies ran while one was open for 12% -> 15% of each run, Pallas kernels for 6% -> 6%
where the time goes in v5:
time: 464 us; the launch traced here: 457 us
  waiting for transfers between devices  173 us (37%)
  Pallas kernels  97.6 us (21%)
  starting transfers between devices  71.6 us (15%)
  matrix products  38.6 us (8%)
  local copies, waits for them, and re-layouts  38.5 us (8%)
  other arithmetic  22.6 us (5%)
  between operations  15.6 us (3%)
    ppermute x42, waiting for transfers between devices, exchange(): return lax.ppermute(array, ('section', axis), pairs)  95.1 us
    ppermute x42, starting transfers between devices, exchange(): return lax.ppermute(array, ('section', axis), pairs)  68.1 us
    pallas_call x2, Pallas kernels, run_forward(): pl.pallas_call(forward_kernel, out_shape=shapes, in_specs=[VMEM, ANY, VME...  47.9 us
    all_gather x1, waiting for transfers between devices, on_device(): packed = lax.all_gather(own, DP, axis=0, tiled=False)  44.9 us
    dot_general x18, matrix products, dot(): return jnp.dot(left, right, preferred_element_type=F32)  38.6 us
    ppermute x1, waiting for transfers between devices, on_device(): top_low = lax.ppermute(input_high[1], 'section', [(1, 0)])  32.9 us
    pallas_call x2, Pallas kernels, run_mix_backward(): pl.pallas_call(functools.partial(mix_backward_kernel, len(earlier)), out_...  20.9 us
    pallas_call x2, Pallas kernels, run_feed_backward(): pl.pallas_call(functools.partial(feed_backward_kernel, len(earlier)), out...  16.1 us
  transfers between devices with their start and end apart: 46, of which 22 were waited for; matrix products, arithmetic and copies ran while one was open for 15% of the time, Pallas kernels for 6%

profile of v5, /device:TPU:0, one launch (start us, length us, event | category | flops | bytes accessed | tf_op | source)
XLA Modules:
  0.0 457.4 jit_solution(17855472146076591146)
XLA Ops:
  41.0 4.7 %collective-permute-done.9 = bf16[2,4,16,2048]{3,2,1,0:T(8,128)(2,1)S(1)} collective-permute-done((bf16[2,4,16,2048]{3,2,1,0:T(8,128)(2,1)S(1)}, bf16[2,4,16,2048]{3,2,1,0:T(8,128)(2,1)S(1)}, u32[]{:S(2)}, u32[]{:S(2)}) %collective-permute-start.9) | collective-permute-done | bytes 524320 | tf_op jit(solution)/shard_map/ppermute | solution.py:802
  47.1 7.6 %collective-permute-done.3 = bf16[2,4,16,2048]{3,2,1,0:T(8,128)(2,1)S(1)} collective-permute-done((bf16[2,4,16,2048]{3,2,1,0:T(8,128)(2,1)S(1)}, bf16[2,4,16,2048]{3,2,1,0:T(8,128)(2,1)S(1)}, u32[]{:S(2)}, u32[]{:S(2)}) %collective-permute-start.3) | collective-permute-done | bytes 524320 | tf_op jit(solution)/shard_map/ppermute | solution.py:802
  54.8 13.5 %collective-permute-done.10.up_got.refs_6_ = bf16[4,4,16,2048]{3,2,1,0:T(8,128)(2,1)S(1)} collective-permute-done((bf16[4,4,16,2048]{3,2,1,0:T(8,128)(2,1)S(1)}, bf16[4,4,16,2048]{3,2,1,0:T(8,128)(2,1)S(1)}, u32[]{:S(2)}, u32[]{:S(2)}) %collective-permute-start.10) | collective-permute-done | bytes 1048608 | tf_op jit(solution)/shard_map/ppermute | solution.py:802
  78.2 3.2 collective-permute-start.5
  85.8 44.9 %all-gather.6.cloned.1.call-done = bf16[6656,1024]{1,0:T(8,128)(2,1)} async-done(((bf16[104,1024]{1,0:T(8,128)(2,1)}), bf16[6656,1024]{1,0:T(8,128)(2,1)}) %all-gather.6.cloned.1.call-update) | async-done | bytes 13631504 | tf_op jit(solution)/shard_map/all_gather | solution.py:910
  130.7 3.9 slice.282
  140.6 24.0 %forward.2 = (bf16[256,1024]{1,0:T(8,128)(2,1)}, bf16[256,1024]{1,0:T(8,128)(2,1)}, f32[256,4224]{1,0:T(8,128)}, f32[256,1536]{1,0:T(8,128)}, bf16[256,1536]{1,0...) custom-call(bf16[256,1024]{1,0:T(8,128)(2,1)} %bitcast.315, ...), custom_call_target="tpu_custom_call" | custom-call | flops 6451200000 | bytes 40000000 | tf_op jit(solution)/shard_map/forward/pallas_call | solution.py:633
  169.6 24.0 %forward.3 = (bf16[256,1024]{1,0:T(8,128)(2,1)}, bf16[256,1024]{1,0:T(8,128)(2,1)}, f32[256,4224]{1,0:T(8,128)}, f32[256,1536]{1,0:T(8,128)}, bf16[256,1536]{1,0...) custom-call(bf16[256,1024]{1,0:T(8,128)(2,1)} %copy-done.18, ...), custom_call_target="tpu_custom_call" | custom-call | flops 6451200000 | bytes 40000000 | tf_op jit(solution)/shard_map/forward/pallas_call | solution.py:633
  209.3 32.9 %collective-permute-done.19.refs_0_ = bf16[256,1024]{1,0:T(8,128)(2,1)} collective-permute-done((bf16[256,1024]{1,0:T(8,128)(2,1)}, bf16[256,1024]{1,0:T(8,128)(2,1)}, u32[]{:S(2)}, u32[]{:S(2)}) %collective-permute-start.19) | collective-permute-done | bytes 524320 | tf_op jit(solution)/shard_map/ppermute | solution.py:951
  243.3 14.8 %feed_backward.3 = (bf16[256,2048]{1,0:T(8,128)(2,1)}, bf16[256,2048]{1,0:T(8,128)(2,1)}, f32[256,1024]{1,0:T(8,128)}, f32[1,1024]{1,0:T(1,128)}) custom-call(s32[1]{0:T(128)S(6)} %sub.29.active, bf16[256,1024]{1,0:T(8,128)(2,1)} %collective-permute-done.19.refs_0_, ...), custom_call_target="tpu_custom_call", output_to_operand_aliasing={{0}: (16, {}), {1}: (17, {}), {2}: (18, {}), {3}: (19, {})} | custom-call | flops 3225600000 | bytes 22000000 | tf_op jit(solution)/shard_map/feed_backward/pallas_call | solution.py:663
  269.2 19.0 %mix_backward.3 = (bf16[256,1024]{1,0:T(8,128)(2,1)}, bf16[256,4224]{1,0:T(8,128)(2,1)}, f32[4,1792]{1,0:T(4,128)}, f32[1,1792]{1,0:T(1,128)}, f32[1,128]{1,0:T(...) custom-call(s32[1]{0:T(128)S(6)} %sub.29.active, ...), custom_call_target="tpu_custom_call", output_to_operand_aliasing={{0}: (15, {}), {1}: (16, {}), {2}: (17, {}), {3}: (18, {}),... | custom-call | flops 1075200000 | bytes 14000000 | tf_op jit(solution)/shard_map/mix_backward/pallas_call | solution.py:700
  293.6 3.3 convolution_convert_fusion.1
  317.8 10.4 %input_backward.3 = (f32[256,1024]{1,0:T(8,128)}, bf16[256,1024]{1,0:T(8,128)(2,1)}, f32[1,1024]{1,0:T(1,128)}) custom-call(s32[1]{0:T(128)S(6)} %sub.29.active, bf16[256,4224]{1,0:T(8,128)(2,1)} %get-tuple-element.131.refs_0_, f32[256,1024]{1,0:T(8,128)} %get-tuple-element.139.refs_0_.refs_1_, ...), custom_call_target="tpu_custom_call", output_to_operand_aliasing={{0}: (7, {}), {1}: (8, {}), {2}: (9, {})} | custom-call | flops 2150400000 | bytes 13000000 | tf_op jit(solution)/shard_map/input_backward/pallas_call | solution.py:732
  340.0 11.7 %collective-permute-done.23 = bf16[512,1024]{1,0:T(8,128)(2,1)} collective-permute-done((bf16[512,1024]{1,0:T(8,128)(2,1)}, bf16[512,1024]{1,0:T(8,128)(2,1)}, u32[]{:S(2)}, u32[]{:S(2)}) %collective-permute-start.23) | collective-permute-done | bytes 1048608 | tf_op jit(solution)/shard_map/ppermute | solution.py:802
  364.6 10.6 %collective-permute-done.30 = bf16[256,2048]{1,0:T(8,128)(2,1)S(1)} collective-permute-done((bf16[256,2048]{1,0:T(8,128)(2,1)S(1)}, bf16[256,2048]{1,0:T(8,128)(2,1)S(1)}, u32[]{:S(2)}, u32[]{:S(2)}) %collective-permute-start.30) | collective-permute-done | bytes 1048608 | tf_op jit(solution)/shard_map/ppermute | solution.py:802
  381.0 18.5 %collective-permute-done.26 = bf16[256,2048]{1,0:T(8,128)(2,1)S(1)} collective-permute-done((bf16[256,2048]{1,0:T(8,128)(2,1)S(1)}, bf16[256,2048]{1,0:T(8,128)(2,1)S(1)}, u32[]{:S(2)}, u32[]{:S(2)}) %collective-permute-start.26) | collective-permute-done | bytes 1048608 | tf_op jit(solution)/shard_map/ppermute | solution.py:802
  399.7 4.5 collective-permute-start.27
  404.1 3.4 collective-permute-done.31
  407.7 3.6 collective-permute-start.32
  411.4 3.5 collective-permute-start.37
  415.0 5.5 %collective-permute-done.32 = bf16[64,4096]{1,0:T(8,128)(2,1)S(1)} collective-permute-done((bf16[64,4096]{1,0:T(8,128)(2,1)S(1)}, bf16[64,4096]{1,0:T(8,128)(2,1)S(1)}, u32[]{:S(2)}, u32[]{:S(2)}) %collective-permute-start.32) | collective-permute-done | bytes 524320 | tf_op jit(solution)/shard_map/ppermute | solution.py:802
  421.0 4.1 collective-permute-done.37
  432.5 4.1 collective-permute-done.42
  439.5 3.1 collective-permute-start.39
  (369 shorter events, 163.1 us)
Async XLA Ops:
  7.2 123.4 %all-gather.6.cloned.1.call-start = ((), (), s32[]{:S(2)}) async-start(), calls=%async_computation.1 | async-start | bytes 13844480 | tf_op jit(solution)/shard_map/all_gather | solution.py:910
  12.0 413.4 %all-gather.4.cloned.1.call-start = ((), (), s32[]{:S(2)}) async-start(), calls=%async_computation | async-start | bytes 3461120 | tf_op jit(solution)/shard_map/all_gather | solution.py:1016
  45.7 22.6 %collective-permute-start.10 = (bf16[4,4,16,2048]{3,2,1,0:T(8,128)(2,1)S(1)}, bf16[4,4,16,2048]{3,2,1,0:T(8,128)(2,1)S(1)}, u32[]{:S(2)}, u32[]{:S(2)}) collective-permute-start(bf16[4,4,16,2048]{3,2,1,0:T(8,128)(2,1)S(1)} %fusion.36.up_own.refs_5_), channel_id=1, source_target_pairs={{0,4},{4,0},{8,12},{12,8},{64,76},{68,72},{72,68},{76,64},{1,5},{5... | collective-permute-start | bytes 3145736 | tf_op jit(solution)/shard_map/ppermute | solution.py:802
  46.9 25.3 %collective-permute-start.16 = (bf16[4,4,32,1024]{3,2,1,0:T(8,128)(2,1)S(1)}, bf16[4,4,32,1024]{3,2,1,0:T(8,128)(2,1)S(1)}, u32[]{:S(2)}, u32[]{:S(2)}) collective-permute-start(bf16[4,4,32,1024]{3,2,1,0:T(8,128)(2,1)S(1)} %slice_dynamic-update-slice_fusion.down_own.refs_8_), channel_id=1, source_target_pairs={{0,1},{1,0},{2,3},{3,2},{64,67},{65,66},{66,65},{67,64},{4,5},{5,4... | collective-permute-start | bytes 3145736 | tf_op jit(solution)/shard_map/ppermute | solution.py:802
  54.8 21.8 %collective-permute-start.4 = (bf16[4,4,16,2048]{3,2,1,0:T(8,128)(2,1)S(1)}, bf16[4,4,16,2048]{3,2,1,0:T(8,128)(2,1)S(1)}, u32[]{:S(2)}, u32[]{:S(2)}) collective-permute-start(bf16[4,4,16,2048]{3,2,1,0:T(8,128)(2,1)S(1)} %slice_dynamic-update-slice_fusion.2.gate_own.refs_2_), channel_id=1, source_target_pairs={{0,16},{16,0},{32,48},{48,32},{64,112},{80,96},{96,80},{112,64},{1... | collective-permute-start | bytes 3145736 | tf_op jit(solution)/shard_map/ppermute | solution.py:802
  70.0 69.2 %collective-permute-start.11 = (bf16[2,4,4,16,2048]{4,3,2,1,0:T(8,128)(2,1)}, bf16[2,4,4,16,2048]{4,3,2,1,0:T(8,128)(2,1)}, u32[]{:S(2)}, u32[]{:S(2)}) collective-permute-start(bf16[2,4,4,16,2048]{4,3,2,1,0:T(8,128)(2,1)} %pad_maximum_fusion.2), channel_id=1, source_target_pairs={{0,12},{4,8},{8,4},{12,0},{64,68},{68,64},{72,76},{76,72},{1,13},{... | collective-permute-start | bytes 6291464 | tf_op jit(solution)/shard_map/ppermute | solution.py:802
  73.9 65.3 %collective-permute-start.17 = (bf16[2,4,4,32,1024]{4,3,2,1,0:T(8,128)(2,1)}, bf16[2,4,4,32,1024]{4,3,2,1,0:T(8,128)(2,1)S(1)}, u32[]{:S(2)}, u32[]{:S(2)}) collective-permute-start(bf16[2,4,4,32,1024]{4,3,2,1,0:T(8,128)(2,1)} %pad_maximum_fusion.3), channel_id=1, source_target_pairs={{0,3},{1,2},{2,1},{3,0},{64,65},{65,64},{66,67},{67,66},{4,7},{5,6... | collective-permute-start | bytes 6291464 | tf_op jit(solution)/shard_map/ppermute | solution.py:802
  78.2 61.0 %collective-permute-start.5 = (bf16[2,4,4,16,2048]{4,3,2,1,0:T(8,128)(2,1)}, bf16[2,4,4,16,2048]{4,3,2,1,0:T(8,128)(2,1)}, u32[]{:S(2)}, u32[]{:S(2)}) collective-permute-start(bf16[2,4,4,16,2048]{4,3,2,1,0:T(8,128)(2,1)} %pad_maximum_fusion.1), channel_id=1, source_target_pairs={{0,48},{16,32},{32,16},{48,0},{64,80},{80,64},{96,112},{112,96},{1... | collective-permute-start | bytes 6291464 | tf_op jit(solution)/shard_map/ppermute | solution.py:802
  200.5 41.7 %collective-permute-start.19 = (bf16[256,1024]{1,0:T(8,128)(2,1)}, bf16[256,1024]{1,0:T(8,128)(2,1)}, u32[]{:S(2)}, u32[]{:S(2)}) collective-permute-start(bf16[256,1024]{1,0:T(8,128)(2,1)} %get-tuple-element.99.refs_7_), channel_id=1, source_target_pairs={{64,0},{65,1},{66,2},{67,3},{68,4},{69,5},{70,6},{71,7},{72,8},{73... | collective-permute-start | bytes 1572872 | tf_op jit(solution)/shard_map/ppermute | solution.py:951
  264.2 26.1 %collective-permute-start.20 = (bf16[1024,1024]{1,0:T(8,128)(2,1)S(1)}, bf16[1024,1024]{1,0:T(8,128)(2,1)}, u32[]{:S(2)}, u32[]{:S(2)}) collective-permute-start(bf16[1024,1024]{1,0:T(8,128)(2,1)S(1)} %convolution_convert_fusion.5), channel_id=1, source_target_pairs={{0,1},{1,0},{2,3},{3,2},{64,67},{65,66},{66,65},{67,64},{4,5},{5,4... | collective-permute-start | bytes 6291464 | tf_op jit(solution)/shard_map/ppermute | solution.py:802
  265.7 26.4 %collective-permute-start.21 = (bf16[512,2048]{1,0:T(8,128)(2,1)}, bf16[512,2048]{1,0:T(8,128)(2,1)}, u32[]{:S(2)}, u32[]{:S(2)}) collective-permute-start(bf16[512,2048]{1,0:T(8,128)(2,1)} %convolution_convert_fusion.3), channel_id=1, source_target_pairs={{0,16},{16,0},{32,48},{48,32},{64,112},{80,96},{96,80},{112,64},{1... | collective-permute-start | bytes 6291464 | tf_op jit(solution)/shard_map/ppermute | solution.py:802
  267.3 26.4 %collective-permute-start.22 = (bf16[512,2048]{1,0:T(8,128)(2,1)}, bf16[512,2048]{1,0:T(8,128)(2,1)}, u32[]{:S(2)}, u32[]{:S(2)}) collective-permute-start(bf16[512,2048]{1,0:T(8,128)(2,1)} %convolution_convert_fusion.2), channel_id=1, source_target_pairs={{0,4},{4,0},{8,12},{12,8},{64,76},{68,72},{72,68},{76,64},{1,5},{5... | collective-permute-start | bytes 6291464 | tf_op jit(solution)/shard_map/ppermute | solution.py:802
  301.3 36.9 %collective-permute-start.24 = (bf16[1024,1024]{1,0:T(8,128)(2,1)}, bf16[1024,1024]{1,0:T(8,128)(2,1)}, u32[]{:S(2)}, u32[]{:S(2)}) collective-permute-start(bf16[1024,1024]{1,0:T(8,128)(2,1)} %convolution_convert_fusion.4), channel_id=1, source_target_pairs={{0,3},{1,2},{2,1},{3,0},{64,65},{65,64},{66,67},{67,66},{4,7},{5,6... | collective-permute-start | bytes 6291464 | tf_op jit(solution)/shard_map/ppermute | solution.py:802
  308.6 25.5 %collective-permute-start.33 = (bf16[256,2048]{1,0:T(8,128)(2,1)}, bf16[256,2048]{1,0:T(8,128)(2,1)}, u32[]{:S(2)}, u32[]{:S(2)}) collective-permute-start(bf16[256,2048]{1,0:T(8,128)(2,1)} %fusion.11), channel_id=1, source_target_pairs={{0,12},{4,8},{8,4},{12,0},{64,68},{68,64},{72,76},{76,72},{1,13},{... | collective-permute-start | bytes 3145736 | tf_op jit(solution)/shard_map/ppermute | solution.py:802
  312.1 39.6 %collective-permute-start.23 = (bf16[512,1024]{1,0:T(8,128)(2,1)}, bf16[512,1024]{1,0:T(8,128)(2,1)}, u32[]{:S(2)}, u32[]{:S(2)}) collective-permute-start(bf16[512,1024]{1,0:T(8,128)(2,1)} %add_convert_fusion.3), channel_id=1, source_target_pairs={{0,3},{1,2},{2,1},{3,0},{64,65},{65,64},{66,67},{67,66},{4,7},{5,6... | collective-permute-start | bytes 3145736 | tf_op jit(solution)/shard_map/ppermute | solution.py:802
  313.3 43.2 %collective-permute-start.29 = (bf16[512,2048]{1,0:T(8,128)(2,1)}, bf16[512,2048]{1,0:T(8,128)(2,1)}, u32[]{:S(2)}, u32[]{:S(2)}) collective-permute-start(bf16[512,2048]{1,0:T(8,128)(2,1)} %convolution_convert_fusion.1), channel_id=1, source_target_pairs={{0,48},{16,32},{32,16},{48,0},{64,80},{80,64},{96,112},{112,96},{1... | collective-permute-start | bytes 6291464 | tf_op jit(solution)/shard_map/ppermute | solution.py:802
  315.4 43.4 %collective-permute-start.34 = (bf16[512,2176]{1,0:T(8,128)(2,1)}, bf16[512,2176]{1,0:T(8,128)(2,1)}, u32[]{:S(2)}, u32[]{:S(2)}) collective-permute-start(bf16[512,2176]{1,0:T(8,128)(2,1)} %convolution_convert_fusion), channel_id=1, source_target_pairs={{0,12},{4,8},{8,4},{12,0},{64,68},{68,64},{72,76},{76,72},{1,13},{... | collective-permute-start | bytes 6684680 | tf_op jit(solution)/shard_map/ppermute | solution.py:802
  334.2 20.1 %collective-permute-start.28 = (bf16[256,2048]{1,0:T(8,128)(2,1)}, bf16[256,2048]{1,0:T(8,128)(2,1)}, u32[]{:S(2)}, u32[]{:S(2)}) collective-permute-start(bf16[256,2048]{1,0:T(8,128)(2,1)} %fusion.9), channel_id=1, source_target_pairs={{0,48},{16,32},{32,16},{48,0},{64,80},{80,64},{96,112},{112,96},{1... | collective-permute-start | bytes 3145736 | tf_op jit(solution)/shard_map/ppermute | solution.py:802
  339.9 20.8 %collective-permute-start.25 = (bf16[512,1024]{1,0:T(8,128)(2,1)S(1)}, bf16[512,1024]{1,0:T(8,128)(2,1)S(1)}, u32[]{:S(2)}, u32[]{:S(2)}) collective-permute-start(bf16[512,1024]{1,0:T(8,128)(2,1)S(1)} %add_convert_fusion.1), channel_id=1, source_target_pairs={{0,1},{1,0},{2,3},{3,2},{64,67},{65,66},{66,65},{67,64},{4,5},{5,4... | collective-permute-start | bytes 3145736 | tf_op jit(solution)/shard_map/ppermute | solution.py:802
  360.6 17.8 %collective-permute-start.35 = (bf16[256,2176]{1,0:T(8,128)(2,1)S(1)}, bf16[256,2176]{1,0:T(8,128)(2,1)S(1)}, u32[]{:S(2)}, u32[]{:S(2)}) collective-permute-start(bf16[256,2176]{1,0:T(8,128)(2,1)S(1)} %fusion.2), channel_id=1, source_target_pairs={{0,4},{4,0},{8,12},{12,8},{64,76},{68,72},{72,68},{76,64},{1,5},{5... | collective-permute-start | bytes 3342344 | tf_op jit(solution)/shard_map/ppermute | solution.py:802
  363.1 36.4 %collective-permute-start.26 = (bf16[256,2048]{1,0:T(8,128)(2,1)S(1)}, bf16[256,2048]{1,0:T(8,128)(2,1)S(1)}, u32[]{:S(2)}, u32[]{:S(2)}) collective-permute-start(bf16[256,2048]{1,0:T(8,128)(2,1)S(1)} %bitcast.322), channel_id=1, source_target_pairs={{0,16},{16,0},{32,48},{48,32},{64,112},{80,96},{96,80},{112,64},{1... | collective-permute-start | bytes 3145736 | tf_op jit(solution)/shard_map/ppermute | solution.py:802
  377.5 30.0 %collective-permute-start.31 = (bf16[128,4096]{1,0:T(8,128)(2,1)S(1)}, bf16[128,4096]{1,0:T(8,128)(2,1)S(1)}, u32[]{:S(2)}, u32[]{:S(2)}) collective-permute-start(bf16[128,4096]{1,0:T(8,128)(2,1)S(1)} %bitcast.323), channel_id=1, source_target_pairs={{0,4},{4,0},{8,12},{12,8},{64,76},{68,72},{72,68},{76,64},{1,5},{5... | collective-permute-start | bytes 3145736 | tf_op jit(solution)/shard_map/ppermute | solution.py:802
  380.7 30.6 %collective-permute-start.36 = (bf16[128,4224]{1,0:T(8,128)(2,1)S(1)}, bf16[128,4224]{1,0:T(8,128)(2,1)S(1)}, u32[]{:S(2)}, u32[]{:S(2)}) collective-permute-start(bf16[128,4224]{1,0:T(8,128)(2,1)S(1)} %bitcast.318), channel_id=1, source_target_pairs={{0,1},{1,0},{2,3},{3,2},{64,67},{65,66},{66,65},{67,64},{4,5},{5,4... | collective-permute-start | bytes 3244040 | tf_op jit(solution)/shard_map/ppermute | solution.py:802
  399.7 21.1 %collective-permute-start.27 = (bf16[128,2048]{1,0:T(8,128)(2,1)S(1)}, bf16[128,2048]{1,0:T(8,128)(2,1)S(1)}, u32[]{:S(2)}, u32[]{:S(2)}) collective-permute-start(bf16[128,2048]{1,0:T(8,128)(2,1)S(1)} %fusion.18), channel_id=1, source_target_pairs={{0,48},{16,32},{32,16},{48,0},{64,80},{80,64},{96,112},{112,96},{1... | collective-permute-start | bytes 1572872 | tf_op jit(solution)/shard_map/ppermute | solution.py:802
  (85 other events, 644.6 us)
Sparse Core Ops, SparseCore 0:
  12.1 118.4 all-gather.5
  336.1 69.5 all-gather.3

commit v6 on v5

--- a/solution.py
+++ b/solution.py
@@ -303,15 +303,25 @@
     return block.reshape(-1, block.shape[-1])
 
 
-def forward_kernel(
-    x, packed, dt_weight, out_weight, heads_weight,
+def forward_kernel(unpack, x, packed, dt_weight, *refs):
+    if unpack:
+        given, results = (None, None), refs[20:22]
+        rest = refs[:20] + refs[22:]
+    else:
+        given, results = refs[:2], (None, None)
+        rest = refs[2:]
+    forward_body(unpack, x, packed, dt_weight, *given, *results, *rest)
+
+
+def forward_body(
+    unpack, x, packed, dt_weight, out_weight, heads_weight, out_result, heads_result,
     places, gate_own, gate_got, gate_far, up_own, up_got, up_far, down_own, down_got, down_far,
     input_gain, kernel, bias, step_bias, decay_log, skip,
     mixer_gain, feed_gain, cosine, sine,
     result_out, normed_out, proj_out, ssm_out, mamba_out, attended_out, middle_out, ffin_out, gate_out,
     upper_out, hidden_out,
     result, normed, proj, ssm, mamba, attended, middle, ffin, gate, upper, hidden,
-    cat, gate_mat, up_mat, down_mat, out_mat, heads_mat, sems, out_sems, feed_sems,
+    cat, gate_mat, up_mat, down_mat, out_mat, heads_mat, mixed, sems, out_sems, feed_sems,
 ):
     leaving = []
 
@@ -325,8 +335,11 @@
         pltpu.make_async_copy(packed.at[:, pl.ds(16 * j, 16), :], cat.at[j], sems.at[j])
         for j in range(4)
     ]
-    copies.append(pltpu.make_async_copy(out_weight, out_mat, sems.at[4]))
-    copies.append(pltpu.make_async_copy(heads_weight, heads_mat, sems.at[5]))
+    if unpack:
+        copies.append(pltpu.make_async_copy(packed.at[:, pl.ds(OUT0, 32), :], mixed, sems.at[4]))
+    else:
+        copies.append(pltpu.make_async_copy(out_weight, out_mat, sems.at[4]))
+        copies.append(pltpu.make_async_copy(heads_weight, heads_mat, sems.at[5]))
     pieces = (gate_own, gate_got, gate_far, up_own, up_got, up_far, down_own, down_got, down_far)
     feeds = feed_copies(places, pieces, (gate_mat, up_mat, down_mat), feed_sems)
     start_all(copies + feeds)
@@ -335,14 +348,7 @@
     proj[:, T0:CAT] = dot(normed[...], dt_weight[...])
     for j in range(4):
         copies[j].wait()
-
-        def columns(tile, carry, j=j):
-            at = pl.multiple_of(tile * 256, 256)
-            block = flat(cat[j, :, :, pl.ds(at, 256)])
-            proj[:, pl.ds(pl.multiple_of(j * 1024 + at, 256), 256)] = dot(normed[...], block)
-            return carry
-
-        lax.fori_loop(0, 4, columns, 0)
+        proj[:, 1024 * j : 1024 * j + 1024] = dot(normed[...], flat(cat[j]))
     leave((normed, normed_out), (proj, proj_out))
 
     def sequence(index, carry):
@@ -353,43 +359,34 @@
 
     lax.fori_loop(0, 2, sequence, 0)
     leave((ssm, ssm_out), (mamba, mamba_out), (attended, attended_out))
-    copies[4].wait()
-    copies[5].wait()
-
-    def joined(tile, carry):
-        at = pl.ds(pl.multiple_of(tile * 256, 256), 256)
-        part = dot(mamba[...], out_mat[:, at]) + dot(attended[...], heads_mat[:, at])
-        middle[:, at] = x[:, at].astype(F32) + part
-        return carry
-
-    lax.fori_loop(0, 4, joined, 0)
+    for copy in copies[4:]:
+        copy.wait()
+    if unpack:
+        wide = mixed[...].astype(F32)
+        out_mat[...] = wide[:, :24].reshape(INNER, WIDTH).astype(BF16)
+        heads_mat[...] = wide[:, 24:].reshape(512, WIDTH).astype(BF16)
+        leave((out_mat, out_result), (heads_mat, heads_result))
+
+    part = dot(mamba[...], out_mat[...]) + dot(attended[...], heads_mat[...])
+    middle[...] = x[...].astype(F32) + part
     value = middle[...]
     ffin[...] = (value * rms(value) * feed_gain[...]).astype(BF16)
     leave((middle, middle_out), (ffin, ffin_out))
     for copy in feeds[:8]:
         copy.wait()
 
-    def feed(tile, carry):
-        at = pl.ds(pl.multiple_of(tile * 256, 256), 256)
+    for half in range(2):
+        at = slice(1024 * half, 1024 * half + 1024)
         low = dot(ffin[...], rows_of(gate_mat[:, :, :, :, at]))
         high = dot(ffin[...], rows_of(up_mat[:, :, :, :, at]))
         gate[:, at] = low
         upper[:, at] = high
         hidden[:, at] = (low * sigmoid(low) * high).astype(BF16)
-        return carry
-
-    lax.fori_loop(0, 8, feed, 0)
     leave((gate, gate_out), (upper, upper_out), (hidden, hidden_out))
     for copy in feeds[8:]:
         copy.wait()
 
-    def last(tile, carry):
-        at = pl.ds(pl.multiple_of(tile * 256, 256), 256)
-        part = dot(hidden[...], rows_of(down_mat[:, :, :, :, at]))
-        result[:, at] = (middle[:, at] + part).astype(BF16)
-        return carry
-
-    lax.fori_loop(0, 4, last, 0)
+    result[...] = (middle[...] + dot(hidden[...], rows_of(down_mat[...]))).astype(BF16)
     leave((result, result_out))
     for copy in leaving:
         copy.wait()
@@ -414,7 +411,7 @@
     gate_in, upper_in, middle_in, feed_gain,
     grad_gate_out, grad_upper_out, grad_middle_out, feed_grad_out,
     grad_gate, grad_upper, grad_middle, feed_grad,
-    gate, upper, middle, gate_mat, up_mat, down_mat, grad_ffin, sems, out_sems, feed_sems,
+    gate, upper, middle, gate_mat, up_mat, down_mat, sems, out_sems, feed_sems,
 ):
     inputs = [
         pltpu.make_async_copy(gate_in, gate, sems.at[0]),
@@ -424,33 +421,28 @@
     pieces = (gate_own, gate_got, gate_far, up_own, up_got, up_far, down_own, down_got, down_far)
     feeds = feed_copies(places, pieces, (gate_mat, up_mat, down_mat), feed_sems)
     start_all(feeds[8:] + inputs + feeds[:8])
-    for copy in feeds[8:] + inputs:
+    for copy in feeds[8:]:
         copy.wait()
 
-    def through(tile, carry):
-        at = pl.ds(pl.multiple_of(tile * 256, 256), 256)
-        block = down_mat[tile // 2, pl.ds(lax.rem(tile, 2) * 2, 2)]
-        grad_hidden = dot_nt(grad_top[...], rows_of(block))
+    for half in range(2):
+        at = slice(1024 * half, 1024 * half + 1024)
+        grad_hidden = dot_nt(grad_top[...], rows_of(down_mat[2 * half : 2 * half + 2]))
+        if half == 0:
+            inputs[0].wait()
+            inputs[1].wait()
         low, high = gate[:, at], upper[:, at]
         slope = sigmoid(low)
         grad_upper[:, at] = (grad_hidden * (low * slope)).astype(BF16)
         part = grad_hidden * high * (slope * (1.0 + low * (1.0 - slope)))
         grad_gate[:, at] = part.astype(BF16)
-        return carry
-
-    lax.fori_loop(0, 8, through, 0)
     leaving = leave_all(((grad_gate, grad_gate_out), (grad_upper, grad_upper_out)), out_sems)
     for copy in feeds[:8]:
         copy.wait()
 
-    def back(tile, carry):
-        at = pl.ds(pl.multiple_of(tile * 256, 256), 256)
-        total = dot_nt(grad_gate[...], rows_of(gate_mat[tile]))
-        grad_ffin[:, at] = total + dot_nt(grad_upper[...], rows_of(up_mat[tile]))
-        return carry
-
-    lax.fori_loop(0, 4, back, 0)
-    grad_part, grad_gain = rms_backward(middle[...], feed_gain[...], grad_ffin[...])
+    grad_ffin = dot_nt(grad_gate[...], rows_of(gate_mat[...]))
+    grad_ffin = grad_ffin + dot_nt(grad_upper[...], rows_of(up_mat[...]))
+    inputs[2].wait()
+    grad_part, grad_gain = rms_backward(middle[...], feed_gain[...], grad_ffin)
     feed_grad[...] = grad_gain
     grad_middle[...] = grad_top[...].astype(F32) + grad_part
     leaving += leave_all(
@@ -488,19 +480,8 @@
     copies[0].wait()
     copies[1].wait()
 
-    def through(tile, carry):
-        at = pl.ds(pl.multiple_of(tile * 256, 256), 256)
-        grad_mamba[:, at] = dot_nt(grad_branch[...], out_mat[at, :])
-        return carry
-
-    lax.fori_loop(0, 6, through, 0)
-
-    def through_heads(tile, carry):
-        at = pl.ds(pl.multiple_of(tile * 256, 256), 256)
-        grad_attended[:, at] = dot_nt(grad_branch[...], heads_mat[at, :])
-        return carry
-
-    lax.fori_loop(0, 2, through_heads, 0)
+    grad_mamba[...] = dot_nt(grad_branch[...], out_mat[...])
+    grad_attended[...] = dot_nt(grad_branch[...], heads_mat[...])
     small = {
         1: kernel_grad,
         2: bias_grad,
@@ -556,28 +537,20 @@
     grad_cat, grad_middle, x, packed, dt_weight, input_gain,
     grad_start_out, start_low_out, input_grad_out,
     grad_start, start_low, input_grad,
-    cat, grad_normed, sems, out_sems,
+    cat, sems, out_sems,
 ):
     copies = [
         pltpu.make_async_copy(packed.at[:, pl.ds(16 * j, 16), :], cat.at[j], sems.at[j])
         for j in range(4)
     ]
     start_all(copies)
-    for copy in copies:
-        copy.wait()
-
-    def back(tile, carry):
-        at = pl.ds(pl.multiple_of(tile * 256, 256), 256)
-        total = dot_nt(grad_cat[:, T0:CAT], dt_weight[at, :])
-        for j in range(4):
-            block = flat(cat[j, pl.ds(tile * 16, 16)])
-            total = total + dot_nt(grad_cat[:, 1024 * j : 1024 * j + 1024], block)
-        grad_normed[:, at] = total
-        return carry
-
-    lax.fori_loop(0, 4, back, 0)
+    grad_normed = dot_nt(grad_cat[:, T0:CAT], dt_weight[...])
+    for j in range(4):
+        copies[j].wait()
+        part = dot_nt(grad_cat[:, 1024 * j : 1024 * j + 1024], flat(cat[j]))
+        grad_normed = grad_normed + part
     state = x[...].astype(F32)
-    grad_state, grad_gain = rms_backward(state, input_gain[...], grad_normed[...])
+    grad_state, grad_gain = rms_backward(state, input_gain[...], grad_normed)
     input_grad[...] = grad_gain
     total = grad_middle[...] + grad_state
     grad_start[...] = total
@@ -616,7 +589,9 @@
 
 
 def run_forward(start, mats, small, rope):
-    packed, dt_weight, out_weight, heads_weight, feeds = mats
+    packed, dt_weight, *given, feeds = mats
+    unpack = not given
+    extra = (shape(INNER, WIDTH, BF16), shape(512, WIDTH, BF16))
     shapes = (
         shape(ROWS, WIDTH, BF16),
         shape(ROWS, WIDTH, BF16),
@@ -631,18 +606,19 @@
         shape(ROWS, FEED, BF16),
     )
     return pl.pallas_call(
-        forward_kernel,
-        out_shape=shapes,
-        in_specs=[VMEM, ANY, VMEM, ANY, ANY, SMEM] + [ANY] * 9 + [VMEM] * 10,
-        out_specs=(ANY,) * len(shapes),
+        functools.partial(forward_kernel, unpack),
+        out_shape=extra + shapes if unpack else shapes,
+        in_specs=[VMEM, ANY, VMEM] + [ANY] * len(given) + [SMEM] + [ANY] * 9 + [VMEM] * 10,
+        out_specs=(ANY,) * (len(shapes) + 2 * unpack),
         scratch_shapes=[
             *mirrored(shapes),
             scratch(4, 64, 16, 1024),
             *FEED_MATS,
             scratch(INNER, WIDTH),
             scratch(512, WIDTH),
+            scratch(64, 32, WIDTH) if unpack else scratch(16, 128),
             pltpu.SemaphoreType.DMA((6,)),
-            pltpu.SemaphoreType.DMA((len(shapes),)),
+            pltpu.SemaphoreType.DMA((len(shapes) + 2,)),
             pltpu.SemaphoreType.DMA((12,)),
         ],
         compiler_params=pltpu.CompilerParams(vmem_limit_bytes=LIMIT),
@@ -650,7 +626,7 @@
             flops=2 * ROWS * 12_600_000, bytes_accessed=40_000_000, transcendentals=2_000_000
         ),
         name="forward",
-    )(start, packed, dt_weight, out_weight, heads_weight, *feeds, *small, *rope)
+    )(start, packed, dt_weight, *given, *feeds, *small, *rope)
 
 
 def run_feed_backward(active, grad_top, mats, gate, upper, middle, feed_gain, earlier=()):
@@ -671,7 +647,6 @@
             scratch(ROWS, FEED, dtype=F32),
             scratch(ROWS, WIDTH, dtype=F32),
             *FEED_MATS,
-            scratch(ROWS, WIDTH, dtype=F32),
             pltpu.SemaphoreType.DMA((3,)),
             pltpu.SemaphoreType.DMA((4,)),
             pltpu.SemaphoreType.DMA((12,)),
@@ -737,7 +712,6 @@
         scratch_shapes=[
             *mirrored(shapes),
             scratch(4, 64, 16, 1024),
-            scratch(ROWS, WIDTH, dtype=F32),
             pltpu.SemaphoreType.DMA((4,)),
             pltpu.SemaphoreType.DMA((3,)),
         ],
@@ -811,12 +785,15 @@
     return exchange(sent, axis, partners(axis, turn)[2][0])
 
 
-def exchanged(part, got, axis, turn):
-    me, (one, two), (swap_one, swap_two) = partners(axis, turn)
-    half = got.shape[0] // 2
-    handed = part([two]) + got[half:].astype(F32)
-    last = exchange(handed.astype(BF16), axis, swap_two)
-    return part([me]) + got[:half].astype(F32) + last.astype(F32)
+def handed_on(part, got, axis, turn):
+    me, (one, two), swaps = partners(axis, turn)
+    return (part([two]) + got[got.shape[0] // 2 :].astype(F32)).astype(BF16)
+
+
+def totalled(part, got, handed, axis, turn):
+    me, found, (swap_one, swap_two) = partners(axis, turn)
+    last = exchange(handed, axis, swap_two)
+    return part([me]) + got[: got.shape[0] // 2].astype(F32) + last.astype(F32)
 
 
 def product_of(left, right, place):
@@ -840,7 +817,7 @@
 def summed_on(array, axis, dim, turn):
     part = quarters_of(array, dim)
     got = first_got(first_sent(part, axis, turn), axis, turn)
-    return exchanged(part, got, axis, turn)
+    return totalled(part, got, handed_on(part, got, axis, turn), axis, turn)
 
 
 def second_summed(parts, order, depth):
@@ -921,8 +898,6 @@
     mats = (
         packed,
         jnp.pad(dt_weight, ((0, 0), (0, 128 - HEADS))),
-        packed[:, OUT0:HEADS0].reshape(INNER, WIDTH),
-        packed[:, HEADS0:DT0].reshape(512, WIDTH),
         (places, *(piece for blocks, found in feeds for piece in blocks)),
     )
     small = prepared_small([piece[0] for piece in pieces])
@@ -931,7 +906,8 @@
     first = lax.axis_index("section") == 0
 
     start_low = layer_input.reshape(rows, width)
-    kept_low = run_forward(start_low, mats, small, rope)
+    out_mat, heads_mat, *kept_low = run_forward(start_low, mats, small, rope)
+    mats = (*mats[:2], out_mat, heads_mat, mats[2])
     start_high = lax.ppermute(kept_low[0], "section", [(0, 1)])
     kept_high = run_forward(start_high, mats, small, rope)
     layer_outputs = jnp.where(first, kept_low[0], kept_high[0]).reshape(1, micro, part, width)
@@ -965,24 +941,21 @@
     grad_low = jnp.where(first, top_low, top_high)
     grad_low, grad_gate, grad_upper = lax.optimization_barrier((grad_low, grad_gate, grad_upper))
     orders = ((2, 0, 1), (0, 1, 2), (1, 2, 0))
+    axes = [DP[order[0]] for order in orders]
     products = [
         product_of(left, right, order[0])
         for left, right, order in zip(
             (hidden_t, ffin_t, ffin_t), (grad_low, grad_gate, grad_upper), orders
         )
     ]
-    sents = [first_sent(p, DP[order[0]], 0) for p, order in zip(products, orders)]
+    sents = [first_sent(p, axis, 0) for p, axis in zip(products, axes)]
     grad_middle, *sents = lax.optimization_barrier((grad_middle, *sents))
-    gots = [first_got(sent, DP[order[0]], 0) for sent, order in zip(sents, orders)]
+    gots = [first_got(sent, axis, 0) for sent, axis in zip(sents, axes)]
     mix = run_mix_backward(
         on_low, grad_middle, mats, kept_low[2], kept_low[3], small, rope, pick, mix_high
     )
     grad_branch, grad_cat, *small_grads = mix
-    grad_branch, grad_cat, *gots = lax.optimization_barrier((grad_branch, grad_cat, *gots))
-    feed_parts = [
-        exchanged(p, got, DP[order[0]], 0) for p, got, order in zip(products, gots, orders)
-    ]
-    products = [
+    mix_products = [
         product_of(left, right, order[0])
         for left, right, order in zip(
             (joined_t, normed_t, normed_t),
@@ -990,14 +963,22 @@
             orders,
         )
     ]
-    sents = [first_sent(p, DP[order[0]], 1) for p, order in zip(products, orders)]
-    grad_middle, *sents = lax.optimization_barrier((grad_middle, *sents))
-    mix_parts = []
-    for p, sent, order in zip(products, sents, orders):
-        got = first_got(sent, DP[order[0]], 1)
-        mix_parts.append(exchanged(p, got, DP[order[0]], 1))
+    mix_sents = [first_sent(p, axis, 1) for p, axis in zip(mix_products, axes)]
+    pending = lax.optimization_barrier((*gots, *mix_sents))
+    gots, mix_sents = pending[:3], pending[3:]
+    mix_gots = [first_got(sent, axis, 1) for sent, axis in zip(mix_sents, axes)]
+    handed = [handed_on(p, got, axis, 0) for p, got, axis in zip(products, gots, axes)]
+    last_middle, *unused = lax.optimization_barrier((grad_middle, *handed))
+    feed_parts = [
+        totalled(p, got, hand, axis, 0)
+        for p, got, hand, axis in zip(products, gots, handed, axes)
+    ]
+    mix_parts = [
+        totalled(p, got, handed_on(p, got, axis, 1), axis, 1)
+        for p, got, axis in zip(mix_products, mix_gots, axes)
+    ]
     grad_start, unused, input_grad = run_input_backward(
-        on_low, grad_cat, grad_middle, start_low, mats, small[0], input_high
+        on_low, grad_cat, last_middle, start_low, mats, small[0], input_high
     )
     small_grads = [input_grad, *small_grads]
     input_g, kernel_g, bias_g, step_g, decay_g, skip_g, mixer_g = small_grads
@@ -1013,7 +994,8 @@
     )
     vector = jnp.concatenate([piece.reshape(-1) for piece in small_grads])
     vector = jnp.pad(vector, (0, -vector.shape[0] % 1024)).reshape(-1, 128)
-    total = jnp.sum(lax.all_gather(vector, DP, axis=0, tiled=False), axis=0).reshape(-1)
+    vectors = lax.all_gather(vector.astype(BF16), DP, axis=0, tiled=False)
+    total = jnp.sum(vectors.astype(F32), axis=0).reshape(-1)
     seconds = [
         second_summed(pair, order, depth)
         for pair, order, depth in zip(zip(feed_parts, mix_parts), orders, (32, 16, 16))

time: 464 us -> 430 us (0.927)
  waiting for transfers between devices: 173 us -> 152 us
  other arithmetic: 22.6 us -> 36.4 us
  Pallas kernels: 97.6 us -> 86.7 us
  starting transfers between devices: 71.6 us -> 61.9 us
  local copies, waits for them, and re-layouts: 38.5 us -> 31.8 us
    ppermute x42, waiting for transfers between devices: 95.1 us -> 73.1 us  [exchange(): return lax.ppermute(array, ('section', axis), pairs)]
    all_gather x1, waiting for transfers between devices: 0.02 us -> 9.7 us  [on_device(): vectors = lax.all_gather(vector.astype(BF16), DP, axis=0, tiled=False)]
    ppermute x42, starting transfers between devices: 68.1 us -> 59 us  [exchange(): return lax.ppermute(array, ('section', axis), pairs)]
    pallas_call x2, Pallas kernels: 47.9 us -> 39 us  [run_forward(): pl.pallas_call(functools.partial(forward_kernel, unpack), out_shape=extra...]
    ppermute x1, waiting for transfers between devices: 32.9 us -> 24.3 us  [on_device(): top_low = lax.ppermute(input_high[1], 'section', [(1, 0)])]
  transfers between devices with their start and end apart: 46 -> 46, of which waited for: 22 -> 20; matrix products, arithmetic and copies ran while one was open for 15% -> 19% of each run, Pallas kernels for 6% -> 6%
where the time goes in v6:
time: 430 us; the launch traced here: 423 us
  waiting for transfers between devices  152 us (35%)
  Pallas kernels  86.7 us (20%)
  starting transfers between devices  61.9 us (14%)
  matrix products  38.7 us (9%)
  other arithmetic  36.4 us (8%)
  local copies, waits for them, and re-layouts  31.8 us (7%)
  between operations  15.4 us (4%)
    ppermute x42, waiting for transfers between devices, exchange(): return lax.ppermute(array, ('section', axis), pairs)  73.1 us
    ppermute x42, starting transfers between devices, exchange(): return lax.ppermute(array, ('section', axis), pairs)  59 us
    all_gather x1, waiting for transfers between devices, on_device(): packed = lax.all_gather(own, DP, axis=0, tiled=False)  45.3 us
    pallas_call x2, Pallas kernels, run_forward(): pl.pallas_call(functools.partial(forward_kernel, unpack), out_shape=extra...  39 us
    dot_general x18, matrix products, dot(): return jnp.dot(left, right, preferred_element_type=F32)  38.7 us
    ppermute x1, waiting for transfers between devices, on_device(): top_low = lax.ppermute(input_high[1], 'section', [(1, 0)])  24.3 us
    pallas_call x2, Pallas kernels, run_mix_backward(): pl.pallas_call(functools.partial(mix_backward_kernel, len(earlier)), out_...  20 us
    pallas_call x2, Pallas kernels, run_input_backward(): pl.pallas_call(functools.partial(input_backward_kernel, len(earlier)), ou...  14.3 us
  transfers between devices with their start and end apart: 46, of which 20 were waited for; matrix products, arithmetic and copies ran while one was open for 19% of the time, Pallas kernels for 6%

profile of v6, /device:TPU:0, one launch (start us, length us, event | category | flops | bytes accessed | tf_op | source)
XLA Modules:
  0.0 423.3 jit_solution(9391327471878925762)
XLA Ops:
  24.3 2.8 collective-permute-start.1
  35.2 2.8 collective-permute-start.9
  41.0 4.7 %collective-permute-done.9 = bf16[2,4,16,2048]{3,2,1,0:T(8,128)(2,1)S(1)} collective-permute-done((bf16[2,4,16,2048]{3,2,1,0:T(8,128)(2,1)S(1)}, bf16[2,4,16,2048]{3,2,1,0:T(8,128)(2,1)S(1)}, u32[]{:S(2)}, u32[]{:S(2)}) %collective-permute-start.9) | collective-permute-done | bytes 524320 | tf_op jit(solution)/shard_map/ppermute | solution.py:776
  47.1 7.6 %collective-permute-done.3 = bf16[2,4,16,2048]{3,2,1,0:T(8,128)(2,1)S(1)} collective-permute-done((bf16[2,4,16,2048]{3,2,1,0:T(8,128)(2,1)S(1)}, bf16[2,4,16,2048]{3,2,1,0:T(8,128)(2,1)S(1)}, u32[]{:S(2)}, u32[]{:S(2)}) %collective-permute-start.3) | collective-permute-done | bytes 524320 | tf_op jit(solution)/shard_map/ppermute | solution.py:776
  54.8 13.5 %collective-permute-done.10.refs_5_.refs_7_.refs_6_ = bf16[4,4,16,2048]{3,2,1,0:T(8,128)(2,1)S(1)} collective-permute-done((bf16[4,4,16,2048]{3,2,1,0:T(8,128)(2,1)S(1)}, bf16[4,4,16,2048]{3,2,1,0:T(8,128)(2,1)S(1)}, u32[]{:S(2)}, u32[]{:S(2)}) %collective-permute-start.10) | collective-permute-done | bytes 1048608 | tf_op jit(solution)/shard_map/ppermute | solution.py:776
  73.8 2.7 collective-permute-start.17
  78.2 2.9 collective-permute-start.5
  85.4 45.3 %all-gather.6.cloned.1.call-done = bf16[6656,1024]{1,0:T(8,128)(2,1)} async-done(((bf16[104,1024]{1,0:T(8,128)(2,1)}), bf16[6656,1024]{1,0:T(8,128)(2,1)}) %all-gather.6.cloned.1.call-update) | async-done | bytes 13631504 | tf_op jit(solution)/shard_map/all_gather | solution.py:887
  135.5 19.6 %forward.2 = (bf16[1536,1024]{1,0:T(8,128)(2,1)}, bf16[512,1024]{1,0:T(8,128)(2,1)}, bf16[256,1024]{1,0:T(8,128)(2,1)}, bf16[256,1024]{1,0:T(8,128)(2,1)}, f32[2...) custom-call(bf16[256,1024]{1,0:T(8,128)(2,1)} %bitcast.296, ...), custom_call_target="tpu_custom_call" | custom-call | flops 6451200000 | bytes 40000000 | tf_op jit(solution)/shard_map/forward/pallas_call | solution.py:608
  159.6 19.4 %forward.3 = (bf16[256,1024]{1,0:T(8,128)(2,1)}, bf16[256,1024]{1,0:T(8,128)(2,1)}, f32[256,4224]{1,0:T(8,128)}, f32[256,1536]{1,0:T(8,128)}, bf16[256,1536]{1,0...) custom-call(bf16[256,1024]{1,0:T(8,128)(2,1)} %copy-done.22, ...), custom_call_target="tpu_custom_call" | custom-call | flops 6451200000 | bytes 40000000 | tf_op jit(solution)/shard_map/forward/pallas_call | solution.py:608
  188.4 6.2 %input_backward.2 = (f32[256,1024]{1,0:T(8,128)}, bf16[256,1024]{1,0:T(8,128)(2,1)}, f32[1,1024]{1,0:T(1,128)}) custom-call(s32[1]{0:T(128)} %bitcast.54.active, bf16[256,4224]{1,0:T(8,128)(2,1)} %get-tuple-element.100.refs_0_.refs_15_, f32[256,1024]{1,0:T(8,128)} %get-tuple-element.97.refs_0_.refs_1_.refs_17_, bf16[256,1024]{1,0:T(8,128)(2,1)} %copy-done.22, ...), custom_call_target="tpu_custom_call" | custom-call | flops 2150400000 | bytes 13000000 | tf_op jit(solution)/shard_map/input_backward/pallas_call | solution.py:707
  202.1 24.3 %collective-permute-done.19.refs_0_ = bf16[256,1024]{1,0:T(8,128)(2,1)S(1)} collective-permute-done((bf16[256,1024]{1,0:T(8,128)(2,1)}, bf16[256,1024]{1,0:T(8,128)(2,1)S(1)}, u32[]{:S(2)}, u32[]{:S(2)}) %collective-permute-start.19) | collective-permute-done | bytes 524320 | tf_op jit(solution)/shard_map/ppermute | solution.py:927
  227.3 11.8 %feed_backward.3 = (bf16[256,2048]{1,0:T(8,128)(2,1)}, bf16[256,2048]{1,0:T(8,128)(2,1)}, f32[256,1024]{1,0:T(8,128)}, f32[1,1024]{1,0:T(1,128)}) custom-call(s32[1]{0:T(128)S(6)} %sub.29.active, bf16[256,1024]{1,0:T(8,128)(2,1)} %copy-done.21, ...), custom_call_target="tpu_custom_call", output_to_operand_aliasing={{0}: (16, {}), {1}: (17, {}), {2}: (18, {}), {3}: (19, {})} | custom-call | flops 3225600000 | bytes 22000000 | tf_op jit(solution)/shard_map/feed_backward/pallas_call | solution.py:639
  248.0 18.3 %mix_backward.3 = (bf16[256,1024]{1,0:T(8,128)(2,1)}, bf16[256,4224]{1,0:T(8,128)(2,1)}, f32[4,1792]{1,0:T(4,128)}, f32[1,1792]{1,0:T(1,128)}, f32[1,128]{1,0:T(...) custom-call(s32[1]{0:T(128)S(6)} %sub.29.active, ...), custom_call_target="tpu_custom_call", output_to_operand_aliasing={{0}: (15, {}), {1}: (16, {}), {2}: (17, {}), {3}: (18, {}),... | custom-call | flops 1075200000 | bytes 14000000 | tf_op jit(solution)/shard_map/mix_backward/pallas_call | solution.py:675
  268.3 2.9 fusion.51
  290.6 2.7 add_convert_fusion.7
  298.6 8.1 %input_backward.3 = (f32[256,1024]{1,0:T(8,128)}, bf16[256,1024]{1,0:T(8,128)(2,1)}, f32[1,1024]{1,0:T(1,128)}) custom-call(s32[1]{0:T(128)S(6)} %sub.29.active, bf16[256,4224]{1,0:T(8,128)(2,1)} %get-tuple-element.128.refs_0_, f32[256,1024]{1,0:T(8,128)} %get-tuple-element.142.refs_0_.refs_1_, ...), custom_call_target="tpu_custom_call", output_to_operand_aliasing={{0}: (7, {}), {1}: (8, {}), {2}: (9, {})} | custom-call | flops 2150400000 | bytes 13000000 | tf_op jit(solution)/shard_map/input_backward/pallas_call | solution.py:707
  311.6 4.5 %collective-permute-done.24 = bf16[1024,1024]{1,0:T(8,128)(2,1)} collective-permute-done((bf16[1024,1024]{1,0:T(8,128)(2,1)}, bf16[1024,1024]{1,0:T(8,128)(2,1)}, u32[]{:S(2)}, u32[]{:S(2)}) %collective-permute-start.24) | collective-permute-done | bytes 2097184 | tf_op jit(solution)/shard_map/ppermute | solution.py:776
  319.0 12.6 %collective-permute-done.23 = bf16[512,1024]{1,0:T(8,128)(2,1)} collective-permute-done((bf16[512,1024]{1,0:T(8,128)(2,1)}, bf16[512,1024]{1,0:T(8,128)(2,1)}, u32[]{:S(2)}, u32[]{:S(2)}) %collective-permute-start.23) | collective-permute-done | bytes 1048608 | tf_op jit(solution)/shard_map/ppermute | solution.py:776
  333.7 3.3 collective-permute-done.28
  348.3 8.2 %collective-permute-done.30 = bf16[256,2048]{1,0:T(8,128)(2,1)S(1)} collective-permute-done((bf16[256,2048]{1,0:T(8,128)(2,1)S(1)}, bf16[256,2048]{1,0:T(8,128)(2,1)S(1)}, u32[]{:S(2)}, u32[]{:S(2)}) %collective-permute-start.30) | collective-permute-done | bytes 1048608 | tf_op jit(solution)/shard_map/ppermute | solution.py:776
  363.6 9.7 %all-gather.4.cloned.1.call-done = bf16[64,104,128]{2,1,0:T(8,128)(2,1)} async-done(((bf16[1,104,128]{2,1,0:T(8,128)(2,1)}), bf16[64,104,128]{2,1,0:T(8,128)(2,1)}) %all-gather.4.cloned.1.call-update) | async-done | bytes 1703952 | tf_op jit(solution)/shard_map/all_gather | solution.py:997
  383.9 5.7 %collective-permute-done.32 = bf16[64,4096]{1,0:T(8,128)(2,1)S(1)} collective-permute-done((bf16[64,4096]{1,0:T(8,128)(2,1)S(1)}, bf16[64,4096]{1,0:T(8,128)(2,1)S(1)}, u32[]{:S(2)}, u32[]{:S(2)}) %collective-permute-start.32) | collective-permute-done | bytes 524320 | tf_op jit(solution)/shard_map/ppermute | solution.py:776
  399.0 5.6 %collective-permute-done.42 = bf16[64,2048]{1,0:T(8,128)(2,1)S(1)} collective-permute-done((bf16[64,2048]{1,0:T(8,128)(2,1)S(1)}, bf16[64,2048]{1,0:T(8,128)(2,1)S(1)}, u32[]{:S(2)}, u32[]{:S(2)}) %collective-permute-start.42) | collective-permute-done | bytes 262176 | tf_op jit(solution)/shard_map/ppermute | solution.py:776
  (356 shorter events, 162.9 us)
Async XLA Ops:
  7.2 123.5 %all-gather.6.cloned.1.call-start = ((), (), s32[]{:S(2)}) async-start(), calls=%async_computation.1 | async-start | bytes 13844480 | tf_op jit(solution)/shard_map/all_gather | solution.py:887
  12.0 361.3 %all-gather.4.cloned.1.call-start = ((), (), s32[]{:S(2)}) async-start(), calls=%async_computation | async-start | bytes 1730560 | tf_op jit(solution)/shard_map/all_gather | solution.py:997
  38.4 16.3 %collective-permute-start.3 = (bf16[2,4,16,2048]{3,2,1,0:T(8,128)(2,1)S(1)}, bf16[2,4,16,2048]{3,2,1,0:T(8,128)(2,1)S(1)}, u32[]{:S(2)}, u32[]{:S(2)}) collective-permute-start(bf16[2,4,16,2048]{3,2,1,0:T(8,128)(2,1)S(1)} %pad_maximum_fusion.9), channel_id=1, source_target_pairs={{0,12},{4,8},{8,4},{12,0},{64,68},{68,64},{72,76},{76,72},{1,13},{... | collective-permute-start | bytes 1572872 | tf_op jit(solution)/shard_map/ppermute | solution.py:776
  45.7 22.6 %collective-permute-start.10 = (bf16[4,4,16,2048]{3,2,1,0:T(8,128)(2,1)S(1)}, bf16[4,4,16,2048]{3,2,1,0:T(8,128)(2,1)S(1)}, u32[]{:S(2)}, u32[]{:S(2)}) collective-permute-start(bf16[4,4,16,2048]{3,2,1,0:T(8,128)(2,1)S(1)} %fusion.38.refs_4_.refs_6_.refs_5_), channel_id=1, source_target_pairs={{0,4},{4,0},{8,12},{12,8},{64,76},{68,72},{72,68},{76,64},{1,5},{5... | collective-permute-start | bytes 3145736 | tf_op jit(solution)/shard_map/ppermute | solution.py:776
  46.9 25.2 %collective-permute-start.16 = (bf16[4,4,32,1024]{3,2,1,0:T(8,128)(2,1)S(1)}, bf16[4,4,32,1024]{3,2,1,0:T(8,128)(2,1)S(1)}, u32[]{:S(2)}, u32[]{:S(2)}) collective-permute-start(bf16[4,4,32,1024]{3,2,1,0:T(8,128)(2,1)S(1)} %slice_dynamic-update-slice_fusion.refs_7_.refs_9_.refs_8_), channel_id=1, source_target_pairs={{0,1},{1,0},{2,3},{3,2},{64,67},{65,66},{66,65},{67,64},{4,5},{5,4... | collective-permute-start | bytes 3145736 | tf_op jit(solution)/shard_map/ppermute | solution.py:776
  54.8 21.7 %collective-permute-start.4 = (bf16[4,4,16,2048]{3,2,1,0:T(8,128)(2,1)S(1)}, bf16[4,4,16,2048]{3,2,1,0:T(8,128)(2,1)S(1)}, u32[]{:S(2)}, u32[]{:S(2)}) collective-permute-start(bf16[4,4,16,2048]{3,2,1,0:T(8,128)(2,1)S(1)} %slice_dynamic-update-slice_fusion.2.refs_1_.refs_3_.refs_2_), channel_id=1, source_target_pairs={{0,16},{16,0},{32,48},{48,32},{64,112},{80,96},{96,80},{112,64},{1... | collective-permute-start | bytes 3145736 | tf_op jit(solution)/shard_map/ppermute | solution.py:776
  70.0 64.2 %collective-permute-start.11 = (bf16[2,4,4,16,2048]{4,3,2,1,0:T(8,128)(2,1)}, bf16[2,4,4,16,2048]{4,3,2,1,0:T(8,128)(2,1)}, u32[]{:S(2)}, u32[]{:S(2)}) collective-permute-start(bf16[2,4,4,16,2048]{4,3,2,1,0:T(8,128)(2,1)} %pad_maximum_fusion.2), channel_id=1, source_target_pairs={{0,12},{4,8},{8,4},{12,0},{64,68},{68,64},{72,76},{76,72},{1,13},{... | collective-permute-start | bytes 6291464 | tf_op jit(solution)/shard_map/ppermute | solution.py:776
  73.8 60.4 %collective-permute-start.17 = (bf16[2,4,4,32,1024]{4,3,2,1,0:T(8,128)(2,1)}, bf16[2,4,4,32,1024]{4,3,2,1,0:T(8,128)(2,1)S(1)}, u32[]{:S(2)}, u32[]{:S(2)}) collective-permute-start(bf16[2,4,4,32,1024]{4,3,2,1,0:T(8,128)(2,1)} %pad_maximum_fusion.3), channel_id=1, source_target_pairs={{0,3},{1,2},{2,1},{3,0},{64,65},{65,64},{66,67},{67,66},{4,7},{5,6... | collective-permute-start | bytes 6291464 | tf_op jit(solution)/shard_map/ppermute | solution.py:776
  78.2 56.0 %collective-permute-start.5 = (bf16[2,4,4,16,2048]{4,3,2,1,0:T(8,128)(2,1)}, bf16[2,4,4,16,2048]{4,3,2,1,0:T(8,128)(2,1)}, u32[]{:S(2)}, u32[]{:S(2)}) collective-permute-start(bf16[2,4,4,16,2048]{4,3,2,1,0:T(8,128)(2,1)} %pad_maximum_fusion.1), channel_id=1, source_target_pairs={{0,48},{16,32},{32,16},{48,0},{64,80},{80,64},{96,112},{112,96},{1... | collective-permute-start | bytes 6291464 | tf_op jit(solution)/shard_map/ppermute | solution.py:776
  194.6 31.8 %collective-permute-start.19 = (bf16[256,1024]{1,0:T(8,128)(2,1)}, bf16[256,1024]{1,0:T(8,128)(2,1)S(1)}, u32[]{:S(2)}, u32[]{:S(2)}) collective-permute-start(bf16[256,1024]{1,0:T(8,128)(2,1)} %get-tuple-element.101.refs_7_), channel_id=1, source_target_pairs={{64,0},{65,1},{66,2},{67,3},{68,4},{69,5},{70,6},{71,7},{72,8},{73... | collective-permute-start | bytes 1572872 | tf_op jit(solution)/shard_map/ppermute | solution.py:927
  245.3 35.9 %collective-permute-start.20 = (bf16[1024,1024]{1,0:T(8,128)(2,1)}, bf16[1024,1024]{1,0:T(8,128)(2,1)}, u32[]{:S(2)}, u32[]{:S(2)}) collective-permute-start(bf16[1024,1024]{1,0:T(8,128)(2,1)} %convolution_convert_fusion.5), channel_id=1, source_target_pairs={{0,1},{1,0},{2,3},{3,2},{64,67},{65,66},{66,65},{67,64},{4,5},{5,4... | collective-permute-start | bytes 6291464 | tf_op jit(solution)/shard_map/ppermute | solution.py:776
  246.8 34.5 %collective-permute-start.21 = (bf16[512,2048]{1,0:T(8,128)(2,1)}, bf16[512,2048]{1,0:T(8,128)(2,1)}, u32[]{:S(2)}, u32[]{:S(2)}) collective-permute-start(bf16[512,2048]{1,0:T(8,128)(2,1)} %convolution_convert_fusion.3), channel_id=1, source_target_pairs={{0,16},{16,0},{32,48},{48,32},{64,112},{80,96},{96,80},{112,64},{1... | collective-permute-start | bytes 6291464 | tf_op jit(solution)/shard_map/ppermute | solution.py:776
  247.7 33.5 %collective-permute-start.22 = (bf16[512,2048]{1,0:T(8,128)(2,1)}, bf16[512,2048]{1,0:T(8,128)(2,1)}, u32[]{:S(2)}, u32[]{:S(2)}) collective-permute-start(bf16[512,2048]{1,0:T(8,128)(2,1)} %convolution_convert_fusion.2), channel_id=1, source_target_pairs={{0,4},{4,0},{8,12},{12,8},{64,76},{68,72},{72,68},{76,64},{1,5},{5... | collective-permute-start | bytes 6291464 | tf_op jit(solution)/shard_map/ppermute | solution.py:776
  281.2 34.9 %collective-permute-start.24 = (bf16[1024,1024]{1,0:T(8,128)(2,1)}, bf16[1024,1024]{1,0:T(8,128)(2,1)}, u32[]{:S(2)}, u32[]{:S(2)}) collective-permute-start(bf16[1024,1024]{1,0:T(8,128)(2,1)} %convolution_convert_fusion.4), channel_id=1, source_target_pairs={{0,3},{1,2},{2,1},{3,0},{64,65},{65,64},{66,67},{67,66},{4,7},{5,6... | collective-permute-start | bytes 6291464 | tf_op jit(solution)/shard_map/ppermute | solution.py:776
  286.4 21.1 %collective-permute-start.33 = (bf16[256,2048]{1,0:T(8,128)(2,1)}, bf16[256,2048]{1,0:T(8,128)(2,1)}, u32[]{:S(2)}, u32[]{:S(2)}) collective-permute-start(bf16[256,2048]{1,0:T(8,128)(2,1)} %fusion.5), channel_id=1, source_target_pairs={{0,12},{4,8},{8,4},{12,0},{64,68},{68,64},{72,76},{76,72},{1,13},{... | collective-permute-start | bytes 3145736 | tf_op jit(solution)/shard_map/ppermute | solution.py:776
  288.9 50.4 %collective-permute-start.29 = (bf16[512,2048]{1,0:T(8,128)(2,1)}, bf16[512,2048]{1,0:T(8,128)(2,1)}, u32[]{:S(2)}, u32[]{:S(2)}) collective-permute-start(bf16[512,2048]{1,0:T(8,128)(2,1)} %convolution_convert_fusion.1), channel_id=1, source_target_pairs={{0,48},{16,32},{32,16},{48,0},{64,80},{80,64},{96,112},{112,96},{1... | collective-permute-start | bytes 6291464 | tf_op jit(solution)/shard_map/ppermute | solution.py:776
  293.3 38.3 %collective-permute-start.23 = (bf16[512,1024]{1,0:T(8,128)(2,1)}, bf16[512,1024]{1,0:T(8,128)(2,1)}, u32[]{:S(2)}, u32[]{:S(2)}) collective-permute-start(bf16[512,1024]{1,0:T(8,128)(2,1)} %add_convert_fusion.7), channel_id=1, source_target_pairs={{0,3},{1,2},{2,1},{3,0},{64,65},{65,64},{66,67},{67,66},{4,7},{5,6... | collective-permute-start | bytes 3145736 | tf_op jit(solution)/shard_map/ppermute | solution.py:776
  294.3 46.8 %collective-permute-start.34 = (bf16[512,2176]{1,0:T(8,128)(2,1)}, bf16[512,2176]{1,0:T(8,128)(2,1)}, u32[]{:S(2)}, u32[]{:S(2)}) collective-permute-start(bf16[512,2176]{1,0:T(8,128)(2,1)} %convolution_convert_fusion), channel_id=1, source_target_pairs={{0,12},{4,8},{8,4},{12,0},{64,68},{68,64},{72,76},{76,72},{1,13},{... | collective-permute-start | bytes 6684680 | tf_op jit(solution)/shard_map/ppermute | solution.py:776
  307.5 29.5 %collective-permute-start.28 = (bf16[256,2048]{1,0:T(8,128)(2,1)}, bf16[256,2048]{1,0:T(8,128)(2,1)}, u32[]{:S(2)}, u32[]{:S(2)}) collective-permute-start(bf16[256,2048]{1,0:T(8,128)(2,1)} %fusion.4), channel_id=1, source_target_pairs={{0,48},{16,32},{32,16},{48,0},{64,80},{80,64},{96,112},{112,96},{1... | collective-permute-start | bytes 3145736 | tf_op jit(solution)/shard_map/ppermute | solution.py:776
  317.8 25.3 %collective-permute-start.25 = (bf16[512,1024]{1,0:T(8,128)(2,1)S(1)}, bf16[512,1024]{1,0:T(8,128)(2,1)S(1)}, u32[]{:S(2)}, u32[]{:S(2)}) collective-permute-start(bf16[512,1024]{1,0:T(8,128)(2,1)S(1)} %add_convert_fusion.5), channel_id=1, source_target_pairs={{0,1},{1,0},{2,3},{3,2},{64,67},{65,66},{66,65},{67,64},{4,5},{5,4... | collective-permute-start | bytes 3145736 | tf_op jit(solution)/shard_map/ppermute | solution.py:776
  343.1 16.7 %collective-permute-start.35 = (bf16[256,2176]{1,0:T(8,128)(2,1)S(1)}, bf16[256,2176]{1,0:T(8,128)(2,1)S(1)}, u32[]{:S(2)}, u32[]{:S(2)}) collective-permute-start(bf16[256,2176]{1,0:T(8,128)(2,1)S(1)} %add_convert_fusion.1), channel_id=1, source_target_pairs={{0,4},{4,0},{8,12},{12,8},{64,76},{68,72},{72,68},{76,64},{1,5},{5... | collective-permute-start | bytes 3342344 | tf_op jit(solution)/shard_map/ppermute | solution.py:776
  346.5 28.6 %collective-permute-start.26 = (bf16[256,2048]{1,0:T(8,128)(2,1)}, bf16[256,2048]{1,0:T(8,128)(2,1)}, u32[]{:S(2)}, u32[]{:S(2)}) collective-permute-start(bf16[256,2048]{1,0:T(8,128)(2,1)} %bitcast.99), channel_id=1, source_target_pairs={{0,16},{16,0},{32,48},{48,32},{64,112},{80,96},{96,80},{112,64},{1... | collective-permute-start | bytes 3145736 | tf_op jit(solution)/shard_map/ppermute | solution.py:776
  359.7 18.2 %collective-permute-start.31 = (bf16[128,4096]{1,0:T(8,128)(2,1)}, bf16[128,4096]{1,0:T(8,128)(2,1)}, u32[]{:S(2)}, u32[]{:S(2)}) collective-permute-start(bf16[128,4096]{1,0:T(8,128)(2,1)} %bitcast.109), channel_id=1, source_target_pairs={{0,4},{4,0},{8,12},{12,8},{64,76},{68,72},{72,68},{76,64},{1,5},{5... | collective-permute-start | bytes 3145736 | tf_op jit(solution)/shard_map/ppermute | solution.py:776
  363.6 17.3 %collective-permute-start.36 = (bf16[128,4224]{1,0:T(8,128)(2,1)}, bf16[128,4224]{1,0:T(8,128)(2,1)}, u32[]{:S(2)}, u32[]{:S(2)}) collective-permute-start(bf16[128,4224]{1,0:T(8,128)(2,1)} %bitcast.119), channel_id=1, source_target_pairs={{0,1},{1,0},{2,3},{3,2},{64,67},{65,66},{66,65},{67,64},{4,5},{5,4... | collective-permute-start | bytes 3244040 | tf_op jit(solution)/shard_map/ppermute | solution.py:776
  (76 other events, 573.8 us)
Sparse Core Ops, SparseCore 0:
  12.1 118.4 all-gather.5
  309.6 63.6 all-gather.3

commit v7 on v6

--- a/solution.py
+++ b/solution.py
@@ -924,10 +924,13 @@
     input_high = run_input_backward(
         on_high, mix_high[1], feed_high[2], start_high, mats, small[0]
     )
-    top_low = lax.ppermute(input_high[1], "section", [(1, 0)])
+    slots = (1, 4, 5, 7, 10)
+    low_top, *tied = lax.optimization_barrier((input_high[1], *(kept_high[s] for s in slots)))
+    tied = dict(zip(slots, tied))
+    top_low = lax.ppermute(low_top, "section", [(1, 0)])
 
     def chosen(slot):
-        return jnp.where(first, kept_low[slot], kept_high[slot])
+        return jnp.where(first, kept_low[slot], tied[slot])
 
     normed_t, ffin_t, hidden_t = (chosen(slot).T for slot in (1, 7, 10))
     joined_t = jnp.concatenate(
@@ -968,7 +971,22 @@
     gots, mix_sents = pending[:3], pending[3:]
     mix_gots = [first_got(sent, axis, 1) for sent, axis in zip(mix_sents, axes)]
     handed = [handed_on(p, got, axis, 0) for p, got, axis in zip(products, gots, axes)]
-    last_middle, *unused = lax.optimization_barrier((grad_middle, *handed))
+    last_middle, *pending = lax.optimization_barrier(
+        (grad_middle, grad_low, grad_gate, grad_upper, grad_branch, grad_cat, *handed)
+    )
+    rights, (late_branch, late_cat), handed = pending[:3], pending[3:5], pending[5:]
+    products = [
+        product_of(left, right, order[0])
+        for left, right, order in zip((hidden_t, ffin_t, ffin_t), rights, orders)
+    ]
+    mix_products = [
+        product_of(left, right, order[0])
+        for left, right, order in zip(
+            (joined_t, normed_t, normed_t),
+            (late_branch, late_cat[:, :2048], late_cat[:, 2048:]),
+            orders,
+        )
+    ]
     feed_parts = [
         totalled(p, got, hand, axis, 0)
         for p, got, hand, axis in zip(products, gots, handed, axes)
@@ -995,14 +1013,19 @@
     vector = jnp.concatenate([piece.reshape(-1) for piece in small_grads])
     vector = jnp.pad(vector, (0, -vector.shape[0] % 1024)).reshape(-1, 128)
     vectors = lax.all_gather(vector.astype(BF16), DP, axis=0, tiled=False)
-    total = jnp.sum(vectors.astype(F32), axis=0).reshape(-1)
     seconds = [
         second_summed(pair, order, depth)
         for pair, order, depth in zip(zip(feed_parts, mix_parts), orders, (32, 16, 16))
     ]
-    total, *seconds = lax.optimization_barrier((total, *seconds))
+    axes = [DP[order[2]] for order in orders]
+    quarters = [quarters_of(array, 0) for array in seconds]
+    gots = [first_got(first_sent(p, axis, 0), axis, 0) for p, axis in zip(quarters, axes)]
+    handed = [handed_on(p, got, axis, 0) for p, got, axis in zip(quarters, gots, axes)]
+    vectors, *unused = lax.optimization_barrier((vectors, *handed))
+    total = jnp.sum(vectors.astype(F32), axis=0).reshape(-1)
     rows_grad, gate_cat, up_cat = (
-        summed_on(array, DP[order[2]], 0, 0) for array, order in zip(seconds, orders)
+        totalled(p, got, hand, axis, 0)
+        for p, got, hand, axis in zip(quarters, gots, handed, axes)
     )
     down_grad, joined_grad = rows_grad[:, :WIDTH], rows_grad[:, WIDTH:]
     gate_grad, up_grad = gate_cat[:, :FEED], up_cat[:, :FEED]

time: 430 us -> 429 us (level)
    ppermute x42, waiting for transfers between devices: 73.1 us -> 91.7 us  [exchange(): return lax.ppermute(array, ('section', axis), pairs)]
    all_gather x1, waiting for transfers between devices: 9.7 us -> 0.01 us  [on_device(): vectors = lax.all_gather(vector.astype(BF16), DP, axis=0, tiled=False)]
    ppermute x1, waiting for transfers between devices: 24.3 us -> 15.4 us  [on_device(): top_low = lax.ppermute(low_top, 'section', [(1, 0)])]
  transfers between devices with their start and end apart: 46 -> 46, of which waited for: 20 -> 22; matrix products, arithmetic and copies ran while one was open for 19% -> 21% of each run, Pallas kernels for 6% -> 6%
where the time goes in v7:
time: 429 us; the launch traced here: 421 us
  waiting for transfers between devices  156 us (36%)
  Pallas kernels  87 us (20%)
  starting transfers between devices  59.9 us (14%)
  matrix products  38.9 us (9%)
  other arithmetic  32.7 us (8%)
  local copies, waits for them, and re-layouts  31.4 us (7%)
  between operations  15.6 us (4%)
    ppermute x42, waiting for transfers between devices, exchange(): return lax.ppermute(array, ('section', axis), pairs)  91.7 us
    ppermute x42, starting transfers between devices, exchange(): return lax.ppermute(array, ('section', axis), pairs)  56.9 us
    all_gather x1, waiting for transfers between devices, on_device(): packed = lax.all_gather(own, DP, axis=0, tiled=False)  48.6 us
    pallas_call x2, Pallas kernels, run_forward(): pl.pallas_call(functools.partial(forward_kernel, unpack), out_shape=extra...  39 us
    dot_general x18, matrix products, dot(): return jnp.dot(left, right, preferred_element_type=F32)  38.9 us
    pallas_call x2, Pallas kernels, run_mix_backward(): pl.pallas_call(functools.partial(mix_backward_kernel, len(earlier)), out_...  19.7 us
    ppermute x1, waiting for transfers between devices, on_device(): top_low = lax.ppermute(low_top, 'section', [(1, 0)])  15.4 us
    pallas_call x2, Pallas kernels, run_input_backward(): pl.pallas_call(functools.partial(input_backward_kernel, len(earlier)), ou...  15 us
  transfers between devices with their start and end apart: 46, of which 22 were waited for; matrix products, arithmetic and copies ran while one was open for 21% of the time, Pallas kernels for 6%

profile of v7, /device:TPU:0, one launch (start us, length us, event | category | flops | bytes accessed | tf_op | source)
XLA Modules:
  0.0 421.4 jit_solution(7691076785289311759)
XLA Ops:
  23.5 3.3 collective-permute-start.13
  40.4 4.6 %collective-permute-done.3 = bf16[2,4,16,2048]{3,2,1,0:T(8,128)(2,1)S(1)} collective-permute-done((bf16[2,4,16,2048]{3,2,1,0:T(8,128)(2,1)S(1)}, bf16[2,4,16,2048]{3,2,1,0:T(8,128)(2,1)S(1)}, u32[]{:S(2)}, u32[]{:S(2)}) %collective-permute-start.3) | collective-permute-done | bytes 524320 | tf_op jit(solution)/shard_map/ppermute | solution.py:776
  46.9 6.9 %collective-permute-done.15 = bf16[2,4,32,1024]{3,2,1,0:T(8,128)(2,1)S(1)} collective-permute-done((bf16[2,4,32,1024]{3,2,1,0:T(8,128)(2,1)S(1)}, bf16[2,4,32,1024]{3,2,1,0:T(8,128)(2,1)S(1)}, u32[]{:S(2)}, u32[]{:S(2)}) %collective-permute-start.15) | collective-permute-done | bytes 524320 | tf_op jit(solution)/shard_map/ppermute | solution.py:776
  54.0 14.3 %collective-permute-done.4.refs_2_.refs_4_.refs_3_ = bf16[4,4,16,2048]{3,2,1,0:T(8,128)(2,1)S(1)} collective-permute-done((bf16[4,4,16,2048]{3,2,1,0:T(8,128)(2,1)S(1)}, bf16[4,4,16,2048]{3,2,1,0:T(8,128)(2,1)S(1)}, u32[]{:S(2)}, u32[]{:S(2)}) %collective-permute-start.4) | collective-permute-done | bytes 1048608 | tf_op jit(solution)/shard_map/ppermute | solution.py:776
  77.1 2.7 collective-permute-start.17
  84.1 48.6 %all-gather.6.cloned.1.call-done = bf16[6656,1024]{1,0:T(8,128)(2,1)} async-done(((bf16[104,1024]{1,0:T(8,128)(2,1)}), bf16[6656,1024]{1,0:T(8,128)(2,1)}) %all-gather.6.cloned.1.call-update) | async-done | bytes 13631504 | tf_op jit(solution)/shard_map/all_gather | solution.py:887
  137.7 19.7 %forward.2 = (bf16[1536,1024]{1,0:T(8,128)(2,1)}, bf16[512,1024]{1,0:T(8,128)(2,1)}, bf16[256,1024]{1,0:T(8,128)(2,1)}, bf16[256,1024]{1,0:T(8,128)(2,1)}, f32[2...) custom-call(bf16[256,1024]{1,0:T(8,128)(2,1)} %bitcast.302, ...), custom_call_target="tpu_custom_call" | custom-call | flops 6451200000 | bytes 40000000 | tf_op jit(solution)/shard_map/forward/pallas_call | solution.py:608
  161.9 19.4 %forward.3 = (bf16[256,1024]{1,0:T(8,128)(2,1)}, bf16[256,1024]{1,0:T(8,128)(2,1)}, f32[256,4224]{1,0:T(8,128)}, f32[256,1536]{1,0:T(8,128)}, bf16[256,1536]{1,0...) custom-call(bf16[256,1024]{1,0:T(8,128)(2,1)} %copy-done.20, ...), custom_call_target="tpu_custom_call" | custom-call | flops 6451200000 | bytes 40000000 | tf_op jit(solution)/shard_map/forward/pallas_call | solution.py:608
  184.6 6.7 %input_backward.2 = (f32[256,1024]{1,0:T(8,128)}, bf16[256,1024]{1,0:T(8,128)(2,1)}, f32[1,1024]{1,0:T(1,128)}) custom-call(s32[1]{0:T(128)} %bitcast.54.active, bf16[256,4224]{1,0:T(8,128)(2,1)} %get-tuple-element.111.refs_0_.refs_15_, f32[256,1024]{1,0:T(8,128)} %get-tuple-element.108.refs_0_.refs_1_.refs_17_, bf16[256,1024]{1,0:T(8,128)(2,1)} %copy-done.20, ...), custom_call_target="tpu_custom_call" | custom-call | flops 2150400000 | bytes 13000000 | tf_op jit(solution)/shard_map/input_backward/pallas_call | solution.py:707
  207.2 15.4 %collective-permute-done.19.refs_0_ = bf16[256,1024]{1,0:T(8,128)(2,1)S(1)} collective-permute-done((bf16[256,1024]{1,0:T(8,128)(2,1)}, bf16[256,1024]{1,0:T(8,128)(2,1)S(1)}, u32[]{:S(2)}, u32[]{:S(2)}) %collective-permute-start.19) | collective-permute-done | bytes 524320 | tf_op jit(solution)/shard_map/ppermute | solution.py:930
  223.4 11.6 %feed_backward.3 = (bf16[256,2048]{1,0:T(8,128)(2,1)}, bf16[256,2048]{1,0:T(8,128)(2,1)}, f32[256,1024]{1,0:T(8,128)}, f32[1,1024]{1,0:T(1,128)}) custom-call(s32[1]{0:T(128)S(6)} %sub.29.active, bf16[256,1024]{1,0:T(8,128)(2,1)} %copy-done.19, ...), custom_call_target="tpu_custom_call", output_to_operand_aliasing={{0}: (16, {}), {1}: (17, {}), {2}: (18, {}), {3}: (19, {})} | custom-call | flops 3225600000 | bytes 22000000 | tf_op jit(solution)/shard_map/feed_backward/pallas_call | solution.py:639
  246.1 18.1 %mix_backward.3 = (bf16[256,1024]{1,0:T(8,128)(2,1)}, bf16[256,4224]{1,0:T(8,128)(2,1)}, f32[4,1792]{1,0:T(4,128)}, f32[1,1792]{1,0:T(1,128)}, f32[1,128]{1,0:T(...) custom-call(s32[1]{0:T(128)S(6)} %sub.29.active, ...), custom_call_target="tpu_custom_call", output_to_operand_aliasing={{0}: (15, {}), {1}: (16, {}), {2}: (17, {}), {3}: (18, {}),... | custom-call | flops 1075200000 | bytes 14000000 | tf_op jit(solution)/shard_map/mix_backward/pallas_call | solution.py:675
  267.1 3.3 convolution_convert_fusion.4
  279.4 2.7 fusion
  282.2 2.7 fusion.1
  284.8 2.7 collective-permute-start.30
  291.7 8.3 %input_backward.3 = (f32[256,1024]{1,0:T(8,128)}, bf16[256,1024]{1,0:T(8,128)(2,1)}, f32[1,1024]{1,0:T(1,128)}) custom-call(s32[1]{0:T(128)S(6)} %sub.29.active, bf16[256,4224]{1,0:T(8,128)(2,1)} %get-tuple-element.165.refs_0_, f32[256,1024]{1,0:T(8,128)} %get-tuple-element.159.refs_0_.refs_1_, ...), custom_call_target="tpu_custom_call", output_to_operand_aliasing={{0}: (7, {}), {1}: (8, {}), {2}: (9, {})} | custom-call | flops 2150400000 | bytes 13000000 | tf_op jit(solution)/shard_map/input_backward/pallas_call | solution.py:707
  312.1 15.4 %collective-permute-done.37 = bf16[512,1024]{1,0:T(8,128)(2,1)} collective-permute-done((bf16[512,1024]{1,0:T(8,128)(2,1)}, bf16[512,1024]{1,0:T(8,128)(2,1)}, u32[]{:S(2)}, u32[]{:S(2)}) %collective-permute-start.37) | collective-permute-done | bytes 1048608 | tf_op jit(solution)/shard_map/ppermute | solution.py:776
  341.3 8.9 %collective-permute-done.39 = bf16[512,1024]{1,0:T(8,128)(2,1)S(1)} collective-permute-done((bf16[512,1024]{1,0:T(8,128)(2,1)S(1)}, bf16[512,1024]{1,0:T(8,128)(2,1)S(1)}, u32[]{:S(2)}, u32[]{:S(2)}) %collective-permute-start.39) | collective-permute-done | bytes 1048608 | tf_op jit(solution)/shard_map/ppermute | solution.py:776
  356.8 16.6 %collective-permute-done.26 = bf16[128,4096]{1,0:T(8,128)(2,1)S(1)} collective-permute-done((bf16[128,4096]{1,0:T(8,128)(2,1)S(1)}, bf16[128,4096]{1,0:T(8,128)(2,1)S(1)}, u32[]{:S(2)}, u32[]{:S(2)}) %collective-permute-start.26) | collective-permute-done | bytes 1048608 | tf_op jit(solution)/shard_map/ppermute | solution.py:776
  376.9 3.3 collective-permute-start.34
  380.2 6.6 %collective-permute-done.27 = bf16[64,4096]{1,0:T(8,128)(2,1)S(1)} collective-permute-done((bf16[64,4096]{1,0:T(8,128)(2,1)S(1)}, bf16[64,4096]{1,0:T(8,128)(2,1)S(1)}, u32[]{:S(2)}, u32[]{:S(2)}) %collective-permute-start.27) | collective-permute-done | bytes 524320 | tf_op jit(solution)/shard_map/ppermute | solution.py:776
  387.1 2.9 collective-permute-start.28
  390.9 3.5 collective-permute-done.28
  (372 shorter events, 157.6 us)
Async XLA Ops:
  7.2 125.6 %all-gather.6.cloned.1.call-start = ((), (), s32[]{:S(2)}) async-start(), calls=%async_computation.1 | async-start | bytes 13844480 | tf_op jit(solution)/shard_map/all_gather | solution.py:887
  12.0 395.4 %all-gather.4.cloned.1.call-start = ((), (), s32[]{:S(2)}) async-start(), calls=%async_computation | async-start | bytes 1730560 | tf_op jit(solution)/shard_map/all_gather | solution.py:1015
  38.0 15.8 %collective-permute-start.15 = (bf16[2,4,32,1024]{3,2,1,0:T(8,128)(2,1)S(1)}, bf16[2,4,32,1024]{3,2,1,0:T(8,128)(2,1)S(1)}, u32[]{:S(2)}, u32[]{:S(2)}) collective-permute-start(bf16[2,4,32,1024]{3,2,1,0:T(8,128)(2,1)S(1)} %pad_maximum_fusion.11), channel_id=1, source_target_pairs={{0,48},{16,32},{32,16},{48,0},{64,80},{80,64},{96,112},{112,96},{1... | collective-permute-start | bytes 1572872 | tf_op jit(solution)/shard_map/ppermute | solution.py:776
  45.1 23.2 %collective-permute-start.4 = (bf16[4,4,16,2048]{3,2,1,0:T(8,128)(2,1)S(1)}, bf16[4,4,16,2048]{3,2,1,0:T(8,128)(2,1)S(1)}, u32[]{:S(2)}, u32[]{:S(2)}) collective-permute-start(bf16[4,4,16,2048]{3,2,1,0:T(8,128)(2,1)S(1)} %slice_dynamic-update-slice_fusion.2.refs_1_.refs_3_.refs_2_), channel_id=1, source_target_pairs={{0,16},{16,0},{32,48},{48,32},{64,112},{80,96},{96,80},{112,64},{1... | collective-permute-start | bytes 3145736 | tf_op jit(solution)/shard_map/ppermute | solution.py:776
  46.1 25.2 %collective-permute-start.10 = (bf16[4,4,16,2048]{3,2,1,0:T(8,128)(2,1)S(1)}, bf16[4,4,16,2048]{3,2,1,0:T(8,128)(2,1)S(1)}, u32[]{:S(2)}, u32[]{:S(2)}) collective-permute-start(bf16[4,4,16,2048]{3,2,1,0:T(8,128)(2,1)S(1)} %fusion.34.refs_4_.refs_6_.refs_5_), channel_id=1, source_target_pairs={{0,4},{4,0},{8,12},{12,8},{64,76},{68,72},{72,68},{76,64},{1,5},{5... | collective-permute-start | bytes 3145736 | tf_op jit(solution)/shard_map/ppermute | solution.py:776
  53.9 21.4 %collective-permute-start.16 = (bf16[4,4,32,1024]{3,2,1,0:T(8,128)(2,1)S(1)}, bf16[4,4,32,1024]{3,2,1,0:T(8,128)(2,1)S(1)}, u32[]{:S(2)}, u32[]{:S(2)}) collective-permute-start(bf16[4,4,32,1024]{3,2,1,0:T(8,128)(2,1)S(1)} %slice_dynamic-update-slice_fusion.refs_7_.refs_9_.refs_8_), channel_id=1, source_target_pairs={{0,1},{1,0},{2,3},{3,2},{64,67},{65,66},{66,65},{67,64},{4,5},{5,4... | collective-permute-start | bytes 3145736 | tf_op jit(solution)/shard_map/ppermute | solution.py:776
  70.0 65.2 %collective-permute-start.5 = (bf16[2,4,4,16,2048]{4,3,2,1,0:T(8,128)(2,1)}, bf16[2,4,4,16,2048]{4,3,2,1,0:T(8,128)(2,1)}, u32[]{:S(2)}, u32[]{:S(2)}) collective-permute-start(bf16[2,4,4,16,2048]{4,3,2,1,0:T(8,128)(2,1)} %pad_maximum_fusion.1), channel_id=1, source_target_pairs={{0,48},{16,32},{32,16},{48,0},{64,80},{80,64},{96,112},{112,96},{1... | collective-permute-start | bytes 6291464 | tf_op jit(solution)/shard_map/ppermute | solution.py:776
  73.0 63.4 %collective-permute-start.11 = (bf16[2,4,4,16,2048]{4,3,2,1,0:T(8,128)(2,1)}, bf16[2,4,4,16,2048]{4,3,2,1,0:T(8,128)(2,1)S(1)}, u32[]{:S(2)}, u32[]{:S(2)}) collective-permute-start(bf16[2,4,4,16,2048]{4,3,2,1,0:T(8,128)(2,1)} %pad_maximum_fusion.2), channel_id=1, source_target_pairs={{0,12},{4,8},{8,4},{12,0},{64,68},{68,64},{72,76},{76,72},{1,13},{... | collective-permute-start | bytes 6291464 | tf_op jit(solution)/shard_map/ppermute | solution.py:776
  77.1 59.3 %collective-permute-start.17 = (bf16[2,4,4,32,1024]{4,3,2,1,0:T(8,128)(2,1)}, bf16[2,4,4,32,1024]{4,3,2,1,0:T(8,128)(2,1)}, u32[]{:S(2)}, u32[]{:S(2)}) collective-permute-start(bf16[2,4,4,32,1024]{4,3,2,1,0:T(8,128)(2,1)} %pad_maximum_fusion.3), channel_id=1, source_target_pairs={{0,3},{1,2},{2,1},{3,0},{64,65},{65,64},{66,67},{67,66},{4,7},{5,6... | collective-permute-start | bytes 6291464 | tf_op jit(solution)/shard_map/ppermute | solution.py:776
  191.4 31.2 %collective-permute-start.19 = (bf16[256,1024]{1,0:T(8,128)(2,1)}, bf16[256,1024]{1,0:T(8,128)(2,1)S(1)}, u32[]{:S(2)}, u32[]{:S(2)}) collective-permute-start(bf16[256,1024]{1,0:T(8,128)(2,1)} %get-tuple-element.118.refs_7_), channel_id=1, source_target_pairs={{64,0},{65,1},{66,2},{67,3},{68,4},{69,5},{70,6},{71,7},{72,8},{73... | collective-permute-start | bytes 1572872 | tf_op jit(solution)/shard_map/ppermute | solution.py:930
  241.1 33.5 %collective-permute-start.20 = (bf16[1024,1024]{1,0:T(8,128)(2,1)S(1)}, bf16[1024,1024]{1,0:T(8,128)(2,1)}, u32[]{:S(2)}, u32[]{:S(2)}) collective-permute-start(bf16[1024,1024]{1,0:T(8,128)(2,1)S(1)} %convolution_convert_fusion.5), channel_id=1, source_target_pairs={{0,1},{1,0},{2,3},{3,2},{64,67},{65,66},{66,65},{67,64},{4,5},{5,4... | collective-permute-start | bytes 6291464 | tf_op jit(solution)/shard_map/ppermute | solution.py:776
  242.6 32.1 %collective-permute-start.21 = (bf16[512,2048]{1,0:T(8,128)(2,1)}, bf16[512,2048]{1,0:T(8,128)(2,1)}, u32[]{:S(2)}, u32[]{:S(2)}) collective-permute-start(bf16[512,2048]{1,0:T(8,128)(2,1)} %convolution_convert_fusion.3), channel_id=1, source_target_pairs={{0,16},{16,0},{32,48},{48,32},{64,112},{80,96},{96,80},{112,64},{1... | collective-permute-start | bytes 6291464 | tf_op jit(solution)/shard_map/ppermute | solution.py:776
  244.1 30.5 %collective-permute-start.22 = (bf16[512,2048]{1,0:T(8,128)(2,1)}, bf16[512,2048]{1,0:T(8,128)(2,1)}, u32[]{:S(2)}, u32[]{:S(2)}) collective-permute-start(bf16[512,2048]{1,0:T(8,128)(2,1)} %convolution_convert_fusion.2), channel_id=1, source_target_pairs={{0,4},{4,0},{8,12},{12,8},{64,76},{68,72},{72,68},{76,64},{1,5},{5... | collective-permute-start | bytes 6291464 | tf_op jit(solution)/shard_map/ppermute | solution.py:776
  274.6 35.6 %collective-permute-start.24 = (bf16[512,2048]{1,0:T(8,128)(2,1)}, bf16[512,2048]{1,0:T(8,128)(2,1)}, u32[]{:S(2)}, u32[]{:S(2)}) collective-permute-start(bf16[512,2048]{1,0:T(8,128)(2,1)} %convolution_convert_fusion.1), channel_id=1, source_target_pairs={{0,48},{16,32},{32,16},{48,0},{64,80},{80,64},{96,112},{112,96},{1... | collective-permute-start | bytes 6291464 | tf_op jit(solution)/shard_map/ppermute | solution.py:776
  284.8 20.4 %collective-permute-start.30 = (bf16[256,2048]{1,0:T(8,128)(2,1)}, bf16[256,2048]{1,0:T(8,128)(2,1)}, u32[]{:S(2)}, u32[]{:S(2)}) collective-permute-start(bf16[256,2048]{1,0:T(8,128)(2,1)} %fusion.1), channel_id=1, source_target_pairs={{0,12},{4,8},{8,4},{12,0},{64,68},{68,64},{72,76},{76,72},{1,13},{... | collective-permute-start | bytes 3145736 | tf_op jit(solution)/shard_map/ppermute | solution.py:776
  287.9 47.0 %collective-permute-start.31 = (bf16[512,2176]{1,0:T(8,128)(2,1)}, bf16[512,2176]{1,0:T(8,128)(2,1)}, u32[]{:S(2)}, u32[]{:S(2)}) collective-permute-start(bf16[512,2176]{1,0:T(8,128)(2,1)} %convolution_convert_fusion), channel_id=1, source_target_pairs={{0,12},{4,8},{8,4},{12,0},{64,68},{68,64},{72,76},{76,72},{1,13},{... | collective-permute-start | bytes 6684680 | tf_op jit(solution)/shard_map/ppermute | solution.py:776
  288.5 44.4 %collective-permute-start.38 = (bf16[1024,1024]{1,0:T(8,128)(2,1)}, bf16[1024,1024]{1,0:T(8,128)(2,1)}, u32[]{:S(2)}, u32[]{:S(2)}) collective-permute-start(bf16[1024,1024]{1,0:T(8,128)(2,1)} %convolution_convert_fusion.4), channel_id=1, source_target_pairs={{0,3},{1,2},{2,1},{3,0},{64,65},{65,64},{66,67},{67,66},{4,7},{5,6... | collective-permute-start | bytes 6291464 | tf_op jit(solution)/shard_map/ppermute | solution.py:776
  290.5 37.0 %collective-permute-start.37 = (bf16[512,1024]{1,0:T(8,128)(2,1)}, bf16[512,1024]{1,0:T(8,128)(2,1)}, u32[]{:S(2)}, u32[]{:S(2)}) collective-permute-start(bf16[512,1024]{1,0:T(8,128)(2,1)} %add_convert_fusion.9), channel_id=1, source_target_pairs={{0,3},{1,2},{2,1},{3,0},{64,65},{65,64},{66,67},{67,66},{4,7},{5,6... | collective-permute-start | bytes 3145736 | tf_op jit(solution)/shard_map/ppermute | solution.py:776
  305.3 25.6 %collective-permute-start.23 = (bf16[256,2048]{1,0:T(8,128)(2,1)}, bf16[256,2048]{1,0:T(8,128)(2,1)S(1)}, u32[]{:S(2)}, u32[]{:S(2)}) collective-permute-start(bf16[256,2048]{1,0:T(8,128)(2,1)} %fusion), channel_id=1, source_target_pairs={{0,48},{16,32},{32,16},{48,0},{64,80},{80,64},{96,112},{112,96},{1... | collective-permute-start | bytes 3145736 | tf_op jit(solution)/shard_map/ppermute | solution.py:776
  312.0 25.2 %collective-permute-start.25 = (bf16[256,2048]{1,0:T(8,128)(2,1)S(1)}, bf16[256,2048]{1,0:T(8,128)(2,1)S(1)}, u32[]{:S(2)}, u32[]{:S(2)}) collective-permute-start(bf16[256,2048]{1,0:T(8,128)(2,1)S(1)} %add_convert_fusion.7), channel_id=1, source_target_pairs={{0,16},{16,0},{32,48},{48,32},{64,112},{80,96},{96,80},{112,64},{1... | collective-permute-start | bytes 3145736 | tf_op jit(solution)/shard_map/ppermute | solution.py:776
  336.8 16.2 %collective-permute-start.32 = (bf16[256,2176]{1,0:T(8,128)(2,1)S(1)}, bf16[256,2176]{1,0:T(8,128)(2,1)S(1)}, u32[]{:S(2)}, u32[]{:S(2)}) collective-permute-start(bf16[256,2176]{1,0:T(8,128)(2,1)S(1)} %add_convert_fusion.1), channel_id=1, source_target_pairs={{0,4},{4,0},{8,12},{12,8},{64,76},{68,72},{72,68},{76,64},{1,5},{5... | collective-permute-start | bytes 3342344 | tf_op jit(solution)/shard_map/ppermute | solution.py:776
  339.4 34.0 %collective-permute-start.26 = (bf16[128,4096]{1,0:T(8,128)(2,1)S(1)}, bf16[128,4096]{1,0:T(8,128)(2,1)S(1)}, u32[]{:S(2)}, u32[]{:S(2)}) collective-permute-start(bf16[128,4096]{1,0:T(8,128)(2,1)S(1)} %bitcast.317), channel_id=1, source_target_pairs={{0,4},{4,0},{8,12},{12,8},{64,76},{68,72},{72,68},{76,64},{1,5},{5... | collective-permute-start | bytes 3145736 | tf_op jit(solution)/shard_map/ppermute | solution.py:776
  352.5 22.8 %collective-permute-start.40 = (bf16[256,2048]{1,0:T(8,128)(2,1)S(1)}, bf16[256,2048]{1,0:T(8,128)(2,1)S(1)}, u32[]{:S(2)}, u32[]{:S(2)}) collective-permute-start(bf16[256,2048]{1,0:T(8,128)(2,1)S(1)} %bitcast.318), channel_id=1, source_target_pairs={{0,16},{16,0},{32,48},{48,32},{64,112},{80,96},{96,80},{112,64},{1... | collective-permute-start | bytes 3145736 | tf_op jit(solution)/shard_map/ppermute | solution.py:776
  356.1 20.7 %collective-permute-start.33 = (bf16[128,4224]{1,0:T(8,128)(2,1)S(1)}, bf16[128,4224]{1,0:T(8,128)(2,1)S(1)}, u32[]{:S(2)}, u32[]{:S(2)}) collective-permute-start(bf16[128,4224]{1,0:T(8,128)(2,1)S(1)} %bitcast.313), channel_id=1, source_target_pairs={{0,1},{1,0},{2,3},{3,2},{64,67},{65,66},{66,65},{67,64},{4,5},{5,4... | collective-permute-start | bytes 3244040 | tf_op jit(solution)/shard_map/ppermute | solution.py:776
  (83 other events, 616.1 us)
Sparse Core Ops, SparseCore 0:
  12.1 120.6 all-gather.5
  305.3 63.7 all-gather.3

commit v8 on v7

--- a/solution.py
+++ b/solution.py
@@ -21,7 +21,7 @@
 BF16 = jnp.bfloat16
 HIDE = -1e30
 Q0, K0, V0, Z0, X0, T0 = 0, 512, 640, 768, 2304, 4096
-OUT0, HEADS0, DT0, PACKED = 64, 88, 96, 104
+OUT0, PACKED = 64, 96
 
 
 def dot(left, right):
@@ -303,25 +303,25 @@
     return block.reshape(-1, block.shape[-1])
 
 
-def forward_kernel(unpack, x, packed, dt_weight, *refs):
+def forward_kernel(unpack, x, packed, *refs):
     if unpack:
-        given, results = (None, None), refs[20:22]
-        rest = refs[:20] + refs[22:]
+        given, results = (None, None), refs[20:23]
+        rest = refs[:20] + refs[23:]
     else:
-        given, results = refs[:2], (None, None)
+        given, results = refs[:2], (None, None, None)
         rest = refs[2:]
-    forward_body(unpack, x, packed, dt_weight, *given, *results, *rest)
+    forward_body(unpack, x, packed, *given, *results, *rest)
 
 
 def forward_body(
-    unpack, x, packed, dt_weight, out_weight, heads_weight, out_result, heads_result,
+    unpack, x, packed, out_weight, heads_weight, dt_result, out_result, heads_result,
     places, gate_own, gate_got, gate_far, up_own, up_got, up_far, down_own, down_got, down_far,
     input_gain, kernel, bias, step_bias, decay_log, skip,
     mixer_gain, feed_gain, cosine, sine,
     result_out, normed_out, proj_out, ssm_out, mamba_out, attended_out, middle_out, ffin_out, gate_out,
     upper_out, hidden_out,
     result, normed, proj, ssm, mamba, attended, middle, ffin, gate, upper, hidden,
-    cat, gate_mat, up_mat, down_mat, out_mat, heads_mat, mixed, sems, out_sems, feed_sems,
+    cat, gate_mat, up_mat, down_mat, out_mat, heads_mat, mixed, dt_mat, sems, out_sems, feed_sems,
 ):
     leaving = []
 
@@ -345,10 +345,13 @@
     start_all(copies + feeds)
     state = x[...].astype(F32)
     normed[...] = (state * rms(state) * input_gain[...]).astype(BF16)
-    proj[:, T0:CAT] = dot(normed[...], dt_weight[...])
     for j in range(4):
         copies[j].wait()
         proj[:, 1024 * j : 1024 * j + 1024] = dot(normed[...], flat(cat[j]))
+    for copy in feeds[4:8]:
+        copy.wait()
+    dt_mat[...] = rows_of(up_mat[:, :, :, :, FEED:])
+    proj[:, T0:CAT] = dot(normed[...], dt_mat[...])
     leave((normed, normed_out), (proj, proj_out))
 
     def sequence(index, carry):
@@ -365,14 +368,14 @@
         wide = mixed[...].astype(F32)
         out_mat[...] = wide[:, :24].reshape(INNER, WIDTH).astype(BF16)
         heads_mat[...] = wide[:, 24:].reshape(512, WIDTH).astype(BF16)
-        leave((out_mat, out_result), (heads_mat, heads_result))
+        leave((dt_mat, dt_result), (out_mat, out_result), (heads_mat, heads_result))
 
     part = dot(mamba[...], out_mat[...]) + dot(attended[...], heads_mat[...])
     middle[...] = x[...].astype(F32) + part
     value = middle[...]
     ffin[...] = (value * rms(value) * feed_gain[...]).astype(BF16)
     leave((middle, middle_out), (ffin, ffin_out))
-    for copy in feeds[:8]:
+    for copy in feeds[:4]:
         copy.wait()
 
     for half in range(2):
@@ -440,7 +443,7 @@
         copy.wait()
 
     grad_ffin = dot_nt(grad_gate[...], rows_of(gate_mat[...]))
-    grad_ffin = grad_ffin + dot_nt(grad_upper[...], rows_of(up_mat[...]))
+    grad_ffin = grad_ffin + dot_nt(grad_upper[...], rows_of(up_mat[:, :, :, :, :FEED]))
     inputs[2].wait()
     grad_part, grad_gain = rms_backward(middle[...], feed_gain[...], grad_ffin)
     feed_grad[...] = grad_gain
@@ -579,7 +582,7 @@
 
 FEED_MATS = (
     scratch(4, 4, 4, 16, FEED),
-    scratch(4, 4, 4, 16, FEED),
+    scratch(4, 4, 4, 16, FEED + 128),
     scratch(4, 4, 4, 32, WIDTH),
 )
 
@@ -589,9 +592,10 @@
 
 
 def run_forward(start, mats, small, rope):
-    packed, dt_weight, *given, feeds = mats
+    packed, *given, feeds = mats
     unpack = not given
-    extra = (shape(INNER, WIDTH, BF16), shape(512, WIDTH, BF16))
+    given = given[1:]
+    extra = (shape(WIDTH, 128, BF16), shape(INNER, WIDTH, BF16), shape(512, WIDTH, BF16))
     shapes = (
         shape(ROWS, WIDTH, BF16),
         shape(ROWS, WIDTH, BF16),
@@ -608,8 +612,8 @@
     return pl.pallas_call(
         functools.partial(forward_kernel, unpack),
         out_shape=extra + shapes if unpack else shapes,
-        in_specs=[VMEM, ANY, VMEM] + [ANY] * len(given) + [SMEM] + [ANY] * 9 + [VMEM] * 10,
-        out_specs=(ANY,) * (len(shapes) + 2 * unpack),
+        in_specs=[VMEM, ANY] + [ANY] * len(given) + [SMEM] + [ANY] * 9 + [VMEM] * 10,
+        out_specs=(ANY,) * (len(shapes) + 3 * unpack),
         scratch_shapes=[
             *mirrored(shapes),
             scratch(4, 64, 16, 1024),
@@ -617,8 +621,9 @@
             scratch(INNER, WIDTH),
             scratch(512, WIDTH),
             scratch(64, 32, WIDTH) if unpack else scratch(16, 128),
+            scratch(WIDTH, 128),
             pltpu.SemaphoreType.DMA((6,)),
-            pltpu.SemaphoreType.DMA((len(shapes) + 2,)),
+            pltpu.SemaphoreType.DMA((len(shapes) + 3,)),
             pltpu.SemaphoreType.DMA((12,)),
         ],
         compiler_params=pltpu.CompilerParams(vmem_limit_bytes=LIMIT),
@@ -626,7 +631,7 @@
             flops=2 * ROWS * 12_600_000, bytes_accessed=40_000_000, transcendentals=2_000_000
         ),
         name="forward",
-    )(start, packed, dt_weight, *given, *feeds, *small, *rope)
+    )(start, packed, *given, *feeds, *small, *rope)
 
 
 def run_feed_backward(active, grad_top, mats, gate, upper, middle, feed_gain, earlier=()):
@@ -724,6 +729,55 @@
     )(active, grad_cat, grad_middle, start, *mats[:2], input_gain, *earlier)
 
 
+def finish_kernel(
+    mine, rows_own, gate_own, up_own, rows_got, gate_got, up_got, rows_last, gate_last, up_last,
+    in_grad, query_grad, key_grad, value_grad, out_grad, heads_grad, gate_grad, up_grad, down_grad,
+):
+    def total(k, own, got, last):
+        depth = own.shape[1]
+        part = own[mine[k]].astype(F32) + got[:depth].astype(F32)
+        return part + last[...].astype(F32)
+
+    value = total(0, rows_own, rows_got, rows_last)
+    down_grad[0] = value[:, :WIDTH]
+    out_grad[0] = value[:24, WIDTH:]
+    heads_grad[0] = value[24:, WIDTH:]
+    value = total(1, gate_own, gate_got, gate_last)
+    gate_grad[0] = value[:, :FEED]
+    query_grad[0] = value[:, FEED : FEED + K0]
+    key_grad[0] = value[:, FEED + K0 : FEED + V0]
+    value_grad[0] = value[:, FEED + V0 : FEED + Z0]
+    in_grad[0, :, : 2048 - Z0] = value[:, FEED + Z0 :]
+    value = total(2, up_own, up_got, up_last)
+    up_grad[0] = value[:, :FEED]
+    in_grad[0, :, 2048 - Z0 :] = value[:, FEED : FEED + T0 + HEADS - 2048]
+
+
+def run_finish(mine, owns, gots, lasts):
+    shapes = tuple(
+        jax.ShapeDtypeStruct((1, *dims), F32)
+        for dims in (
+            (16, T0 + HEADS - Z0),
+            (16, 512),
+            (16, 128),
+            (16, 128),
+            (24, WIDTH),
+            (8, WIDTH),
+            (16, FEED),
+            (16, FEED),
+            (32, WIDTH),
+        )
+    )
+    return pl.pallas_call(
+        finish_kernel,
+        out_shape=shapes,
+        in_specs=[SMEM] + [VMEM] * 9,
+        out_specs=(VMEM,) * 9,
+        compiler_params=pltpu.CompilerParams(vmem_limit_bytes=LIMIT // 2),
+        name="finish",
+    )(mine, *owns, *gots, *lasts)
+
+
 def rope_tables():
     position = jnp.arange(LEN).astype(F32)
     inverse = 10000.0 ** (-(jnp.arange(32).astype(F32) * 2.0) / 64)
@@ -826,7 +880,7 @@
     rest = [0, 1, 2]
     rest.remove(order[0])
     array = array.reshape(4, 4, depth, width)
-    array = summed_on(array, DP[order[1]], rest.index(order[1]), 0).astype(BF16)
+    array = summed_on(array, DP[order[1]], rest.index(order[1]), 1).astype(BF16)
     return array.reshape(4, depth, width)
 
 
@@ -874,30 +928,27 @@
     cat = jnp.concatenate(
         [query_weight[0], key_weight[0], value_weight[0], in_weight[0, :, :3328]], axis=1
     )
-    steps = jnp.pad(in_weight[0, :, 3328:].reshape(1, -1), ((0, 7), (0, 1024 - 16 * HEADS)))
+    steps = jnp.pad(in_weight[0, :, 3328:], ((0, 0), (0, 128 - HEADS)))
     own = jnp.concatenate(
         [
             *column_blocks(cat),
             out_weight[0],
             heads_weight[0],
-            steps,
         ],
         axis=0,
     )
     packed = lax.all_gather(own, DP, axis=0, tiled=False)
-    dt_weight = packed[:, DT0, : 16 * HEADS].reshape(WIDTH, HEADS)
     feeds = [
-        gathered(weight[0], order)
-        for weight, order in (
-            (gate_weight, (0, 1, 2)),
-            (up_weight, (1, 2, 0)),
-            (down_weight, (2, 0, 1)),
+        gathered(block, order)
+        for block, order in (
+            (gate_weight[0], (0, 1, 2)),
+            (jnp.concatenate([up_weight[0], steps], axis=1), (1, 2, 0)),
+            (down_weight[0], (2, 0, 1)),
         )
     ]
     places = jnp.stack([place for blocks, found in feeds for place in found]).astype(jnp.int32)
     mats = (
         packed,
-        jnp.pad(dt_weight, ((0, 0), (0, 128 - HEADS))),
         (places, *(piece for blocks, found in feeds for piece in blocks)),
     )
     small = prepared_small([piece[0] for piece in pieces])
@@ -906,8 +957,8 @@
     first = lax.axis_index("section") == 0
 
     start_low = layer_input.reshape(rows, width)
-    out_mat, heads_mat, *kept_low = run_forward(start_low, mats, small, rope)
-    mats = (*mats[:2], out_mat, heads_mat, mats[2])
+    dt_weight, out_mat, heads_mat, *kept_low = run_forward(start_low, mats, small, rope)
+    mats = (packed, dt_weight, out_mat, heads_mat, mats[1])
     start_high = lax.ppermute(kept_low[0], "section", [(0, 1)])
     kept_high = run_forward(start_high, mats, small, rope)
     layer_outputs = jnp.where(first, kept_low[0], kept_high[0]).reshape(1, micro, part, width)
@@ -1019,17 +1070,16 @@
     ]
     axes = [DP[order[2]] for order in orders]
     quarters = [quarters_of(array, 0) for array in seconds]
-    gots = [first_got(first_sent(p, axis, 0), axis, 0) for p, axis in zip(quarters, axes)]
+    sents = [first_sent(p, axis, 0) for p, axis in zip(quarters, axes)]
+    gots = [first_got(sent, axis, 0) for sent, axis in zip(sents, axes)]
+    vectors, *unused = lax.optimization_barrier((vectors, *sents))
+    total = jnp.sum(vectors.astype(F32), axis=0).reshape(-1)
     handed = [handed_on(p, got, axis, 0) for p, got, axis in zip(quarters, gots, axes)]
-    vectors, *unused = lax.optimization_barrier((vectors, *handed))
-    total = jnp.sum(vectors.astype(F32), axis=0).reshape(-1)
-    rows_grad, gate_cat, up_cat = (
-        totalled(p, got, hand, axis, 0)
-        for p, got, hand, axis in zip(quarters, gots, handed, axes)
-    )
-    down_grad, joined_grad = rows_grad[:, :WIDTH], rows_grad[:, WIDTH:]
-    gate_grad, up_grad = gate_cat[:, :FEED], up_cat[:, :FEED]
-    cat_grad = jnp.concatenate([gate_cat[:, FEED:], up_cat[:, FEED:]], axis=1)
+    lasts = [
+        exchange(hand, axis, partners(axis, 0)[2][1]) for hand, axis in zip(handed, axes)
+    ]
+    mine = jnp.stack([lax.axis_index(axis) for axis in axes]).astype(jnp.int32)
+    mat_grads = run_finish(mine, seconds, gots, lasts)
 
     summed, at = ([], 0)
     for piece in small_grads:
@@ -1038,15 +1088,7 @@
     return (
         layer_outputs,
         grad_start.reshape(1, micro, part, width),
-        cat_grad[None, :, Z0 : T0 + HEADS],
-        cat_grad[None, :, :K0],
-        cat_grad[None, :, K0:V0],
-        cat_grad[None, :, V0:Z0],
-        joined_grad[None, :24],
-        joined_grad[None, 24:],
-        gate_grad[None],
-        up_grad[None],
-        down_grad[None],
+        *mat_grads,
         *summed,
     )
 

time: 429 us -> 441 us (1.028)
  starting transfers between devices: 59.9 us -> 100 us
  waiting for transfers between devices: 156 us -> 139 us
  local copies, waits for them, and re-layouts: 31.4 us -> 23.1 us
    all_gather x1, waiting for transfers between devices: 48.6 us -> 0.01 us  [on_device(): packed = lax.all_gather(own, DP, axis=0, tiled=False)]
    ppermute x42, starting transfers between devices: 56.9 us -> 96.9 us  [exchange(): return lax.ppermute(array, ('section', axis), pairs)]
    ppermute x42, waiting for transfers between devices: 91.7 us -> 120 us  [exchange(): return lax.ppermute(array, ('section', axis), pairs)]
    broadcast_in_dim x7 -> x0, local copies, waits for them, and re-layouts: 4.49 us -> none  [the longest x1 0.67 us: on_device(): gate_grad[None]]
  transfers between devices with their start and end apart: 46 -> 46, of which waited for: 22 -> 20; matrix products, arithmetic and copies ran while one was open for 21% -> 17% of each run, Pallas kernels for 6% -> 6%
where the time goes in v8:
time: 441 us; the launch traced here: 435 us
  waiting for transfers between devices  139 us (32%)
  starting transfers between devices  100 us (23%)
  Pallas kernels  89.2 us (20%)
  matrix products  37.1 us (8%)
  other arithmetic  30.5 us (7%)
  local copies, waits for them, and re-layouts  23.1 us (5%)
  between operations  15.5 us (4%)
    ppermute x42, waiting for transfers between devices, exchange(): return lax.ppermute(array, ('section', axis), pairs)  120 us
    ppermute x42, starting transfers between devices, exchange(): return lax.ppermute(array, ('section', axis), pairs)  96.9 us
    pallas_call x2, Pallas kernels, run_forward(): pl.pallas_call(functools.partial(forward_kernel, unpack), out_shape=extra...  39.5 us
    dot_general x18, matrix products, dot(): return jnp.dot(left, right, preferred_element_type=F32)  37.1 us
    pallas_call x2, Pallas kernels, run_mix_backward(): pl.pallas_call(functools.partial(mix_backward_kernel, len(earlier)), out_...  19.9 us
    ppermute x1, waiting for transfers between devices, on_device(): top_low = lax.ppermute(low_top, 'section', [(1, 0)])  19.6 us
    pallas_call x2, Pallas kernels, run_input_backward(): pl.pallas_call(functools.partial(input_backward_kernel, len(earlier)), ou...  14.8 us
    pallas_call x2, Pallas kernels, run_feed_backward(): pl.pallas_call(functools.partial(feed_backward_kernel, len(earlier)), out...  13.5 us
  transfers between devices with their start and end apart: 46, of which 20 were waited for; matrix products, arithmetic and copies ran while one was open for 17% of the time, Pallas kernels for 6%

profile of v8, /device:TPU:0, one launch (start us, length us, event | category | flops | bytes accessed | tf_op | source)
XLA Modules:
  0.0 434.7 jit_solution(6193614821570731952)
XLA Ops:
  38.4 3.4 collective-permute-start.9
  45.6 11.3 %collective-permute-done.9 = bf16[2,4,16,2176]{3,2,1,0:T(8,128)(2,1)S(1)} collective-permute-done((bf16[2,4,16,2176]{3,2,1,0:T(8,128)(2,1)S(1)}, bf16[2,4,16,2176]{3,2,1,0:T(8,128)(2,1)S(1)}, u32[]{:S(2)}, u32[]{:S(2)}) %collective-permute-start.9) | collective-permute-done | bytes 557088 | tf_op jit(solution)/shard_map/ppermute | solution.py:830
  57.3 9.6 %collective-permute-done.4.refs_2_.refs_4_.refs_3_ = bf16[4,4,16,2048]{3,2,1,0:T(8,128)(2,1)S(1)} collective-permute-done((bf16[4,4,16,2048]{3,2,1,0:T(8,128)(2,1)S(1)}, bf16[4,4,16,2048]{3,2,1,0:T(8,128)(2,1)S(1)}, u32[]{:S(2)}, u32[]{:S(2)}) %collective-permute-start.4) | collective-permute-done | bytes 1048608 | tf_op jit(solution)/shard_map/ppermute | solution.py:830
  74.7 28.0 %collective-permute-start.11 = (bf16[2,4,4,16,2176]{4,3,2,1,0:T(8,128)(2,1)}, bf16[2,4,4,16,2176]{4,3,2,1,0:T(8,128)(2,1)S(1)}, u32[]{:S(2)}, u32[]{:S(2)}) collective-permute-start(bf16[2,4,4,16,2176]{4,3,2,1,0:T(8,128)(2,1)} %pad_maximum_fusion), channel_id=1, source_target_pairs={{0,12},{4,8},{8,4},{12,0},{64,68},{68,64},{72,76},{76,72},{1,13},{... | collective-permute-start | bytes 6684680 | tf_op jit(solution)/shard_map/ppermute | solution.py:830
  104.3 6.2 %collective-permute-start.17 = (bf16[2,4,4,32,1024]{4,3,2,1,0:T(8,128)(2,1)}, bf16[2,4,4,32,1024]{4,3,2,1,0:T(8,128)(2,1)}, u32[]{:S(2)}, u32[]{:S(2)}) collective-permute-start(bf16[2,4,4,32,1024]{4,3,2,1,0:T(8,128)(2,1)} %pad_maximum_fusion.3), channel_id=1, source_target_pairs={{0,3},{1,2},{2,1},{3,0},{64,65},{65,64},{66,67},{67,66},{4,7},{5,6... | collective-permute-start | bytes 6291464 | tf_op jit(solution)/shard_map/ppermute | solution.py:830
  114.9 15.0 %collective-permute-done.5.refs_3_.refs_5_.refs_4_ = bf16[2,4,4,16,2048]{4,3,2,1,0:T(8,128)(2,1)} collective-permute-done((bf16[2,4,4,16,2048]{4,3,2,1,0:T(8,128)(2,1)}, bf16[2,4,4,16,2048]{4,3,2,1,0:T(8,128)(2,1)}, u32[]{:S(2)}, u32[]{:S(2)}) %collective-permute-start.5) | collective-permute-done | bytes 2097184 | tf_op jit(solution)/shard_map/ppermute | solution.py:830
  129.9 7.8 %collective-permute-done.17.refs_9_.refs_11_.refs_10_ = bf16[2,4,4,32,1024]{4,3,2,1,0:T(8,128)(2,1)} collective-permute-done((bf16[2,4,4,32,1024]{4,3,2,1,0:T(8,128)(2,1)}, bf16[2,4,4,32,1024]{4,3,2,1,0:T(8,128)(2,1)}, u32[]{:S(2)}, u32[]{:S(2)}) %collective-permute-start.17) | collective-permute-done | bytes 2097184 | tf_op jit(solution)/shard_map/ppermute | solution.py:830
  140.8 19.7 %forward.2 = (bf16[1024,128]{1,0:T(8,128)(2,1)}, bf16[1536,1024]{1,0:T(8,128)(2,1)}, bf16[512,1024]{1,0:T(8,128)(2,1)}, bf16[256,1024]{1,0:T(8,128)(2,1)}, bf16[...) custom-call(bf16[256,1024]{1,0:T(8,128)(2,1)} %bitcast.285, ...), custom_call_target="tpu_custom_call" | custom-call | flops 6451200000 | bytes 40000000 | tf_op jit(solution)/shard_map/forward/pallas_call | solution.py:612
  165.1 19.7 %forward.3 = (bf16[256,1024]{1,0:T(8,128)(2,1)}, bf16[256,1024]{1,0:T(8,128)(2,1)}, f32[256,4224]{1,0:T(8,128)}, f32[256,1536]{1,0:T(8,128)}, bf16[256,1536]{1,0...) custom-call(bf16[256,1024]{1,0:T(8,128)(2,1)} %copy-done.19, ...), custom_call_target="tpu_custom_call" | custom-call | flops 6451200000 | bytes 40000000 | tf_op jit(solution)/shard_map/forward/pallas_call | solution.py:612
  188.3 6.7 %input_backward.2 = (f32[256,1024]{1,0:T(8,128)}, bf16[256,1024]{1,0:T(8,128)(2,1)}, f32[1,1024]{1,0:T(1,128)}) custom-call(s32[1]{0:T(128)} %bitcast.56.active, bf16[256,4224]{1,0:T(8,128)(2,1)} %get-tuple-element.121.refs_0_.refs_15_, f32[256,1024]{1,0:T(8,128)} %get-tuple-element.118.refs_0_.refs_1_.refs_17_, bf16[256,1024]{1,0:T(8,128)(2,1)} %copy-done.19, ...), custom_call_target="tpu_custom_call" | custom-call | flops 2150400000 | bytes 13000000 | tf_op jit(solution)/shard_map/input_backward/pallas_call | solution.py:712
  207.0 19.6 %collective-permute-done.19.refs_0_ = bf16[256,1024]{1,0:T(8,128)(2,1)} collective-permute-done((bf16[256,1024]{1,0:T(8,128)(2,1)}, bf16[256,1024]{1,0:T(8,128)(2,1)}, u32[]{:S(2)}, u32[]{:S(2)}) %collective-permute-start.19) | collective-permute-done | bytes 524320 | tf_op jit(solution)/shard_map/ppermute | solution.py:981
  227.7 11.9 %feed_backward.3 = (bf16[256,2048]{1,0:T(8,128)(2,1)}, bf16[256,2048]{1,0:T(8,128)(2,1)}, f32[256,1024]{1,0:T(8,128)}, f32[1,1024]{1,0:T(1,128)}) custom-call(s32[1]{0:T(128)S(6)} %sub.29.active, bf16[256,1024]{1,0:T(8,128)(2,1)} %collective-permute-done.19.refs_0_, ...), custom_call_target="tpu_custom_call", output_to_operand_aliasing={{0}: (16, {}), {1}: (17, {}), {2}: (18, {}), {3}: (19, {})} | custom-call | flops 3225600000 | bytes 22000000 | tf_op jit(solution)/shard_map/feed_backward/pallas_call | solution.py:644
  249.8 18.2 %mix_backward.3 = (bf16[256,1024]{1,0:T(8,128)(2,1)}, bf16[256,4224]{1,0:T(8,128)(2,1)}, f32[4,1792]{1,0:T(4,128)}, f32[1,1792]{1,0:T(1,128)}, f32[1,128]{1,0:T(...) custom-call(s32[1]{0:T(128)S(6)} %sub.29.active, ...), custom_call_target="tpu_custom_call", output_to_operand_aliasing={{0}: (15, {}), {1}: (16, {}), {2}: (17, {}), {3}: (18, {}),... | custom-call | flops 1075200000 | bytes 14000000 | tf_op jit(solution)/shard_map/mix_backward/pallas_call | solution.py:680
  270.9 3.2 convolution_convert_fusion.4
  278.3 3.7 collective-permute-start.24
  290.6 3.3 collective-permute-start.29
  300.0 8.1 %input_backward.3 = (f32[256,1024]{1,0:T(8,128)}, bf16[256,1024]{1,0:T(8,128)(2,1)}, f32[1,1024]{1,0:T(1,128)}) custom-call(s32[1]{0:T(128)S(6)} %sub.29.active, bf16[256,4224]{1,0:T(8,128)(2,1)} %get-tuple-element.180.refs_0_, f32[256,1024]{1,0:T(8,128)} %get-tuple-element.170.refs_0_.refs_1_, ...), custom_call_target="tpu_custom_call", output_to_operand_aliasing={{0}: (7, {}), {1}: (8, {}), {2}: (9, {})} | custom-call | flops 2150400000 | bytes 13000000 | tf_op jit(solution)/shard_map/input_backward/pallas_call | solution.py:712
  316.5 12.5 %collective-permute-done.23 = bf16[512,1024]{1,0:T(8,128)(2,1)} collective-permute-done((bf16[512,1024]{1,0:T(8,128)(2,1)}, bf16[512,1024]{1,0:T(8,128)(2,1)}, u32[]{:S(2)}, u32[]{:S(2)}) %collective-permute-start.23) | collective-permute-done | bytes 1048608 | tf_op jit(solution)/shard_map/ppermute | solution.py:830
  331.0 3.4 collective-permute-done.33
  343.8 20.1 %collective-permute-done.30 = bf16[256,2048]{1,0:T(8,128)(2,1)S(1)} collective-permute-done((bf16[256,2048]{1,0:T(8,128)(2,1)S(1)}, bf16[256,2048]{1,0:T(8,128)(2,1)S(1)}, u32[]{:S(2)}, u32[]{:S(2)}) %collective-permute-start.30) | collective-permute-done | bytes 1048608 | tf_op jit(solution)/shard_map/ppermute | solution.py:830
  371.2 5.6 %collective-permute-start.36 = (bf16[128,4224]{1,0:T(8,128)(2,1)S(1)}, bf16[128,4224]{1,0:T(8,128)(2,1)S(1)}, u32[]{:S(2)}, u32[]{:S(2)}) collective-permute-start(bf16[128,4224]{1,0:T(8,128)(2,1)S(1)} %bitcast.291), channel_id=1, source_target_pairs={{0,3},{1,2},{2,1},{3,0},{64,65},{65,64},{66,67},{67,66},{4,7},{5,6... | collective-permute-start | bytes 3244040 | tf_op jit(solution)/shard_map/ppermute | solution.py:830
  379.8 9.0 %collective-permute-done.31 = bf16[128,4096]{1,0:T(8,128)(2,1)S(1)} collective-permute-done((bf16[128,4096]{1,0:T(8,128)(2,1)S(1)}, bf16[128,4096]{1,0:T(8,128)(2,1)S(1)}, u32[]{:S(2)}, u32[]{:S(2)}) %collective-permute-start.31) | collective-permute-done | bytes 1048608 | tf_op jit(solution)/shard_map/ppermute | solution.py:830
  389.2 9.2 %collective-permute-done.36 = bf16[128,4224]{1,0:T(8,128)(2,1)S(1)} collective-permute-done((bf16[128,4224]{1,0:T(8,128)(2,1)S(1)}, bf16[128,4224]{1,0:T(8,128)(2,1)S(1)}, u32[]{:S(2)}, u32[]{:S(2)}) %collective-permute-start.36) | collective-permute-done | bytes 1081376 | tf_op jit(solution)/shard_map/ppermute | solution.py:830
  403.0 5.1 %collective-permute-done.37 = bf16[64,4224]{1,0:T(8,128)(2,1)S(1)} collective-permute-done((bf16[64,4224]{1,0:T(8,128)(2,1)S(1)}, bf16[64,4224]{1,0:T(8,128)(2,1)S(1)}, u32[]{:S(2)}, u32[]{:S(2)}) %collective-permute-start.37) | collective-permute-done | bytes 540704 | tf_op jit(solution)/shard_map/ppermute | solution.py:830
  (360 shorter events, 158.6 us)
Async XLA Ops:
  7.2 132.3 %all-gather.6.cloned.1.call-start = ((), (), s32[]{:S(2)}) async-start(), calls=%async_computation.1 | async-start | bytes 12779520 | tf_op jit(solution)/shard_map/all_gather | solution.py:940
  11.2 399.8 %all-gather.4.cloned.1.call-start = ((), (), s32[]{:S(2)}) async-start(), calls=%async_computation | async-start | bytes 1730560 | tf_op jit(solution)/shard_map/all_gather | solution.py:1066
  36.0 21.1 %collective-permute-start.15 = (bf16[2,4,32,1024]{3,2,1,0:T(8,128)(2,1)S(1)}, bf16[2,4,32,1024]{3,2,1,0:T(8,128)(2,1)S(1)}, u32[]{:S(2)}, u32[]{:S(2)}) collective-permute-start(bf16[2,4,32,1024]{3,2,1,0:T(8,128)(2,1)S(1)} %pad_maximum_fusion.11), channel_id=1, source_target_pairs={{0,48},{16,32},{32,16},{48,0},{64,80},{80,64},{96,112},{112,96},{1... | collective-permute-start | bytes 1572872 | tf_op jit(solution)/shard_map/ppermute | solution.py:830
  44.8 22.1 %collective-permute-start.4 = (bf16[4,4,16,2048]{3,2,1,0:T(8,128)(2,1)S(1)}, bf16[4,4,16,2048]{3,2,1,0:T(8,128)(2,1)S(1)}, u32[]{:S(2)}, u32[]{:S(2)}) collective-permute-start(bf16[4,4,16,2048]{3,2,1,0:T(8,128)(2,1)S(1)} %slice_dynamic-update-slice_fusion.2.refs_1_.refs_3_.refs_2_), channel_id=1, source_target_pairs={{0,16},{16,0},{32,48},{48,32},{64,112},{80,96},{96,80},{112,64},{1... | collective-permute-start | bytes 3145736 | tf_op jit(solution)/shard_map/ppermute | solution.py:830
  57.2 45.4 %collective-permute-start.16 = (bf16[4,4,32,1024]{3,2,1,0:T(8,128)(2,1)S(1)}, bf16[4,4,32,1024]{3,2,1,0:T(8,128)(2,1)S(1)}, u32[]{:S(2)}, u32[]{:S(2)}) collective-permute-start(bf16[4,4,32,1024]{3,2,1,0:T(8,128)(2,1)S(1)} %slice_dynamic-update-slice_fusion.refs_7_.refs_9_.refs_8_), channel_id=1, source_target_pairs={{0,1},{1,0},{2,3},{3,2},{64,67},{65,66},{66,65},{67,64},{4,5},{5,4... | collective-permute-start | bytes 3145736 | tf_op jit(solution)/shard_map/ppermute | solution.py:830
  68.6 61.3 %collective-permute-start.5 = (bf16[2,4,4,16,2048]{4,3,2,1,0:T(8,128)(2,1)}, bf16[2,4,4,16,2048]{4,3,2,1,0:T(8,128)(2,1)}, u32[]{:S(2)}, u32[]{:S(2)}) collective-permute-start(bf16[2,4,4,16,2048]{4,3,2,1,0:T(8,128)(2,1)} %pad_maximum_fusion.2), channel_id=1, source_target_pairs={{0,48},{16,32},{32,16},{48,0},{64,80},{80,64},{96,112},{112,96},{1... | collective-permute-start | bytes 6291464 | tf_op jit(solution)/shard_map/ppermute | solution.py:830
  74.7 64.8 %collective-permute-start.11 = (bf16[2,4,4,16,2176]{4,3,2,1,0:T(8,128)(2,1)}, bf16[2,4,4,16,2176]{4,3,2,1,0:T(8,128)(2,1)S(1)}, u32[]{:S(2)}, u32[]{:S(2)}) collective-permute-start(bf16[2,4,4,16,2176]{4,3,2,1,0:T(8,128)(2,1)} %pad_maximum_fusion), channel_id=1, source_target_pairs={{0,12},{4,8},{8,4},{12,0},{64,68},{68,64},{72,76},{76,72},{1,13},{... | collective-permute-start | bytes 6684680 | tf_op jit(solution)/shard_map/ppermute | solution.py:830
  104.3 33.4 %collective-permute-start.17 = (bf16[2,4,4,32,1024]{4,3,2,1,0:T(8,128)(2,1)}, bf16[2,4,4,32,1024]{4,3,2,1,0:T(8,128)(2,1)}, u32[]{:S(2)}, u32[]{:S(2)}) collective-permute-start(bf16[2,4,4,32,1024]{4,3,2,1,0:T(8,128)(2,1)} %pad_maximum_fusion.3), channel_id=1, source_target_pairs={{0,3},{1,2},{2,1},{3,0},{64,65},{65,64},{66,67},{67,66},{4,7},{5,6... | collective-permute-start | bytes 6291464 | tf_op jit(solution)/shard_map/ppermute | solution.py:830
  195.0 31.6 %collective-permute-start.19 = (bf16[256,1024]{1,0:T(8,128)(2,1)}, bf16[256,1024]{1,0:T(8,128)(2,1)}, u32[]{:S(2)}, u32[]{:S(2)}) collective-permute-start(bf16[256,1024]{1,0:T(8,128)(2,1)} %get-tuple-element.129.refs_7_), channel_id=1, source_target_pairs={{64,0},{65,1},{66,2},{67,3},{68,4},{69,5},{70,6},{71,7},{72,8},{73... | collective-permute-start | bytes 1572872 | tf_op jit(solution)/shard_map/ppermute | solution.py:981
  245.8 32.5 %collective-permute-start.20 = (bf16[1024,1024]{1,0:T(8,128)(2,1)}, bf16[1024,1024]{1,0:T(8,128)(2,1)}, u32[]{:S(2)}, u32[]{:S(2)}) collective-permute-start(bf16[1024,1024]{1,0:T(8,128)(2,1)} %convolution_convert_fusion.5), channel_id=1, source_target_pairs={{0,1},{1,0},{2,3},{3,2},{64,67},{65,66},{66,65},{67,64},{4,5},{5,4... | collective-permute-start | bytes 6291464 | tf_op jit(solution)/shard_map/ppermute | solution.py:830
  246.2 32.1 %collective-permute-start.21 = (bf16[512,2048]{1,0:T(8,128)(2,1)}, bf16[512,2048]{1,0:T(8,128)(2,1)}, u32[]{:S(2)}, u32[]{:S(2)}) collective-permute-start(bf16[512,2048]{1,0:T(8,128)(2,1)} %convolution_convert_fusion.3), channel_id=1, source_target_pairs={{0,16},{16,0},{32,48},{48,32},{64,112},{80,96},{96,80},{112,64},{1... | collective-permute-start | bytes 6291464 | tf_op jit(solution)/shard_map/ppermute | solution.py:830
  248.0 30.3 %collective-permute-start.22 = (bf16[512,2048]{1,0:T(8,128)(2,1)}, bf16[512,2048]{1,0:T(8,128)(2,1)}, u32[]{:S(2)}, u32[]{:S(2)}) collective-permute-start(bf16[512,2048]{1,0:T(8,128)(2,1)} %convolution_convert_fusion.2), channel_id=1, source_target_pairs={{0,4},{4,0},{8,12},{12,8},{64,76},{68,72},{72,68},{76,64},{1,5},{5... | collective-permute-start | bytes 6291464 | tf_op jit(solution)/shard_map/ppermute | solution.py:830
  278.3 34.9 %collective-permute-start.24 = (bf16[1024,1024]{1,0:T(8,128)(2,1)}, bf16[1024,1024]{1,0:T(8,128)(2,1)}, u32[]{:S(2)}, u32[]{:S(2)}) collective-permute-start(bf16[1024,1024]{1,0:T(8,128)(2,1)} %convolution_convert_fusion.4), channel_id=1, source_target_pairs={{0,3},{1,2},{2,1},{3,0},{64,65},{65,64},{66,67},{67,66},{4,7},{5,6... | collective-permute-start | bytes 6291464 | tf_op jit(solution)/shard_map/ppermute | solution.py:830
  290.5 38.4 %collective-permute-start.23 = (bf16[512,1024]{1,0:T(8,128)(2,1)}, bf16[512,1024]{1,0:T(8,128)(2,1)}, u32[]{:S(2)}, u32[]{:S(2)}) collective-permute-start(bf16[512,1024]{1,0:T(8,128)(2,1)} %add_convert_fusion.9), channel_id=1, source_target_pairs={{0,3},{1,2},{2,1},{3,0},{64,65},{65,64},{66,67},{67,66},{4,7},{5,6... | collective-permute-start | bytes 3145736 | tf_op jit(solution)/shard_map/ppermute | solution.py:830
  290.6 45.8 %collective-permute-start.29 = (bf16[512,2048]{1,0:T(8,128)(2,1)}, bf16[512,2048]{1,0:T(8,128)(2,1)}, u32[]{:S(2)}, u32[]{:S(2)}) collective-permute-start(bf16[512,2048]{1,0:T(8,128)(2,1)} %convolution_convert_fusion.1), channel_id=1, source_target_pairs={{0,48},{16,32},{32,16},{48,0},{64,80},{80,64},{96,112},{112,96},{1... | collective-permute-start | bytes 6291464 | tf_op jit(solution)/shard_map/ppermute | solution.py:830
  293.9 44.4 %collective-permute-start.34 = (bf16[512,2176]{1,0:T(8,128)(2,1)}, bf16[512,2176]{1,0:T(8,128)(2,1)}, u32[]{:S(2)}, u32[]{:S(2)}) collective-permute-start(bf16[512,2176]{1,0:T(8,128)(2,1)} %convolution_convert_fusion), channel_id=1, source_target_pairs={{0,12},{4,8},{8,4},{12,0},{64,68},{68,64},{72,76},{76,72},{1,13},{... | collective-permute-start | bytes 6684680 | tf_op jit(solution)/shard_map/ppermute | solution.py:830
  309.6 24.8 %collective-permute-start.33 = (bf16[256,2048]{1,0:T(8,128)(2,1)S(1)}, bf16[256,2048]{1,0:T(8,128)(2,1)S(1)}, u32[]{:S(2)}, u32[]{:S(2)}) collective-permute-start(bf16[256,2048]{1,0:T(8,128)(2,1)S(1)} %copy-done.21), channel_id=1, source_target_pairs={{0,12},{4,8},{8,4},{12,0},{64,68},{68,64},{72,76},{76,72},{1,13},{... | collective-permute-start | bytes 3145736 | tf_op jit(solution)/shard_map/ppermute | solution.py:830
  315.1 25.9 %collective-permute-start.25 = (bf16[512,1024]{1,0:T(8,128)(2,1)S(1)}, bf16[512,1024]{1,0:T(8,128)(2,1)S(1)}, u32[]{:S(2)}, u32[]{:S(2)}) collective-permute-start(bf16[512,1024]{1,0:T(8,128)(2,1)S(1)} %add_convert_fusion.7), channel_id=1, source_target_pairs={{0,1},{1,0},{2,3},{3,2},{64,67},{65,66},{66,65},{67,64},{4,5},{5,4... | collective-permute-start | bytes 3145736 | tf_op jit(solution)/shard_map/ppermute | solution.py:830
  338.2 25.8 %collective-permute-start.30 = (bf16[256,2048]{1,0:T(8,128)(2,1)S(1)}, bf16[256,2048]{1,0:T(8,128)(2,1)S(1)}, u32[]{:S(2)}, u32[]{:S(2)}) collective-permute-start(bf16[256,2048]{1,0:T(8,128)(2,1)S(1)} %add_convert_fusion.4), channel_id=1, source_target_pairs={{0,16},{16,0},{32,48},{48,32},{64,112},{80,96},{96,80},{112,64},{1... | collective-permute-start | bytes 3145736 | tf_op jit(solution)/shard_map/ppermute | solution.py:830
  340.1 29.0 %collective-permute-start.35 = (bf16[256,2176]{1,0:T(8,128)(2,1)S(1)}, bf16[256,2176]{1,0:T(8,128)(2,1)S(1)}, u32[]{:S(2)}, u32[]{:S(2)}) collective-permute-start(bf16[256,2176]{1,0:T(8,128)(2,1)S(1)} %add_convert_fusion.1), channel_id=1, source_target_pairs={{0,4},{4,0},{8,12},{12,8},{64,76},{68,72},{72,68},{76,64},{1,5},{5... | collective-permute-start | bytes 3342344 | tf_op jit(solution)/shard_map/ppermute | solution.py:830
  343.3 33.5 %collective-permute-start.26 = (bf16[256,2048]{1,0:T(8,128)(2,1)S(1)}, bf16[256,2048]{1,0:T(8,128)(2,1)S(1)}, u32[]{:S(2)}, u32[]{:S(2)}) collective-permute-start(bf16[256,2048]{1,0:T(8,128)(2,1)S(1)} %bitcast.295), channel_id=1, source_target_pairs={{0,48},{16,32},{32,16},{48,0},{64,80},{80,64},{96,112},{112,96},{1... | collective-permute-start | bytes 3145736 | tf_op jit(solution)/shard_map/ppermute | solution.py:830
  366.3 22.5 %collective-permute-start.31 = (bf16[128,4096]{1,0:T(8,128)(2,1)S(1)}, bf16[128,4096]{1,0:T(8,128)(2,1)S(1)}, u32[]{:S(2)}, u32[]{:S(2)}) collective-permute-start(bf16[128,4096]{1,0:T(8,128)(2,1)S(1)} %bitcast.296), channel_id=1, source_target_pairs={{0,12},{4,8},{8,4},{12,0},{64,68},{68,64},{72,76},{76,72},{1,13},{... | collective-permute-start | bytes 3145736 | tf_op jit(solution)/shard_map/ppermute | solution.py:830
  371.2 27.3 %collective-permute-start.36 = (bf16[128,4224]{1,0:T(8,128)(2,1)S(1)}, bf16[128,4224]{1,0:T(8,128)(2,1)S(1)}, u32[]{:S(2)}, u32[]{:S(2)}) collective-permute-start(bf16[128,4224]{1,0:T(8,128)(2,1)S(1)} %bitcast.291), channel_id=1, source_target_pairs={{0,3},{1,2},{2,1},{3,0},{64,65},{65,64},{66,67},{67,66},{4,7},{5,6... | collective-permute-start | bytes 3244040 | tf_op jit(solution)/shard_map/ppermute | solution.py:830
  376.9 22.7 %collective-permute-start.27 = (bf16[128,2048]{1,0:T(8,128)(2,1)S(1)}, bf16[128,2048]{1,0:T(8,128)(2,1)S(1)}, u32[]{:S(2)}, u32[]{:S(2)}) collective-permute-start(bf16[128,2048]{1,0:T(8,128)(2,1)S(1)} %fusion.9), channel_id=1, source_target_pairs={{0,16},{16,0},{32,48},{48,32},{64,112},{80,96},{96,80},{112,64},{1... | collective-permute-start | bytes 1572872 | tf_op jit(solution)/shard_map/ppermute | solution.py:830
  (84 other events, 698.1 us)
Sparse Core Ops, SparseCore 0:
  11.5 115.4 all-gather.5
  309.7 63.6 all-gather.3

commit v9 on v8

--- a/solution.py
+++ b/solution.py
@@ -21,7 +21,7 @@
 BF16 = jnp.bfloat16
 HIDE = -1e30
 Q0, K0, V0, Z0, X0, T0 = 0, 512, 640, 768, 2304, 4096
-OUT0, PACKED = 64, 96
+OUT0, HEADS0, DT0, PACKED = 64, 88, 96, 104
 
 
 def dot(left, right):
@@ -303,25 +303,25 @@
     return block.reshape(-1, block.shape[-1])
 
 
-def forward_kernel(unpack, x, packed, *refs):
+def forward_kernel(unpack, x, packed, dt_weight, *refs):
     if unpack:
-        given, results = (None, None), refs[20:23]
-        rest = refs[:20] + refs[23:]
+        given, results = (None, None), refs[20:22]
+        rest = refs[:20] + refs[22:]
     else:
-        given, results = refs[:2], (None, None, None)
+        given, results = refs[:2], (None, None)
         rest = refs[2:]
-    forward_body(unpack, x, packed, *given, *results, *rest)
+    forward_body(unpack, x, packed, dt_weight, *given, *results, *rest)
 
 
 def forward_body(
-    unpack, x, packed, out_weight, heads_weight, dt_result, out_result, heads_result,
+    unpack, x, packed, dt_weight, out_weight, heads_weight, out_result, heads_result,
     places, gate_own, gate_got, gate_far, up_own, up_got, up_far, down_own, down_got, down_far,
     input_gain, kernel, bias, step_bias, decay_log, skip,
     mixer_gain, feed_gain, cosine, sine,
     result_out, normed_out, proj_out, ssm_out, mamba_out, attended_out, middle_out, ffin_out, gate_out,
     upper_out, hidden_out,
     result, normed, proj, ssm, mamba, attended, middle, ffin, gate, upper, hidden,
-    cat, gate_mat, up_mat, down_mat, out_mat, heads_mat, mixed, dt_mat, sems, out_sems, feed_sems,
+    cat, gate_mat, up_mat, down_mat, out_mat, heads_mat, mixed, sems, out_sems, feed_sems,
 ):
     leaving = []
 
@@ -345,13 +345,10 @@
     start_all(copies + feeds)
     state = x[...].astype(F32)
     normed[...] = (state * rms(state) * input_gain[...]).astype(BF16)
+    proj[:, T0:CAT] = dot(normed[...], dt_weight[...])
     for j in range(4):
         copies[j].wait()
         proj[:, 1024 * j : 1024 * j + 1024] = dot(normed[...], flat(cat[j]))
-    for copy in feeds[4:8]:
-        copy.wait()
-    dt_mat[...] = rows_of(up_mat[:, :, :, :, FEED:])
-    proj[:, T0:CAT] = dot(normed[...], dt_mat[...])
     leave((normed, normed_out), (proj, proj_out))
 
     def sequence(index, carry):
@@ -368,14 +365,14 @@
         wide = mixed[...].astype(F32)
         out_mat[...] = wide[:, :24].reshape(INNER, WIDTH).astype(BF16)
         heads_mat[...] = wide[:, 24:].reshape(512, WIDTH).astype(BF16)
-        leave((dt_mat, dt_result), (out_mat, out_result), (heads_mat, heads_result))
+        leave((out_mat, out_result), (heads_mat, heads_result))
 
     part = dot(mamba[...], out_mat[...]) + dot(attended[...], heads_mat[...])
     middle[...] = x[...].astype(F32) + part
     value = middle[...]
     ffin[...] = (value * rms(value) * feed_gain[...]).astype(BF16)
     leave((middle, middle_out), (ffin, ffin_out))
-    for copy in feeds[:4]:
+    for copy in feeds[:8]:
         copy.wait()
 
     for half in range(2):
@@ -443,7 +440,7 @@
         copy.wait()
 
     grad_ffin = dot_nt(grad_gate[...], rows_of(gate_mat[...]))
-    grad_ffin = grad_ffin + dot_nt(grad_upper[...], rows_of(up_mat[:, :, :, :, :FEED]))
+    grad_ffin = grad_ffin + dot_nt(grad_upper[...], rows_of(up_mat[...]))
     inputs[2].wait()
     grad_part, grad_gain = rms_backward(middle[...], feed_gain[...], grad_ffin)
     feed_grad[...] = grad_gain
@@ -582,7 +579,7 @@
 
 FEED_MATS = (
     scratch(4, 4, 4, 16, FEED),
-    scratch(4, 4, 4, 16, FEED + 128),
+    scratch(4, 4, 4, 16, FEED),
     scratch(4, 4, 4, 32, WIDTH),
 )
 
@@ -592,10 +589,9 @@
 
 
 def run_forward(start, mats, small, rope):
-    packed, *given, feeds = mats
+    packed, dt_weight, *given, feeds = mats
     unpack = not given
-    given = given[1:]
-    extra = (shape(WIDTH, 128, BF16), shape(INNER, WIDTH, BF16), shape(512, WIDTH, BF16))
+    extra = (shape(INNER, WIDTH, BF16), shape(512, WIDTH, BF16))
     shapes = (
         shape(ROWS, WIDTH, BF16),
         shape(ROWS, WIDTH, BF16),
@@ -612,8 +608,8 @@
     return pl.pallas_call(
         functools.partial(forward_kernel, unpack),
         out_shape=extra + shapes if unpack else shapes,
-        in_specs=[VMEM, ANY] + [ANY] * len(given) + [SMEM] + [ANY] * 9 + [VMEM] * 10,
-        out_specs=(ANY,) * (len(shapes) + 3 * unpack),
+        in_specs=[VMEM, ANY, VMEM] + [ANY] * len(given) + [SMEM] + [ANY] * 9 + [VMEM] * 10,
+        out_specs=(ANY,) * (len(shapes) + 2 * unpack),
         scratch_shapes=[
             *mirrored(shapes),
             scratch(4, 64, 16, 1024),
@@ -621,9 +617,8 @@
             scratch(INNER, WIDTH),
             scratch(512, WIDTH),
             scratch(64, 32, WIDTH) if unpack else scratch(16, 128),
-            scratch(WIDTH, 128),
             pltpu.SemaphoreType.DMA((6,)),
-            pltpu.SemaphoreType.DMA((len(shapes) + 3,)),
+            pltpu.SemaphoreType.DMA((len(shapes) + 2,)),
             pltpu.SemaphoreType.DMA((12,)),
         ],
         compiler_params=pltpu.CompilerParams(vmem_limit_bytes=LIMIT),
@@ -631,7 +626,7 @@
             flops=2 * ROWS * 12_600_000, bytes_accessed=40_000_000, transcendentals=2_000_000
         ),
         name="forward",
-    )(start, packed, *given, *feeds, *small, *rope)
+    )(start, packed, dt_weight, *given, *feeds, *small, *rope)
 
 
 def run_feed_backward(active, grad_top, mats, gate, upper, middle, feed_gain, earlier=()):
@@ -880,7 +875,7 @@
     rest = [0, 1, 2]
     rest.remove(order[0])
     array = array.reshape(4, 4, depth, width)
-    array = summed_on(array, DP[order[1]], rest.index(order[1]), 1).astype(BF16)
+    array = summed_on(array, DP[order[1]], rest.index(order[1]), 0).astype(BF16)
     return array.reshape(4, depth, width)
 
 
@@ -928,27 +923,30 @@
     cat = jnp.concatenate(
         [query_weight[0], key_weight[0], value_weight[0], in_weight[0, :, :3328]], axis=1
     )
-    steps = jnp.pad(in_weight[0, :, 3328:], ((0, 0), (0, 128 - HEADS)))
+    steps = jnp.pad(in_weight[0, :, 3328:].reshape(1, -1), ((0, 7), (0, 1024 - 16 * HEADS)))
     own = jnp.concatenate(
         [
             *column_blocks(cat),
             out_weight[0],
             heads_weight[0],
+            steps,
         ],
         axis=0,
     )
     packed = lax.all_gather(own, DP, axis=0, tiled=False)
+    dt_weight = packed[:, DT0, : 16 * HEADS].reshape(WIDTH, HEADS)
     feeds = [
-        gathered(block, order)
-        for block, order in (
-            (gate_weight[0], (0, 1, 2)),
-            (jnp.concatenate([up_weight[0], steps], axis=1), (1, 2, 0)),
-            (down_weight[0], (2, 0, 1)),
+        gathered(weight[0], order)
+        for weight, order in (
+            (gate_weight, (0, 1, 2)),
+            (up_weight, (1, 2, 0)),
+            (down_weight, (2, 0, 1)),
         )
     ]
     places = jnp.stack([place for blocks, found in feeds for place in found]).astype(jnp.int32)
     mats = (
         packed,
+        jnp.pad(dt_weight, ((0, 0), (0, 128 - HEADS))),
         (places, *(piece for blocks, found in feeds for piece in blocks)),
     )
     small = prepared_small([piece[0] for piece in pieces])
@@ -957,8 +955,8 @@
     first = lax.axis_index("section") == 0
 
     start_low = layer_input.reshape(rows, width)
-    dt_weight, out_mat, heads_mat, *kept_low = run_forward(start_low, mats, small, rope)
-    mats = (packed, dt_weight, out_mat, heads_mat, mats[1])
+    out_mat, heads_mat, *kept_low = run_forward(start_low, mats, small, rope)
+    mats = (*mats[:2], out_mat, heads_mat, mats[2])
     start_high = lax.ppermute(kept_low[0], "section", [(0, 1)])
     kept_high = run_forward(start_high, mats, small, rope)
     layer_outputs = jnp.where(first, kept_low[0], kept_high[0]).reshape(1, micro, part, width)

time: 441 us -> 424 us (0.961)
  starting transfers between devices: 100 us -> 64 us
  waiting for transfers between devices: 139 us -> 157 us
    all_gather x1, waiting for transfers between devices: 0.01 us -> 48.7 us  [on_device(): packed = lax.all_gather(own, DP, axis=0, tiled=False)]
    ppermute x42, starting transfers between devices: 96.9 us -> 60.9 us  [exchange(): return lax.ppermute(array, ('section', axis), pairs)]
    ppermute x42, waiting for transfers between devices: 120 us -> 89.1 us  [exchange(): return lax.ppermute(array, ('section', axis), pairs)]
  transfers between devices with their start and end apart: 46 -> 46, of which waited for: 20 -> 20; matrix products, arithmetic and copies ran while one was open for 17% -> 18% of each run, Pallas kernels for 6% -> 6%
where the time goes in v9:
time: 424 us; the launch traced here: 418 us
  waiting for transfers between devices  157 us (37%)
  Pallas kernels  88.7 us (21%)
  starting transfers between devices  64 us (15%)
  matrix products  37.1 us (9%)
  other arithmetic  28.7 us (7%)
  local copies, waits for them, and re-layouts  26.5 us (6%)
  between operations  15.5 us (4%)
    ppermute x42, waiting for transfers between devices, exchange(): return lax.ppermute(array, ('section', axis), pairs)  89.1 us
    ppermute x42, starting transfers between devices, exchange(): return lax.ppermute(array, ('section', axis), pairs)  60.9 us
    all_gather x1, waiting for transfers between devices, on_device(): packed = lax.all_gather(own, DP, axis=0, tiled=False)  48.7 us
    pallas_call x2, Pallas kernels, run_forward(): pl.pallas_call(functools.partial(forward_kernel, unpack), out_shape=extra...  39.2 us
    dot_general x18, matrix products, dot(): return jnp.dot(left, right, preferred_element_type=F32)  37.1 us
    pallas_call x2, Pallas kernels, run_mix_backward(): pl.pallas_call(functools.partial(mix_backward_kernel, len(earlier)), out_...  19.7 us
    ppermute x1, waiting for transfers between devices, on_device(): top_low = lax.ppermute(low_top, 'section', [(1, 0)])  19.4 us
    pallas_call x2, Pallas kernels, run_input_backward(): pl.pallas_call(functools.partial(input_backward_kernel, len(earlier)), ou...  14.8 us
  transfers between devices with their start and end apart: 46, of which 20 were waited for; matrix products, arithmetic and copies ran while one was open for 18% of the time, Pallas kernels for 6%

profile of v9, /device:TPU:0, one launch (start us, length us, event | category | flops | bytes accessed | tf_op | source)
XLA Modules:
  0.0 417.6 jit_solution(10114879173623629225)
XLA Ops:
  23.5 3.3 collective-permute-start.13
  40.4 4.6 %collective-permute-done.3 = bf16[2,4,16,2048]{3,2,1,0:T(8,128)(2,1)S(1)} collective-permute-done((bf16[2,4,16,2048]{3,2,1,0:T(8,128)(2,1)S(1)}, bf16[2,4,16,2048]{3,2,1,0:T(8,128)(2,1)S(1)}, u32[]{:S(2)}, u32[]{:S(2)}) %collective-permute-start.3) | collective-permute-done | bytes 524320 | tf_op jit(solution)/shard_map/ppermute | solution.py:825
  46.9 6.9 %collective-permute-done.15 = bf16[2,4,32,1024]{3,2,1,0:T(8,128)(2,1)S(1)} collective-permute-done((bf16[2,4,32,1024]{3,2,1,0:T(8,128)(2,1)S(1)}, bf16[2,4,32,1024]{3,2,1,0:T(8,128)(2,1)S(1)}, u32[]{:S(2)}, u32[]{:S(2)}) %collective-permute-start.15) | collective-permute-done | bytes 524320 | tf_op jit(solution)/shard_map/ppermute | solution.py:825
  54.0 14.3 %collective-permute-done.4.refs_2_.refs_4_.refs_3_ = bf16[4,4,16,2048]{3,2,1,0:T(8,128)(2,1)S(1)} collective-permute-done((bf16[4,4,16,2048]{3,2,1,0:T(8,128)(2,1)S(1)}, bf16[4,4,16,2048]{3,2,1,0:T(8,128)(2,1)S(1)}, u32[]{:S(2)}, u32[]{:S(2)}) %collective-permute-start.4) | collective-permute-done | bytes 1048608 | tf_op jit(solution)/shard_map/ppermute | solution.py:825
  77.1 2.7 collective-permute-start.17
  84.1 48.7 %all-gather.6.cloned.1.call-done = bf16[6656,1024]{1,0:T(8,128)(2,1)} async-done(((bf16[104,1024]{1,0:T(8,128)(2,1)}), bf16[6656,1024]{1,0:T(8,128)(2,1)}) %all-gather.6.cloned.1.call-update) | async-done | bytes 13631504 | tf_op jit(solution)/shard_map/all_gather | solution.py:936
  137.7 19.7 %forward.2 = (bf16[1536,1024]{1,0:T(8,128)(2,1)}, bf16[512,1024]{1,0:T(8,128)(2,1)}, bf16[256,1024]{1,0:T(8,128)(2,1)}, bf16[256,1024]{1,0:T(8,128)(2,1)}, f32[2...) custom-call(bf16[256,1024]{1,0:T(8,128)(2,1)} %bitcast.281, ...), custom_call_target="tpu_custom_call" | custom-call | flops 6451200000 | bytes 40000000 | tf_op jit(solution)/shard_map/forward/pallas_call | solution.py:608
  161.9 19.5 %forward.3 = (bf16[256,1024]{1,0:T(8,128)(2,1)}, bf16[256,1024]{1,0:T(8,128)(2,1)}, f32[256,4224]{1,0:T(8,128)}, f32[256,1536]{1,0:T(8,128)}, bf16[256,1536]{1,0...) custom-call(bf16[256,1024]{1,0:T(8,128)(2,1)} %copy-done.19, ...), custom_call_target="tpu_custom_call" | custom-call | flops 6451200000 | bytes 40000000 | tf_op jit(solution)/shard_map/forward/pallas_call | solution.py:608
  184.8 6.7 %input_backward.2 = (f32[256,1024]{1,0:T(8,128)}, bf16[256,1024]{1,0:T(8,128)(2,1)}, f32[1,1024]{1,0:T(1,128)}) custom-call(s32[1]{0:T(128)} %bitcast.54.active, bf16[256,4224]{1,0:T(8,128)(2,1)} %get-tuple-element.120.refs_0_.refs_15_, f32[256,1024]{1,0:T(8,128)} %get-tuple-element.117.refs_0_.refs_1_.refs_17_, bf16[256,1024]{1,0:T(8,128)(2,1)} %copy-done.19, ...), custom_call_target="tpu_custom_call" | custom-call | flops 2150400000 | bytes 13000000 | tf_op jit(solution)/shard_map/input_backward/pallas_call | solution.py:707
  203.6 19.4 %collective-permute-done.19.refs_0_ = bf16[256,1024]{1,0:T(8,128)(2,1)} collective-permute-done((bf16[256,1024]{1,0:T(8,128)(2,1)}, bf16[256,1024]{1,0:T(8,128)(2,1)}, u32[]{:S(2)}, u32[]{:S(2)}) %collective-permute-start.19) | collective-permute-done | bytes 524320 | tf_op jit(solution)/shard_map/ppermute | solution.py:979
  224.1 11.8 %feed_backward.3 = (bf16[256,2048]{1,0:T(8,128)(2,1)}, bf16[256,2048]{1,0:T(8,128)(2,1)}, f32[256,1024]{1,0:T(8,128)}, f32[1,1024]{1,0:T(1,128)}) custom-call(s32[1]{0:T(128)S(6)} %sub.29.active, bf16[256,1024]{1,0:T(8,128)(2,1)} %collective-permute-done.19.refs_0_, ...), custom_call_target="tpu_custom_call", output_to_operand_aliasing={{0}: (16, {}), {1}: (17, {}), {2}: (18, {}), {3}: (19, {})} | custom-call | flops 3225600000 | bytes 22000000 | tf_op jit(solution)/shard_map/feed_backward/pallas_call | solution.py:639
  247.1 18.0 %mix_backward.3 = (bf16[256,1024]{1,0:T(8,128)(2,1)}, bf16[256,4224]{1,0:T(8,128)(2,1)}, f32[4,1792]{1,0:T(4,128)}, f32[1,1792]{1,0:T(1,128)}, f32[1,128]{1,0:T(...) custom-call(s32[1]{0:T(128)S(6)} %sub.29.active, ...), custom_call_target="tpu_custom_call", output_to_operand_aliasing={{0}: (15, {}), {1}: (16, {}), {2}: (17, {}), {3}: (18, {}),... | custom-call | flops 1075200000 | bytes 14000000 | tf_op jit(solution)/shard_map/mix_backward/pallas_call | solution.py:675
  268.1 3.3 convolution_convert_fusion.4
  280.4 2.7 fusion
  283.1 2.7 fusion.1
  290.6 2.9 collective-permute-start.34
  297.1 8.1 %input_backward.3 = (f32[256,1024]{1,0:T(8,128)}, bf16[256,1024]{1,0:T(8,128)(2,1)}, f32[1,1024]{1,0:T(1,128)}) custom-call(s32[1]{0:T(128)S(6)} %sub.29.active, bf16[256,4224]{1,0:T(8,128)(2,1)} %get-tuple-element.178.refs_0_, f32[256,1024]{1,0:T(8,128)} %get-tuple-element.168.refs_0_.refs_1_, ...), custom_call_target="tpu_custom_call", output_to_operand_aliasing={{0}: (7, {}), {1}: (8, {}), {2}: (9, {})} | custom-call | flops 2150400000 | bytes 13000000 | tf_op jit(solution)/shard_map/input_backward/pallas_call | solution.py:707
  311.9 13.8 %collective-permute-done.23 = bf16[512,1024]{1,0:T(8,128)(2,1)} collective-permute-done((bf16[512,1024]{1,0:T(8,128)(2,1)}, bf16[512,1024]{1,0:T(8,128)(2,1)}, u32[]{:S(2)}, u32[]{:S(2)}) %collective-permute-start.23) | collective-permute-done | bytes 1048608 | tf_op jit(solution)/shard_map/ppermute | solution.py:825
  327.8 3.3 collective-permute-done.33
  342.4 8.1 %collective-permute-done.30 = bf16[256,2048]{1,0:T(8,128)(2,1)S(1)} collective-permute-done((bf16[256,2048]{1,0:T(8,128)(2,1)S(1)}, bf16[256,2048]{1,0:T(8,128)(2,1)S(1)}, u32[]{:S(2)}, u32[]{:S(2)}) %collective-permute-start.30) | collective-permute-done | bytes 1048608 | tf_op jit(solution)/shard_map/ppermute | solution.py:825
  356.4 15.2 %collective-permute-done.26 = bf16[256,2048]{1,0:T(8,128)(2,1)S(1)} collective-permute-done((bf16[256,2048]{1,0:T(8,128)(2,1)S(1)}, bf16[256,2048]{1,0:T(8,128)(2,1)S(1)}, u32[]{:S(2)}, u32[]{:S(2)}) %collective-permute-start.26) | collective-permute-done | bytes 1048608 | tf_op jit(solution)/shard_map/ppermute | solution.py:825
  373.9 4.0 collective-permute-done.31
  380.7 3.1 collective-permute-start.37
  385.0 3.8 collective-permute-done.32
  (366 shorter events, 155.4 us)
Async XLA Ops:
  7.2 125.6 %all-gather.6.cloned.1.call-start = ((), (), s32[]{:S(2)}) async-start(), calls=%async_computation.1 | async-start | bytes 13844480 | tf_op jit(solution)/shard_map/all_gather | solution.py:936
  12.0 380.6 %all-gather.4.cloned.1.call-start = ((), (), s32[]{:S(2)}) async-start(), calls=%async_computation | async-start | bytes 1730560 | tf_op jit(solution)/shard_map/all_gather | solution.py:1064
  38.0 15.8 %collective-permute-start.15 = (bf16[2,4,32,1024]{3,2,1,0:T(8,128)(2,1)S(1)}, bf16[2,4,32,1024]{3,2,1,0:T(8,128)(2,1)S(1)}, u32[]{:S(2)}, u32[]{:S(2)}) collective-permute-start(bf16[2,4,32,1024]{3,2,1,0:T(8,128)(2,1)S(1)} %pad_maximum_fusion.11), channel_id=1, source_target_pairs={{0,48},{16,32},{32,16},{48,0},{64,80},{80,64},{96,112},{112,96},{1... | collective-permute-start | bytes 1572872 | tf_op jit(solution)/shard_map/ppermute | solution.py:825
  45.1 23.2 %collective-permute-start.4 = (bf16[4,4,16,2048]{3,2,1,0:T(8,128)(2,1)S(1)}, bf16[4,4,16,2048]{3,2,1,0:T(8,128)(2,1)S(1)}, u32[]{:S(2)}, u32[]{:S(2)}) collective-permute-start(bf16[4,4,16,2048]{3,2,1,0:T(8,128)(2,1)S(1)} %slice_dynamic-update-slice_fusion.2.refs_1_.refs_3_.refs_2_), channel_id=1, source_target_pairs={{0,16},{16,0},{32,48},{48,32},{64,112},{80,96},{96,80},{112,64},{1... | collective-permute-start | bytes 3145736 | tf_op jit(solution)/shard_map/ppermute | solution.py:825
  46.1 25.2 %collective-permute-start.10 = (bf16[4,4,16,2048]{3,2,1,0:T(8,128)(2,1)S(1)}, bf16[4,4,16,2048]{3,2,1,0:T(8,128)(2,1)S(1)}, u32[]{:S(2)}, u32[]{:S(2)}) collective-permute-start(bf16[4,4,16,2048]{3,2,1,0:T(8,128)(2,1)S(1)} %fusion.33.refs_4_.refs_6_.refs_5_), channel_id=1, source_target_pairs={{0,4},{4,0},{8,12},{12,8},{64,76},{68,72},{72,68},{76,64},{1,5},{5... | collective-permute-start | bytes 3145736 | tf_op jit(solution)/shard_map/ppermute | solution.py:825
  53.9 21.4 %collective-permute-start.16 = (bf16[4,4,32,1024]{3,2,1,0:T(8,128)(2,1)S(1)}, bf16[4,4,32,1024]{3,2,1,0:T(8,128)(2,1)S(1)}, u32[]{:S(2)}, u32[]{:S(2)}) collective-permute-start(bf16[4,4,32,1024]{3,2,1,0:T(8,128)(2,1)S(1)} %slice_dynamic-update-slice_fusion.refs_7_.refs_9_.refs_8_), channel_id=1, source_target_pairs={{0,1},{1,0},{2,3},{3,2},{64,67},{65,66},{66,65},{67,64},{4,5},{5,4... | collective-permute-start | bytes 3145736 | tf_op jit(solution)/shard_map/ppermute | solution.py:825
  70.0 65.2 %collective-permute-start.5 = (bf16[2,4,4,16,2048]{4,3,2,1,0:T(8,128)(2,1)}, bf16[2,4,4,16,2048]{4,3,2,1,0:T(8,128)(2,1)}, u32[]{:S(2)}, u32[]{:S(2)}) collective-permute-start(bf16[2,4,4,16,2048]{4,3,2,1,0:T(8,128)(2,1)} %pad_maximum_fusion.1), channel_id=1, source_target_pairs={{0,48},{16,32},{32,16},{48,0},{64,80},{80,64},{96,112},{112,96},{1... | collective-permute-start | bytes 6291464 | tf_op jit(solution)/shard_map/ppermute | solution.py:825
  72.9 63.4 %collective-permute-start.11 = (bf16[2,4,4,16,2048]{4,3,2,1,0:T(8,128)(2,1)}, bf16[2,4,4,16,2048]{4,3,2,1,0:T(8,128)(2,1)S(1)}, u32[]{:S(2)}, u32[]{:S(2)}) collective-permute-start(bf16[2,4,4,16,2048]{4,3,2,1,0:T(8,128)(2,1)} %pad_maximum_fusion.2), channel_id=1, source_target_pairs={{0,12},{4,8},{8,4},{12,0},{64,68},{68,64},{72,76},{76,72},{1,13},{... | collective-permute-start | bytes 6291464 | tf_op jit(solution)/shard_map/ppermute | solution.py:825
  77.1 59.3 %collective-permute-start.17 = (bf16[2,4,4,32,1024]{4,3,2,1,0:T(8,128)(2,1)}, bf16[2,4,4,32,1024]{4,3,2,1,0:T(8,128)(2,1)}, u32[]{:S(2)}, u32[]{:S(2)}) collective-permute-start(bf16[2,4,4,32,1024]{4,3,2,1,0:T(8,128)(2,1)} %pad_maximum_fusion.3), channel_id=1, source_target_pairs={{0,3},{1,2},{2,1},{3,0},{64,65},{65,64},{66,67},{67,66},{4,7},{5,6... | collective-permute-start | bytes 6291464 | tf_op jit(solution)/shard_map/ppermute | solution.py:825
  191.5 31.4 %collective-permute-start.19 = (bf16[256,1024]{1,0:T(8,128)(2,1)}, bf16[256,1024]{1,0:T(8,128)(2,1)}, u32[]{:S(2)}, u32[]{:S(2)}) collective-permute-start(bf16[256,1024]{1,0:T(8,128)(2,1)} %get-tuple-element.127.refs_7_), channel_id=1, source_target_pairs={{64,0},{65,1},{66,2},{67,3},{68,4},{69,5},{70,6},{71,7},{72,8},{73... | collective-permute-start | bytes 1572872 | tf_op jit(solution)/shard_map/ppermute | solution.py:979
  242.1 33.4 %collective-permute-start.20 = (bf16[1024,1024]{1,0:T(8,128)(2,1)}, bf16[1024,1024]{1,0:T(8,128)(2,1)}, u32[]{:S(2)}, u32[]{:S(2)}) collective-permute-start(bf16[1024,1024]{1,0:T(8,128)(2,1)} %convolution_convert_fusion.5), channel_id=1, source_target_pairs={{0,1},{1,0},{2,3},{3,2},{64,67},{65,66},{66,65},{67,64},{4,5},{5,4... | collective-permute-start | bytes 6291464 | tf_op jit(solution)/shard_map/ppermute | solution.py:825
  243.6 32.0 %collective-permute-start.21 = (bf16[512,2048]{1,0:T(8,128)(2,1)}, bf16[512,2048]{1,0:T(8,128)(2,1)}, u32[]{:S(2)}, u32[]{:S(2)}) collective-permute-start(bf16[512,2048]{1,0:T(8,128)(2,1)} %convolution_convert_fusion.3), channel_id=1, source_target_pairs={{0,16},{16,0},{32,48},{48,32},{64,112},{80,96},{96,80},{112,64},{1... | collective-permute-start | bytes 6291464 | tf_op jit(solution)/shard_map/ppermute | solution.py:825
  245.1 30.5 %collective-permute-start.22 = (bf16[512,2048]{1,0:T(8,128)(2,1)}, bf16[512,2048]{1,0:T(8,128)(2,1)}, u32[]{:S(2)}, u32[]{:S(2)}) collective-permute-start(bf16[512,2048]{1,0:T(8,128)(2,1)} %convolution_convert_fusion.2), channel_id=1, source_target_pairs={{0,4},{4,0},{8,12},{12,8},{64,76},{68,72},{72,68},{76,64},{1,5},{5... | collective-permute-start | bytes 6291464 | tf_op jit(solution)/shard_map/ppermute | solution.py:825
  275.6 34.4 %collective-permute-start.24 = (bf16[1024,1024]{1,0:T(8,128)(2,1)}, bf16[1024,1024]{1,0:T(8,128)(2,1)}, u32[]{:S(2)}, u32[]{:S(2)}) collective-permute-start(bf16[1024,1024]{1,0:T(8,128)(2,1)} %convolution_convert_fusion.4), channel_id=1, source_target_pairs={{0,3},{1,2},{2,1},{3,0},{64,65},{65,64},{66,67},{67,66},{4,7},{5,6... | collective-permute-start | bytes 6291464 | tf_op jit(solution)/shard_map/ppermute | solution.py:825
  285.8 20.9 %collective-permute-start.28 = (bf16[256,2048]{1,0:T(8,128)(2,1)}, bf16[256,2048]{1,0:T(8,128)(2,1)}, u32[]{:S(2)}, u32[]{:S(2)}) collective-permute-start(bf16[256,2048]{1,0:T(8,128)(2,1)} %fusion), channel_id=1, source_target_pairs={{0,48},{16,32},{32,16},{48,0},{64,80},{80,64},{96,112},{112,96},{1... | collective-permute-start | bytes 3145736 | tf_op jit(solution)/shard_map/ppermute | solution.py:825
  288.2 37.5 %collective-permute-start.23 = (bf16[512,1024]{1,0:T(8,128)(2,1)}, bf16[512,1024]{1,0:T(8,128)(2,1)}, u32[]{:S(2)}, u32[]{:S(2)}) collective-permute-start(bf16[512,1024]{1,0:T(8,128)(2,1)} %add_convert_fusion.9), channel_id=1, source_target_pairs={{0,3},{1,2},{2,1},{3,0},{64,65},{65,64},{66,67},{67,66},{4,7},{5,6... | collective-permute-start | bytes 3145736 | tf_op jit(solution)/shard_map/ppermute | solution.py:825
  289.5 43.7 %collective-permute-start.29 = (bf16[512,2048]{1,0:T(8,128)(2,1)}, bf16[512,2048]{1,0:T(8,128)(2,1)}, u32[]{:S(2)}, u32[]{:S(2)}) collective-permute-start(bf16[512,2048]{1,0:T(8,128)(2,1)} %convolution_convert_fusion.1), channel_id=1, source_target_pairs={{0,48},{16,32},{32,16},{48,0},{64,80},{80,64},{96,112},{112,96},{1... | collective-permute-start | bytes 6291464 | tf_op jit(solution)/shard_map/ppermute | solution.py:825
  290.6 44.4 %collective-permute-start.34 = (bf16[512,2176]{1,0:T(8,128)(2,1)}, bf16[512,2176]{1,0:T(8,128)(2,1)}, u32[]{:S(2)}, u32[]{:S(2)}) collective-permute-start(bf16[512,2176]{1,0:T(8,128)(2,1)} %convolution_convert_fusion), channel_id=1, source_target_pairs={{0,12},{4,8},{8,4},{12,0},{64,68},{68,64},{72,76},{76,72},{1,13},{... | collective-permute-start | bytes 6684680 | tf_op jit(solution)/shard_map/ppermute | solution.py:825
  306.7 24.4 %collective-permute-start.33 = (bf16[256,2048]{1,0:T(8,128)(2,1)S(1)}, bf16[256,2048]{1,0:T(8,128)(2,1)S(1)}, u32[]{:S(2)}, u32[]{:S(2)}) collective-permute-start(bf16[256,2048]{1,0:T(8,128)(2,1)S(1)} %copy-done.21), channel_id=1, source_target_pairs={{0,12},{4,8},{8,4},{12,0},{64,68},{68,64},{72,76},{76,72},{1,13},{... | collective-permute-start | bytes 3145736 | tf_op jit(solution)/shard_map/ppermute | solution.py:825
  311.8 26.2 %collective-permute-start.25 = (bf16[512,1024]{1,0:T(8,128)(2,1)S(1)}, bf16[512,1024]{1,0:T(8,128)(2,1)S(1)}, u32[]{:S(2)}, u32[]{:S(2)}) collective-permute-start(bf16[512,1024]{1,0:T(8,128)(2,1)S(1)} %add_convert_fusion.7), channel_id=1, source_target_pairs={{0,1},{1,0},{2,3},{3,2},{64,67},{65,66},{66,65},{67,64},{4,5},{5,4... | collective-permute-start | bytes 3145736 | tf_op jit(solution)/shard_map/ppermute | solution.py:825
  336.7 17.4 %collective-permute-start.35 = (bf16[256,2176]{1,0:T(8,128)(2,1)S(1)}, bf16[256,2176]{1,0:T(8,128)(2,1)S(1)}, u32[]{:S(2)}, u32[]{:S(2)}) collective-permute-start(bf16[256,2176]{1,0:T(8,128)(2,1)S(1)} %add_convert_fusion.1), channel_id=1, source_target_pairs={{0,4},{4,0},{8,12},{12,8},{64,76},{68,72},{72,68},{76,64},{1,5},{5... | collective-permute-start | bytes 3342344 | tf_op jit(solution)/shard_map/ppermute | solution.py:825
  340.3 31.3 %collective-permute-start.26 = (bf16[256,2048]{1,0:T(8,128)(2,1)S(1)}, bf16[256,2048]{1,0:T(8,128)(2,1)S(1)}, u32[]{:S(2)}, u32[]{:S(2)}) collective-permute-start(bf16[256,2048]{1,0:T(8,128)(2,1)S(1)} %bitcast.290), channel_id=1, source_target_pairs={{0,16},{16,0},{32,48},{48,32},{64,112},{80,96},{96,80},{112,64},{1... | collective-permute-start | bytes 3145736 | tf_op jit(solution)/shard_map/ppermute | solution.py:825
  352.9 25.1 %collective-permute-start.31 = (bf16[128,4096]{1,0:T(8,128)(2,1)S(1)}, bf16[128,4096]{1,0:T(8,128)(2,1)S(1)}, u32[]{:S(2)}, u32[]{:S(2)}) collective-permute-start(bf16[128,4096]{1,0:T(8,128)(2,1)S(1)} %bitcast.291), channel_id=1, source_target_pairs={{0,4},{4,0},{8,12},{12,8},{64,76},{68,72},{72,68},{76,64},{1,5},{5... | collective-permute-start | bytes 3145736 | tf_op jit(solution)/shard_map/ppermute | solution.py:825
  356.3 24.3 %collective-permute-start.36 = (bf16[128,4224]{1,0:T(8,128)(2,1)S(1)}, bf16[128,4224]{1,0:T(8,128)(2,1)S(1)}, u32[]{:S(2)}, u32[]{:S(2)}) collective-permute-start(bf16[128,4224]{1,0:T(8,128)(2,1)S(1)} %bitcast.286), channel_id=1, source_target_pairs={{0,1},{1,0},{2,3},{3,2},{64,67},{65,66},{66,65},{67,64},{4,5},{5,4... | collective-permute-start | bytes 3244040 | tf_op jit(solution)/shard_map/ppermute | solution.py:825
  (85 other events, 660.3 us)
Sparse Core Ops, SparseCore 0:
  12.1 120.6 all-gather.5
  306.8 63.2 all-gather.3

commit v10 on v9

--- a/solution.py
+++ b/solution.py
@@ -1015,10 +1015,10 @@
             orders,
         )
     ]
-    mix_sents = [first_sent(p, axis, 1) for p, axis in zip(mix_products, axes)]
+    mix_sents = [first_sent(p, axis, 0) for p, axis in zip(mix_products, axes)]
     pending = lax.optimization_barrier((*gots, *mix_sents))
     gots, mix_sents = pending[:3], pending[3:]
-    mix_gots = [first_got(sent, axis, 1) for sent, axis in zip(mix_sents, axes)]
+    mix_gots = [first_got(sent, axis, 0) for sent, axis in zip(mix_sents, axes)]
     handed = [handed_on(p, got, axis, 0) for p, got, axis in zip(products, gots, axes)]
     last_middle, *pending = lax.optimization_barrier(
         (grad_middle, grad_low, grad_gate, grad_upper, grad_branch, grad_cat, *handed)
@@ -1041,7 +1041,7 @@
         for p, got, hand, axis in zip(products, gots, handed, axes)
     ]
     mix_parts = [
-        totalled(p, got, handed_on(p, got, axis, 1), axis, 1)
+        totalled(p, got, handed_on(p, got, axis, 0), axis, 0)
         for p, got, axis in zip(mix_products, mix_gots, axes)
     ]
     grad_start, unused, input_grad = run_input_backward(

time: 424 us -> 433 us (1.021)
  starting transfers between devices: 64 us -> 69.6 us
    ppermute x42, starting transfers between devices: 60.9 us -> 66.5 us  [exchange(): return lax.ppermute(array, ('section', axis), pairs)]
  transfers between devices with their start and end apart: 46 -> 46, of which waited for: 20 -> 22; matrix products, arithmetic and copies ran while one was open for 18% -> 18% of each run, Pallas kernels for 6% -> 6%
where the time goes in v10:
time: 433 us; the launch traced here: 426 us
  waiting for transfers between devices  161 us (37%)
  Pallas kernels  88.4 us (20%)
  starting transfers between devices  69.6 us (16%)
  matrix products  37.1 us (9%)
  other arithmetic  29 us (7%)
  local copies, waits for them, and re-layouts  26 us (6%)
  between operations  15.5 us (4%)
    ppermute x42, waiting for transfers between devices, exchange(): return lax.ppermute(array, ('section', axis), pairs)  89.6 us
    ppermute x42, starting transfers between devices, exchange(): return lax.ppermute(array, ('section', axis), pairs)  66.5 us
    all_gather x1, waiting for transfers between devices, on_device(): packed = lax.all_gather(own, DP, axis=0, tiled=False)  48.6 us
    pallas_call x2, Pallas kernels, run_forward(): pl.pallas_call(functools.partial(forward_kernel, unpack), out_shape=extra...  39.1 us
    dot_general x18, matrix products, dot(): return jnp.dot(left, right, preferred_element_type=F32)  37.1 us
    ppermute x1, waiting for transfers between devices, on_device(): top_low = lax.ppermute(low_top, 'section', [(1, 0)])  22.4 us
    pallas_call x2, Pallas kernels, run_mix_backward(): pl.pallas_call(functools.partial(mix_backward_kernel, len(earlier)), out_...  19.7 us
    pallas_call x2, Pallas kernels, run_input_backward(): pl.pallas_call(functools.partial(input_backward_kernel, len(earlier)), ou...  14.8 us
  transfers between devices with their start and end apart: 46, of which 22 were waited for; matrix products, arithmetic and copies ran while one was open for 18% of the time, Pallas kernels for 6%

profile of v10, /device:TPU:0, one launch (start us, length us, event | category | flops | bytes accessed | tf_op | source)
XLA Modules:
  0.0 426.2 jit_solution(14094472020487669022)
XLA Ops:
  23.5 3.3 collective-permute-start.13
  40.4 4.6 %collective-permute-done.3 = bf16[2,4,16,2048]{3,2,1,0:T(8,128)(2,1)S(1)} collective-permute-done((bf16[2,4,16,2048]{3,2,1,0:T(8,128)(2,1)S(1)}, bf16[2,4,16,2048]{3,2,1,0:T(8,128)(2,1)S(1)}, u32[]{:S(2)}, u32[]{:S(2)}) %collective-permute-start.3) | collective-permute-done | bytes 524320 | tf_op jit(solution)/shard_map/ppermute | solution.py:825
  46.9 6.9 %collective-permute-done.15 = bf16[2,4,32,1024]{3,2,1,0:T(8,128)(2,1)S(1)} collective-permute-done((bf16[2,4,32,1024]{3,2,1,0:T(8,128)(2,1)S(1)}, bf16[2,4,32,1024]{3,2,1,0:T(8,128)(2,1)S(1)}, u32[]{:S(2)}, u32[]{:S(2)}) %collective-permute-start.15) | collective-permute-done | bytes 524320 | tf_op jit(solution)/shard_map/ppermute | solution.py:825
  54.0 14.3 %collective-permute-done.4.refs_2_.refs_4_.refs_3_ = bf16[4,4,16,2048]{3,2,1,0:T(8,128)(2,1)S(1)} collective-permute-done((bf16[4,4,16,2048]{3,2,1,0:T(8,128)(2,1)S(1)}, bf16[4,4,16,2048]{3,2,1,0:T(8,128)(2,1)S(1)}, u32[]{:S(2)}, u32[]{:S(2)}) %collective-permute-start.4) | collective-permute-done | bytes 1048608 | tf_op jit(solution)/shard_map/ppermute | solution.py:825
  84.2 48.6 %all-gather.6.cloned.1.call-done = bf16[6656,1024]{1,0:T(8,128)(2,1)} async-done(((bf16[104,1024]{1,0:T(8,128)(2,1)}), bf16[6656,1024]{1,0:T(8,128)(2,1)}) %all-gather.6.cloned.1.call-update) | async-done | bytes 13631504 | tf_op jit(solution)/shard_map/all_gather | solution.py:936
  137.7 19.7 %forward.2 = (bf16[1536,1024]{1,0:T(8,128)(2,1)}, bf16[512,1024]{1,0:T(8,128)(2,1)}, bf16[256,1024]{1,0:T(8,128)(2,1)}, bf16[256,1024]{1,0:T(8,128)(2,1)}, f32[2...) custom-call(bf16[256,1024]{1,0:T(8,128)(2,1)} %bitcast.281, ...), custom_call_target="tpu_custom_call" | custom-call | flops 6451200000 | bytes 40000000 | tf_op jit(solution)/shard_map/forward/pallas_call | solution.py:608
  161.9 19.4 %forward.3 = (bf16[256,1024]{1,0:T(8,128)(2,1)}, bf16[256,1024]{1,0:T(8,128)(2,1)}, f32[256,4224]{1,0:T(8,128)}, f32[256,1536]{1,0:T(8,128)}, bf16[256,1536]{1,0...) custom-call(bf16[256,1024]{1,0:T(8,128)(2,1)} %copy-done.19, ...), custom_call_target="tpu_custom_call" | custom-call | flops 6451200000 | bytes 40000000 | tf_op jit(solution)/shard_map/forward/pallas_call | solution.py:608
  184.7 6.7 %input_backward.2 = (f32[256,1024]{1,0:T(8,128)}, bf16[256,1024]{1,0:T(8,128)(2,1)}, f32[1,1024]{1,0:T(1,128)}) custom-call(s32[1]{0:T(128)} %bitcast.54.active, bf16[256,4224]{1,0:T(8,128)(2,1)} %get-tuple-element.120.refs_0_.refs_15_, f32[256,1024]{1,0:T(8,128)} %get-tuple-element.117.refs_0_.refs_1_.refs_17_, bf16[256,1024]{1,0:T(8,128)(2,1)} %copy-done.19, ...), custom_call_target="tpu_custom_call" | custom-call | flops 2150400000 | bytes 13000000 | tf_op jit(solution)/shard_map/input_backward/pallas_call | solution.py:707
  203.6 22.4 %collective-permute-done.19.refs_0_ = bf16[256,1024]{1,0:T(8,128)(2,1)S(1)} collective-permute-done((bf16[256,1024]{1,0:T(8,128)(2,1)}, bf16[256,1024]{1,0:T(8,128)(2,1)S(1)}, u32[]{:S(2)}, u32[]{:S(2)}) %collective-permute-start.19) | collective-permute-done | bytes 524320 | tf_op jit(solution)/shard_map/ppermute | solution.py:979
  226.8 11.6 %feed_backward.3 = (bf16[256,2048]{1,0:T(8,128)(2,1)}, bf16[256,2048]{1,0:T(8,128)(2,1)}, f32[256,1024]{1,0:T(8,128)}, f32[1,1024]{1,0:T(1,128)}) custom-call(s32[1]{0:T(128)S(6)} %sub.29.active, bf16[256,1024]{1,0:T(8,128)(2,1)} %copy-done.18, ...), custom_call_target="tpu_custom_call", output_to_operand_aliasing={{0}: (16, {}), {1}: (17, {}), {2}: (18, {}), {3}: (19, {})} | custom-call | flops 3225600000 | bytes 22000000 | tf_op jit(solution)/shard_map/feed_backward/pallas_call | solution.py:639
  249.4 18.0 %mix_backward.3 = (bf16[256,1024]{1,0:T(8,128)(2,1)}, bf16[256,4224]{1,0:T(8,128)(2,1)}, f32[4,1792]{1,0:T(4,128)}, f32[1,1792]{1,0:T(1,128)}, f32[1,128]{1,0:T(...) custom-call(s32[1]{0:T(128)S(6)} %sub.29.active, ...), custom_call_target="tpu_custom_call", output_to_operand_aliasing={{0}: (15, {}), {1}: (16, {}), {2}: (17, {}), {3}: (18, {}),... | custom-call | flops 1075200000 | bytes 14000000 | tf_op jit(solution)/shard_map/mix_backward/pallas_call | solution.py:675
  270.4 3.3 convolution_convert_fusion.4
  298.3 8.1 %input_backward.3 = (f32[256,1024]{1,0:T(8,128)}, bf16[256,1024]{1,0:T(8,128)(2,1)}, f32[1,1024]{1,0:T(1,128)}) custom-call(s32[1]{0:T(128)S(6)} %sub.29.active, bf16[256,4224]{1,0:T(8,128)(2,1)} %get-tuple-element.178.refs_0_, f32[256,1024]{1,0:T(8,128)} %get-tuple-element.168.refs_0_.refs_1_, ...), custom_call_target="tpu_custom_call", output_to_operand_aliasing={{0}: (7, {}), {1}: (8, {}), {2}: (9, {})} | custom-call | flops 2150400000 | bytes 13000000 | tf_op jit(solution)/shard_map/input_backward/pallas_call | solution.py:707
  307.9 6.4 %collective-permute-done.28 = bf16[256,2048]{1,0:T(8,128)(2,1)} collective-permute-done((bf16[256,2048]{1,0:T(8,128)(2,1)}, bf16[256,2048]{1,0:T(8,128)(2,1)}, u32[]{:S(2)}, u32[]{:S(2)}) %collective-permute-start.28) | collective-permute-done | bytes 1048608 | tf_op jit(solution)/shard_map/ppermute | solution.py:825
  320.1 5.2 %collective-permute-done.24 = bf16[1024,1024]{1,0:T(8,128)(2,1)} collective-permute-done((bf16[1024,1024]{1,0:T(8,128)(2,1)}, bf16[1024,1024]{1,0:T(8,128)(2,1)}, u32[]{:S(2)}, u32[]{:S(2)}) %collective-permute-start.24) | collective-permute-done | bytes 2097184 | tf_op jit(solution)/shard_map/ppermute | solution.py:825
  345.9 11.2 %collective-permute-done.30 = bf16[256,2048]{1,0:T(8,128)(2,1)S(1)} collective-permute-done((bf16[256,2048]{1,0:T(8,128)(2,1)S(1)}, bf16[256,2048]{1,0:T(8,128)(2,1)S(1)}, u32[]{:S(2)}, u32[]{:S(2)}) %collective-permute-start.30) | collective-permute-done | bytes 1048608 | tf_op jit(solution)/shard_map/ppermute | solution.py:825
  359.9 12.4 %collective-permute-done.35 = bf16[256,2176]{1,0:T(8,128)(2,1)S(1)} collective-permute-done((bf16[256,2176]{1,0:T(8,128)(2,1)S(1)}, bf16[256,2176]{1,0:T(8,128)(2,1)S(1)}, u32[]{:S(2)}, u32[]{:S(2)}) %collective-permute-start.35) | collective-permute-done | bytes 1114144 | tf_op jit(solution)/shard_map/ppermute | solution.py:825
  375.3 4.0 collective-permute-done.31
  379.5 5.6 %collective-permute-start.32 = (bf16[64,4096]{1,0:T(8,128)(2,1)S(1)}, bf16[64,4096]{1,0:T(8,128)(2,1)S(1)}, u32[]{:S(2)}, u32[]{:S(2)}) collective-permute-start(bf16[64,4096]{1,0:T(8,128)(2,1)S(1)} %fusion.6), channel_id=1, source_target_pairs={{0,12},{4,8},{8,4},{12,0},{64,68},{68,64},{72,76},{76,72},{1,13},{... | collective-permute-start | bytes 1572872 | tf_op jit(solution)/shard_map/ppermute | solution.py:825
  385.2 6.5 %collective-permute-done.36 = bf16[128,4224]{1,0:T(8,128)(2,1)S(1)} collective-permute-done((bf16[128,4224]{1,0:T(8,128)(2,1)S(1)}, bf16[128,4224]{1,0:T(8,128)(2,1)S(1)}, u32[]{:S(2)}, u32[]{:S(2)}) %collective-permute-start.36) | collective-permute-done | bytes 1081376 | tf_op jit(solution)/shard_map/ppermute | solution.py:825
  391.9 3.3 collective-permute-start.37
  397.7 4.8 %collective-permute-done.37 = bf16[64,4224]{1,0:T(8,128)(2,1)S(1)} collective-permute-done((bf16[64,4224]{1,0:T(8,128)(2,1)S(1)}, bf16[64,4224]{1,0:T(8,128)(2,1)S(1)}, u32[]{:S(2)}, u32[]{:S(2)}) %collective-permute-start.37) | collective-permute-done | bytes 540704 | tf_op jit(solution)/shard_map/ppermute | solution.py:825
  408.1 3.2 collective-permute-start.42
  414.4 3.3 collective-permute-done.43.up_last
  (360 shorter events, 157.7 us)
Async XLA Ops:
  7.2 125.5 %all-gather.6.cloned.1.call-start = ((), (), s32[]{:S(2)}) async-start(), calls=%async_computation.1 | async-start | bytes 13844480 | tf_op jit(solution)/shard_map/all_gather | solution.py:936
  12.0 391.0 %all-gather.4.cloned.1.call-start = ((), (), s32[]{:S(2)}) async-start(), calls=%async_computation | async-start | bytes 1730560 | tf_op jit(solution)/shard_map/all_gather | solution.py:1064
  45.1 23.2 %collective-permute-start.4 = (bf16[4,4,16,2048]{3,2,1,0:T(8,128)(2,1)S(1)}, bf16[4,4,16,2048]{3,2,1,0:T(8,128)(2,1)S(1)}, u32[]{:S(2)}, u32[]{:S(2)}) collective-permute-start(bf16[4,4,16,2048]{3,2,1,0:T(8,128)(2,1)S(1)} %slice_dynamic-update-slice_fusion.2.refs_1_.refs_3_.refs_2_), channel_id=1, source_target_pairs={{0,16},{16,0},{32,48},{48,32},{64,112},{80,96},{96,80},{112,64},{1... | collective-permute-start | bytes 3145736 | tf_op jit(solution)/shard_map/ppermute | solution.py:825
  46.1 25.2 %collective-permute-start.10 = (bf16[4,4,16,2048]{3,2,1,0:T(8,128)(2,1)S(1)}, bf16[4,4,16,2048]{3,2,1,0:T(8,128)(2,1)S(1)}, u32[]{:S(2)}, u32[]{:S(2)}) collective-permute-start(bf16[4,4,16,2048]{3,2,1,0:T(8,128)(2,1)S(1)} %fusion.33.refs_4_.refs_6_.refs_5_), channel_id=1, source_target_pairs={{0,4},{4,0},{8,12},{12,8},{64,76},{68,72},{72,68},{76,64},{1,5},{5... | collective-permute-start | bytes 3145736 | tf_op jit(solution)/shard_map/ppermute | solution.py:825
  53.9 21.5 %collective-permute-start.16 = (bf16[4,4,32,1024]{3,2,1,0:T(8,128)(2,1)S(1)}, bf16[4,4,32,1024]{3,2,1,0:T(8,128)(2,1)S(1)}, u32[]{:S(2)}, u32[]{:S(2)}) collective-permute-start(bf16[4,4,32,1024]{3,2,1,0:T(8,128)(2,1)S(1)} %slice_dynamic-update-slice_fusion.refs_7_.refs_9_.refs_8_), channel_id=1, source_target_pairs={{0,1},{1,0},{2,3},{3,2},{64,67},{65,66},{66,65},{67,64},{4,5},{5,4... | collective-permute-start | bytes 3145736 | tf_op jit(solution)/shard_map/ppermute | solution.py:825
  70.0 65.1 %collective-permute-start.5 = (bf16[2,4,4,16,2048]{4,3,2,1,0:T(8,128)(2,1)}, bf16[2,4,4,16,2048]{4,3,2,1,0:T(8,128)(2,1)}, u32[]{:S(2)}, u32[]{:S(2)}) collective-permute-start(bf16[2,4,4,16,2048]{4,3,2,1,0:T(8,128)(2,1)} %pad_maximum_fusion.1), channel_id=1, source_target_pairs={{0,48},{16,32},{32,16},{48,0},{64,80},{80,64},{96,112},{112,96},{1... | collective-permute-start | bytes 6291464 | tf_op jit(solution)/shard_map/ppermute | solution.py:825
  73.0 63.4 %collective-permute-start.11 = (bf16[2,4,4,16,2048]{4,3,2,1,0:T(8,128)(2,1)}, bf16[2,4,4,16,2048]{4,3,2,1,0:T(8,128)(2,1)S(1)}, u32[]{:S(2)}, u32[]{:S(2)}) collective-permute-start(bf16[2,4,4,16,2048]{4,3,2,1,0:T(8,128)(2,1)} %pad_maximum_fusion.2), channel_id=1, source_target_pairs={{0,12},{4,8},{8,4},{12,0},{64,68},{68,64},{72,76},{76,72},{1,13},{... | collective-permute-start | bytes 6291464 | tf_op jit(solution)/shard_map/ppermute | solution.py:825
  77.1 59.3 %collective-permute-start.17 = (bf16[2,4,4,32,1024]{4,3,2,1,0:T(8,128)(2,1)}, bf16[2,4,4,32,1024]{4,3,2,1,0:T(8,128)(2,1)}, u32[]{:S(2)}, u32[]{:S(2)}) collective-permute-start(bf16[2,4,4,32,1024]{4,3,2,1,0:T(8,128)(2,1)} %pad_maximum_fusion.3), channel_id=1, source_target_pairs={{0,3},{1,2},{2,1},{3,0},{64,65},{65,64},{66,67},{67,66},{4,7},{5,6... | collective-permute-start | bytes 6291464 | tf_op jit(solution)/shard_map/ppermute | solution.py:825
  194.7 31.3 %collective-permute-start.19 = (bf16[256,1024]{1,0:T(8,128)(2,1)}, bf16[256,1024]{1,0:T(8,128)(2,1)S(1)}, u32[]{:S(2)}, u32[]{:S(2)}) collective-permute-start(bf16[256,1024]{1,0:T(8,128)(2,1)} %get-tuple-element.127.refs_7_), channel_id=1, source_target_pairs={{64,0},{65,1},{66,2},{67,3},{68,4},{69,5},{70,6},{71,7},{72,8},{73... | collective-permute-start | bytes 1572872 | tf_op jit(solution)/shard_map/ppermute | solution.py:979
  244.6 33.3 %collective-permute-start.20 = (bf16[1024,1024]{1,0:T(8,128)(2,1)}, bf16[1024,1024]{1,0:T(8,128)(2,1)}, u32[]{:S(2)}, u32[]{:S(2)}) collective-permute-start(bf16[1024,1024]{1,0:T(8,128)(2,1)} %convolution_convert_fusion.5), channel_id=1, source_target_pairs={{0,1},{1,0},{2,3},{3,2},{64,67},{65,66},{66,65},{67,64},{4,5},{5,4... | collective-permute-start | bytes 6291464 | tf_op jit(solution)/shard_map/ppermute | solution.py:825
  246.1 31.8 %collective-permute-start.21 = (bf16[512,2048]{1,0:T(8,128)(2,1)}, bf16[512,2048]{1,0:T(8,128)(2,1)}, u32[]{:S(2)}, u32[]{:S(2)}) collective-permute-start(bf16[512,2048]{1,0:T(8,128)(2,1)} %convolution_convert_fusion.3), channel_id=1, source_target_pairs={{0,16},{16,0},{32,48},{48,32},{64,112},{80,96},{96,80},{112,64},{1... | collective-permute-start | bytes 6291464 | tf_op jit(solution)/shard_map/ppermute | solution.py:825
  247.4 30.5 %collective-permute-start.22 = (bf16[512,2048]{1,0:T(8,128)(2,1)}, bf16[512,2048]{1,0:T(8,128)(2,1)}, u32[]{:S(2)}, u32[]{:S(2)}) collective-permute-start(bf16[512,2048]{1,0:T(8,128)(2,1)} %convolution_convert_fusion.2), channel_id=1, source_target_pairs={{0,4},{4,0},{8,12},{12,8},{64,76},{68,72},{72,68},{76,64},{1,5},{5... | collective-permute-start | bytes 6291464 | tf_op jit(solution)/shard_map/ppermute | solution.py:825
  277.9 47.3 %collective-permute-start.24 = (bf16[1024,1024]{1,0:T(8,128)(2,1)}, bf16[1024,1024]{1,0:T(8,128)(2,1)}, u32[]{:S(2)}, u32[]{:S(2)}) collective-permute-start(bf16[1024,1024]{1,0:T(8,128)(2,1)} %convolution_convert_fusion.4), channel_id=1, source_target_pairs={{0,1},{1,0},{2,3},{3,2},{64,67},{65,66},{66,65},{67,64},{4,5},{5,4... | collective-permute-start | bytes 6291464 | tf_op jit(solution)/shard_map/ppermute | solution.py:825
  286.7 27.6 %collective-permute-start.28 = (bf16[256,2048]{1,0:T(8,128)(2,1)}, bf16[256,2048]{1,0:T(8,128)(2,1)}, u32[]{:S(2)}, u32[]{:S(2)}) collective-permute-start(bf16[256,2048]{1,0:T(8,128)(2,1)} %fusion), channel_id=1, source_target_pairs={{0,48},{16,32},{32,16},{48,0},{64,80},{80,64},{96,112},{112,96},{1... | collective-permute-start | bytes 3145736 | tf_op jit(solution)/shard_map/ppermute | solution.py:825
  289.1 40.0 %collective-permute-start.23 = (bf16[512,1024]{1,0:T(8,128)(2,1)}, bf16[512,1024]{1,0:T(8,128)(2,1)}, u32[]{:S(2)}, u32[]{:S(2)}) collective-permute-start(bf16[512,1024]{1,0:T(8,128)(2,1)} %add_convert_fusion.9), channel_id=1, source_target_pairs={{0,3},{1,2},{2,1},{3,0},{64,65},{65,64},{66,67},{67,66},{4,7},{5,6... | collective-permute-start | bytes 3145736 | tf_op jit(solution)/shard_map/ppermute | solution.py:825
  291.8 41.4 %collective-permute-start.29 = (bf16[512,2048]{1,0:T(8,128)(2,1)}, bf16[512,2048]{1,0:T(8,128)(2,1)}, u32[]{:S(2)}, u32[]{:S(2)}) collective-permute-start(bf16[512,2048]{1,0:T(8,128)(2,1)} %convolution_convert_fusion.1), channel_id=1, source_target_pairs={{0,16},{16,0},{32,48},{48,32},{64,112},{80,96},{96,80},{112,64},{1... | collective-permute-start | bytes 6291464 | tf_op jit(solution)/shard_map/ppermute | solution.py:825
  292.4 45.6 %collective-permute-start.34 = (bf16[512,2176]{1,0:T(8,128)(2,1)}, bf16[512,2176]{1,0:T(8,128)(2,1)}, u32[]{:S(2)}, u32[]{:S(2)}) collective-permute-start(bf16[512,2176]{1,0:T(8,128)(2,1)} %convolution_convert_fusion), channel_id=1, source_target_pairs={{0,4},{4,0},{8,12},{12,8},{64,76},{68,72},{72,68},{76,64},{1,5},{5... | collective-permute-start | bytes 6684680 | tf_op jit(solution)/shard_map/ppermute | solution.py:825
  335.0 22.1 %collective-permute-start.30 = (bf16[256,2048]{1,0:T(8,128)(2,1)S(1)}, bf16[256,2048]{1,0:T(8,128)(2,1)S(1)}, u32[]{:S(2)}, u32[]{:S(2)}) collective-permute-start(bf16[256,2048]{1,0:T(8,128)(2,1)S(1)} %add_convert_fusion.4), channel_id=1, source_target_pairs={{0,48},{16,32},{32,16},{48,0},{64,80},{80,64},{96,112},{112,96},{1... | collective-permute-start | bytes 3145736 | tf_op jit(solution)/shard_map/ppermute | solution.py:825
  339.8 32.5 %collective-permute-start.35 = (bf16[256,2176]{1,0:T(8,128)(2,1)S(1)}, bf16[256,2176]{1,0:T(8,128)(2,1)S(1)}, u32[]{:S(2)}, u32[]{:S(2)}) collective-permute-start(bf16[256,2176]{1,0:T(8,128)(2,1)S(1)} %add_convert_fusion.1), channel_id=1, source_target_pairs={{0,12},{4,8},{8,4},{12,0},{64,68},{68,64},{72,76},{76,72},{1,13},{... | collective-permute-start | bytes 3342344 | tf_op jit(solution)/shard_map/ppermute | solution.py:825
  345.8 28.7 %collective-permute-start.26 = (bf16[256,2048]{1,0:T(8,128)(2,1)S(1)}, bf16[256,2048]{1,0:T(8,128)(2,1)S(1)}, u32[]{:S(2)}, u32[]{:S(2)}) collective-permute-start(bf16[256,2048]{1,0:T(8,128)(2,1)S(1)} %bitcast.289), channel_id=1, source_target_pairs={{0,16},{16,0},{32,48},{48,32},{64,112},{80,96},{96,80},{112,64},{1... | collective-permute-start | bytes 3145736 | tf_op jit(solution)/shard_map/ppermute | solution.py:825
  359.4 20.0 %collective-permute-start.31 = (bf16[128,4096]{1,0:T(8,128)(2,1)S(1)}, bf16[128,4096]{1,0:T(8,128)(2,1)S(1)}, u32[]{:S(2)}, u32[]{:S(2)}) collective-permute-start(bf16[128,4096]{1,0:T(8,128)(2,1)S(1)} %bitcast.290), channel_id=1, source_target_pairs={{0,4},{4,0},{8,12},{12,8},{64,76},{68,72},{72,68},{76,64},{1,5},{5... | collective-permute-start | bytes 3145736 | tf_op jit(solution)/shard_map/ppermute | solution.py:825
  374.4 17.3 %collective-permute-start.36 = (bf16[128,4224]{1,0:T(8,128)(2,1)S(1)}, bf16[128,4224]{1,0:T(8,128)(2,1)S(1)}, u32[]{:S(2)}, u32[]{:S(2)}) collective-permute-start(bf16[128,4224]{1,0:T(8,128)(2,1)S(1)} %bitcast.286), channel_id=1, source_target_pairs={{0,1},{1,0},{2,3},{3,2},{64,67},{65,66},{66,65},{67,64},{4,5},{5,4... | collective-permute-start | bytes 3244040 | tf_op jit(solution)/shard_map/ppermute | solution.py:825
  374.7 20.5 %collective-permute-start.27 = (bf16[128,2048]{1,0:T(8,128)(2,1)S(1)}, bf16[128,2048]{1,0:T(8,128)(2,1)S(1)}, u32[]{:S(2)}, u32[]{:S(2)}) collective-permute-start(bf16[128,2048]{1,0:T(8,128)(2,1)S(1)} %fusion.9), channel_id=1, source_target_pairs={{0,48},{16,32},{32,16},{48,0},{64,80},{80,64},{96,112},{112,96},{1... | collective-permute-start | bytes 1572872 | tf_op jit(solution)/shard_map/ppermute | solution.py:825
  379.5 17.8 %collective-permute-start.32 = (bf16[64,4096]{1,0:T(8,128)(2,1)S(1)}, bf16[64,4096]{1,0:T(8,128)(2,1)S(1)}, u32[]{:S(2)}, u32[]{:S(2)}) collective-permute-start(bf16[64,4096]{1,0:T(8,128)(2,1)S(1)} %fusion.6), channel_id=1, source_target_pairs={{0,12},{4,8},{8,4},{12,0},{64,68},{68,64},{72,76},{76,72},{1,13},{... | collective-permute-start | bytes 1572872 | tf_op jit(solution)/shard_map/ppermute | solution.py:825
  (82 other events, 667.4 us)
Sparse Core Ops, SparseCore 0:
  12.1 120.5 all-gather.5
  308.0 64.4 all-gather.3
